TPU v7x, 32 devices: a whole 2x2x4 slice. The times are simulated.
32 devices in a mesh: dp: 4 (over y, core), fsdp: 8 (over z, x).
Axes of the slice: x: 2, y: 2, z: 4, core: 2. Of those that a mesh axis runs over, the one named last changes fastest.
Arguments:
- latent: bfloat16 [182272, 256], P(('dp', 'fsdp')), may hold values from -6 to 6
- actions: int32 [182272], P(('dp', 'fsdp')), may hold values from 0 to 3
- value_bins: int32 [182272], P(('dp', 'fsdp')), may hold values from 0 to 600
- chance_codes: int32 [182272], P(('dp', 'fsdp')), may hold values from 0 to 31
- step_mask: int32 [182272], P(('dp', 'fsdp')), may hold values 0 or 1
- stem_weight: bfloat16 [256, 256], P('fsdp'), may hold values from -0.375 to 0.375
- action_table: bfloat16 [4, 256], P(None, 'fsdp'), may hold values from -6 to 6
- stem_bias: bfloat16 [256], P('fsdp'), may hold values from -4 to 4
- stem_gain: bfloat16 [256], P('fsdp'), may hold values from 0.099609375 to 1.8984375
- stem_shift: bfloat16 [256], P('fsdp'), may hold values from -3 to 3
- block_weight: bfloat16 [10, 256, 256], P(None, 'fsdp'), may hold values from -0.375 to 0.375
- block_gain: bfloat16 [10, 256], P(None, 'fsdp'), may hold values from 0.099609375 to 1.8984375
- block_shift: bfloat16 [10, 256], P(None, 'fsdp'), may hold values from -3 to 3
- block_bias: bfloat16 [10, 256], P(None, 'fsdp'), may hold values from -3 to 3
- value_weight: bfloat16 [256, 601], P('fsdp'), may hold values from -0.375 to 0.375
- value_bias: bfloat16 [601], replicated, may hold values from -4 to 4
- chance_weight: bfloat16 [256, 32], P('fsdp'), may hold values from -0.375 to 0.375
- chance_bias: bfloat16 [32], replicated, may hold values from -4 to 4
Outputs:
- latents: bfloat16 [182272, 256], P(('dp', 'fsdp'))
- value_logits: bfloat16 [182272, 601], P(('dp', 'fsdp'))
- chance_logits: bfloat16 [182272, 32], P(('dp', 'fsdp'))
- loss: float32 [], replicated
- latent_grad: bfloat16 [182272, 256], P(('dp', 'fsdp'))
- stem_weight_grad: float32 [256, 256], P('fsdp')
- action_table_grad: float32 [4, 256], P(None, 'fsdp')
- stem_bias_grad: float32 [256], P('fsdp')
- stem_gain_grad: float32 [256], P('fsdp')
- stem_shift_grad: float32 [256], P('fsdp')
- block_weight_grad: float32 [10, 256, 256], P(None, 'fsdp')
- block_gain_grad: float32 [10, 256], P(None, 'fsdp')
- block_shift_grad: float32 [10, 256], P(None, 'fsdp')
- block_bias_grad: float32 [10, 256], P(None, 'fsdp')
- value_weight_grad: float32 [256, 601], P('fsdp')
- value_bias_grad: float32 [601], replicated
- chance_weight_grad: float32 [256, 32], P('fsdp')
- chance_bias_grad: float32 [32], replicated
All inputs are finite; a program needn't handle non-finite values. No bound on the sum of `step_mask` on one device may be relied on, other than what follows from the above.
Results may differ from a plain program's by a relative error of at most 0.009.
Values may be sent and summed in bfloat16 or wider, within the bound.
No kernel may reach another device: no remote copies, remote signals or barrier semaphores. Data moves between devices by JAX's collectives and lax.ppermute only.
A program may use at most 192 MiB of HBM per device.

v0:
```python
import jax
import jax.numpy as jnp
from jax import lax
from jax.sharding import PartitionSpec as P


def norm_act(values, gain, shift):
    center = values - jnp.mean(values, axis=-1, keepdims=True)
    spread = jnp.mean(center * center, axis=-1, keepdims=True)
    return jax.nn.gelu(center * lax.rsqrt(spread + 1e-05) * gain + shift, approximate=True)


def left_product(left, right):
    return lax.dot_general(
        left, right, (((0,), (0,)), ((), ())), preferred_element_type=jnp.float32
    )


def right_product(left, right):
    return lax.dot_general(
        left, right, (((1,), (1,)), ((), ())), preferred_element_type=jnp.float32
    )


def cross_rows(logits, target):
    row_max = jnp.max(logits, axis=-1, keepdims=True)
    shifted = logits - row_max
    expon = jnp.exp(shifted)
    row_total = jnp.sum(expon, axis=-1, keepdims=True)
    target_hot = (target[:, None] == jnp.arange(logits.shape[1], dtype=jnp.int32)[None, :]).astype(
        jnp.float32
    )
    loss_rows = jnp.log(row_total[:, 0]) - jnp.sum(shifted * target_hot, axis=-1)
    return (loss_rows, expon / row_total - target_hot)


def per_device(
    latent,
    actions,
    value_bins,
    chance_codes,
    step_mask,
    stem_weight,
    action_table,
    stem_bias,
    stem_gain,
    stem_shift,
    block_weight,
    block_gain,
    block_shift,
    block_bias,
    value_weight,
    value_bias,
    chance_weight,
    chance_bias,
):
    outer = (
        lax.all_gather(stem_weight, "fsdp", axis=0, tiled=True),
        lax.all_gather(action_table, "fsdp", axis=1, tiled=True),
        lax.all_gather(stem_bias, "fsdp", axis=0, tiled=True),
        lax.all_gather(stem_gain, "fsdp", axis=0, tiled=True),
        lax.all_gather(stem_shift, "fsdp", axis=0, tiled=True),
        lax.all_gather(value_weight, "fsdp", axis=0, tiled=True),
        lax.all_gather(chance_weight, "fsdp", axis=0, tiled=True),
    )
    w_stem, w_action, b_stem, g_stem, s_stem, w_value, w_chance = outer
    moves = w_action.shape[0]
    onehot = (actions[:, None] == jnp.arange(moves, dtype=jnp.int32)[None, :]).astype(jnp.bfloat16)
    pre = (
        jnp.dot(latent, w_stem, preferred_element_type=jnp.float32)
        + jnp.dot(onehot, w_action, preferred_element_type=jnp.float32)
        + b_stem.astype(jnp.float32)
    )
    stream, stem_back = jax.vjp(
        norm_act, pre, g_stem.astype(jnp.float32), s_stem.astype(jnp.float32)
    )
    stacked = (block_weight, block_gain, block_shift, block_bias)

    def fetch_forward(params_block):
        return (
            lax.all_gather(params_block[0], "fsdp", axis=0, tiled=True),
            lax.all_gather(params_block[1], "fsdp", axis=0, tiled=True),
            lax.all_gather(params_block[2], "fsdp", axis=0, tiled=True),
            lax.all_gather(params_block[3], "fsdp", axis=0, tiled=True),
        )

    def fetch_backward(params_block):
        return (
            lax.all_gather(params_block[0], "fsdp", axis=0, tiled=True),
            lax.all_gather(params_block[1], "fsdp", axis=0, tiled=True),
            lax.all_gather(params_block[2], "fsdp", axis=0, tiled=True),
            lax.all_gather(params_block[3], "fsdp", axis=0, tiled=True),
        )

    def forward_step(current, params_block):
        w_block, g_block, s_block, b_block = fetch_forward(params_block)
        activated = norm_act(
            current, g_block.astype(jnp.float32), s_block.astype(jnp.float32)
        ).astype(jnp.bfloat16)
        updated = (
            current
            + jnp.dot(activated, w_block, preferred_element_type=jnp.float32)
            + b_block.astype(jnp.float32)
        )
        return (updated, current)

    final, inputs = lax.scan(forward_step, stream, tuple(stacked))
    rounded = final.astype(jnp.bfloat16)
    value_full = jnp.dot(rounded, w_value, preferred_element_type=jnp.float32) + value_bias.astype(
        jnp.float32
    )
    chance_full = jnp.dot(
        rounded, w_chance, preferred_element_type=jnp.float32
    ) + chance_bias.astype(jnp.float32)
    weight_rows = step_mask.astype(jnp.float32)
    loss_value, grad_value = cross_rows(value_full, value_bins)
    loss_chance, grad_chance = cross_rows(chance_full, chance_codes)
    loss_part = jnp.sum(weight_rows * (loss_value + loss_chance))
    grad_value = grad_value * weight_rows[:, None]
    grad_chance = grad_chance * weight_rows[:, None]
    loss_total, value_bias_sum, chance_bias_sum = lax.psum(
        (loss_part, jnp.sum(grad_value, axis=0), jnp.sum(grad_chance, axis=0)), ("dp", "fsdp")
    )
    grad_scale = 1.0 / (latent.shape[0] * lax.axis_size("dp") * lax.axis_size("fsdp"))
    value_low = grad_value.astype(jnp.bfloat16)
    chance_low = grad_chance.astype(jnp.bfloat16)
    head_value_grad = left_product(rounded, value_low)
    head_chance_grad = left_product(rounded, chance_low)
    d_stream = right_product(value_low, w_value) + right_product(chance_low, w_chance)

    def backward_step(d_current, saved):
        current = saved[0]
        w_block, g_block, s_block, b_block = fetch_backward(saved[1:])
        activated, act_back = jax.vjp(
            norm_act, current, g_block.astype(jnp.float32), s_block.astype(jnp.float32)
        )
        d_low = d_current.astype(jnp.bfloat16)
        d_weight = left_product(activated.astype(jnp.bfloat16), d_low)
        d_bias = jnp.sum(d_current, axis=0)
        d_activated = right_product(d_low, w_block)
        d_input, d_gain, d_shift = act_back(d_activated)
        grads_block = (d_weight, d_gain, d_shift, d_bias)
        grads_block = (
            lax.psum_scatter(
                grads_block[0].astype(jnp.bfloat16), "fsdp", scatter_dimension=0, tiled=True
            ).astype(jnp.float32),
            lax.psum_scatter(
                grads_block[1].astype(jnp.bfloat16), "fsdp", scatter_dimension=0, tiled=True
            ).astype(jnp.float32),
            lax.psum_scatter(
                grads_block[2].astype(jnp.bfloat16), "fsdp", scatter_dimension=0, tiled=True
            ).astype(jnp.float32),
            lax.psum_scatter(
                grads_block[3].astype(jnp.bfloat16), "fsdp", scatter_dimension=0, tiled=True
            ).astype(jnp.float32),
        )
        return (d_current + d_input, tuple(grads_block))

    d_stream, block_sums = lax.scan(
        backward_step, d_stream, (inputs,) + tuple(stacked), reverse=True
    )
    d_pre, d_gain_stem, d_shift_stem = stem_back(d_stream)
    d_pre_low = d_pre.astype(jnp.bfloat16)
    d_stem_weight = left_product(latent, d_pre_low)
    d_action = left_product(onehot, d_pre_low)
    latent_grad = right_product(d_pre_low, w_stem).astype(jnp.bfloat16)
    outer_sums = (
        lax.psum_scatter(d_stem_weight, "fsdp", scatter_dimension=0, tiled=True),
        lax.psum_scatter(d_action, "fsdp", scatter_dimension=1, tiled=True),
        lax.psum_scatter(jnp.sum(d_pre, axis=0), "fsdp", scatter_dimension=0, tiled=True),
        lax.psum_scatter(d_gain_stem, "fsdp", scatter_dimension=0, tiled=True),
        lax.psum_scatter(d_shift_stem, "fsdp", scatter_dimension=0, tiled=True),
        lax.psum_scatter(head_value_grad, "fsdp", scatter_dimension=0, tiled=True),
        lax.psum_scatter(head_chance_grad, "fsdp", scatter_dimension=0, tiled=True),
    )
    summed = lax.psum(tuple(outer_sums) + tuple(block_sums), "dp")
    scaled = tuple((item * grad_scale for item in summed))
    latents = final.astype(jnp.bfloat16)
    return (
        latents,
        value_full.astype(jnp.bfloat16),
        chance_full.astype(jnp.bfloat16),
        loss_total * grad_scale,
        latent_grad,
        scaled[0],
        scaled[1],
        scaled[2],
        scaled[3],
        scaled[4],
        scaled[7],
        scaled[8],
        scaled[9],
        scaled[10],
        scaled[5],
        value_bias_sum * grad_scale,
        scaled[6],
        chance_bias_sum * grad_scale,
    )


def solution(mesh):
    placed = (
        P(("dp", "fsdp"), None),
        P(("dp", "fsdp")),
        P(("dp", "fsdp")),
        P(("dp", "fsdp")),
        P(("dp", "fsdp")),
        P("fsdp", None),
        P(None, "fsdp"),
        P("fsdp"),
        P("fsdp"),
        P("fsdp"),
        P(None, "fsdp", None),
        P(None, "fsdp"),
        P(None, "fsdp"),
        P(None, "fsdp"),
        P("fsdp", None),
        P(),
        P("fsdp", None),
        P(),
    )
    return jax.shard_map(
        per_device,
        mesh=mesh,
        in_specs=placed,
        out_specs=(
            P(("dp", "fsdp"), None),
            P(("dp", "fsdp"), None),
            P(("dp", "fsdp"), None),
            P(),
            P(("dp", "fsdp"), None),
            P("fsdp", None),
            P(None, "fsdp"),
            P("fsdp"),
            P("fsdp"),
            P("fsdp"),
            P(None, "fsdp", None),
            P(None, "fsdp"),
            P(None, "fsdp"),
            P(None, "fsdp"),
            P("fsdp", None),
            P(),
            P("fsdp", None),
            P(),
        ),
        check_vma=False,
    )
```

profile of v0, /device:TPU:0, one launch (start us, length us, event | category | flops | bytes accessed | tf_op | source)
XLA Modules:
  0.0 2319.5 jit_solution(11059191878110190017)
XLA Ops:
  12.7 23.1 all-reduce.21
  35.8 30.7 %all_gather.60 = bf16[256,256]{1,0:T(8,128)(2,1)S(1)} all-gather(bf16[32,256]{1,0:T(8,128)(2,1)} %param.27), channel_id=1, replica_groups=mesh['dp'=4,'fsdp'=8] {'fsdp'}, dimensions={0}, use_global_device_ids=true | all-gather | bytes 147456 | tf_op jit(solution)/shard_map/all_gather | solution.py:58
  66.5 16.6 all-gather.7
  95.6 676.9 %while.34 = (s32[]{:T(128)}, f32[5696,256]{1,0:T(8,128)}, f32[10,5696,256]{2,1,0:T(8,128)}, bf16[10,32]{1,0:T(8,128)(2,1)}, bf16[10,32]{1,0:T(8,128)(2,1)}, /*in...) while((s32[]{:T(128)}, f32[5696,256]{1,0:T(8,128)}, ...), condition=%wide.region_5.6_spmd, body=%wide.region_2.5_spmd.sunk | while | flops 774298688 | bytes 41359048 | solution.py:107
  98.9 19.0 all-reduce.25
  124.2 30.5 %all-gather.10 = bf16[1,256,256]{2,1,0:T(8,128)(2,1)S(1)} all-gather(bf16[1,32,256]{2,1,0:T(8,128)(2,1)S(1)} %constant_dynamic-slice_fusion.9), channel_id=4, replica_groups=mesh['dp'=4,'fsdp'=8] {'fsdp'}, dimensions={1}, use_global_device_ids=true | all-gather | bytes 147456 | tf_op jit(solution)/shard_map/while/body/eval_jaxpr/all_gather | solution.py:81
  167.5 17.3 all-reduce.25
  191.1 30.5 %all-gather.10 = bf16[1,256,256]{2,1,0:T(8,128)(2,1)S(1)} all-gather(bf16[1,32,256]{2,1,0:T(8,128)(2,1)S(1)} %constant_dynamic-slice_fusion.9), channel_id=4, replica_groups=mesh['dp'=4,'fsdp'=8] {'fsdp'}, dimensions={1}, use_global_device_ids=true | all-gather | bytes 147456 | tf_op jit(solution)/shard_map/while/body/eval_jaxpr/all_gather | solution.py:81
  234.4 19.0 all-reduce.25
  259.6 30.5 %all-gather.10 = bf16[1,256,256]{2,1,0:T(8,128)(2,1)S(1)} all-gather(bf16[1,32,256]{2,1,0:T(8,128)(2,1)S(1)} %constant_dynamic-slice_fusion.9), channel_id=4, replica_groups=mesh['dp'=4,'fsdp'=8] {'fsdp'}, dimensions={1}, use_global_device_ids=true | all-gather | bytes 147456 | tf_op jit(solution)/shard_map/while/body/eval_jaxpr/all_gather | solution.py:81
  302.9 17.3 all-reduce.25
  326.5 30.5 %all-gather.10 = bf16[1,256,256]{2,1,0:T(8,128)(2,1)S(1)} all-gather(bf16[1,32,256]{2,1,0:T(8,128)(2,1)S(1)} %constant_dynamic-slice_fusion.9), channel_id=4, replica_groups=mesh['dp'=4,'fsdp'=8] {'fsdp'}, dimensions={1}, use_global_device_ids=true | all-gather | bytes 147456 | tf_op jit(solution)/shard_map/while/body/eval_jaxpr/all_gather | solution.py:81
  369.7 19.0 all-reduce.25
  395.0 30.6 %all-gather.10 = bf16[1,256,256]{2,1,0:T(8,128)(2,1)S(1)} all-gather(bf16[1,32,256]{2,1,0:T(8,128)(2,1)S(1)} %constant_dynamic-slice_fusion.9), channel_id=4, replica_groups=mesh['dp'=4,'fsdp'=8] {'fsdp'}, dimensions={1}, use_global_device_ids=true | all-gather | bytes 147456 | tf_op jit(solution)/shard_map/while/body/eval_jaxpr/all_gather | solution.py:81
  438.3 17.4 all-reduce.25
  462.0 30.5 %all-gather.10 = bf16[1,256,256]{2,1,0:T(8,128)(2,1)S(1)} all-gather(bf16[1,32,256]{2,1,0:T(8,128)(2,1)S(1)} %constant_dynamic-slice_fusion.9), channel_id=4, replica_groups=mesh['dp'=4,'fsdp'=8] {'fsdp'}, dimensions={1}, use_global_device_ids=true | all-gather | bytes 147456 | tf_op jit(solution)/shard_map/while/body/eval_jaxpr/all_gather | solution.py:81
  505.2 18.9 all-reduce.25
  530.4 30.6 %all-gather.10 = bf16[1,256,256]{2,1,0:T(8,128)(2,1)S(1)} all-gather(bf16[1,32,256]{2,1,0:T(8,128)(2,1)S(1)} %constant_dynamic-slice_fusion.9), channel_id=4, replica_groups=mesh['dp'=4,'fsdp'=8] {'fsdp'}, dimensions={1}, use_global_device_ids=true | all-gather | bytes 147456 | tf_op jit(solution)/shard_map/while/body/eval_jaxpr/all_gather | solution.py:81
  573.8 17.3 all-reduce.25
  597.2 30.6 %all-gather.10 = bf16[1,256,256]{2,1,0:T(8,128)(2,1)S(1)} all-gather(bf16[1,32,256]{2,1,0:T(8,128)(2,1)S(1)} %constant_dynamic-slice_fusion.9), channel_id=4, replica_groups=mesh['dp'=4,'fsdp'=8] {'fsdp'}, dimensions={1}, use_global_device_ids=true | all-gather | bytes 147456 | tf_op jit(solution)/shard_map/while/body/eval_jaxpr/all_gather | solution.py:81
  640.5 18.9 all-reduce.25
  665.7 30.6 %all-gather.10 = bf16[1,256,256]{2,1,0:T(8,128)(2,1)S(1)} all-gather(bf16[1,32,256]{2,1,0:T(8,128)(2,1)S(1)} %constant_dynamic-slice_fusion.9), channel_id=4, replica_groups=mesh['dp'=4,'fsdp'=8] {'fsdp'}, dimensions={1}, use_global_device_ids=true | all-gather | bytes 147456 | tf_op jit(solution)/shard_map/while/body/eval_jaxpr/all_gather | solution.py:81
  709.0 17.3 all-reduce.25
  732.5 30.5 %all-gather.10 = bf16[1,256,256]{2,1,0:T(8,128)(2,1)S(1)} all-gather(bf16[1,32,256]{2,1,0:T(8,128)(2,1)S(1)} %constant_dynamic-slice_fusion.9), channel_id=4, replica_groups=mesh['dp'=4,'fsdp'=8] {'fsdp'}, dimensions={1}, use_global_device_ids=true | all-gather | bytes 147456 | tf_op jit(solution)/shard_map/while/body/eval_jaxpr/all_gather | solution.py:81
  775.5 30.5 %all_gather.66 = bf16[256,32]{1,0:T(8,128)(2,1)S(1)} all-gather(bf16[32,32]{1,0:T(8,128)(2,1)S(1)} %copy-done.39), channel_id=1, replica_groups=mesh['dp'=4,'fsdp'=8] {'fsdp'}, dimensions={0}, use_global_device_ids=true | all-gather | bytes 18432 | tf_op jit(solution)/shard_map/all_gather | solution.py:64
  806.1 31.0 %all_gather.65 = bf16[256,601]{1,0:T(8,128)(2,1)S(1)} all-gather(bf16[32,601]{1,0:T(8,128)(2,1)S(1)} %copy-done.35), channel_id=1, replica_groups=mesh['dp'=4,'fsdp'=8] {'fsdp'}, dimensions={0}, use_global_device_ids=true | all-gather | bytes 346176 | tf_op jit(solution)/shard_map/all_gather | solution.py:63
  860.9 1140.3 %while.35 = (s32[]{:T(128)}, f32[5696,256]{1,0:T(8,128)}, f32[10,32,256]{2,1,0:T(8,128)S(1)}, f32[10,32]{1,0:T(8,128)S(1)}, f32[10,32]{1,0:T(8,128)S(1)}, /*inde...) while((s32[]{:T(128)}, f32[5696,256]{1,0:T(8,128)}, ...), condition=%wide.region_26.27_spmd, body=%wide.region_14.26_spmd.sunk | while | flops 1588068352 | bytes 100678608 | solution.py:159
  872.5 19.0 all-reduce.26
  899.8 30.5 %all-gather.11 = bf16[1,256,256]{2,1,0:T(8,128)(2,1)S(1)} all-gather(bf16[1,32,256]{2,1,0:T(8,128)(2,1)S(1)} %constant_dynamic-slice_fusion.10), channel_id=6, replica_groups=mesh['dp'=4,'fsdp'=8] {'fsdp'}, dimensions={1}, use_global_device_ids=true | all-gather | bytes 147456 | tf_op jit(solution)/shard_map/while/body/eval_jaxpr/all_gather | solution.py:89
  947.3 17.3 all-reduce.27
  986.5 19.0 all-reduce.26
  1013.8 30.6 %all-gather.11 = bf16[1,256,256]{2,1,0:T(8,128)(2,1)S(1)} all-gather(bf16[1,32,256]{2,1,0:T(8,128)(2,1)S(1)} %constant_dynamic-slice_fusion.10), channel_id=6, replica_groups=mesh['dp'=4,'fsdp'=8] {'fsdp'}, dimensions={1}, use_global_device_ids=true | all-gather | bytes 147456 | tf_op jit(solution)/shard_map/while/body/eval_jaxpr/all_gather | solution.py:89
  1061.3 17.3 all-reduce.27
  1100.5 19.0 all-reduce.26
  1127.8 30.6 %all-gather.11 = bf16[1,256,256]{2,1,0:T(8,128)(2,1)S(1)} all-gather(bf16[1,32,256]{2,1,0:T(8,128)(2,1)S(1)} %constant_dynamic-slice_fusion.10), channel_id=6, replica_groups=mesh['dp'=4,'fsdp'=8] {'fsdp'}, dimensions={1}, use_global_device_ids=true | all-gather | bytes 147456 | tf_op jit(solution)/shard_map/while/body/eval_jaxpr/all_gather | solution.py:89
  1175.4 17.3 all-reduce.27
  1214.4 19.1 all-reduce.26
  1241.9 30.5 %all-gather.11 = bf16[1,256,256]{2,1,0:T(8,128)(2,1)S(1)} all-gather(bf16[1,32,256]{2,1,0:T(8,128)(2,1)S(1)} %constant_dynamic-slice_fusion.10), channel_id=6, replica_groups=mesh['dp'=4,'fsdp'=8] {'fsdp'}, dimensions={1}, use_global_device_ids=true | all-gather | bytes 147456 | tf_op jit(solution)/shard_map/while/body/eval_jaxpr/all_gather | solution.py:89
  1289.4 17.2 all-reduce.27
  1328.4 19.0 all-reduce.26
  1355.9 30.6 %all-gather.11 = bf16[1,256,256]{2,1,0:T(8,128)(2,1)S(1)} all-gather(bf16[1,32,256]{2,1,0:T(8,128)(2,1)S(1)} %constant_dynamic-slice_fusion.10), channel_id=6, replica_groups=mesh['dp'=4,'fsdp'=8] {'fsdp'}, dimensions={1}, use_global_device_ids=true | all-gather | bytes 147456 | tf_op jit(solution)/shard_map/while/body/eval_jaxpr/all_gather | solution.py:89
  1403.4 17.2 all-reduce.27
  1442.4 19.1 all-reduce.26
  1469.9 30.5 %all-gather.11 = bf16[1,256,256]{2,1,0:T(8,128)(2,1)S(1)} all-gather(bf16[1,32,256]{2,1,0:T(8,128)(2,1)S(1)} %constant_dynamic-slice_fusion.10), channel_id=6, replica_groups=mesh['dp'=4,'fsdp'=8] {'fsdp'}, dimensions={1}, use_global_device_ids=true | all-gather | bytes 147456 | tf_op jit(solution)/shard_map/while/body/eval_jaxpr/all_gather | solution.py:89
  1517.4 17.3 all-reduce.27
  1556.4 19.0 all-reduce.26
  1583.9 30.6 %all-gather.11 = bf16[1,256,256]{2,1,0:T(8,128)(2,1)S(1)} all-gather(bf16[1,32,256]{2,1,0:T(8,128)(2,1)S(1)} %constant_dynamic-slice_fusion.10), channel_id=6, replica_groups=mesh['dp'=4,'fsdp'=8] {'fsdp'}, dimensions={1}, use_global_device_ids=true | all-gather | bytes 147456 | tf_op jit(solution)/shard_map/while/body/eval_jaxpr/all_gather | solution.py:89
  1631.4 17.2 all-reduce.27
  1670.4 19.0 all-reduce.26
  1697.8 30.6 %all-gather.11 = bf16[1,256,256]{2,1,0:T(8,128)(2,1)S(1)} all-gather(bf16[1,32,256]{2,1,0:T(8,128)(2,1)S(1)} %constant_dynamic-slice_fusion.10), channel_id=6, replica_groups=mesh['dp'=4,'fsdp'=8] {'fsdp'}, dimensions={1}, use_global_device_ids=true | all-gather | bytes 147456 | tf_op jit(solution)/shard_map/while/body/eval_jaxpr/all_gather | solution.py:89
  1745.4 17.2 all-reduce.27
  1784.4 19.1 all-reduce.26
  1811.9 30.6 %all-gather.11 = bf16[1,256,256]{2,1,0:T(8,128)(2,1)S(1)} all-gather(bf16[1,32,256]{2,1,0:T(8,128)(2,1)S(1)} %constant_dynamic-slice_fusion.10), channel_id=6, replica_groups=mesh['dp'=4,'fsdp'=8] {'fsdp'}, dimensions={1}, use_global_device_ids=true | all-gather | bytes 147456 | tf_op jit(solution)/shard_map/while/body/eval_jaxpr/all_gather | solution.py:89
  1859.4 17.2 all-reduce.27
  1898.4 19.1 all-reduce.26
  1925.9 30.6 %all-gather.11 = bf16[1,256,256]{2,1,0:T(8,128)(2,1)S(1)} all-gather(bf16[1,32,256]{2,1,0:T(8,128)(2,1)S(1)} %constant_dynamic-slice_fusion.10), channel_id=6, replica_groups=mesh['dp'=4,'fsdp'=8] {'fsdp'}, dimensions={1}, use_global_device_ids=true | all-gather | bytes 147456 | tf_op jit(solution)/shard_map/while/body/eval_jaxpr/all_gather | solution.py:89
  1973.4 17.2 all-reduce.27
  2042.5 19.1 all-reduce.18
  2062.5 37.2 %all-reduce.17 = (f32[]{:T(128)}, f32[601]{0:T(1024)S(1)}, f32[32]{0:T(128)S(1)}) all-reduce(f32[]{:T(128)} %multiply_reduce_fusion.7, f32[601]{0:T(1024)S(1)} %copy-done.36, f32[32]{0:T(128)S(1)} %get-tuple-element.434), channel_id=1, replica_groups=mesh['dp'=4,'fsdp'=8] {'dp','fsdp'}, use_global_device_ids=true, to_apply=%region_13.14 | all-reduce | flops 634 | bytes 5072 | tf_op jit(solution)/shard_map/psum | solution.py:121
  2102.2 42.5 %reduce-scatter.14.cloned.1.call-done = f32[32,256]{1,0:T(8,128)} async-done(((f32[256,256]{1,0:T(8,128)}), f32[32,256]{1,0:T(8,128)}) %reduce-scatter.14.cloned.1.call-update) | async-done | bytes 32784
  2145.5 62.3 %reduce-scatter.12.cloned.1.call-done = f32[32,32]{1,0:T(8,128)} async-done(((f32[256,32]{1,0:T(8,128)}), f32[32,32]{1,0:T(8,128)}) %reduce-scatter.12.cloned.1.call-update) | async-done | bytes 4112 | tf_op jit(solution)/shard_map/reduce_scatter | solution.py:174
  2207.8 12.6 all-reduce.19
  2224.1 48.4 %reduce-scatter.10.cloned.1.call-done = f32[32,601]{1,0:T(8,128)} async-done(((f32[256,601]{1,0:T(8,128)}), f32[32,601]{1,0:T(8,128)}) %reduce-scatter.10.cloned.1.call-update) | async-done | bytes 76944 | tf_op jit(solution)/shard_map/reduce_scatter | solution.py:173
  2273.0 34.1 %all-reduce.30.cloned.1.call-done = (f32[10,32,256]{2,1,0:T(8,128)}, f32[32,601]{1,0:T(8,128)}) async-done(((f32[10,32,256]{2,1,0:T(8,128)}, f32[32,601]{1,0:T(8,128)}), (f32[10,32,256]{2,1,0:T(8,128)}, f32[32,601]{1,0:T(8,128)})) %all-reduce.30.cloned.1.call-update) | async-done | bytes 404624 | tf_op jit(solution)/shard_map/psum | solution.py:176
  (661 shorter events, 735.5 us)
Async XLA Ops:
  8.0 75.2 %copy-start = (bf16[5696,256]{1,0:T(8,128)(2,1)S(1)}, bf16[5696,256]{1,0:T(8,128)(2,1)}, u32[]{:S(2)}) copy-start(bf16[5696,256]{1,0:T(8,128)(2,1)} %param.22) | copy-start | bytes 8749060
  66.5 17.6 copy-start.10
  85.8 9.7 copy-start.2
  85.8 9.7 copy-start.12
  89.3 6.2 copy-start.22
  89.3 6.2 copy-start.18
  89.4 6.2 copy-start.37
  89.4 6.2 copy-start.40
  89.4 6.2 copy-start.34
  772.5 3.0 copy-start.39
  772.5 33.5 %copy-start.43 = (bf16[32]{0:T(256)(128)(2,1)S(1)}, bf16[32]{0:T(256)(128)(2,1)}, u32[]{:S(2)}) copy-start(bf16[32]{0:T(256)(128)(2,1)} %param.39) | copy-start | bytes 196
  772.5 33.5 %copy-start.31 = (s32[5696]{0:T(1024)S(1)}, s32[5696]{0:T(1024)}, u32[]{:S(2)}) copy-start(s32[5696]{0:T(1024)} %param.26) | copy-start | bytes 68356
  772.5 33.6 %copy-start.42 = (bf16[601]{0:T(1024)(128)(2,1)S(1)}, bf16[601]{0:T(1024)(128)(2,1)}, u32[]{:S(2)}) copy-start(bf16[601]{0:T(1024)(128)(2,1)} %param.37) | copy-start | bytes 3610
  772.5 33.6 %copy-start.35 = (bf16[32,601]{1,0:T(8,128)(2,1)S(1)}, bf16[32,601]{1,0:T(8,128)(2,1)}, u32[]{:S(2)}) copy-start(bf16[32,601]{1,0:T(8,128)(2,1)} %param.36) | copy-start | bytes 115396
  775.5 79.9 %copy-start.6 = (bf16[5696,256]{1,0:T(8,128)(2,1)}, bf16[5696,256]{1,0:T(8,128)(2,1)S(1)}, u32[]{:S(2)}) copy-start(bf16[5696,256]{1,0:T(8,128)(2,1)S(1)} %convert_element_type.162) | copy-start | bytes 8749060
  806.0 50.8 %copy-start.20 = (f32[5696]{0:T(1024)}, f32[5696]{0:T(1024)S(1)}, u32[]{:S(2)}) copy-start(f32[5696]{0:T(1024)S(1)} %convert_element_type.167) | copy-start | bytes 68356
  844.5 8.3 copy-start.24
  852.7 4.1 copy-start.29
  856.7 4.1 copy-start.7
  856.7 4.1 copy-start.14
  856.9 4.0 copy-start.16
  860.9 1140.3 %copy-start.13 = (f32[5696]{0:T(1024)S(1)}, f32[5696]{0:T(1024)}, u32[]{:S(2)}) copy-start(f32[5696]{0:T(1024)} %copy-done.12) | copy-start | bytes 68356
  860.9 1140.3 %copy-start.19 = (f32[5696]{0:T(1024)S(1)}, f32[5696]{0:T(1024)}, u32[]{:S(2)}) copy-start(f32[5696]{0:T(1024)} %copy-done.18) | copy-start | bytes 68356
  860.9 1140.3 %copy-start.38 = (f32[256]{0:T(256)S(1)}, f32[256]{0:T(256)}, u32[]{:S(2)}) copy-start(f32[256]{0:T(256)} %copy-done.37) | copy-start | bytes 3076
  860.9 1140.3 %copy-start.41 = (f32[256]{0:T(256)S(1)}, f32[256]{0:T(256)}, u32[]{:S(2)}) copy-start(f32[256]{0:T(256)} %copy-done.40) | copy-start | bytes 3076
  861.1 113.3 %reduce-scatter.18.cloned.1.call-start = ((), (), s32[]{:S(2)}) async-start(), calls=%async_computation.10 | async-start | bytes 147456 | tf_op jit(solution)/shard_map/while/body/eval_jaxpr/reduce_scatter | solution.py:144
  939.0 7.7 copy-start.1
  975.2 113.3 %reduce-scatter.18.cloned.1.call-start = ((), (), s32[]{:S(2)}) async-start(), calls=%async_computation.10 | async-start | bytes 147456 | tf_op jit(solution)/shard_map/while/body/eval_jaxpr/reduce_scatter | solution.py:144
  1053.0 7.7 copy-start.1
  1089.2 113.3 %reduce-scatter.18.cloned.1.call-start = ((), (), s32[]{:S(2)}) async-start(), calls=%async_computation.10 | async-start | bytes 147456 | tf_op jit(solution)/shard_map/while/body/eval_jaxpr/reduce_scatter | solution.py:144
  1167.0 7.7 copy-start.1
  1203.2 113.3 %reduce-scatter.18.cloned.1.call-start = ((), (), s32[]{:S(2)}) async-start(), calls=%async_computation.10 | async-start | bytes 147456 | tf_op jit(solution)/shard_map/while/body/eval_jaxpr/reduce_scatter | solution.py:144
  1281.0 7.7 copy-start.1
  1317.2 113.3 %reduce-scatter.18.cloned.1.call-start = ((), (), s32[]{:S(2)}) async-start(), calls=%async_computation.10 | async-start | bytes 147456 | tf_op jit(solution)/shard_map/while/body/eval_jaxpr/reduce_scatter | solution.py:144
  1395.1 7.7 copy-start.1
  1431.2 113.3 %reduce-scatter.18.cloned.1.call-start = ((), (), s32[]{:S(2)}) async-start(), calls=%async_computation.10 | async-start | bytes 147456 | tf_op jit(solution)/shard_map/while/body/eval_jaxpr/reduce_scatter | solution.py:144
  1509.0 7.7 copy-start.1
  1545.2 113.3 %reduce-scatter.18.cloned.1.call-start = ((), (), s32[]{:S(2)}) async-start(), calls=%async_computation.10 | async-start | bytes 147456 | tf_op jit(solution)/shard_map/while/body/eval_jaxpr/reduce_scatter | solution.py:144
  1623.0 7.7 copy-start.1
  1659.2 113.2 %reduce-scatter.18.cloned.1.call-start = ((), (), s32[]{:S(2)}) async-start(), calls=%async_computation.10 | async-start | bytes 147456 | tf_op jit(solution)/shard_map/while/body/eval_jaxpr/reduce_scatter | solution.py:144
  1737.0 7.7 copy-start.1
  1773.2 113.3 %reduce-scatter.18.cloned.1.call-start = ((), (), s32[]{:S(2)}) async-start(), calls=%async_computation.10 | async-start | bytes 147456 | tf_op jit(solution)/shard_map/while/body/eval_jaxpr/reduce_scatter | solution.py:144
  1851.0 7.7 copy-start.1
  1887.2 113.3 %reduce-scatter.18.cloned.1.call-start = ((), (), s32[]{:S(2)}) async-start(), calls=%async_computation.10 | async-start | bytes 147456 | tf_op jit(solution)/shard_map/while/body/eval_jaxpr/reduce_scatter | solution.py:144
  1965.0 7.7 copy-start.1
  2001.2 9.6 copy-start.9
  2001.2 100.2 %reduce-scatter.16.cloned.1.call-start = ((), (), s32[]{:S(2)}) async-start(), calls=%async_computation.8 | async-start | bytes 147456
  2001.2 9.6 copy-start.23
  2001.2 9.6 copy-start.3
  2015.3 4.1 copy-start.27
  2017.8 7.3 copy-start.15
  2017.8 7.3 copy-start.17
  2017.8 7.3 copy-start.21
  2017.8 7.3 copy-start.30
  2021.3 123.3 %reduce-scatter.14.cloned.1.call-start = ((), (), s32[]{:S(2)}) async-start(), calls=%async_computation.7 | async-start | bytes 294912
  2025.1 182.8 %reduce-scatter.12.cloned.1.call-start = ((), (), s32[]{:S(2)}) async-start(), calls=%async_computation.6 | async-start | bytes 147456 | tf_op jit(solution)/shard_map/reduce_scatter | solution.py:174
  2028.8 7.4 copy-start.11
  2028.8 243.7 %reduce-scatter.10.cloned.1.call-start = ((), (), s32[]{:S(2)}) async-start(), calls=%async_computation.5 | async-start | bytes 737280 | tf_op jit(solution)/shard_map/reduce_scatter | solution.py:173
  2036.1 25.7 %copy-start.25 = (f32[5696]{0:T(1024)S(1)}, f32[5696]{0:T(1024)}, u32[]{:S(2)}) copy-start(f32[5696]{0:T(1024)} %copy-done.24) | copy-start | bytes 68356
  2036.1 25.7 %copy-start.28 = (f32[5696]{0:T(1024)S(1)}, f32[5696]{0:T(1024)}, u32[]{:S(2)}) copy-start(f32[5696]{0:T(1024)} %get-tuple-element.430) | copy-start | bytes 68356
  2036.1 25.7 %copy-start.32 = (s32[5696]{0:T(1024)S(1)}, s32[5696]{0:T(1024)}, u32[]{:S(2)}) copy-start(s32[5696]{0:T(1024)} %param.26) | copy-start | bytes 68356
  2036.1 26.3 %copy-start.36 = (f32[601]{0:T(1024)S(1)}, f32[601]{0:T(1024)}, u32[]{:S(2)}) copy-start(f32[601]{0:T(1024)} %get-tuple-element.507) | copy-start | bytes 7216
  2036.2 271.0 %all-reduce.30.cloned.1.call-start = ((), (), s32[]{:S(2)}) async-start(), calls=%async_computation.9 | async-start | bytes 819200 | tf_op jit(solution)/shard_map/psum | solution.py:176
  2036.2 4.4 copy-start.8
  (4 other events, 7.6 us)
Sparse Core Ops, SparseCore 0:
  899.2 58.1 reduce-scatter.17
  1013.2 58.0 reduce-scatter.17
  1127.2 58.1 reduce-scatter.17
  1241.3 58.0 reduce-scatter.17
  1355.3 58.1 reduce-scatter.17
  1469.3 58.0 reduce-scatter.17
  1583.2 58.1 reduce-scatter.17
  1697.2 58.1 reduce-scatter.17
  1811.3 58.1 reduce-scatter.17
  1925.3 58.1 reduce-scatter.17
Sparse Core Ops, SparseCore 1:
  2021.4 59.6 reduce-scatter.15
  2084.3 60.3 reduce-scatter.13
  2147.8 59.9 reduce-scatter.11
  2211.1 61.3 reduce-scatter.9
  2275.6 31.4 all-reduce.29
where the time goes:
time: 2330 us; the launch traced here: 2320 us
  blocking collectives  1360 us (58%)
  other arithmetic  356 us (15%)
  matrix products  254 us (11%)
  waiting for transfers between devices  188 us (8%)
  local copies, waits for them, and re-layouts  124 us (5%)
    while x30, blocking collectives  544 us
    all_gather x10, blocking collectives, fetch_backward(): lax.all_gather(params_block[0], 'fsdp', axis=0, tiled=True)  305 us
    all_gather x10, blocking collectives, fetch_forward(): lax.all_gather(params_block[0], 'fsdp', axis=0, tiled=True)  305 us
    dot_general x13, matrix products, right_product(): lax.dot_general(left, right, (((1,), (1,)), ((), ())), preferred_element_...  97.1 us
    reduce_sum x10, other arithmetic, backward_step(): d_bias = jnp.sum(d_current, axis=0)  95.4 us
    reduce_sum x21, other arithmetic, norm_act(): spread = jnp.mean(center * center, axis=-1, keepdims=True)  90.5 us
    dot_general x13, matrix products, left_product(): lax.dot_general(left, right, (((0,), (0,)), ((), ())), preferred_element_...  89.8 us
    reduce_sum x11, other arithmetic, norm_act(): center * lax.rsqrt(spread + 1e-05) * gain + shift  85.8 us
  transfers between devices with their start and end apart: 15, of which 4 were waited for; matrix products, arithmetic and copies ran while one was open for 13% of the time, Pallas kernels for 0%

commit v1 on v0

v1 whole, which is shorter than its diff:
```python
import functools
import jax
import jax.numpy as jnp
from jax import lax
from jax.experimental import pallas as pl
from jax.experimental.pallas import tpu as pltpu
from jax.sharding import PartitionSpec as P

F32 = jnp.float32
BF16 = jnp.bfloat16
WIDTH = 256
UNIT = 16
TILE = 1440
HEAD_CHUNK = 240
SPLIT = 3
K0 = 2 * 0.7978845608028654
K1 = 8 * 0.7978845608028654 * 0.044715


def mm(a, b):
    return lax.dot_general(a, b, (((1,), (0,)), ((), ())), preferred_element_type=F32)


def mm_nt(a, b):
    return lax.dot_general(a, b, (((1,), (1,)), ((), ())), preferred_element_type=F32)


def mm_tn(a, b):
    return lax.dot_general(a, b, (((0,), (0,)), ((), ())), preferred_element_type=F32)


def norm_gelu(s, gain8, gain_slope, shift_half):
    mean = jnp.sum(s, axis=1, keepdims=True) * (1.0 / WIDTH)
    center = s - mean
    r = lax.rsqrt(jnp.sum(center * center, axis=1, keepdims=True) + WIDTH * 1e-5)
    n = center * r
    h = n * gain8 + shift_half
    y = h * h
    t = jnp.tanh(h * (K0 + K1 * y))
    e1 = 1.0 + t
    bend = (h * (y + K0 / (3 * K1))) * (1.0 - t)
    slope = (e1 * gain_slope) * (1.0 / (3 * K1) + bend)
    return h * e1, n.astype(BF16), slope.astype(BF16), jnp.broadcast_to(r, (UNIT, 128))


def scales(vec_ref, at, layers):
    gain = vec_ref[pl.ds(at, 1), :]
    return gain * 8.0, gain * (8.0 * 3 * K1), vec_ref[pl.ds(at + layers, 1), :] * 0.5


def norm_back(da, slope, n, r):
    w = da * slope.astype(F32)
    m1 = jnp.sum(w, axis=1, keepdims=True) * (1.0 / WIDTH)
    w16 = w.astype(BF16)
    wn = w16 * n
    wide = (wn[:, 0:128] + wn[:, 128:256]).astype(F32)
    m2 = jnp.sum(wide, axis=1, keepdims=True)
    m1 = jnp.broadcast_to(m1, (UNIT, 128)).astype(BF16)
    m2 = jnp.broadcast_to(m2, (UNIT, 128)).astype(BF16)
    halves = [
        (w[:, k:k + 128] - (m1 + n[:, k:k + 128] * m2).astype(F32)) * r for k in (0, 128)
    ]
    return jnp.concatenate(halves, axis=1), w, wn


def forward_chunk(base, size, s_ref, save, i, scale, w, bias):
    act_ref, n_ref, slope_ref, r_ref = save
    for u in range(0, size, UNIT):
        rows = pl.ds(base + u, UNIT)
        act, n, slope, r = norm_gelu(s_ref[rows, :], *scale)
        act_ref[i, rows, :] = act.astype(BF16)
        n_ref[i, rows, :] = n
        slope_ref[i, rows, :] = slope
        r_ref[i, rows, :] = r
    out = mm(act_ref[i, pl.ds(base, size), :], w)
    for u in range(0, size, UNIT):
        rows = pl.ds(base + u, UNIT)
        s_ref[rows, :] = s_ref[rows, :] + (out[u:u + UNIT, :] + bias)


def forward_layers(chunk_rows, first, last, layers, s_ref, save, vec_ref, w_ref, w_at, save_at):
    def layer(i, carry):
        scale = scales(vec_ref, 7 + i, layers)
        bias = vec_ref[pl.ds(7 + 2 * layers + i, 1), :]
        def chunk(c, carry):
            base = pl.multiple_of(c * chunk_rows, UNIT)
            forward_chunk(base, chunk_rows, s_ref, save, i - save_at, scale, w_ref[i - w_at], bias)
            return carry
        return lax.fori_loop(0, TILE // chunk_rows, chunk, carry)
    lax.fori_loop(first, last, layer, 0)


def column_sums(parts):
    total = parts[0]
    for part in parts[1:]:
        total = total + part
    return total.astype(F32)


GROUP = 3


def backward_chunk(base, size, s_ref, low_ref, save, i, w, gw_ref, g_at):
    act_ref, n_ref, slope_ref, r_ref = save
    zero = jnp.zeros((UNIT, WIDTH), F32)
    shift, gain, bias = zero, zero, zero
    low = low_ref[pl.ds(base, size), :]
    da = mm_nt(low, w)
    gw_ref[g_at] += mm_tn(act_ref[i, pl.ds(base, size), :], low)
    held = []
    for u in range(0, size, UNIT):
        rows = pl.ds(base + u, UNIT)
        d_in, wf, wn = norm_back(da[u:u + UNIT, :], slope_ref[i, rows, :], n_ref[i, rows, :], r_ref[i, rows, :])
        shift = shift + wf
        held.append(wn)
        if len(held) == GROUP:
            gain = gain + column_sums(held)
            held = []
        ds = s_ref[rows, :]
        bias = bias + ds
        ds = ds + d_in
        s_ref[rows, :] = ds
        low_ref[rows, :] = ds.astype(BF16)
    return gain, shift, bias


def fold(x):
    return jnp.sum(x, axis=0, keepdims=True)


def backward_layers(chunk_rows, first, last, layers, s_ref, low_ref, save, w_ref, w_at, save_at, gw_ref, gv_ref, g_at):
    def layer(j, carry):
        i = last - 1 - j
        def chunk(c, carry):
            base = pl.multiple_of(c * chunk_rows, UNIT)
            sums = backward_chunk(base, chunk_rows, s_ref, low_ref, save, i - save_at, w_ref[i - w_at], gw_ref, i - g_at)
            for k in range(3):
                gv_ref[pl.ds(7 + k * layers + i, 1), :] += fold(sums[k])
            return carry
        return lax.fori_loop(0, TILE // chunk_rows, chunk, carry)
    lax.fori_loop(0, last - first, layer, 0)


def cross(logits, target, mask, lane):
    top = jnp.max(logits, axis=1, keepdims=True)
    shifted = logits - top
    expon = jnp.exp(shifted)
    total = jnp.sum(expon, axis=1, keepdims=True)
    hit = lane == target
    grad = expon * (mask * (1.0 / total))
    grad = grad - jnp.where(hit, mask, 0.0)
    return jnp.log(total), jnp.where(hit, shifted, 0.0), grad


def heads_chunk(base, nq, s_ref, low_ref, col_ref, w_ref, w_at, hb_ref, latents_ref, value_ref, chance_ref, dlog_ref, loss_ref, ghb_ref):
    size = HEAD_CHUNK
    span = pl.ds(base, size)
    lane_v = lax.broadcasted_iota(jnp.int32, (1, 640), 1).astype(F32)
    lane_c = lane_v[:, 0:128]
    bias_v = hb_ref[0:1, 0:640]
    bias_c = hb_ref[0:1, 640:768]
    lat = s_ref[span, :].astype(BF16)
    latents_ref[span, :] = lat
    full = [mm(lat, w_ref[w_at + k]) for k in range(3)]
    loss = jnp.zeros((UNIT, 128), F32)
    sum_v = jnp.zeros((UNIT, 640), F32)
    sum_c = jnp.zeros((UNIT, 128), F32)
    for u in range(0, size, UNIT):
        rows = pl.ds(base + u, UNIT)
        parts = [f[u:u + UNIT, :] for f in full]
        value = jnp.concatenate([parts[0], parts[1], parts[2][:, 0:128]], axis=1) + bias_v
        chance = parts[2][:, 128:256] + bias_c
        value_ref[rows, :] = value[:, 0:nq].astype(BF16)
        chance_ref[rows, :] = chance[:, 0:chance_ref.shape[1]].astype(BF16)
        bins, codes, mask = (col_ref[k, rows, :] for k in range(3))
        wide = lambda x: jnp.concatenate([x] * 5, axis=1)
        log_v, at_v, grad_v = cross(value, wide(bins), wide(mask), lane_v)
        log_c, at_c, grad_c = cross(chance, codes, mask, lane_c)
        hits = at_c
        for k in range(5):
            hits = hits + at_v[:, k * 128:(k + 1) * 128]
        loss = loss + mask * ((log_v + log_c) * (1.0 / 128) - hits)
        sum_v = sum_v + grad_v
        sum_c = sum_c + grad_c
        dlog_ref[0, rows, :] = grad_v[:, 0:256].astype(BF16)
        dlog_ref[1, rows, :] = grad_v[:, 256:512].astype(BF16)
        dlog_ref[2, rows, 0:128] = grad_v[:, 512:640].astype(BF16)
        dlog_ref[2, rows, 128:256] = grad_c.astype(BF16)
    loss_ref[...] += loss
    ghb_ref[:, 0:640] += sum_v
    ghb_ref[:, 640:768] += sum_c
    ds = mm_nt(dlog_ref[0, span, :], w_ref[w_at])
    ds += mm_nt(dlog_ref[1, span, :], w_ref[w_at + 1])
    ds += mm_nt(dlog_ref[2, span, :], w_ref[w_at + 2])
    s_ref[span, :] = ds
    low_ref[span, :] = ds.astype(BF16)


def spread_columns(ints, col_ref):
    k = lax.broadcasted_iota(jnp.int32, (16, 384), 0)
    j = lax.broadcasted_iota(jnp.int32, (16, 384), 1) >> 7
    pick = jnp.where((j == 0) & (k == 1), 32.0, 0.0) + jnp.where(
        ((j == 0) & (k == 2)) | ((j == 1) & (k == 3)) | ((j == 2) & (k == 4)), 1.0, 0.0
    )
    cols = mm_tn(ints, pick.astype(BF16))
    for c in range(3):
        col_ref[c] = cols[0:TILE, c * 128:(c + 1) * 128]


def unpack_vec(w, vec_ref):
    vec_ref[...] = w[:, 0:128].astype(F32).T


def moves_hot(ints):
    rows = lax.broadcasted_iota(jnp.int32, ints.shape, 0).astype(F32)
    return jnp.where((rows == ints[0:1, :].astype(F32)) | (rows == 4.0), 1.0, 0.0).astype(BF16)


def table_of(vec_ref):
    rows = lax.broadcasted_iota(jnp.int32, (16, WIDTH), 0)
    return jnp.where(rows < 5, vec_ref[0:16, :], 0.0).astype(BF16)


def stem_forward(chunk_rows, latent_ref, hot_ref, vec_ref, w, s_ref, n_ref, slope_ref, r_ref, n_at):
    table = table_of(vec_ref)
    scale = scales(vec_ref, 5, 1)
    def chunk(c, carry):
        base = pl.multiple_of(c * chunk_rows, UNIT)
        span = pl.ds(base, chunk_rows)
        pre = mm(latent_ref[span, :], w) + mm(hot_ref[span, :], table)
        for u in range(0, chunk_rows, UNIT):
            rows = pl.ds(base + u, UNIT)
            act, n, slope, r = norm_gelu(pre[u:u + UNIT, :], *scale)
            s_ref[rows, :] = act
            n_ref[n_at, rows, :] = n
            slope_ref[n_at, rows, :] = slope
            r_ref[n_at, rows, :] = r
        return carry
    lax.fori_loop(0, TILE // chunk_rows, chunk, 0)


def stem_backward(chunk_rows, latent_ref, hot, s_ref, low_ref, n_ref, slope_ref, r_ref, n_at, w, lgrad_ref, gw_ref, g_at, gv_ref):
    def chunk(c, carry):
        base = pl.multiple_of(c * chunk_rows, UNIT)
        span = pl.ds(base, chunk_rows)
        shift = jnp.zeros((UNIT, WIDTH), F32)
        gain = shift
        held = []
        for u in range(0, chunk_rows, UNIT):
            rows = pl.ds(base + u, UNIT)
            d_in, wf, wn = norm_back(s_ref[rows, :], slope_ref[n_at, rows, :], n_ref[n_at, rows, :], r_ref[n_at, rows, :])
            shift = shift + wf
            held.append(wn)
            if len(held) == GROUP:
                gain = gain + column_sums(held)
                held = []
            low_ref[rows, :] = d_in.astype(BF16)
        low = low_ref[span, :]
        lgrad_ref[span, :] = mm_nt(low, w).astype(BF16)
        gw_ref[g_at] += mm_tn(latent_ref[span, :], low)
        gv_ref[5:6, :] += fold(gain)
        gv_ref[6:7, :] += fold(shift)
        return carry
    lax.fori_loop(0, TILE // chunk_rows, chunk, 0)
    rows = lax.broadcasted_iota(jnp.int32, (16, WIDTH), 0)
    gv_ref[0:16, :] += jnp.where(rows < 5, mm(hot[:, 0:TILE], low_ref[...]), 0.0)


def clean_latent(latent_ref, lat_ref, rows_dev):
    lat_ref[...] = latent_ref[...]
    steps = -(-rows_dev // TILE)
    tail = rows_dev - (steps - 1) * TILE
    if tail < TILE:
        @pl.when(pl.program_id(0) == steps - 1)
        def _():
            lat_ref[tail:TILE, :] = jnp.zeros((TILE - tail, WIDTH), BF16)


def split_low(x):
    high = x.astype(BF16)
    return high, (x - high.astype(F32)).astype(BF16)


def put_pieces(out_refs, spot, at, matrix):
    rows = out_refs[0].shape[1]
    if len(out_refs) == 1:
        out_refs[0][at] = matrix(pl.ds(0, rows))
    else:
        for k, ref in enumerate(out_refs):
            ref[at] = matrix(pl.ds(pl.multiple_of((spot ^ k) * rows, rows), rows))


def assemble_kernel(pieces, first, spots_ref, *refs):
    ins, (front_ref, own_ref) = refs[:pieces], refs[pieces:]
    rows = ins[0].shape[1]
    for k, ref in enumerate(ins):
        span = pl.ds(pl.multiple_of((spots_ref[1] ^ k) * rows, rows), rows)
        for m in range(ref.shape[0]):
            if m < first:
                front_ref[m, span, :] = ref[m]
            else:
                own_ref[m - first, span, :] = ref[m]


def first_kernel(layers, rows_dev, latent_ref, ints_ref, w_ref, act_ref, n_ref, slope_ref, r_ref, s_ref, vec_ref, lat_ref, hot_ref):
    @pl.when(pl.program_id(0) == 0)
    def _():
        unpack_vec(w_ref[0], vec_ref)

    clean_latent(latent_ref, lat_ref, rows_dev)
    hot_ref[...] = moves_hot(ints_ref[0]).T[0:TILE]
    stem_forward(720, lat_ref, hot_ref, vec_ref, w_ref[1], s_ref, n_ref, slope_ref, r_ref, SPLIT)
    forward_layers(1440, 0, SPLIT, layers, s_ref, (act_ref, n_ref, slope_ref, r_ref), vec_ref, w_ref, -2, 0)


def middle_kernel(
    layers, nq, sources, pieces, spots_ref, s_in_ref, ints_ref, vec_ref, hb_ref, *refs
):
    src = refs[:sources]
    latents_ref, value_ref, chance_ref, ds_ref, gv_ref, rep_ref = refs[sources:sources + 6]
    outs = refs[sources + 6:sources + 6 + pieces]
    w_ref, col_ref, act_ref, n_ref, slope_ref, r_ref, low_ref, dlog_ref, gw_ref, ghb_ref, loss_ref = refs[sources + 6 + pieces:]
    blocks = layers - SPLIT
    step = pl.program_id(0)

    @pl.when(step == 0)
    def _():
        for ref in (gw_ref, gv_ref, ghb_ref, loss_ref):
            ref[...] = jnp.zeros_like(ref)
        each = src[0].shape[0]
        for d, ref in enumerate(src):
            for m in range(each):
                w_ref[(spots_ref[0] ^ d) * each + m if sources > 1 else m] = ref[m]

    spread_columns(ints_ref[0], col_ref)
    ds_ref[...] = s_in_ref[...]
    save = (act_ref, n_ref, slope_ref, r_ref)
    forward_layers(1440, SPLIT, layers, layers, ds_ref, save, vec_ref, w_ref, SPLIT, SPLIT)

    def head(c, carry):
        base = pl.multiple_of(c * HEAD_CHUNK, UNIT)
        heads_chunk(base, nq, ds_ref, low_ref, col_ref, w_ref, blocks, hb_ref, latents_ref, value_ref, chance_ref, dlog_ref, loss_ref, ghb_ref)
        return carry

    lax.fori_loop(0, TILE // HEAD_CHUNK, head, 0)

    def head_grad(k, carry):
        gw_ref[blocks + k] += mm_tn(latents_ref[...], dlog_ref[k])
        return carry

    lax.fori_loop(0, 3, head_grad, 0)
    backward_layers(1440, SPLIT, layers, layers, ds_ref, low_ref, save, w_ref, SPLIT, SPLIT, gw_ref, gv_ref, SPLIT)

    @pl.when(step == pl.num_programs(0) - 1)
    def _():
        def put(m, carry):
            put_pieces(outs, spots_ref[1], m, lambda rows: gw_ref[m, rows, :].astype(BF16))
            return carry

        lax.fori_loop(0, blocks + 3, put, 0)
        sums = fold(ghb_ref[...])
        row = lax.broadcasted_iota(jnp.int32, (8, WIDTH), 0)
        total = jnp.where(row == 3, jnp.concatenate([fold(loss_ref[...]), jnp.zeros((1, 128), F32)], axis=1), 0.0)
        for k in range(3):
            total = jnp.where(row == k, sums[:, k * 256:(k + 1) * 256], total)
        high, low = split_low(total)
        rep_ref[...] = jnp.concatenate([high, low], axis=0)


def last_kernel(
    layers, pieces, rows_dev, spots_ref, latent_ref, ints_ref, ds_in_ref, act_ref, n_ref, slope_ref, r_ref, w_ref, gv_in_ref, *refs
):
    lgrad_ref = refs[0]
    outs = refs[1:1 + pieces]
    lat_ref, ds_ref, low_ref, gw_ref, gv_ref = refs[1 + pieces:]
    step = pl.program_id(0)

    @pl.when(step == 0)
    def _():
        gw_ref[...] = jnp.zeros_like(gw_ref)
        gv_ref[...] = gv_in_ref[...]

    clean_latent(latent_ref, lat_ref, rows_dev)
    ds_ref[...] = ds_in_ref[...]
    low_ref[...] = ds_in_ref[...].astype(BF16)
    backward_layers(1440, 0, SPLIT, layers, ds_ref, low_ref, (act_ref, n_ref, slope_ref, r_ref), w_ref, -2, 0, gw_ref, gv_ref, -1)
    stem_backward(720, lat_ref, moves_hot(ints_ref[0]), ds_ref, low_ref, n_ref, slope_ref, r_ref, SPLIT, w_ref[1], lgrad_ref, gw_ref, 0, gv_ref)

    @pl.when(step == pl.num_programs(0) - 1)
    def _():
        for m in range(SPLIT + 1):
            put_pieces(outs, spots_ref[1], m, lambda rows: gw_ref[m, rows, :].astype(BF16))
        wide = jnp.concatenate([gv_ref[...], jnp.zeros((128 - gv_ref.shape[0], WIDTH), F32)], axis=0).T
        high, low = split_low(wide)
        gw_ref[0] = jnp.concatenate([high, low], axis=1).astype(F32)
        put_pieces(outs, spots_ref[1], SPLIT + 1, lambda rows: gw_ref[0, rows, :].astype(BF16))


def sum_kernel(count, split, *refs):
    ins, out_ref = refs[:count], refs[count]
    for m in range(out_ref.shape[0]):
        total = ins[0][m].astype(F32)
        for ref in ins[1:]:
            total = total + ref[m].astype(F32)
        if m == split:
            high, low = split_low(total[:, 0:128] + total[:, 128:256])
            out_ref[m] = jnp.concatenate([high, low], axis=1)
        else:
            out_ref[m] = total.astype(BF16)


def sum_rep_kernel(count, *refs):
    ins, out_ref = refs[:count], refs[count]
    total = ins[0][...].astype(F32)
    for ref in ins[1:]:
        total = total + ref[...].astype(F32)
    high, low = split_low(total[0:8] + total[8:16])
    out_ref[...] = jnp.concatenate([high, low], axis=0)


SMEM = pl.BlockSpec(memory_space=pltpu.SMEM)
VMEM = pl.BlockSpec(memory_space=pltpu.VMEM)


def params(mib):
    return pltpu.CompilerParams(vmem_limit_bytes=mib << 20)


def tiled(shape, dim):
    block = shape[:dim] + (TILE,) + shape[dim + 1:]
    return pl.BlockSpec(block, lambda i: (0,) * dim + (i,) + (0,) * (len(shape) - dim - 1))


def whole(shape):
    return pl.BlockSpec(shape, lambda i: (0,) * len(shape))


def once(shape):
    return pl.BlockSpec(shape, lambda i: (0,) * len(shape), pipeline_mode=pl.Buffered(1))


def struct(shape, dtype):
    return jax.ShapeDtypeStruct(shape, dtype)


def exchange(x, axis, size):
    return [lax.ppermute(x, axis, [(i, i ^ k) for i in range(size)]) for k in range(1, size)]


def send_pieces(pieces, axis):
    size = len(pieces)
    return [lax.ppermute(pieces[k], axis, [(i, i ^ k) for i in range(size)]) for k in range(1, size)]


def per_device(
    latent, actions, value_bins, chance_codes, step_mask, stem_weight, action_table, stem_bias, stem_gain, stem_shift,
    block_weight, block_gain, block_shift, block_bias, value_weight, value_bias, chance_weight, chance_bias,
):
    n_dp, n_fsdp = lax.axis_size("dp"), lax.axis_size("fsdp")
    rows_dev = latent.shape[0]
    layers, shard = block_weight.shape[0], block_weight.shape[1]
    nq, nc = value_weight.shape[1], chance_weight.shape[1]
    moves = action_table.shape[0]
    steps = -(-rows_dev // TILE)
    padded = steps * TILE
    fast = shard % 16 == 0 and n_dp & (n_dp - 1) == 0 and n_fsdp & (n_fsdp - 1) == 0
    dp, fsdp = lax.axis_index("dp"), lax.axis_index("fsdp")
    spots = jnp.stack([dp, fsdp]).astype(jnp.int32)

    vectors = jnp.concatenate(
        [action_table, stem_bias[None], stem_gain[None], stem_shift[None], block_gain, block_shift, block_bias], axis=0
    )
    vectors = jnp.pad(vectors.T, ((0, 0), (0, WIDTH - vectors.shape[0])))
    head = jnp.concatenate(
        [value_weight, jnp.zeros((shard, 640 - nq), BF16), chance_weight, jnp.zeros((shard, 128 - nc), BF16)], axis=1
    )
    head = jnp.stack([head[:, k * WIDTH:(k + 1) * WIDTH] for k in range(3)])
    front = jnp.concatenate([vectors[None], stem_weight[None], block_weight[:SPLIT]], axis=0)
    back = jnp.concatenate([block_weight[SPLIT:], head], axis=0)
    n_front, n_back = front.shape[0], back.shape[0]
    if fast:
        each = -(-n_back // n_dp)
        back = jnp.pad(back, ((0, each * n_dp - n_back), (0, 0), (0, 0)))
        mine = jnp.concatenate([front, lax.dynamic_slice_in_dim(back, dp * each, each, 0)], axis=0)
        got = [mine] + exchange(mine, "fsdp", n_fsdp)
        w_front, own = pl.pallas_call(
            functools.partial(assemble_kernel, n_fsdp, n_front),
            in_specs=[SMEM] + [VMEM] * n_fsdp,
            out_specs=[VMEM] * 2,
            out_shape=[struct((n_front, WIDTH, WIDTH), BF16), struct((each, WIDTH, WIDTH), BF16)],
            name="assemble",
        )(spots, *got)
        sources = [own] + exchange(own, "dp", n_dp)
        pieces, piece_rows = n_fsdp, shard
    else:
        w_front = lax.all_gather(front, "fsdp", axis=1, tiled=True)
        sources = [lax.all_gather(back, "fsdp", axis=1, tiled=True)]
        pieces, piece_rows = 1, WIDTH

    ints = jnp.stack([actions, value_bins >> 5, value_bins & 31, chance_codes, step_mask])
    ints = jnp.pad(ints.astype(BF16), ((0, 11), (0, padded - rows_dev))).reshape(16, steps, TILE).transpose(1, 0, 2)
    width = -(-TILE // 128) * 128
    ints = jnp.pad(ints, ((0, 0), (0, 0), (0, width - TILE)))
    ints_spec = pl.BlockSpec((1, 16, width), lambda i: (i, 0, 0))
    low = lambda n: jnp.full((n,), -1e30, F32)
    head_bias = jnp.concatenate([value_bias.astype(F32), low(640 - nq), chance_bias.astype(F32), low(128 - nc)])
    head_bias = jnp.broadcast_to(head_bias[None], (8, 3 * WIDTH))

    saved = [
        struct((SPLIT, padded, WIDTH), BF16),
        struct((SPLIT + 1, padded, WIDTH), BF16),
        struct((SPLIT + 1, padded, WIDTH), BF16),
        struct((SPLIT + 1, padded, 128), F32),
    ]
    stream = struct((padded, WIDTH), F32)
    scratch = pltpu.VMEM
    *held, s_mid, vec = pl.pallas_call(
        functools.partial(first_kernel, layers, rows_dev),
        grid=(steps,),
        in_specs=[tiled((rows_dev, WIDTH), 0), ints_spec, once(w_front.shape)],
        out_specs=[tiled(x.shape, 1) for x in saved] + [tiled(stream.shape, 0), whole((128, WIDTH))],
        out_shape=saved + [stream, struct((128, WIDTH), F32)],
        scratch_shapes=[scratch((TILE, WIDTH), BF16), scratch((TILE, 16), BF16)],
        compiler_params=params(60),
        cost_estimate=pl.CostEstimate(flops=4 * rows_dev * WIDTH * WIDTH * 40, bytes_accessed=60 << 20, transcendentals=0),
        name="first",
    )(latent, ints, w_front)

    blocks = layers - SPLIT
    latents, value_logits, chance_logits, ds_mid, gv_mid, rep, *parts_mid = pl.pallas_call(
        functools.partial(middle_kernel, layers, nq, len(sources), pieces),
        grid=(steps,),
        in_specs=[SMEM, tiled(stream.shape, 0), ints_spec, once(vec.shape), once(head_bias.shape)]
        + [once(x.shape) for x in sources],
        out_specs=[
            tiled((rows_dev, WIDTH), 0), tiled((rows_dev, nq), 0), tiled((rows_dev, nc), 0), tiled(stream.shape, 0),
            whole((48, WIDTH)), whole((16, WIDTH)),
        ] + [whole((blocks + 3, piece_rows, WIDTH))] * pieces,
        out_shape=[
            struct((rows_dev, WIDTH), BF16), struct((rows_dev, nq), BF16), struct((rows_dev, nc), BF16), stream,
            struct((48, WIDTH), F32), struct((16, WIDTH), BF16),
        ] + [struct((blocks + 3, piece_rows, WIDTH), BF16)] * pieces,
        scratch_shapes=[
            scratch((sources[0].shape[0] * len(sources), WIDTH, WIDTH), BF16),
            scratch((3, TILE, 128), F32),
            scratch((blocks, TILE, WIDTH), BF16),
            scratch((blocks, TILE, WIDTH), BF16),
            scratch((blocks, TILE, WIDTH), BF16),
            scratch((blocks, TILE, 128), F32),
            scratch((TILE, WIDTH), BF16),
            scratch((3, TILE, WIDTH), BF16),
            scratch((blocks + 3, WIDTH, WIDTH), F32),
            scratch((UNIT, 3 * WIDTH), F32),
            scratch((UNIT, 128), F32),
        ],
        compiler_params=params(62),
        cost_estimate=pl.CostEstimate(flops=4 * rows_dev * WIDTH * WIDTH * 200, bytes_accessed=40 << 20, transcendentals=0),
        name="middle",
    )(spots, s_mid, ints, vec, head_bias, *sources)

    latent_grad, *parts_end = pl.pallas_call(
        functools.partial(last_kernel, layers, pieces, rows_dev),
        grid=(steps,),
        in_specs=[SMEM, tiled((rows_dev, WIDTH), 0), ints_spec, tiled(stream.shape, 0)]
        + [tiled(x.shape, 1) for x in saved]
        + [once(w_front.shape), once((48, WIDTH))],
        out_specs=[tiled((rows_dev, WIDTH), 0)] + [whole((SPLIT + 2, piece_rows, WIDTH))] * pieces,
        out_shape=[struct((rows_dev, WIDTH), BF16)] + [struct((SPLIT + 2, piece_rows, WIDTH), BF16)] * pieces,
        scratch_shapes=[
            scratch((TILE, WIDTH), BF16),
            scratch((TILE, WIDTH), F32),
            scratch((TILE, WIDTH), BF16),
            scratch((SPLIT + 1, WIDTH, WIDTH), F32),
            scratch((48, WIDTH), F32),
        ],
        compiler_params=params(60),
        cost_estimate=pl.CostEstimate(flops=4 * rows_dev * WIDTH * WIDTH * 40, bytes_accessed=60 << 20, transcendentals=0),
        name="last",
    )(spots, latent, ints, ds_mid, *held, w_front, gv_mid)

    if fast:
        def add(arrays, split, name):
            return pl.pallas_call(
                functools.partial(sum_kernel, len(arrays), split),
                in_specs=[VMEM] * len(arrays), out_specs=VMEM,
                out_shape=struct(arrays[0].shape, BF16), name=name,
            )(*arrays)

        def add_rep(arrays, name):
            return pl.pallas_call(
                functools.partial(sum_rep_kernel, len(arrays)),
                in_specs=[VMEM] * len(arrays), out_specs=VMEM,
                out_shape=struct(arrays[0].shape, BF16), name=name,
            )(*arrays)

        mid = add([parts_mid[0]] + send_pieces(parts_mid, "fsdp"), -1, "sum_mid")
        rep = add_rep([rep] + exchange(rep, "fsdp", n_fsdp), "sum_rep")
        end = add([parts_end[0]] + send_pieces(parts_end, "fsdp"), SPLIT + 1, "sum_end")
        total = lambda x: sum((y.astype(F32) for y in exchange(x, "dp", n_dp)), x.astype(F32))
        mid, rep, end = total(mid), total(rep), total(end)
    else:
        scatter = lambda x: lax.psum(
            lax.psum_scatter(x, "fsdp", scatter_dimension=1, tiled=True).astype(F32), "dp"
        )
        mid, end = scatter(parts_mid[0]), scatter(parts_end[0])
        rep = lax.psum(rep.astype(F32), ("dp", "fsdp"))

    scale = 1.0 / (rows_dev * n_dp * n_fsdp)
    rep = (rep[0:8] + rep[8:16]) * scale
    head_grad = jnp.concatenate([mid[blocks + k] for k in range(3)], axis=1) * scale
    small = (end[SPLIT + 1, :, 0:128] + end[SPLIT + 1, :, 128:256]).T * scale
    bias_sums = rep[0:3].reshape(3 * WIDTH)
    at = moves + 3
    gain = block_gain.astype(F32)
    return (
        latents,
        value_logits,
        chance_logits,
        jnp.sum(rep[3]),
        latent_grad,
        end[0] * scale,
        small[0:moves],
        small[moves],
        small[moves + 1] / stem_gain.astype(F32),
        small[moves + 2] / (16.0 * stem_gain.astype(F32)),
        jnp.concatenate([end[1:SPLIT + 1], mid[:blocks]], axis=0) * scale,
        small[at:at + layers] / gain,
        small[at + layers:at + 2 * layers] / (16.0 * gain),
        small[at + 2 * layers:at + 3 * layers],
        head_grad[:, 0:nq],
        bias_sums[0:nq],
        head_grad[:, 640:640 + nc],
        bias_sums[640:640 + nc],
    )


def solution(mesh):
    placed = (
        P(("dp", "fsdp"), None),
        P(("dp", "fsdp")),
        P(("dp", "fsdp")),
        P(("dp", "fsdp")),
        P(("dp", "fsdp")),
        P("fsdp", None),
        P(None, "fsdp"),
        P("fsdp"),
        P("fsdp"),
        P("fsdp"),
        P(None, "fsdp", None),
        P(None, "fsdp"),
        P(None, "fsdp"),
        P(None, "fsdp"),
        P("fsdp", None),
        P(),
        P("fsdp", None),
        P(),
    )
    return jax.shard_map(
        per_device,
        mesh=mesh,
        in_specs=placed,
        out_specs=(
            P(("dp", "fsdp"), None),
            P(("dp", "fsdp"), None),
            P(("dp", "fsdp"), None),
            P(),
            P(("dp", "fsdp"), None),
            P("fsdp", None),
            P(None, "fsdp"),
            P("fsdp"),
            P("fsdp"),
            P("fsdp"),
            P(None, "fsdp", None),
            P(None, "fsdp"),
            P(None, "fsdp"),
            P(None, "fsdp"),
            P("fsdp", None),
            P(),
            P("fsdp", None),
            P(),
        ),
        check_vma=False,
    )
```

time: 2330 us -> 318 us (0.14)
  blocking collectives: 1360 us -> 0 us
  other arithmetic: 356 us -> 11.1 us
  matrix products: 254 us -> 0 us
  Pallas kernels: 0 us -> 174 us
  waiting for transfers between devices: 188 us -> 30.4 us
  local copies, waits for them, and re-layouts: 124 us -> 30.6 us
  starting transfers between devices: 0.25 us -> 64.8 us
    all_gather x24 -> x0, blocking collectives: 720 us -> none  [the longest x10 305 us: fetch_backward(): lax.all_gather(params_block[0], 'fsdp', axis=0, tiled=True)]
    while x30 -> x0, blocking collectives: 544 us -> none
    reduce_sum x60 -> x1, other arithmetic: 335 us -> 0.6 us  [per_device(): jnp.sum(rep[3])]
    dot_general x40 -> x0, matrix products: 252 us -> none  [the longest x13 97.1 us: right_product(): lax.dot_general(left, right, (((1,), (1,)), ((), ())), preferred_element_...]
    pallas_call x0 -> x7, Pallas kernels: none -> 174 us  [the longest x1 104 us: per_device(): pl.pallas_call(functools.partial(middle_kernel, layers, nq, len(sources),...]
    reduce_scatter x12 -> x0, waiting for transfers between devices: 111 us -> none  [the longest x1 62.3 us: per_device(): lax.psum_scatter(head_chance_grad, 'fsdp', scatter_dimension=0, tiled=True)]
    while x180 -> x0, local copies, waits for them, and re-layouts: 70.9 us -> none
    ppermute x0 -> x40, starting transfers between devices: none -> 64.8 us  [the longest x26 41 us: exchange(): lax.ppermute(x, axis, [(i, i ^ k) for i in range(size)])]
  transfers between devices with their start and end apart: 15 -> 40, of which waited for: 4 -> 10; matrix products, arithmetic and copies ran while one was open for 13% -> 8% of each run, Pallas kernels for 0% -> 20%
where the time goes in v1:
time: 318 us; the launch traced here: 313 us
  Pallas kernels  174 us (55%)
  starting transfers between devices  64.8 us (20%)
  local copies, waits for them, and re-layouts  30.6 us (10%)
  waiting for transfers between devices  30.4 us (10%)
  other arithmetic  11.1 us (3%)
    pallas_call x1, Pallas kernels, per_device(): pl.pallas_call(functools.partial(middle_kernel, layers, nq, len(sources),...  104 us
    ppermute x26, starting transfers between devices, exchange(): lax.ppermute(x, axis, [(i, i ^ k) for i in range(size)])  41 us
    pallas_call x1, Pallas kernels, per_device(): pl.pallas_call(functools.partial(first_kernel, layers, rows_dev), grid=(s...  34.1 us
    pallas_call x1, Pallas kernels, per_device(): pl.pallas_call(functools.partial(last_kernel, layers, pieces, rows_dev),...  27.9 us
    ppermute x14, starting transfers between devices, send_pieces(): lax.ppermute(pieces[k], axis, [(i, i ^ k) for i in range(size)])  23.8 us
    unnamed x110, local copies, waits for them, and re-layouts  21.9 us
    ppermute x14, waiting for transfers between devices, send_pieces(): lax.ppermute(pieces[k], axis, [(i, i ^ k) for i in range(size)])  18.6 us
    ppermute x26, waiting for transfers between devices, exchange(): lax.ppermute(x, axis, [(i, i ^ k) for i in range(size)])  11.8 us
  transfers between devices with their start and end apart: 40, of which 10 were waited for; matrix products, arithmetic and copies ran while one was open for 8% of the time, Pallas kernels for 20%

profile of v1, /device:TPU:0, one launch (start us, length us, event | category | flops | bytes accessed | tf_op | source)
XLA Modules:
  0.0 312.5 jit_solution(3779617550496356348)
XLA Ops:
  0.7 0.8 slice.84
  1.5 0.9 slice.85
  2.4 0.8 copy.55
  3.1 0.8 copy.51
  3.9 0.8 copy.52
  4.7 0.8 copy.54
  5.4 0.8 copy.56
  6.2 0.8 copy.57
  7.0 0.8 copy.53
  8.0 0.8 fusion.12
  9.6 6.0 %collective-permute-start.6 = (bf16[8,32,256]{2,1,0:T(8,128)(2,1)S(1)}, bf16[8,32,256]{2,1,0:T(8,128)(2,1)S(1)}, u32[]{:S(2)}, u32[]{:S(2)}) collective-permute-start(bf16[8,32,256]{2,1,0:T(8,128)(2,1)S(1)} %pad_maximum_fusion.refs_0_), channel_id=1, source_target_pairs={{0,7},{1,6},{2,5},{3,4},{4,3},{5,2},{6,1},{7,0},{8,15},{9,14},{10,... | collective-permute-start | bytes 393224 | tf_op jit(solution)/shard_map/ppermute | solution.py:447
  15.8 0.8 collective-permute-start.4
  16.6 2.0 collective-permute-start.3
  18.6 2.3 collective-permute-start.2
  20.9 0.7 and_convert_fusion
  21.7 9.7 %collective-permute-start.1 = (bf16[8,32,256]{2,1,0:T(8,128)(2,1)S(1)}, bf16[8,32,256]{2,1,0:T(8,128)(2,1)S(1)}, u32[]{:S(2)}, u32[]{:S(2)}) collective-permute-start(bf16[8,32,256]{2,1,0:T(8,128)(2,1)S(1)} %pad_maximum_fusion.refs_0_), channel_id=1, source_target_pairs={{0,2},{1,3},{2,0},{3,1},{4,6},{5,7},{6,4},{7,5},{8,10},{9,11},{10,... | collective-permute-start | bytes 393224 | tf_op jit(solution)/shard_map/ppermute | solution.py:447
  31.4 1.4 collective-permute-start
  34.6 0.7 convert.20
  35.4 0.7 convert.23
  36.2 0.7 convert.24
  38.3 0.8 collective-permute-done.1.refs_2_
  40.5 2.3 assemble.1
  42.8 1.6 collective-permute-start.8
  44.7 34.1 %first.1 = (bf16[3,5760,256]{2,1,0:T(8,128)(2,1)}, bf16[4,5760,256]{2,1,0:T(8,128)(2,1)}, bf16[4,5760,256]{2,1,0:T(8,128)(2,1)}, f32[4,5760,128]{2,1,0:T(8,128)}...) custom-call(bf16[5696,256]{1,0:T(8,128)(2,1)} %latent_ref.3, bf16[4,16,1536]{2,1,0:T(8,128)(2,1)} %pad.17.ints_ref, ...), custom_call_target="tpu_custom_call" | custom-call | flops 59726888960 | bytes 62914560 | tf_op jit(solution)/shard_map/first/pallas_call | solution.py:517
  79.9 104.5 %middle.1 = (bf16[5696,256]{1,0:T(8,128)(2,1)}, bf16[5696,601]{1,0:T(8,128)(2,1)}, bf16[5696,32]{1,0:T(8,128)(2,1)}, f32[5760,256]{1,0:T(8,128)}, f32[48,256]{1,...) custom-call(s32[2]{0:T(128)} %pad_add_fusion.spots_ref, ...), custom_call_target="tpu_custom_call" | custom-call | flops 298634444800 | bytes 41943040 | tf_op jit(solution)/shard_map/middle/pallas_call | solution.py:530
  184.3 2.7 collective-permute-start.16
  187.0 1.3 collective-permute-start.15
  188.4 1.1 collective-permute-start.14
  189.5 2.6 collective-permute-start.13
  192.3 1.9 collective-permute-start.11
  194.2 1.3 collective-permute-start.10
  195.6 1.2 collective-permute-done.12.refs_3_
  196.8 1.3 collective-permute-done.10.refs_1_
  198.7 1.4 sum_rep.1
  200.2 1.6 collective-permute-start.18
  202.0 27.9 %last.1 = (bf16[5696,256]{1,0:T(8,128)(2,1)}, bf16[5,32,256]{2,1,0:T(8,128)(2,1)}, bf16[5,32,256]{2,1,0:T(8,128)(2,1)}, bf16[5,32,256]{2,1,0:T(8,128)(2,1)}, bf1...) custom-call(s32[2]{0:T(128)} %pad_add_fusion.spots_ref, ...), custom_call_target="tpu_custom_call" | custom-call | flops 59726888960 | bytes 62914560 | tf_op jit(solution)/shard_map/last/pallas_call | solution.py:561
  229.9 1.4 collective-permute-start.20
  231.9 1.9 copy.60
  233.8 10.5 %copy.59 = bf16[5696,601]{0,1:T(8,128)(2,1)} copy(bf16[5696,601]{1,0:T(8,128)(2,1)} %get-tuple-element.99) | data formatting | bytes 13693184
  244.4 1.7 collective-permute-start.22
  246.1 1.6 collective-permute-start.23
  247.6 2.1 collective-permute-start.24
  249.8 2.3 collective-permute-start.25
  252.2 1.7 collective-permute-start.26
  254.4 1.4 collective-permute-start.30
  255.8 1.9 collective-permute-done.23.refs_4_
  257.8 3.4 %collective-permute-done.24.refs_5_ = bf16[5,32,256]{2,1,0:T(8,128)(2,1)S(1)} collective-permute-done((bf16[5,32,256]{2,1,0:T(8,128)(2,1)S(1)}, bf16[5,32,256]{2,1,0:T(8,128)(2,1)S(1)}, u32[]{:S(2)}, u32[]{:S(2)}) %collective-permute-start.24) | collective-permute-done | bytes 81952 | tf_op jit(solution)/shard_map/ppermute | solution.py:452
  261.9 1.9 sum_end.1
  263.7 1.5 collective-permute-start.28
  266.2 2.5 collective-permute-done.29
  268.7 3.2 %collective-permute-start.32 = (bf16[10,32,256]{2,1,0:T(8,128)(2,1)S(1)}, bf16[10,32,256]{2,1,0:T(8,128)(2,1)S(1)}, u32[]{:S(2)}, u32[]{:S(2)}) collective-permute-start(bf16[10,32,256]{2,1,0:T(8,128)(2,1)S(1)} %copy-done.42), channel_id=1, source_target_pairs={{0,3},{1,2},{2,1},{3,0},{4,7},{5,6},{6,5},{7,4},{8,11},{9,10},{10,... | collective-permute-start | bytes 491528 | tf_op jit(solution)/shard_map/ppermute | solution.py:452
  271.9 2.1 collective-permute-start.33
  274.1 1.6 collective-permute-start.34
  275.6 0.9 convert_add_fusion.1
  276.7 2.3 collective-permute-start.35
  279.0 1.8 collective-permute-start.36
  284.8 8.9 %collective-permute-done.33.refs_4_ = bf16[10,32,256]{2,1,0:T(8,128)(2,1)S(1)} collective-permute-done((bf16[10,32,256]{2,1,0:T(8,128)(2,1)S(1)}, bf16[10,32,256]{2,1,0:T(8,128)(2,1)S(1)}, u32[]{:S(2)}, u32[]{:S(2)}) %collective-permute-start.33) | collective-permute-done | bytes 163872 | tf_op jit(solution)/shard_map/ppermute | solution.py:452
  293.7 4.4 %collective-permute-done.34.refs_5_ = bf16[10,32,256]{2,1,0:T(8,128)(2,1)S(1)} collective-permute-done((bf16[10,32,256]{2,1,0:T(8,128)(2,1)S(1)}, bf16[10,32,256]{2,1,0:T(8,128)(2,1)S(1)}, u32[]{:S(2)}, u32[]{:S(2)}) %collective-permute-start.34) | collective-permute-done | bytes 163872 | tf_op jit(solution)/shard_map/ppermute | solution.py:452
  298.9 2.2 sum_mid.1
  301.7 1.3 collective-permute-start.37
  303.5 4.3 %collective-permute-done.39 = bf16[10,32,256]{2,1,0:T(8,128)(2,1)S(1)} collective-permute-done((bf16[10,32,256]{2,1,0:T(8,128)(2,1)}, bf16[10,32,256]{2,1,0:T(8,128)(2,1)S(1)}, u32[]{:S(2)}, u32[]{:S(2)}) %collective-permute-start.39) | collective-permute-done | bytes 163872 | tf_op jit(solution)/shard_map/ppermute | solution.py:447
  307.8 1.6 collective-permute-done.38
  309.5 1.0 convert_add_fusion
  311.8 0.8 maximum_multiply_fusion
  (187 shorter events, 18.5 us)
Async XLA Ops:
  9.6 29.6 %copy-start.1 = (bf16[8,32,256]{2,1,0:T(8,128)(2,1)}, bf16[8,32,256]{2,1,0:T(8,128)(2,1)S(1)}, u32[]{:S(2)}) copy-start(bf16[8,32,256]{2,1,0:T(8,128)(2,1)S(1)} %pad_maximum_fusion.refs_0_) | copy-start | bytes 393220
  9.6 12.1 %collective-permute-start.6 = (bf16[8,32,256]{2,1,0:T(8,128)(2,1)S(1)}, bf16[8,32,256]{2,1,0:T(8,128)(2,1)S(1)}, u32[]{:S(2)}, u32[]{:S(2)}) collective-permute-start(bf16[8,32,256]{2,1,0:T(8,128)(2,1)S(1)} %pad_maximum_fusion.refs_0_), channel_id=1, source_target_pairs={{0,7},{1,6},{2,5},{3,4},{4,3},{5,2},{6,1},{7,0},{8,15},{9,14},{10,... | collective-permute-start | bytes 393224 | tf_op jit(solution)/shard_map/ppermute | solution.py:447
  15.6 15.7 %collective-permute-start.5 = (bf16[8,32,256]{2,1,0:T(8,128)(2,1)S(1)}, bf16[8,32,256]{2,1,0:T(8,128)(2,1)S(1)}, u32[]{:S(2)}, u32[]{:S(2)}) collective-permute-start(bf16[8,32,256]{2,1,0:T(8,128)(2,1)S(1)} %pad_maximum_fusion.refs_0_), channel_id=1, source_target_pairs={{0,6},{1,7},{2,4},{3,5},{4,2},{5,3},{6,0},{7,1},{8,14},{9,15},{10,... | collective-permute-start | bytes 393224 | tf_op jit(solution)/shard_map/ppermute | solution.py:447
  15.8 22.5 %collective-permute-start.4 = (bf16[8,32,256]{2,1,0:T(8,128)(2,1)S(1)}, bf16[8,32,256]{2,1,0:T(8,128)(2,1)S(1)}, u32[]{:S(2)}, u32[]{:S(2)}) collective-permute-start(bf16[8,32,256]{2,1,0:T(8,128)(2,1)S(1)} %pad_maximum_fusion.refs_0_), channel_id=1, source_target_pairs={{0,5},{1,4},{2,7},{3,6},{4,1},{5,0},{6,3},{7,2},{8,13},{9,12},{10,... | collective-permute-start | bytes 393224 | tf_op jit(solution)/shard_map/ppermute | solution.py:447
  16.6 21.7 %collective-permute-start.3 = (bf16[8,32,256]{2,1,0:T(8,128)(2,1)S(1)}, bf16[8,32,256]{2,1,0:T(8,128)(2,1)S(1)}, u32[]{:S(2)}, u32[]{:S(2)}) collective-permute-start(bf16[8,32,256]{2,1,0:T(8,128)(2,1)S(1)} %pad_maximum_fusion.refs_0_), channel_id=1, source_target_pairs={{0,4},{1,5},{2,6},{3,7},{4,0},{5,1},{6,2},{7,3},{8,12},{9,13},{10,... | collective-permute-start | bytes 393224 | tf_op jit(solution)/shard_map/ppermute | solution.py:447
  18.6 19.7 %collective-permute-start.2 = (bf16[8,32,256]{2,1,0:T(8,128)(2,1)S(1)}, bf16[8,32,256]{2,1,0:T(8,128)(2,1)S(1)}, u32[]{:S(2)}, u32[]{:S(2)}) collective-permute-start(bf16[8,32,256]{2,1,0:T(8,128)(2,1)S(1)} %pad_maximum_fusion.refs_0_), channel_id=1, source_target_pairs={{0,3},{1,2},{2,1},{3,0},{4,7},{5,6},{6,5},{7,4},{8,11},{9,10},{10,... | collective-permute-start | bytes 393224 | tf_op jit(solution)/shard_map/ppermute | solution.py:447
  21.7 17.5 %copy-start.9 = (bf16[8,32,256]{2,1,0:T(8,128)(2,1)}, bf16[8,32,256]{2,1,0:T(8,128)(2,1)S(1)}, u32[]{:S(2)}) copy-start(bf16[8,32,256]{2,1,0:T(8,128)(2,1)S(1)} %collective-permute-done.6.refs_7_) | copy-start | bytes 393220
  21.7 17.5 %collective-permute-start.1 = (bf16[8,32,256]{2,1,0:T(8,128)(2,1)S(1)}, bf16[8,32,256]{2,1,0:T(8,128)(2,1)S(1)}, u32[]{:S(2)}, u32[]{:S(2)}) collective-permute-start(bf16[8,32,256]{2,1,0:T(8,128)(2,1)S(1)} %pad_maximum_fusion.refs_0_), channel_id=1, source_target_pairs={{0,2},{1,3},{2,0},{3,1},{4,6},{5,7},{6,4},{7,5},{8,10},{9,11},{10,... | collective-permute-start | bytes 393224 | tf_op jit(solution)/shard_map/ppermute | solution.py:447
  31.4 7.8 %collective-permute-start = (bf16[8,32,256]{2,1,0:T(8,128)(2,1)S(1)}, bf16[8,32,256]{2,1,0:T(8,128)(2,1)S(1)}, u32[]{:S(2)}, u32[]{:S(2)}) collective-permute-start(bf16[8,32,256]{2,1,0:T(8,128)(2,1)S(1)} %pad_maximum_fusion.refs_0_), channel_id=1, source_target_pairs={{0,1},{1,0},{2,3},{3,2},{4,5},{5,4},{6,7},{7,6},{8,9},{9,8},{10,11... | collective-permute-start | bytes 393224 | tf_op jit(solution)/shard_map/ppermute | solution.py:447
  42.8 36.0 %collective-permute-start.9 = (bf16[3,256,256]{2,1,0:T(8,128)(2,1)}, bf16[3,256,256]{2,1,0:T(8,128)(2,1)S(1)}, u32[]{:S(2)}, u32[]{:S(2)}) collective-permute-start(bf16[3,256,256]{2,1,0:T(8,128)(2,1)} %get-tuple-element.52.refs_0_), channel_id=1, source_target_pairs={{0,24},{8,16},{16,8},{24,0},{1,25},{9,17},{17,9},{25,1},{2,26},{10... | collective-permute-start | bytes 1179656 | tf_op jit(solution)/shard_map/ppermute | solution.py:447
  42.8 36.0 %collective-permute-start.8 = (bf16[3,256,256]{2,1,0:T(8,128)(2,1)}, bf16[3,256,256]{2,1,0:T(8,128)(2,1)S(1)}, u32[]{:S(2)}, u32[]{:S(2)}) collective-permute-start(bf16[3,256,256]{2,1,0:T(8,128)(2,1)} %get-tuple-element.52.refs_0_), channel_id=1, source_target_pairs={{0,16},{8,24},{16,0},{24,8},{1,17},{9,25},{17,1},{25,9},{2,18},{10... | collective-permute-start | bytes 1179656 | tf_op jit(solution)/shard_map/ppermute | solution.py:447
  44.4 34.5 %collective-permute-start.7 = (bf16[3,256,256]{2,1,0:T(8,128)(2,1)}, bf16[3,256,256]{2,1,0:T(8,128)(2,1)S(1)}, u32[]{:S(2)}, u32[]{:S(2)}) collective-permute-start(bf16[3,256,256]{2,1,0:T(8,128)(2,1)} %get-tuple-element.52.refs_0_), channel_id=1, source_target_pairs={{0,8},{8,0},{16,24},{24,16},{1,9},{9,1},{17,25},{25,17},{2,10},{10... | collective-permute-start | bytes 1179656 | tf_op jit(solution)/shard_map/ppermute | solution.py:447
  184.3 8.0 %collective-permute-start.16 = (bf16[16,256]{1,0:T(8,128)(2,1)}, bf16[16,256]{1,0:T(8,128)(2,1)S(1)}, u32[]{:S(2)}, u32[]{:S(2)}) collective-permute-start(bf16[16,256]{1,0:T(8,128)(2,1)} %get-tuple-element.56.refs_0_), channel_id=1, source_target_pairs={{0,7},{1,6},{2,5},{3,4},{4,3},{5,2},{6,1},{7,0},{8,15},{9,14},{10,... | collective-permute-start | bytes 24584 | tf_op jit(solution)/shard_map/ppermute | solution.py:447
  187.0 7.2 %collective-permute-start.15 = (bf16[16,256]{1,0:T(8,128)(2,1)}, bf16[16,256]{1,0:T(8,128)(2,1)S(1)}, u32[]{:S(2)}, u32[]{:S(2)}) collective-permute-start(bf16[16,256]{1,0:T(8,128)(2,1)} %get-tuple-element.56.refs_0_), channel_id=1, source_target_pairs={{0,6},{1,7},{2,4},{3,5},{4,2},{5,3},{6,0},{7,1},{8,14},{9,15},{10,... | collective-permute-start | bytes 24584 | tf_op jit(solution)/shard_map/ppermute | solution.py:447
  188.4 7.2 %collective-permute-start.14 = (bf16[16,256]{1,0:T(8,128)(2,1)}, bf16[16,256]{1,0:T(8,128)(2,1)S(1)}, u32[]{:S(2)}, u32[]{:S(2)}) collective-permute-start(bf16[16,256]{1,0:T(8,128)(2,1)} %get-tuple-element.56.refs_0_), channel_id=1, source_target_pairs={{0,5},{1,4},{2,7},{3,6},{4,1},{5,0},{6,3},{7,2},{8,13},{9,12},{10,... | collective-permute-start | bytes 24584 | tf_op jit(solution)/shard_map/ppermute | solution.py:447
  189.5 6.1 %collective-permute-start.13 = (bf16[16,256]{1,0:T(8,128)(2,1)}, bf16[16,256]{1,0:T(8,128)(2,1)S(1)}, u32[]{:S(2)}, u32[]{:S(2)}) collective-permute-start(bf16[16,256]{1,0:T(8,128)(2,1)} %get-tuple-element.56.refs_0_), channel_id=1, source_target_pairs={{0,4},{1,5},{2,6},{3,7},{4,0},{5,1},{6,2},{7,3},{8,12},{9,13},{10,... | collective-permute-start | bytes 24584 | tf_op jit(solution)/shard_map/ppermute | solution.py:447
  192.1 4.8 %collective-permute-start.12 = (bf16[16,256]{1,0:T(8,128)(2,1)}, bf16[16,256]{1,0:T(8,128)(2,1)S(1)}, u32[]{:S(2)}, u32[]{:S(2)}) collective-permute-start(bf16[16,256]{1,0:T(8,128)(2,1)} %get-tuple-element.56.refs_0_), channel_id=1, source_target_pairs={{0,3},{1,2},{2,1},{3,0},{4,7},{5,6},{6,5},{7,4},{8,11},{9,10},{10,... | collective-permute-start | bytes 24584 | tf_op jit(solution)/shard_map/ppermute | solution.py:447
  192.3 4.5 %collective-permute-start.11 = (bf16[16,256]{1,0:T(8,128)(2,1)}, bf16[16,256]{1,0:T(8,128)(2,1)S(1)}, u32[]{:S(2)}, u32[]{:S(2)}) collective-permute-start(bf16[16,256]{1,0:T(8,128)(2,1)} %get-tuple-element.56.refs_0_), channel_id=1, source_target_pairs={{0,2},{1,3},{2,0},{3,1},{4,6},{5,7},{6,4},{7,5},{8,10},{9,11},{10,... | collective-permute-start | bytes 24584 | tf_op jit(solution)/shard_map/ppermute | solution.py:447
  194.2 3.9 %collective-permute-start.10 = (bf16[16,256]{1,0:T(8,128)(2,1)}, bf16[16,256]{1,0:T(8,128)(2,1)S(1)}, u32[]{:S(2)}, u32[]{:S(2)}) collective-permute-start(bf16[16,256]{1,0:T(8,128)(2,1)} %get-tuple-element.56.refs_0_), channel_id=1, source_target_pairs={{0,1},{1,0},{2,3},{3,2},{4,5},{5,4},{6,7},{7,6},{8,9},{9,8},{10,11... | collective-permute-start | bytes 24584 | tf_op jit(solution)/shard_map/ppermute | solution.py:447
  200.2 44.2 %collective-permute-start.19 = (bf16[16,256]{1,0:T(8,128)(2,1)}, bf16[16,256]{1,0:T(8,128)(2,1)S(1)}, u32[]{:S(2)}, u32[]{:S(2)}) collective-permute-start(bf16[16,256]{1,0:T(8,128)(2,1)} %sum_rep.1), channel_id=1, source_target_pairs={{0,24},{8,16},{16,8},{24,0},{1,25},{9,17},{17,9},{25,1},{2,26},{10... | collective-permute-start | bytes 24584 | tf_op jit(solution)/shard_map/ppermute | solution.py:447
  200.2 45.9 %collective-permute-start.18 = (bf16[16,256]{1,0:T(8,128)(2,1)}, bf16[16,256]{1,0:T(8,128)(2,1)S(1)}, u32[]{:S(2)}, u32[]{:S(2)}) collective-permute-start(bf16[16,256]{1,0:T(8,128)(2,1)} %sum_rep.1), channel_id=1, source_target_pairs={{0,16},{8,24},{16,0},{24,8},{1,17},{9,25},{17,1},{25,9},{2,18},{10... | collective-permute-start | bytes 24584 | tf_op jit(solution)/shard_map/ppermute | solution.py:447
  201.7 45.9 %collective-permute-start.17 = (bf16[16,256]{1,0:T(8,128)(2,1)}, bf16[16,256]{1,0:T(8,128)(2,1)S(1)}, u32[]{:S(2)}, u32[]{:S(2)}) collective-permute-start(bf16[16,256]{1,0:T(8,128)(2,1)} %sum_rep.1), channel_id=1, source_target_pairs={{0,8},{8,0},{16,24},{24,16},{1,9},{9,1},{17,25},{25,17},{2,10},{10... | collective-permute-start | bytes 24584 | tf_op jit(solution)/shard_map/ppermute | solution.py:447
  202.0 29.8 %copy-start = (bf16[5696,32]{1,0:T(8,128)(2,1)S(1)}, bf16[5696,32]{1,0:T(8,128)(2,1)}, u32[]{:S(2)}) copy-start(bf16[5696,32]{1,0:T(8,128)(2,1)} %get-tuple-element.100) | copy-start | bytes 1093636
  229.9 19.9 %collective-permute-start.20 = (bf16[5,32,256]{2,1,0:T(8,128)(2,1)}, bf16[5,32,256]{2,1,0:T(8,128)(2,1)S(1)}, u32[]{:S(2)}, u32[]{:S(2)}) collective-permute-start(bf16[5,32,256]{2,1,0:T(8,128)(2,1)} %get-tuple-element.65), channel_id=1, source_target_pairs={{0,1},{1,0},{2,3},{3,2},{4,5},{5,4},{6,7},{7,6},{8,9},{9,8},{10,11... | collective-permute-start | bytes 245768 | tf_op jit(solution)/shard_map/ppermute | solution.py:452
  231.3 20.8 %collective-permute-start.21 = (bf16[5,32,256]{2,1,0:T(8,128)(2,1)}, bf16[5,32,256]{2,1,0:T(8,128)(2,1)S(1)}, u32[]{:S(2)}, u32[]{:S(2)}) collective-permute-start(bf16[5,32,256]{2,1,0:T(8,128)(2,1)} %get-tuple-element.66), channel_id=1, source_target_pairs={{0,2},{1,3},{2,0},{3,1},{4,6},{5,7},{6,4},{7,5},{8,10},{9,11},{10,... | collective-permute-start | bytes 245768 | tf_op jit(solution)/shard_map/ppermute | solution.py:452
  233.7 10.7 %copy-start.49 = (bf16[5,32,256]{2,1,0:T(8,128)(2,1)S(1)}, bf16[5,32,256]{2,1,0:T(8,128)(2,1)}, u32[]{:S(2)}) copy-start(bf16[5,32,256]{2,1,0:T(8,128)(2,1)} %get-tuple-element.67) | copy-start | bytes 245764
  233.7 12.4 %copy-start.48 = (bf16[5,32,256]{2,1,0:T(8,128)(2,1)S(1)}, bf16[5,32,256]{2,1,0:T(8,128)(2,1)}, u32[]{:S(2)}) copy-start(bf16[5,32,256]{2,1,0:T(8,128)(2,1)} %get-tuple-element.68) | copy-start | bytes 245764
  233.7 13.9 %copy-start.47 = (bf16[5,32,256]{2,1,0:T(8,128)(2,1)S(1)}, bf16[5,32,256]{2,1,0:T(8,128)(2,1)}, u32[]{:S(2)}) copy-start(bf16[5,32,256]{2,1,0:T(8,128)(2,1)} %get-tuple-element.69) | copy-start | bytes 245764
  233.7 16.0 %copy-start.25 = (bf16[16,256]{1,0:T(8,128)(2,1)S(1)}, bf16[16,256]{1,0:T(8,128)(2,1)}, u32[]{:S(2)}) copy-start(bf16[16,256]{1,0:T(8,128)(2,1)} %sum_rep.1) | copy-start | bytes 24580
  233.7 16.1 %copy-start.46 = (bf16[5,32,256]{2,1,0:T(8,128)(2,1)S(1)}, bf16[5,32,256]{2,1,0:T(8,128)(2,1)}, u32[]{:S(2)}) copy-start(bf16[5,32,256]{2,1,0:T(8,128)(2,1)} %get-tuple-element.70) | copy-start | bytes 245764
  233.7 18.4 %copy-start.45 = (bf16[5,32,256]{2,1,0:T(8,128)(2,1)S(1)}, bf16[5,32,256]{2,1,0:T(8,128)(2,1)}, u32[]{:S(2)}) copy-start(bf16[5,32,256]{2,1,0:T(8,128)(2,1)} %get-tuple-element.71) | copy-start | bytes 245764
  233.7 20.7 %copy-start.44 = (bf16[10,32,256]{2,1,0:T(8,128)(2,1)S(1)}, bf16[10,32,256]{2,1,0:T(8,128)(2,1)}, u32[]{:S(2)}) copy-start(bf16[10,32,256]{2,1,0:T(8,128)(2,1)} %get-tuple-element.73) | copy-start | bytes 491524
  233.8 24.0 %copy-start.43 = (bf16[10,32,256]{2,1,0:T(8,128)(2,1)S(1)}, bf16[10,32,256]{2,1,0:T(8,128)(2,1)}, u32[]{:S(2)}) copy-start(bf16[10,32,256]{2,1,0:T(8,128)(2,1)} %get-tuple-element.74) | copy-start | bytes 491524
  233.8 34.9 %copy-start.42 = (bf16[10,32,256]{2,1,0:T(8,128)(2,1)S(1)}, bf16[10,32,256]{2,1,0:T(8,128)(2,1)}, u32[]{:S(2)}) copy-start(bf16[10,32,256]{2,1,0:T(8,128)(2,1)} %get-tuple-element.75) | copy-start | bytes 491524
  233.8 38.2 %copy-start.41 = (bf16[10,32,256]{2,1,0:T(8,128)(2,1)S(1)}, bf16[10,32,256]{2,1,0:T(8,128)(2,1)}, u32[]{:S(2)}) copy-start(bf16[10,32,256]{2,1,0:T(8,128)(2,1)} %get-tuple-element.76) | copy-start | bytes 491524
  233.8 40.3 %copy-start.40 = (bf16[10,32,256]{2,1,0:T(8,128)(2,1)S(1)}, bf16[10,32,256]{2,1,0:T(8,128)(2,1)}, u32[]{:S(2)}) copy-start(bf16[10,32,256]{2,1,0:T(8,128)(2,1)} %get-tuple-element.77) | copy-start | bytes 491524
  233.8 42.8 %copy-start.24 = (bf16[10,32]{0,1:T(8,128)(2,1)S(1)}, bf16[10,32]{0,1:T(8,128)(2,1)}, u32[]{:S(2)}) copy-start(bf16[10,32]{0,1:T(8,128)(2,1)} %copy-done.23) | copy-start | bytes 1924
  233.8 42.9 %copy-start.39 = (bf16[10,32,256]{2,1,0:T(8,128)(2,1)S(1)}, bf16[10,32,256]{2,1,0:T(8,128)(2,1)}, u32[]{:S(2)}) copy-start(bf16[10,32,256]{2,1,0:T(8,128)(2,1)} %get-tuple-element.78) | copy-start | bytes 491524
  233.8 45.2 %copy-start.38 = (bf16[10,32,256]{2,1,0:T(8,128)(2,1)S(1)}, bf16[10,32,256]{2,1,0:T(8,128)(2,1)}, u32[]{:S(2)}) copy-start(bf16[10,32,256]{2,1,0:T(8,128)(2,1)} %get-tuple-element.79) | copy-start | bytes 491524
  233.8 69.2 %copy-start.34 = (bf16[32]{0:T(256)(128)(2,1)S(1)}, bf16[32]{0:T(256)(128)(2,1)}, u32[]{:S(2)}) copy-start(bf16[32]{0:T(256)(128)(2,1)} %param.26) | copy-start | bytes 196
  244.4 10.1 %collective-permute-start.22 = (bf16[5,32,256]{2,1,0:T(8,128)(2,1)S(1)}, bf16[5,32,256]{2,1,0:T(8,128)(2,1)S(1)}, u32[]{:S(2)}, u32[]{:S(2)}) collective-permute-start(bf16[5,32,256]{2,1,0:T(8,128)(2,1)S(1)} %copy-done.49), channel_id=1, source_target_pairs={{0,3},{1,2},{2,1},{3,0},{4,7},{5,6},{6,5},{7,4},{8,11},{9,10},{10,... | collective-permute-start | bytes 245768 | tf_op jit(solution)/shard_map/ppermute | solution.py:452
  246.1 11.6 %collective-permute-start.23 = (bf16[5,32,256]{2,1,0:T(8,128)(2,1)S(1)}, bf16[5,32,256]{2,1,0:T(8,128)(2,1)S(1)}, u32[]{:S(2)}, u32[]{:S(2)}) collective-permute-start(bf16[5,32,256]{2,1,0:T(8,128)(2,1)S(1)} %copy-done.48), channel_id=1, source_target_pairs={{0,4},{1,5},{2,6},{3,7},{4,0},{5,1},{6,2},{7,3},{8,12},{9,13},{10,... | collective-permute-start | bytes 245768 | tf_op jit(solution)/shard_map/ppermute | solution.py:452
  247.6 13.5 %collective-permute-start.24 = (bf16[5,32,256]{2,1,0:T(8,128)(2,1)S(1)}, bf16[5,32,256]{2,1,0:T(8,128)(2,1)S(1)}, u32[]{:S(2)}, u32[]{:S(2)}) collective-permute-start(bf16[5,32,256]{2,1,0:T(8,128)(2,1)S(1)} %copy-done.47), channel_id=1, source_target_pairs={{0,5},{1,4},{2,7},{3,6},{4,1},{5,0},{6,3},{7,2},{8,13},{9,12},{10,... | collective-permute-start | bytes 245768 | tf_op jit(solution)/shard_map/ppermute | solution.py:452
  249.8 11.4 %copy-start.16 = (bf16[5,32,256]{2,1,0:T(8,128)(2,1)}, bf16[5,32,256]{2,1,0:T(8,128)(2,1)S(1)}, u32[]{:S(2)}) copy-start(bf16[5,32,256]{2,1,0:T(8,128)(2,1)S(1)} %collective-permute-done.20.refs_1_) | copy-start | bytes 245764
  249.8 11.3 %collective-permute-start.25 = (bf16[5,32,256]{2,1,0:T(8,128)(2,1)S(1)}, bf16[5,32,256]{2,1,0:T(8,128)(2,1)S(1)}, u32[]{:S(2)}, u32[]{:S(2)}) collective-permute-start(bf16[5,32,256]{2,1,0:T(8,128)(2,1)S(1)} %copy-done.46), channel_id=1, source_target_pairs={{0,6},{1,7},{2,4},{3,5},{4,2},{5,3},{6,0},{7,1},{8,14},{9,15},{10,... | collective-permute-start | bytes 245768 | tf_op jit(solution)/shard_map/ppermute | solution.py:452
  252.1 9.0 %copy-start.17 = (bf16[5,32,256]{2,1,0:T(8,128)(2,1)}, bf16[5,32,256]{2,1,0:T(8,128)(2,1)S(1)}, u32[]{:S(2)}) copy-start(bf16[5,32,256]{2,1,0:T(8,128)(2,1)S(1)} %collective-permute-done.21.refs_2_) | copy-start | bytes 245764
  252.2 9.0 %collective-permute-start.26 = (bf16[5,32,256]{2,1,0:T(8,128)(2,1)S(1)}, bf16[5,32,256]{2,1,0:T(8,128)(2,1)S(1)}, u32[]{:S(2)}, u32[]{:S(2)}) collective-permute-start(bf16[5,32,256]{2,1,0:T(8,128)(2,1)S(1)} %copy-done.45), channel_id=1, source_target_pairs={{0,7},{1,6},{2,5},{3,4},{4,3},{5,2},{6,1},{7,0},{8,15},{9,14},{10,... | collective-permute-start | bytes 245768 | tf_op jit(solution)/shard_map/ppermute | solution.py:452
  253.9 58.6 %copy-start.33 = (f32[768]{0:T(1024)}, f32[768]{0:T(1024)S(1)}, u32[]{:S(2)}) copy-start(f32[768]{0:T(1024)S(1)} %reshape.49) | copy-start | bytes 9220
  254.4 22.2 %collective-permute-start.30 = (bf16[10,32,256]{2,1,0:T(8,128)(2,1)S(1)}, bf16[10,32,256]{2,1,0:T(8,128)(2,1)S(1)}, u32[]{:S(2)}, u32[]{:S(2)}) collective-permute-start(bf16[10,32,256]{2,1,0:T(8,128)(2,1)S(1)} %copy-done.44), channel_id=1, source_target_pairs={{0,1},{1,0},{2,3},{3,2},{4,5},{5,4},{6,7},{7,6},{8,9},{9,8},{10,11... | collective-permute-start | bytes 491528 | tf_op jit(solution)/shard_map/ppermute | solution.py:452
  257.7 21.3 %collective-permute-start.31 = (bf16[10,32,256]{2,1,0:T(8,128)(2,1)S(1)}, bf16[10,32,256]{2,1,0:T(8,128)(2,1)S(1)}, u32[]{:S(2)}, u32[]{:S(2)}) collective-permute-start(bf16[10,32,256]{2,1,0:T(8,128)(2,1)S(1)} %copy-done.43), channel_id=1, source_target_pairs={{0,2},{1,3},{2,0},{3,1},{4,6},{5,7},{6,4},{7,5},{8,10},{9,11},{10,... | collective-permute-start | bytes 491528 | tf_op jit(solution)/shard_map/ppermute | solution.py:452
  263.7 5.0 %collective-permute-start.29 = (bf16[5,32,256]{2,1,0:T(8,128)(2,1)}, bf16[5,32,256]{2,1,0:T(8,128)(2,1)S(1)}, u32[]{:S(2)}, u32[]{:S(2)}) collective-permute-start(bf16[5,32,256]{2,1,0:T(8,128)(2,1)} %sum_end.1), channel_id=1, source_target_pairs={{0,24},{8,16},{16,8},{24,0},{1,25},{9,17},{17,9},{25,1},{2,26},{10... | collective-permute-start | bytes 245768 | tf_op jit(solution)/shard_map/ppermute | solution.py:447
  263.7 8.2 %collective-permute-start.28 = (bf16[5,32,256]{2,1,0:T(8,128)(2,1)}, bf16[5,32,256]{2,1,0:T(8,128)(2,1)S(1)}, u32[]{:S(2)}, u32[]{:S(2)}) collective-permute-start(bf16[5,32,256]{2,1,0:T(8,128)(2,1)} %sum_end.1), channel_id=1, source_target_pairs={{0,16},{8,24},{16,0},{24,8},{1,17},{9,25},{17,1},{25,9},{2,18},{10... | collective-permute-start | bytes 245768 | tf_op jit(solution)/shard_map/ppermute | solution.py:447
  265.2 8.9 %collective-permute-start.27 = (bf16[5,32,256]{2,1,0:T(8,128)(2,1)}, bf16[5,32,256]{2,1,0:T(8,128)(2,1)S(1)}, u32[]{:S(2)}, u32[]{:S(2)}) collective-permute-start(bf16[5,32,256]{2,1,0:T(8,128)(2,1)} %sum_end.1), channel_id=1, source_target_pairs={{0,8},{8,0},{16,24},{24,16},{1,9},{9,1},{17,25},{25,17},{2,10},{10... | collective-permute-start | bytes 245768 | tf_op jit(solution)/shard_map/ppermute | solution.py:447
  268.7 16.1 %collective-permute-start.32 = (bf16[10,32,256]{2,1,0:T(8,128)(2,1)S(1)}, bf16[10,32,256]{2,1,0:T(8,128)(2,1)S(1)}, u32[]{:S(2)}, u32[]{:S(2)}) collective-permute-start(bf16[10,32,256]{2,1,0:T(8,128)(2,1)S(1)} %copy-done.42), channel_id=1, source_target_pairs={{0,3},{1,2},{2,1},{3,0},{4,7},{5,6},{6,5},{7,4},{8,11},{9,10},{10,... | collective-permute-start | bytes 491528 | tf_op jit(solution)/shard_map/ppermute | solution.py:452
  271.9 21.8 %collective-permute-start.33 = (bf16[10,32,256]{2,1,0:T(8,128)(2,1)S(1)}, bf16[10,32,256]{2,1,0:T(8,128)(2,1)S(1)}, u32[]{:S(2)}, u32[]{:S(2)}) collective-permute-start(bf16[10,32,256]{2,1,0:T(8,128)(2,1)S(1)} %copy-done.41), channel_id=1, source_target_pairs={{0,4},{1,5},{2,6},{3,7},{4,0},{5,1},{6,2},{7,3},{8,12},{9,13},{10,... | collective-permute-start | bytes 491528 | tf_op jit(solution)/shard_map/ppermute | solution.py:452
  274.1 24.1 %collective-permute-start.34 = (bf16[10,32,256]{2,1,0:T(8,128)(2,1)S(1)}, bf16[10,32,256]{2,1,0:T(8,128)(2,1)S(1)}, u32[]{:S(2)}, u32[]{:S(2)}) collective-permute-start(bf16[10,32,256]{2,1,0:T(8,128)(2,1)S(1)} %copy-done.40), channel_id=1, source_target_pairs={{0,5},{1,4},{2,7},{3,6},{4,1},{5,0},{6,3},{7,2},{8,13},{9,12},{10,... | collective-permute-start | bytes 491528 | tf_op jit(solution)/shard_map/ppermute | solution.py:452
  276.7 21.5 %copy-start.2 = (bf16[10,32,256]{2,1,0:T(8,128)(2,1)}, bf16[10,32,256]{2,1,0:T(8,128)(2,1)S(1)}, u32[]{:S(2)}) copy-start(bf16[10,32,256]{2,1,0:T(8,128)(2,1)S(1)} %collective-permute-done.30.refs_1_) | copy-start | bytes 491524
  276.7 21.4 %collective-permute-start.35 = (bf16[10,32,256]{2,1,0:T(8,128)(2,1)S(1)}, bf16[10,32,256]{2,1,0:T(8,128)(2,1)S(1)}, u32[]{:S(2)}, u32[]{:S(2)}) collective-permute-start(bf16[10,32,256]{2,1,0:T(8,128)(2,1)S(1)} %copy-done.39), channel_id=1, source_target_pairs={{0,6},{1,7},{2,4},{3,5},{4,2},{5,3},{6,0},{7,1},{8,14},{9,15},{10,... | collective-permute-start | bytes 491528 | tf_op jit(solution)/shard_map/ppermute | solution.py:452
  279.0 19.2 %copy-start.3 = (bf16[10,32,256]{2,1,0:T(8,128)(2,1)}, bf16[10,32,256]{2,1,0:T(8,128)(2,1)S(1)}, u32[]{:S(2)}) copy-start(bf16[10,32,256]{2,1,0:T(8,128)(2,1)S(1)} %collective-permute-done.31.refs_2_) | copy-start | bytes 491524
  279.0 19.1 %collective-permute-start.36 = (bf16[10,32,256]{2,1,0:T(8,128)(2,1)S(1)}, bf16[10,32,256]{2,1,0:T(8,128)(2,1)S(1)}, u32[]{:S(2)}, u32[]{:S(2)}) collective-permute-start(bf16[10,32,256]{2,1,0:T(8,128)(2,1)S(1)} %copy-done.38), channel_id=1, source_target_pairs={{0,7},{1,6},{2,5},{3,4},{4,3},{5,2},{6,1},{7,0},{8,15},{9,14},{10,... | collective-permute-start | bytes 491528 | tf_op jit(solution)/shard_map/ppermute | solution.py:452
  284.8 13.4 %copy-start.4 = (bf16[10,32,256]{2,1,0:T(8,128)(2,1)}, bf16[10,32,256]{2,1,0:T(8,128)(2,1)S(1)}, u32[]{:S(2)}) copy-start(bf16[10,32,256]{2,1,0:T(8,128)(2,1)S(1)} %collective-permute-done.32.refs_3_) | copy-start | bytes 491524
  301.1 6.7 %collective-permute-start.39 = (bf16[10,32,256]{2,1,0:T(8,128)(2,1)}, bf16[10,32,256]{2,1,0:T(8,128)(2,1)S(1)}, u32[]{:S(2)}, u32[]{:S(2)}) collective-permute-start(bf16[10,32,256]{2,1,0:T(8,128)(2,1)} %sum_mid.1), channel_id=1, source_target_pairs={{0,24},{8,16},{16,8},{24,0},{1,25},{9,17},{17,9},{25,1},{2,26},{10... | collective-permute-start | bytes 491528 | tf_op jit(solution)/shard_map/ppermute | solution.py:447
  301.1 8.3 %collective-permute-start.38 = (bf16[10,32,256]{2,1,0:T(8,128)(2,1)}, bf16[10,32,256]{2,1,0:T(8,128)(2,1)S(1)}, u32[]{:S(2)}, u32[]{:S(2)}) collective-permute-start(bf16[10,32,256]{2,1,0:T(8,128)(2,1)} %sum_mid.1), channel_id=1, source_target_pairs={{0,16},{8,24},{16,0},{24,8},{1,17},{9,25},{17,1},{25,9},{2,18},{10... | collective-permute-start | bytes 491528 | tf_op jit(solution)/shard_map/ppermute | solution.py:447
  301.7 7.8 %collective-permute-start.37 = (bf16[10,32,256]{2,1,0:T(8,128)(2,1)}, bf16[10,32,256]{2,1,0:T(8,128)(2,1)S(1)}, u32[]{:S(2)}, u32[]{:S(2)}) collective-permute-start(bf16[10,32,256]{2,1,0:T(8,128)(2,1)} %sum_mid.1), channel_id=1, source_target_pairs={{0,8},{8,0},{16,24},{24,16},{1,9},{9,1},{17,25},{25,17},{2,10},{10... | collective-permute-start | bytes 491528 | tf_op jit(solution)/shard_map/ppermute | solution.py:447
  (26 other events, 57.0 us)

commit v2 on v1

v2 whole, which is shorter than its diff:
```python
import functools
import jax
import jax.numpy as jnp
from jax import lax
from jax.experimental import pallas as pl
from jax.experimental.pallas import tpu as pltpu
from jax.sharding import PartitionSpec as P

F32 = jnp.float32
BF16 = jnp.bfloat16
WIDTH = 256
UNIT = 16
TILE = 1920
CHUNK = 640
PARTS = TILE // CHUNK
HEAD_CHUNK = 384
SPLIT = 4
K0 = 2 * 0.7978845608028654
K1 = 8 * 0.7978845608028654 * 0.044715


def mm(a, b):
    return lax.dot_general(a, b, (((1,), (0,)), ((), ())), preferred_element_type=F32)


def mm_nt(a, b):
    return lax.dot_general(a, b, (((1,), (1,)), ((), ())), preferred_element_type=F32)


def mm_tn(a, b):
    return lax.dot_general(a, b, (((0,), (0,)), ((), ())), preferred_element_type=F32)


def norm_gelu(s, gain8, gain_slope, shift_half):
    mean = jnp.sum(s, axis=1, keepdims=True) * (1.0 / WIDTH)
    center = s - mean
    r = lax.rsqrt(jnp.sum(center * center, axis=1, keepdims=True) + WIDTH * 1e-5)
    n = center * r
    h = n * gain8 + shift_half
    y = h * h
    t = jnp.tanh(h * (K0 + K1 * y))
    e1 = 1.0 + t
    bend = (h * (y + K0 / (3 * K1))) * (1.0 - t)
    slope = (e1 * gain_slope) * (1.0 / (3 * K1) + bend)
    return h * e1, n.astype(BF16), slope.astype(BF16), jnp.broadcast_to(r, (UNIT, 128))


def scales(vec_ref, at, layers):
    gain = vec_ref[pl.ds(at, 1), :]
    return gain * 8.0, gain * (8.0 * 3 * K1), vec_ref[pl.ds(at + layers, 1), :] * 0.5


def norm_back(da, slope, n, r):
    w = da * slope.astype(F32)
    m1 = jnp.sum(w, axis=1, keepdims=True) * (1.0 / WIDTH)
    w16 = w.astype(BF16)
    wn = w16 * n
    wide = (wn[:, 0:128] + wn[:, 128:256]).astype(F32)
    m2 = jnp.sum(wide, axis=1, keepdims=True)
    m1 = jnp.broadcast_to(m1, (UNIT, 128)).astype(BF16)
    m2 = jnp.broadcast_to(m2, (UNIT, 128)).astype(BF16)
    halves = [
        (w[:, k:k + 128] - (m1 + n[:, k:k + 128] * m2).astype(F32)) * r for k in (0, 128)
    ]
    return jnp.concatenate(halves, axis=1), w, wn


def rows_of(c):
    return pl.multiple_of(c * CHUNK, UNIT)


def activate(base, s_ref, save, i, scale):
    act_ref, n_ref, slope_ref, r_ref = save
    for u in range(0, CHUNK, UNIT):
        rows = pl.ds(base + u, UNIT)
        act, n, slope, r = norm_gelu(s_ref[rows, :], *scale)
        act_ref[i, rows, :] = act.astype(BF16)
        n_ref[i, rows, :] = n
        slope_ref[i, rows, :] = slope
        r_ref[i, rows, :] = r


def forward_layers(first, last, layers, s_ref, save, vec_ref, w_ref, w_at, save_at):
    act_ref = save[0]

    def product(t):
        i, c = first + lax.div(t, PARTS), lax.rem(t, PARTS)
        return mm(act_ref[i - save_at, pl.ds(rows_of(c), CHUNK), :], w_ref[i - w_at])

    def activation(t):
        i, c = first + lax.div(t, PARTS), lax.rem(t, PARTS)
        activate(rows_of(c), s_ref, save, i - save_at, scales(vec_ref, 7 + i, layers))

    def residual(t, out):
        i, c = first + lax.div(t, PARTS), lax.rem(t, PARTS)
        bias = vec_ref[pl.ds(7 + 2 * layers + i, 1), :]
        for u in range(0, CHUNK, UNIT):
            rows = pl.ds(rows_of(c) + u, UNIT)
            s_ref[rows, :] = s_ref[rows, :] + (out[u:u + UNIT, :] + bias)

    def body(t, carry):
        out = product(t - 1)
        activation(t)
        residual(t - 1, out)
        return carry

    steps = (last - first) * PARTS
    activation(jnp.int32(0))
    lax.fori_loop(1, steps, body, 0)
    end = jnp.int32(steps - 1)
    residual(end, product(end))


def column_sums(parts):
    total = parts[0]
    for part in parts[1:]:
        total = total + part
    return total.astype(F32)


GROUP = 4


def fold(x):
    return jnp.sum(x, axis=0, keepdims=True)


def backward_layers(first, last, layers, s_ref, low_ref, da_ref, save, w_ref, w_at, save_at, gw_ref, gv_ref, g_at):
    act_ref, n_ref, slope_ref, r_ref = save
    steps = (last - first) * PARTS

    def place(t):
        return last - 1 - lax.div(t, PARTS), rows_of(lax.rem(t, PARTS))

    def product(t):
        i, base = place(t)
        return mm_nt(low_ref[pl.ds(base, CHUNK), :], w_ref[i - w_at])

    def body(t, carry):
        i, base = place(t)
        following = product(jnp.minimum(t + 1, steps - 1))
        gw_ref[i - g_at] += mm_tn(act_ref[i - save_at, pl.ds(base, CHUNK), :], low_ref[pl.ds(base, CHUNK), :])
        zero = jnp.zeros((UNIT, WIDTH), F32)
        shift, gain, bias = zero, zero, zero
        held = []
        for u in range(0, CHUNK, UNIT):
            rows = pl.ds(base + u, UNIT)
            at = (i - save_at, rows, slice(None))
            d_in, wf, wn = norm_back(da_ref[u:u + UNIT, :], slope_ref[at], n_ref[at], r_ref[at])
            shift = shift + wf
            held.append(wn)
            if len(held) == GROUP:
                gain = gain + column_sums(held)
                held = []
            ds = s_ref[rows, :]
            bias = bias + ds
            ds = ds + d_in
            s_ref[rows, :] = ds
            low_ref[rows, :] = ds.astype(BF16)
        da_ref[...] = following
        for k, x in enumerate((gain, shift, bias)):
            gv_ref[pl.ds(7 + k * layers + i, 1), :] += fold(x)
        return carry

    da_ref[...] = product(jnp.int32(0))
    lax.fori_loop(0, steps, body, 0)


def cross(logits, target, mask, lanes):
    top = functools.reduce(jnp.maximum, logits)
    shifted = [x - jnp.max(top, axis=1, keepdims=True) for x in logits]
    expon = [jnp.exp(x) for x in shifted]
    total = jnp.sum(functools.reduce(jnp.add, expon), axis=1, keepdims=True)
    weight = mask * (1.0 / total)
    hits = jnp.zeros_like(mask)
    grads = []
    for x, e, lane in zip(shifted, expon, lanes):
        hit = lane == target
        hits = jnp.where(hit, x, hits)
        grads.append(e * weight - jnp.where(hit, mask, 0.0))
    return jnp.log(total), hits, grads


def heads_chunk(c, nq, s_ref, low_ref, col_ref, w_ref, w_at, hb_ref, latents_ref, value_ref, chance_ref, dlog_ref, wide_ref, loss_ref, ghb_ref):
    size = HEAD_CHUNK
    base = pl.multiple_of(c * size, 128)
    span = pl.ds(base, size)
    lane = lax.broadcasted_iota(jnp.int32, (1, 128), 1).astype(F32)
    lanes = [lane + 128.0 * k for k in range(5)]
    bias = [hb_ref[0:1, k * 128:(k + 1) * 128] for k in range(6)]
    lat = s_ref[span, :].astype(BF16)
    latents_ref[span, :] = lat
    full = [mm(lat, w_ref[w_at + k]) for k in range(3)]
    loss = jnp.zeros((UNIT, 128), F32)
    sums = [jnp.zeros((UNIT, 128), F32)] * 6
    for u in range(0, size, UNIT):
        rows = pl.ds(base + u, UNIT)
        logits = [full[k // 2][u:u + UNIT, (k % 2) * 128:(k % 2 + 1) * 128] + bias[k] for k in range(6)]
        for k in range(6):
            wide_ref[k, u:u + UNIT, :] = logits[k].astype(BF16)
        bins, codes, mask = (col_ref[k, rows, :] for k in range(3))
        log_v, at_v, grad_v = cross(logits[:5], bins, mask, lanes)
        log_c, at_c, grad_c = cross(logits[5:], codes, mask, lanes[:1])
        loss = loss + mask * ((log_v + log_c) * (1.0 / 128) - (at_v + at_c))
        for k, grad in enumerate(grad_v + grad_c):
            sums[k] = sums[k] + grad
            dlog_ref[k // 2, rows, (k % 2) * 128:(k % 2 + 1) * 128] = grad.astype(BF16)
    loss_ref[...] += loss
    for k in range(6):
        ghb_ref[:, k * 128:(k + 1) * 128] += sums[k]
    for k in range(5):
        height = min(128, nq - k * 128)
        value_ref[k * 128:k * 128 + height, span] = wide_ref[k].T[0:height, :]
    chance_ref[:, span] = wide_ref[5].T[0:chance_ref.shape[0], :]
    ds = mm_nt(dlog_ref[0, span, :], w_ref[w_at])
    ds += mm_nt(dlog_ref[1, span, :], w_ref[w_at + 1])
    ds += mm_nt(dlog_ref[2, span, :], w_ref[w_at + 2])
    s_ref[span, :] = ds
    low_ref[span, :] = ds.astype(BF16)


def spread_columns(ints, col_ref):
    k = lax.broadcasted_iota(jnp.int32, (16, 384), 0)
    j = lax.broadcasted_iota(jnp.int32, (16, 384), 1) >> 7
    pick = jnp.where((j == 0) & (k == 1), 32.0, 0.0) + jnp.where(
        ((j == 0) & (k == 2)) | ((j == 1) & (k == 3)) | ((j == 2) & (k == 4)), 1.0, 0.0
    )
    cols = mm_tn(ints, pick.astype(BF16))
    for c in range(3):
        col_ref[c] = cols[:, c * 128:(c + 1) * 128]


def unpack_vec(w, vec_ref):
    vec_ref[...] = w[:, 0:128].astype(F32).T


def moves_hot(ints):
    rows = lax.broadcasted_iota(jnp.int32, ints.shape, 0).astype(F32)
    return jnp.where((rows == ints[0:1, :].astype(F32)) | (rows == 4.0), 1.0, 0.0).astype(BF16)


def table_of(vec_ref):
    rows = lax.broadcasted_iota(jnp.int32, (16, WIDTH), 0)
    return jnp.where(rows < 5, vec_ref[0:16, :], 0.0).astype(BF16)


def stem_forward(latent_ref, hot_ref, vec_ref, w, s_ref, n_ref, slope_ref, r_ref, n_at):
    table = table_of(vec_ref)
    scale = scales(vec_ref, 5, 1)

    def chunk(c, carry):
        base = rows_of(c)
        span = pl.ds(base, CHUNK)
        pre = mm(latent_ref[span, :], w) + mm(hot_ref[span, :], table)
        for u in range(0, CHUNK, UNIT):
            rows = pl.ds(base + u, UNIT)
            act, n, slope, r = norm_gelu(pre[u:u + UNIT, :], *scale)
            s_ref[rows, :] = act
            n_ref[n_at, rows, :] = n
            slope_ref[n_at, rows, :] = slope
            r_ref[n_at, rows, :] = r
        return carry

    lax.fori_loop(0, PARTS, chunk, 0)


def stem_backward(latent_ref, hot_ref, s_ref, low_ref, n_ref, slope_ref, r_ref, n_at, w, lgrad_ref, gw_ref, g_at, gv_ref):
    def chunk(c, carry):
        base = rows_of(c)
        span = pl.ds(base, CHUNK)
        shift = jnp.zeros((UNIT, WIDTH), F32)
        gain = shift
        held = []
        for u in range(0, CHUNK, UNIT):
            rows = pl.ds(base + u, UNIT)
            d_in, wf, wn = norm_back(s_ref[rows, :], slope_ref[n_at, rows, :], n_ref[n_at, rows, :], r_ref[n_at, rows, :])
            shift = shift + wf
            held.append(wn)
            if len(held) == GROUP:
                gain = gain + column_sums(held)
                held = []
            low_ref[rows, :] = d_in.astype(BF16)
        low = low_ref[span, :]
        lgrad_ref[span, :] = mm_nt(low, w).astype(BF16)
        gw_ref[g_at] += mm_tn(latent_ref[span, :], low)
        gv_ref[0:16, :] += mm_tn(hot_ref[span, :], low)
        gv_ref[5:6, :] += fold(gain)
        gv_ref[6:7, :] += fold(shift)
        return carry

    lax.fori_loop(0, PARTS, chunk, 0)


def clean_latent(latent_ref, lat_ref, rows_dev):
    lat_ref[...] = latent_ref[...]
    steps = -(-rows_dev // TILE)
    tail = rows_dev - (steps - 1) * TILE
    if tail < TILE:
        @pl.when(pl.program_id(0) == steps - 1)
        def _():
            lat_ref[tail:TILE, :] = jnp.zeros((TILE - tail, WIDTH), BF16)


def split_low(x):
    high = x.astype(BF16)
    return high, (x - high.astype(F32)).astype(BF16)


def join_pieces(pieces_ref, w_ref):
    rows = pieces_ref.shape[2]
    for f in range(pieces_ref.shape[0]):
        for m in range(pieces_ref.shape[1]):
            w_ref[m, f * rows:(f + 1) * rows, :] = pieces_ref[f, m]


def cut_pieces(out_ref, m, source_ref, at):
    rows = out_ref.shape[2]
    for f in range(out_ref.shape[0]):
        out_ref[f, m] = source_ref[at, f * rows:(f + 1) * rows, :].astype(BF16)


def first_kernel(layers, rows_dev, latent_ref, ints_ref, front_ref, act_ref, n_ref, slope_ref, r_ref, s_ref, vec_ref, w_ref, lat_ref, hot_ref):
    @pl.when(pl.program_id(0) == 0)
    def _():
        join_pieces(front_ref, w_ref)
        unpack_vec(w_ref[0], vec_ref)

    clean_latent(latent_ref, lat_ref, rows_dev)
    hot_ref[...] = moves_hot(ints_ref[0]).T
    stem_forward(lat_ref, hot_ref, vec_ref, w_ref[1], s_ref, n_ref, slope_ref, r_ref, SPLIT)
    forward_layers(0, SPLIT, layers, s_ref, (act_ref, n_ref, slope_ref, r_ref), vec_ref, w_ref, -2, 0)


def middle_kernel(
    layers, nq, s_in_ref, ints_ref, vec_ref, hb_ref, w_ref,
    latents_ref, value_ref, chance_ref, ds_ref, gv_ref, rep_ref, out_ref,
    col_ref, act_ref, n_ref, slope_ref, r_ref, low_ref, da_ref, dlog_ref, wide_ref, gw_ref, ghb_ref, loss_ref,
):
    blocks = layers - SPLIT
    step = pl.program_id(0)

    @pl.when(step == 0)
    def _():
        for ref in (gw_ref, gv_ref, ghb_ref, loss_ref):
            ref[...] = jnp.zeros_like(ref)

    spread_columns(ints_ref[0], col_ref)
    ds_ref[...] = s_in_ref[...]
    save = (act_ref, n_ref, slope_ref, r_ref)
    forward_layers(SPLIT, layers, layers, ds_ref, save, vec_ref, w_ref, SPLIT, SPLIT)

    def head(c, carry):
        heads_chunk(c, nq, ds_ref, low_ref, col_ref, w_ref, blocks, hb_ref, latents_ref, value_ref, chance_ref, dlog_ref, wide_ref, loss_ref, ghb_ref)
        return carry

    lax.fori_loop(0, TILE // HEAD_CHUNK, head, 0)

    def head_grad(k, carry):
        gw_ref[blocks + k] += mm_tn(latents_ref[...], dlog_ref[k])
        return carry

    lax.fori_loop(0, 3, head_grad, 0)
    backward_layers(SPLIT, layers, layers, ds_ref, low_ref, da_ref, save, w_ref, SPLIT, SPLIT, gw_ref, gv_ref, SPLIT)

    @pl.when(step == pl.num_programs(0) - 1)
    def _():
        def put(m, carry):
            cut_pieces(out_ref, m, gw_ref, m)
            return carry

        lax.fori_loop(0, blocks + 3, put, 0)
        sums = fold(ghb_ref[...])
        row = lax.broadcasted_iota(jnp.int32, (8, WIDTH), 0)
        total = jnp.where(row == 3, jnp.concatenate([fold(loss_ref[...]), jnp.zeros((1, 128), F32)], axis=1), 0.0)
        for k in range(3):
            total = jnp.where(row == k, sums[:, k * 256:(k + 1) * 256], total)
        rep_ref[...] = total


def last_kernel(
    layers, rows_dev, latent_ref, ints_ref, ds_in_ref, act_ref, n_ref, slope_ref, r_ref, front_ref, gv_in_ref,
    lgrad_ref, out_ref, w_ref, lat_ref, hot_ref, ds_ref, low_ref, da_ref, gw_ref, gv_ref,
):
    step = pl.program_id(0)

    @pl.when(step == 0)
    def _():
        join_pieces(front_ref, w_ref)
        gw_ref[...] = jnp.zeros_like(gw_ref)
        gv_ref[...] = gv_in_ref[...]

    clean_latent(latent_ref, lat_ref, rows_dev)
    hot_ref[...] = moves_hot(ints_ref[0]).T
    ds_ref[...] = ds_in_ref[...]
    low_ref[...] = ds_in_ref[...].astype(BF16)
    backward_layers(0, SPLIT, layers, ds_ref, low_ref, da_ref, (act_ref, n_ref, slope_ref, r_ref), w_ref, -2, 0, gw_ref, gv_ref, -1)
    stem_backward(lat_ref, hot_ref, ds_ref, low_ref, n_ref, slope_ref, r_ref, SPLIT, w_ref[1], lgrad_ref, gw_ref, 0, gv_ref)

    @pl.when(step == pl.num_programs(0) - 1)
    def _():
        for m in range(SPLIT + 1):
            cut_pieces(out_ref, m, gw_ref, m)
        wide = jnp.concatenate([gv_ref[...], jnp.zeros((128 - gv_ref.shape[0], WIDTH), F32)], axis=0).T
        high, low = split_low(wide)
        gw_ref[0] = jnp.concatenate([high, low], axis=1).astype(F32)
        cut_pieces(out_ref, SPLIT + 1, gw_ref, 0)


def sum_kernel(split, in_ref, out_ref):
    for m in range(out_ref.shape[0]):
        total = in_ref[0, m].astype(F32)
        for f in range(1, in_ref.shape[0]):
            total = total + in_ref[f, m].astype(F32)
        if m == split:
            high, low = split_low(total[:, 0:128] + total[:, 128:256])
            out_ref[m] = jnp.concatenate([high, low], axis=1)
        else:
            out_ref[m] = total.astype(BF16)


VMEM = pl.BlockSpec(memory_space=pltpu.VMEM)


def params(mib):
    return pltpu.CompilerParams(vmem_limit_bytes=mib << 20)


def tiled(shape, dim):
    block = shape[:dim] + (TILE,) + shape[dim + 1:]
    return pl.BlockSpec(block, lambda i: (0,) * dim + (i,) + (0,) * (len(shape) - dim - 1))


def whole(shape):
    return pl.BlockSpec(shape, lambda i: (0,) * len(shape))


def once(shape):
    return pl.BlockSpec(shape, lambda i: (0,) * len(shape), pipeline_mode=pl.Buffered(1))


def struct(shape, dtype):
    return jax.ShapeDtypeStruct(shape, dtype)


def exchange(x, axis, size):
    return [lax.ppermute(x, axis, [(i, i ^ k) for i in range(size)]) for k in range(1, size)]


def per_device(
    latent, actions, value_bins, chance_codes, step_mask, stem_weight, action_table, stem_bias, stem_gain, stem_shift,
    block_weight, block_gain, block_shift, block_bias, value_weight, value_bias, chance_weight, chance_bias,
):
    n_dp, n_fsdp = lax.axis_size("dp"), lax.axis_size("fsdp")
    rows_dev = latent.shape[0]
    layers, shard = block_weight.shape[0], block_weight.shape[1]
    nq, nc = value_weight.shape[1], chance_weight.shape[1]
    moves = action_table.shape[0]
    steps = -(-rows_dev // TILE)
    padded = steps * TILE
    fast = shard % 16 == 0 and n_dp & (n_dp - 1) == 0

    vectors = jnp.concatenate(
        [action_table, stem_bias[None], stem_gain[None], stem_shift[None], block_gain, block_shift, block_bias], axis=0
    )
    vectors = jnp.pad(vectors.T, ((0, 0), (0, WIDTH - vectors.shape[0])))
    head = jnp.concatenate(
        [value_weight, jnp.zeros((shard, 640 - nq), BF16), chance_weight, jnp.zeros((shard, 128 - nc), BF16)], axis=1
    )
    head = jnp.stack([head[:, k * WIDTH:(k + 1) * WIDTH] for k in range(3)])
    front = jnp.concatenate([vectors[None], stem_weight[None], block_weight[:SPLIT]], axis=0)
    back = jnp.concatenate([block_weight[SPLIT:], head], axis=0)
    if fast:
        pieces, piece_rows = n_fsdp, shard
        w_front = lax.all_to_all(jnp.broadcast_to(front[None], (n_fsdp,) + front.shape), "fsdp", 0, 0)
    else:
        pieces, piece_rows = 1, WIDTH
        w_front = lax.all_gather(front, "fsdp", axis=1, tiled=True)[None]
    w_back = lax.all_gather(back, "fsdp", axis=1, tiled=True)

    ints = jnp.stack([actions, value_bins >> 5, value_bins & 31, chance_codes, step_mask])
    ints = jnp.pad(ints.astype(BF16), ((0, 11), (0, padded - rows_dev))).reshape(16, steps, TILE).transpose(1, 0, 2)
    ints_spec = pl.BlockSpec((1, 16, TILE), lambda i: (i, 0, 0))
    low = lambda n: jnp.full((n,), -1e30, F32)
    head_bias = jnp.concatenate([value_bias.astype(F32), low(640 - nq), chance_bias.astype(F32), low(128 - nc)])
    head_bias = jnp.broadcast_to(head_bias[None], (8, 3 * WIDTH))

    saved = [
        struct((SPLIT, padded, WIDTH), BF16),
        struct((SPLIT + 1, padded, WIDTH), BF16),
        struct((SPLIT + 1, padded, WIDTH), BF16),
        struct((SPLIT + 1, padded, 128), F32),
    ]
    stream = struct((padded, WIDTH), F32)
    scratch = pltpu.VMEM
    front_shape = w_front.shape[1:2] + (WIDTH, WIDTH)
    *held, s_mid, vec = pl.pallas_call(
        functools.partial(first_kernel, layers, rows_dev),
        grid=(steps,),
        in_specs=[tiled((rows_dev, WIDTH), 0), ints_spec, once(w_front.shape)],
        out_specs=[tiled(x.shape, 1) for x in saved] + [tiled(stream.shape, 0), whole((128, WIDTH))],
        out_shape=saved + [stream, struct((128, WIDTH), F32)],
        scratch_shapes=[scratch(front_shape, BF16), scratch((TILE, WIDTH), BF16), scratch((TILE, 16), BF16)],
        compiler_params=params(62),
        cost_estimate=pl.CostEstimate(flops=rows_dev * WIDTH * WIDTH * 200, bytes_accessed=60 << 20, transcendentals=0),
        name="first",
    )(latent, ints, w_front)

    blocks = layers - SPLIT
    latents, value_logits, chance_logits, ds_mid, gv_mid, rep, parts_mid = pl.pallas_call(
        functools.partial(middle_kernel, layers, nq),
        grid=(steps,),
        in_specs=[tiled(stream.shape, 0), ints_spec, once(vec.shape), once(head_bias.shape), once(w_back.shape)],
        out_specs=[
            tiled((rows_dev, WIDTH), 0), tiled((nq, rows_dev), 1), tiled((nc, rows_dev), 1), tiled(stream.shape, 0),
            whole((48, WIDTH)), whole((8, WIDTH)), whole((pieces, blocks + 3, piece_rows, WIDTH)),
        ],
        out_shape=[
            struct((rows_dev, WIDTH), BF16), struct((nq, rows_dev), BF16), struct((nc, rows_dev), BF16), stream,
            struct((48, WIDTH), F32), struct((8, WIDTH), F32), struct((pieces, blocks + 3, piece_rows, WIDTH), BF16),
        ],
        scratch_shapes=[
            scratch((3, TILE, 128), F32),
            scratch((blocks, TILE, WIDTH), BF16),
            scratch((blocks, TILE, WIDTH), BF16),
            scratch((blocks, TILE, WIDTH), BF16),
            scratch((blocks, TILE, 128), F32),
            scratch((TILE, WIDTH), BF16),
            scratch((CHUNK, WIDTH), F32),
            scratch((3, TILE, WIDTH), BF16),
            scratch((6, HEAD_CHUNK, 128), BF16),
            scratch((blocks + 3, WIDTH, WIDTH), F32),
            scratch((UNIT, 3 * WIDTH), F32),
            scratch((UNIT, 128), F32),
        ],
        compiler_params=params(62),
        cost_estimate=pl.CostEstimate(flops=rows_dev * WIDTH * WIDTH * 600, bytes_accessed=40 << 20, transcendentals=0),
        name="middle",
    )(s_mid, ints, vec, head_bias, w_back)

    latent_grad, parts_end = pl.pallas_call(
        functools.partial(last_kernel, layers, rows_dev),
        grid=(steps,),
        in_specs=[tiled((rows_dev, WIDTH), 0), ints_spec, tiled(stream.shape, 0)]
        + [tiled(x.shape, 1) for x in saved]
        + [once(w_front.shape), once((48, WIDTH))],
        out_specs=[tiled((rows_dev, WIDTH), 0), whole((pieces, SPLIT + 2, piece_rows, WIDTH))],
        out_shape=[struct((rows_dev, WIDTH), BF16), struct((pieces, SPLIT + 2, piece_rows, WIDTH), BF16)],
        scratch_shapes=[
            scratch(front_shape, BF16),
            scratch((TILE, WIDTH), BF16),
            scratch((TILE, 16), BF16),
            scratch((TILE, WIDTH), F32),
            scratch((TILE, WIDTH), BF16),
            scratch((CHUNK, WIDTH), F32),
            scratch((SPLIT + 1, WIDTH, WIDTH), F32),
            scratch((48, WIDTH), F32),
        ],
        compiler_params=params(62),
        cost_estimate=pl.CostEstimate(flops=rows_dev * WIDTH * WIDTH * 150, bytes_accessed=60 << 20, transcendentals=0),
        name="last",
    )(latent, ints, ds_mid, *held, w_front, gv_mid)

    rep = lax.psum(rep, ("dp", "fsdp"))
    if fast:
        def reduce(parts, split, name):
            got = lax.all_to_all(parts, "fsdp", 0, 0)
            mine = pl.pallas_call(
                functools.partial(sum_kernel, split), in_specs=[VMEM], out_specs=VMEM,
                out_shape=struct(parts.shape[1:], BF16), name=name,
            )(got)
            return sum((y.astype(F32) for y in exchange(mine, "dp", n_dp)), mine.astype(F32))

        mid, end = reduce(parts_mid, -1, "sum_mid"), reduce(parts_end, SPLIT + 1, "sum_end")
    else:
        scatter = lambda x: lax.psum(
            lax.psum_scatter(x[0], "fsdp", scatter_dimension=1, tiled=True).astype(F32), "dp"
        )
        mid, end = scatter(parts_mid), scatter(parts_end)

    scale = 1.0 / (rows_dev * n_dp * n_fsdp)
    rep = rep * scale
    head_grad = jnp.concatenate([mid[blocks + k] for k in range(3)], axis=1) * scale
    small = (end[SPLIT + 1, :, 0:128] + end[SPLIT + 1, :, 128:256]).T * scale
    bias_sums = rep[0:3].reshape(3 * WIDTH)
    at = moves + 3
    gain = block_gain.astype(F32)
    return (
        latents,
        value_logits.T,
        chance_logits.T,
        jnp.sum(rep[3]),
        latent_grad,
        end[0] * scale,
        small[0:moves],
        small[moves],
        small[moves + 1] / stem_gain.astype(F32),
        small[moves + 2] / (16.0 * stem_gain.astype(F32)),
        jnp.concatenate([end[1:SPLIT + 1], mid[:blocks]], axis=0) * scale,
        small[at:at + layers] / gain,
        small[at + layers:at + 2 * layers] / (16.0 * gain),
        small[at + 2 * layers:at + 3 * layers],
        head_grad[:, 0:nq],
        bias_sums[0:nq],
        head_grad[:, 640:640 + nc],
        bias_sums[640:640 + nc],
    )


def solution(mesh):
    placed = (
        P(("dp", "fsdp"), None),
        P(("dp", "fsdp")),
        P(("dp", "fsdp")),
        P(("dp", "fsdp")),
        P(("dp", "fsdp")),
        P("fsdp", None),
        P(None, "fsdp"),
        P("fsdp"),
        P("fsdp"),
        P("fsdp"),
        P(None, "fsdp", None),
        P(None, "fsdp"),
        P(None, "fsdp"),
        P(None, "fsdp"),
        P("fsdp", None),
        P(),
        P("fsdp", None),
        P(),
    )
    return jax.shard_map(
        per_device,
        mesh=mesh,
        in_specs=placed,
        out_specs=(
            P(("dp", "fsdp"), None),
            P(("dp", "fsdp"), None),
            P(("dp", "fsdp"), None),
            P(),
            P(("dp", "fsdp"), None),
            P("fsdp", None),
            P(None, "fsdp"),
            P("fsdp"),
            P("fsdp"),
            P("fsdp"),
            P(None, "fsdp", None),
            P(None, "fsdp"),
            P(None, "fsdp"),
            P(None, "fsdp"),
            P("fsdp", None),
            P(),
            P("fsdp", None),
            P(),
        ),
        check_vma=False,
    )
```

time: 318 us -> 338 us (1.063); the launches traced: 313 us -> 337 us
  blocking collectives: 0 us -> 72.2 us
  starting transfers between devices: 64.8 us -> 15.2 us
  local copies, waits for them, and re-layouts: 30.6 us -> 14.8 us
  between operations: 1.31 us -> 14.2 us
  Pallas kernels: 174 us -> 182 us
    psum x0 -> x1, blocking collectives: none -> 48.3 us  [per_device(): rep = lax.psum(rep, ('dp', 'fsdp'))]
    ppermute x26 -> x6, starting transfers between devices: 41 us -> 4.32 us  [exchange(): lax.ppermute(x, axis, [(i, i ^ k) for i in range(size)])]
    all_to_all x0 -> x1, blocking collectives: none -> 23.9 us  [reduce(): got = lax.all_to_all(parts, 'fsdp', 0, 0)]
    ppermute x14 -> x0, starting transfers between devices: 23.8 us -> none  [send_pieces(): lax.ppermute(pieces[k], axis, [(i, i ^ k) for i in range(size)])]
    ppermute x14 -> x0, waiting for transfers between devices: 18.6 us -> none  [send_pieces(): lax.ppermute(pieces[k], axis, [(i, i ^ k) for i in range(size)])]
    unnamed x110 -> x17, local copies, waits for them, and re-layouts: 21.9 us -> 4.72 us
    all_to_all x0 -> x2, waiting for transfers between devices: none -> 15.5 us  [the longest x1 15.5 us: per_device(): lax.all_to_all(jnp.broadcast_to(front[None], (n_fsdp,) + front.shape), 'f...]
    all_to_all x0 -> x2, starting transfers between devices: none -> 10.8 us  [the longest x1 7.25 us: per_device(): lax.all_to_all(jnp.broadcast_to(front[None], (n_fsdp,) + front.shape), 'f...]
  transfers between devices with their start and end apart: 40 -> 9, of which waited for: 10 -> 5; matrix products, arithmetic and copies ran while one was open for 8% -> 4% of each run, Pallas kernels for 20% -> 13%
where the time goes in v2:
time: 338 us; the launch traced here: 337 us
  Pallas kernels  182 us (54%)
  blocking collectives  72.2 us (21%)
  waiting for transfers between devices  27.1 us (8%)
  starting transfers between devices  15.2 us (4%)
  local copies, waits for them, and re-layouts  14.8 us (4%)
  between operations  14.2 us (4%)
  other arithmetic  11.1 us (3%)
    pallas_call x1, Pallas kernels, per_device(): pl.pallas_call(functools.partial(middle_kernel, layers, nq), grid=(steps,...  100 us
    psum x1, blocking collectives, per_device(): rep = lax.psum(rep, ('dp', 'fsdp'))  48.3 us
    pallas_call x1, Pallas kernels, per_device(): pl.pallas_call(functools.partial(first_kernel, layers, rows_dev), grid=(s...  42.7 us
    pallas_call x1, Pallas kernels, per_device(): pl.pallas_call(functools.partial(last_kernel, layers, rows_dev), grid=(st...  35.1 us
    all_to_all x1, blocking collectives, reduce(): got = lax.all_to_all(parts, 'fsdp', 0, 0)  23.9 us
    all_to_all x1, waiting for transfers between devices, per_device(): lax.all_to_all(jnp.broadcast_to(front[None], (n_fsdp,) + front.shape), 'f...  15.5 us
    ppermute x6, waiting for transfers between devices, exchange(): lax.ppermute(x, axis, [(i, i ^ k) for i in range(size)])  11.5 us
    all_to_all x1, starting transfers between devices, per_device(): lax.all_to_all(jnp.broadcast_to(front[None], (n_fsdp,) + front.shape), 'f...  7.25 us
  transfers between devices with their start and end apart: 9, of which 5 were waited for; matrix products, arithmetic and copies ran while one was open for 4% of the time, Pallas kernels for 13%

profile of v2, /device:TPU:0, one launch (start us, length us, event | category | flops | bytes accessed | tf_op | source)
XLA Modules:
  0.0 336.5 jit_solution(5273362467675183521)
XLA Ops:
  7.2 3.1 concatenate.21
  10.3 0.1 copy.43
  10.4 0.9 slice.78
  11.2 0.7 pad_maximum_fusion.1
  11.9 1.0 broadcast_in_dim.44
  12.9 7.3 %all-to-all-start = ((bf16[8,6,32,256]{3,2,1,0:T(8,128)(2,1)}), bf16[8,6,32,256]{3,2,1,0:T(8,128)(2,1)S(1)}, u32[]{:S(2)}, u32[]{:S(2)}) async-start(bf16[8,6,32,256]{3,2,1,0:T(8,128)(2,1)} %broadcast_in_dim.44), calls=%async_computation | async-start | bytes 1572864 | tf_op jit(solution)/shard_map/all_to_all | solution.py:474
  20.2 0.0 all-gather.2.cloned.1.call-start
  20.2 0.9 slice.79
  21.1 0.1 pad_slice_fusion
  21.2 0.8 slice_bitcast_fusion.4
  22.0 0.7 pad_maximum_fusion
  22.7 0.0 all-gather.2.cloned.1.call-update
  22.7 0.7 and_convert_fusion
  23.5 0.7 convert.20
  24.2 0.7 convert.23
  25.0 0.7 convert.24
  25.8 0.2 stack.38
  26.0 0.7 copy.51
  26.7 0.7 convert_element_type.42
  27.4 0.7 convert_element_type.43
  28.0 0.1 pad_maximum_fusion.4
  28.1 15.5 %all-to-all-done.front_ref = bf16[8,6,32,256]{3,2,1,0:T(8,128)(2,1)S(1)} async-done(((bf16[8,6,32,256]{3,2,1,0:T(8,128)(2,1)}), bf16[8,6,32,256]{3,2,1,0:T(8,128)(2,1)S(1)}, u32[]{:S(2)}, u32[]{:S(2)}) %all-to-all-start) | async-done | bytes 786464 | tf_op jit(solution)/shard_map/all_to_all | solution.py:474
  43.6 0.9 copy-done.1
  44.5 42.7 %first.1 = (bf16[4,5760,256]{2,1,0:T(8,128)(2,1)}, bf16[5,5760,256]{2,1,0:T(8,128)(2,1)}, bf16[5,5760,256]{2,1,0:T(8,128)(2,1)}, f32[5,5760,128]{2,1,0:T(8,128)}...) custom-call(bf16[5696,256]{1,0:T(8,128)(2,1)} %latent_ref.3, bf16[3,16,1920]{2,1,0:T(8,128)(2,1)} %bitcast.38, ...), custom_call_target="tpu_custom_call" | custom-call | flops 74658611200 | bytes 62914560 | tf_op jit(solution)/shard_map/first/pallas_call | solution.py:496
  87.2 0.0 all-gather.2.cloned.1.call-done.w_ref
  87.2 0.6 broadcast_in_dim.47.hb_ref
  87.8 100.1 %middle.1 = (bf16[5696,256]{1,0:T(8,128)(2,1)}, bf16[601,5696]{1,0:T(8,128)(2,1)}, bf16[32,5696]{1,0:T(8,128)(2,1)}, f32[5760,256]{1,0:T(8,128)}, f32[48,256]{1,...) custom-call(f32[5760,256]{1,0:T(8,128)} %get-tuple-element.33.s_in_ref, bf16[3,16,1920]{2,1,0:T(8,128)(2,1)} %bitcast.39, ...), custom_call_target="tpu_custom_call" | custom-call | flops 223975833600 | bytes 41943040 | tf_op jit(solution)/shard_map/middle/pallas_call | solution.py:509
  188.0 0.0 copy-start.2
  188.0 0.0 copy-start.3
  188.0 35.1 %last.1 = (bf16[5696,256]{1,0:T(8,128)(2,1)}, bf16[8,6,32,256]{3,2,1,0:T(8,128)(2,1)}) custom-call(bf16[5696,256]{1,0:T(8,128)(2,1)} %latent_ref.3, bf16[3,16,1920]{2,1,0:T(8,128)(2,1)} %bitcast.40, f32[5760,256]{1,0:T(8,128)} %get-tuple-element.39.ds_in_ref, bf16[4,5760,256]{2,1,0:T(8,128)(2,1)} %get-tuple-element.40.act_ref, ...), custom_call_target="tpu_custom_call" | custom-call | flops 55993958400 | bytes 62914560 | tf_op jit(solution)/shard_map/last/pallas_call | solution.py:540
  223.1 0.0 copy-start.5
  223.2 23.9 %all_to_all.15.in_ref = bf16[8,6,32,256]{3,2,1,0:T(8,128)(2,1)} all-to-all(bf16[8,6,32,256]{3,2,1,0:T(8,128)(2,1)} %get-tuple-element.46), channel_id=1, replica_groups=mesh['dp'=4,'fsdp'=8] {'fsdp'}, dimensions={0} | all-to-all | bytes 1572864 | tf_op jit(solution)/shard_map/all_to_all | solution.py:566
  247.0 3.6 %all-to-all-start.2 = ((bf16[8,9,32,256]{3,2,1,0:T(8,128)(2,1)}), bf16[8,9,32,256]{3,2,1,0:T(8,128)(2,1)S(1)}, u32[]{:S(2)}, u32[]{:S(2)}) async-start(bf16[8,9,32,256]{3,2,1,0:T(8,128)(2,1)} %get-tuple-element.47), calls=%async_computation.2 | async-start | bytes 2359296 | tf_op jit(solution)/shard_map/all_to_all | solution.py:566
  250.6 0.1 copy.44
  250.7 48.3 %psum.7 = f32[8,256]{1,0:T(8,128)S(1)} all-reduce(f32[8,256]{1,0:T(8,128)S(1)} %copy-done.3), channel_id=1, replica_groups=mesh['dp'=4,'fsdp'=8] {'dp','fsdp'}, use_global_device_ids=true, to_apply=%region_0.1 | all-reduce | flops 2048 | bytes 16384 | tf_op jit(solution)/shard_map/psum | solution.py:563
  299.1 0.5 slice.103
  299.6 1.9 sum_end.1
  301.5 2.3 collective-permute-start.1
  303.8 0.1 collective-permute-start.2
  303.9 0.6 slice_reduce_fusion.3
  304.5 3.1 collective-permute-done.1
  307.6 1.7 collective-permute-done.2
  309.4 0.9 convert_add_fusion.1
  310.4 0.1 fusion.1
  310.4 0.7 copy.46
  311.1 0.7 copy.47
  311.8 0.7 copy.48
  312.5 0.7 copy.45
  313.1 0.7 slice_reduce_fusion
  313.8 0.6 fusion
  314.4 0.0 all-to-all-done.2.in_ref
  314.4 1.0 copy-done
  315.5 2.1 sum_mid.1
  317.6 0.1 collective-permute-start.3
  317.7 1.6 collective-permute-start.4
  319.3 0.1 collective-permute-start.5
  319.4 0.5 multiply_divide_fusion
  320.0 0.0 collective-permute-done.3
  320.0 4.6 %collective-permute-done.4 = bf16[9,32,256]{2,1,0:T(8,128)(2,1)S(1)} collective-permute-done((bf16[9,32,256]{2,1,0:T(8,128)(2,1)}, bf16[9,32,256]{2,1,0:T(8,128)(2,1)S(1)}, u32[]{:S(2)}, u32[]{:S(2)}) %collective-permute-start.4) | collective-permute-done | bytes 147488 | tf_op jit(solution)/shard_map/ppermute | solution.py:446
  324.6 2.1 collective-permute-done.5
  326.6 1.0 convert_add_fusion
  327.7 0.6 slice.122
  328.3 0.6 slice.124
  328.9 0.8 maximum_multiply_fusion
  (28 shorter events, 0.2 us)
Async XLA Ops:
  12.9 30.7 %all-to-all-start = ((bf16[8,6,32,256]{3,2,1,0:T(8,128)(2,1)}), bf16[8,6,32,256]{3,2,1,0:T(8,128)(2,1)S(1)}, u32[]{:S(2)}, u32[]{:S(2)}) async-start(bf16[8,6,32,256]{3,2,1,0:T(8,128)(2,1)} %broadcast_in_dim.44), calls=%async_computation | async-start | bytes 1572864 | tf_op jit(solution)/shard_map/all_to_all | solution.py:474
  20.2 67.1 %all-gather.2.cloned.1.call-start = ((), (), s32[]{:S(2)}) async-start(), calls=%async_computation.3 | async-start | bytes 1327104 | tf_op jit(solution)/shard_map/all_gather | solution.py:478
  43.6 0.9 copy-start.1
  188.0 62.6 %copy-start.2 = (bf16[10,32]{1,0:T(8,128)(2,1)S(1)}, bf16[10,32]{1,0:T(8,128)(2,1)}, u32[]{:S(2)}) copy-start(bf16[10,32]{1,0:T(8,128)(2,1)} %param.29) | copy-start | bytes 1924
  188.0 62.7 %copy-start.3 = (f32[8,256]{1,0:T(8,128)S(1)}, f32[8,256]{1,0:T(8,128)}, u32[]{:S(2)}) copy-start(f32[8,256]{1,0:T(8,128)} %get-tuple-element.38) | copy-start | bytes 24580
  223.1 96.3 %copy-start.5 = (bf16[32]{0:T(256)(128)(2,1)S(1)}, bf16[32]{0:T(256)(128)(2,1)}, u32[]{:S(2)}) copy-start(bf16[32]{0:T(256)(128)(2,1)} %param.26) | copy-start | bytes 196
  247.0 67.4 %all-to-all-start.2 = ((bf16[8,9,32,256]{3,2,1,0:T(8,128)(2,1)}), bf16[8,9,32,256]{3,2,1,0:T(8,128)(2,1)S(1)}, u32[]{:S(2)}, u32[]{:S(2)}) async-start(bf16[8,9,32,256]{3,2,1,0:T(8,128)(2,1)} %get-tuple-element.47), calls=%async_computation.2 | async-start | bytes 2359296 | tf_op jit(solution)/shard_map/all_to_all | solution.py:566
  299.1 30.6 %copy-start.4 = (f32[768]{0:T(1024)}, f32[768]{0:T(1024)S(1)}, u32[]{:S(2)}) copy-start(f32[768]{0:T(1024)S(1)} %reshape.50) | copy-start | bytes 9220
  301.5 3.1 collective-permute-start
  301.5 6.2 %collective-permute-start.1 = (bf16[6,32,256]{2,1,0:T(8,128)(2,1)}, bf16[6,32,256]{2,1,0:T(8,128)(2,1)S(1)}, u32[]{:S(2)}, u32[]{:S(2)}) collective-permute-start(bf16[6,32,256]{2,1,0:T(8,128)(2,1)} %sum_end.1), channel_id=1, source_target_pairs={{0,16},{8,24},{16,0},{24,8},{1,17},{9,25},{17,1},{25,9},{2,18},{10... | collective-permute-start | bytes 294920 | tf_op jit(solution)/shard_map/ppermute | solution.py:446
  303.8 5.6 %collective-permute-start.2 = (bf16[6,32,256]{2,1,0:T(8,128)(2,1)}, bf16[6,32,256]{2,1,0:T(8,128)(2,1)S(1)}, u32[]{:S(2)}, u32[]{:S(2)}) collective-permute-start(bf16[6,32,256]{2,1,0:T(8,128)(2,1)} %sum_end.1), channel_id=1, source_target_pairs={{0,24},{8,16},{16,8},{24,0},{1,25},{9,17},{17,9},{25,1},{2,26},{10... | collective-permute-start | bytes 294920 | tf_op jit(solution)/shard_map/ppermute | solution.py:446
  314.4 1.0 copy-start
  317.6 2.4 collective-permute-start.3
  317.7 6.9 %collective-permute-start.4 = (bf16[9,32,256]{2,1,0:T(8,128)(2,1)}, bf16[9,32,256]{2,1,0:T(8,128)(2,1)S(1)}, u32[]{:S(2)}, u32[]{:S(2)}) collective-permute-start(bf16[9,32,256]{2,1,0:T(8,128)(2,1)} %sum_mid.1), channel_id=1, source_target_pairs={{0,16},{8,24},{16,0},{24,8},{1,17},{9,25},{17,1},{25,9},{2,18},{10... | collective-permute-start | bytes 442376 | tf_op jit(solution)/shard_map/ppermute | solution.py:446
  319.3 7.3 %collective-permute-start.5 = (bf16[9,32,256]{2,1,0:T(8,128)(2,1)}, bf16[9,32,256]{2,1,0:T(8,128)(2,1)S(1)}, u32[]{:S(2)}, u32[]{:S(2)}) collective-permute-start(bf16[9,32,256]{2,1,0:T(8,128)(2,1)} %sum_mid.1), channel_id=1, source_target_pairs={{0,24},{8,16},{16,8},{24,0},{1,25},{9,17},{17,9},{25,1},{2,26},{10... | collective-permute-start | bytes 442376 | tf_op jit(solution)/shard_map/ppermute | solution.py:446
Sparse Core Ops, SparseCore 0:
  23.8 43.4 all-gather.1

commit v3 on v2

--- a/solution.py
+++ b/solution.py
@@ -80,7 +80,7 @@
         r_ref[i, rows, :] = r
 
 
-def forward_layers(first, last, layers, s_ref, save, vec_ref, w_ref, w_at, save_at):
+def forward_layers(first, last, layers, s_ref, save, vec_ref, w_ref, w_at, save_at, after=None):
     act_ref = save[0]
 
     def product(t):
@@ -102,6 +102,8 @@
         out = product(t - 1)
         activation(t)
         residual(t - 1, out)
+        if after is not None:
+            after(first + lax.div(t, PARTS), lax.rem(t, PARTS))
         return carry
 
     steps = (last - first) * PARTS
@@ -125,7 +127,7 @@
     return jnp.sum(x, axis=0, keepdims=True)
 
 
-def backward_layers(first, last, layers, s_ref, low_ref, da_ref, save, w_ref, w_at, save_at, gw_ref, gv_ref, g_at):
+def backward_layers(first, last, layers, s_ref, low_ref, da_ref, save, w_ref, w_at, save_at, gw_ref, gv_ref, g_at, after=None):
     act_ref, n_ref, slope_ref, r_ref = save
     steps = (last - first) * PARTS
 
@@ -160,6 +162,8 @@
         da_ref[...] = following
         for k, x in enumerate((gain, shift, bias)):
             gv_ref[pl.ds(7 + k * layers + i, 1), :] += fold(x)
+        if after is not None:
+            after(i, lax.rem(t, PARTS))
         return carry
 
     da_ref[...] = product(jnp.int32(0))
@@ -319,16 +323,70 @@
         out_ref[f, m] = source_ref[at, f * rows:(f + 1) * rows, :].astype(BF16)
 
 
-def first_kernel(layers, rows_dev, latent_ref, ints_ref, front_ref, act_ref, n_ref, slope_ref, r_ref, s_ref, vec_ref, w_ref, lat_ref, hot_ref):
-    @pl.when(pl.program_id(0) == 0)
+def copies(refs, away, sems, i, span, inward):
+    out = []
+    for k, (near, far) in enumerate(zip(refs, away)):
+        ends = (far.at[i, span, :], near.at[i]) if inward else (near.at[i], far.at[i, span, :])
+        out.append(pltpu.make_async_copy(*ends, sems.at[i, k]))
+    return out
+
+
+def tile_span(step):
+    return pl.ds(pl.multiple_of(step * TILE, 128), TILE)
+
+
+def first_kernel(
+    layers, rows_dev, latent_ref, ints_ref, front_ref, n_out, slope_out, r_out, act_out, s_ref, vec_ref,
+    w_ref, lat_ref, hot_ref, n_ref, slope_ref, r_ref, act_ref, sems,
+):
+    step, steps = pl.program_id(0), pl.num_programs(0)
+    span = tile_span(step)
+    refs, away = (n_ref, slope_ref, r_ref, act_ref), (n_out, slope_out, r_out, act_out)
+
+    def start(i, count=4):
+        for copy in copies(refs[:count], away, sems, i, span, False):
+            copy.start()
+
+    def wait(i, count=4):
+        for copy in copies(refs[:count], away, sems, i, span, False):
+            copy.wait()
+
+    @pl.when(step == 0)
     def _():
         join_pieces(front_ref, w_ref)
         unpack_vec(w_ref[0], vec_ref)
 
     clean_latent(latent_ref, lat_ref, rows_dev)
     hot_ref[...] = moves_hot(ints_ref[0]).T
+
+    @pl.when(step > 0)
+    def _():
+        wait(SPLIT, 3)
+
     stem_forward(lat_ref, hot_ref, vec_ref, w_ref[1], s_ref, n_ref, slope_ref, r_ref, SPLIT)
-    forward_layers(0, SPLIT, layers, s_ref, (act_ref, n_ref, slope_ref, r_ref), vec_ref, w_ref, -2, 0)
+    start(SPLIT, 3)
+
+    def after(i, c):
+        @pl.when(c == PARTS - 1)
+        def _():
+            start(i)
+
+            @pl.when((step > 0) & (i < SPLIT - 1))
+            def _():
+                wait(i + 1)
+
+    @pl.when(step > 0)
+    def _():
+        wait(0)
+
+    save = (act_ref, n_ref, slope_ref, r_ref)
+    forward_layers(0, SPLIT, layers, s_ref, save, vec_ref, w_ref, -2, 0, after)
+
+    @pl.when(step == steps - 1)
+    def _():
+        wait(SPLIT, 3)
+        for i in range(SPLIT):
+            wait(i)
 
 
 def middle_kernel(
@@ -375,16 +433,34 @@
         for k in range(3):
             total = jnp.where(row == k, sums[:, k * 256:(k + 1) * 256], total)
         rep_ref[...] = total
+        if out_ref.shape[1] > blocks + 3:
+            high, low = split_low(total)
+            halves = jnp.concatenate([high, low], axis=0)
+            for f in range(out_ref.shape[0]):
+                out_ref[f, blocks + 3, 0:16, :] = halves
+                out_ref[f, blocks + 3, 16:, :] = jnp.zeros_like(out_ref[f, blocks + 3, 16:, :])
 
 
 def last_kernel(
-    layers, rows_dev, latent_ref, ints_ref, ds_in_ref, act_ref, n_ref, slope_ref, r_ref, front_ref, gv_in_ref,
-    lgrad_ref, out_ref, w_ref, lat_ref, hot_ref, ds_ref, low_ref, da_ref, gw_ref, gv_ref,
+    layers, rows_dev, latent_ref, ints_ref, ds_in_ref, n_in, slope_in, r_in, act_in, front_ref, gv_in_ref,
+    lgrad_ref, out_ref, w_ref, lat_ref, hot_ref, ds_ref, low_ref, da_ref, n_ref, slope_ref, r_ref, act_ref, gw_ref, gv_ref, sems,
 ):
-    step = pl.program_id(0)
+    step, steps = pl.program_id(0), pl.num_programs(0)
+    refs, away = (n_ref, slope_ref, r_ref, act_ref), (n_in, slope_in, r_in, act_in)
+
+    def start(i, to, count=4):
+        for copy in copies(refs[:count], away, sems, i, tile_span(to), True):
+            copy.start()
+
+    def wait(i, count=4):
+        for copy in copies(refs[:count], away, sems, i, tile_span(step), True):
+            copy.wait()
 
     @pl.when(step == 0)
     def _():
+        for i in reversed(range(SPLIT)):
+            start(i, 0)
+        start(SPLIT, 0, 3)
         join_pieces(front_ref, w_ref)
         gw_ref[...] = jnp.zeros_like(gw_ref)
         gv_ref[...] = gv_in_ref[...]
@@ -393,10 +469,29 @@
     hot_ref[...] = moves_hot(ints_ref[0]).T
     ds_ref[...] = ds_in_ref[...]
     low_ref[...] = ds_in_ref[...].astype(BF16)
-    backward_layers(0, SPLIT, layers, ds_ref, low_ref, da_ref, (act_ref, n_ref, slope_ref, r_ref), w_ref, -2, 0, gw_ref, gv_ref, -1)
+
+    def after(i, c):
+        @pl.when(c == PARTS - 1)
+        def _():
+            @pl.when(step < steps - 1)
+            def _():
+                start(i, step + 1)
+
+            @pl.when(i > 0)
+            def _():
+                wait(i - 1)
+
+    wait(SPLIT - 1)
+    save = (act_ref, n_ref, slope_ref, r_ref)
+    backward_layers(0, SPLIT, layers, ds_ref, low_ref, da_ref, save, w_ref, -2, 0, gw_ref, gv_ref, -1, after)
+    wait(SPLIT, 3)
     stem_backward(lat_ref, hot_ref, ds_ref, low_ref, n_ref, slope_ref, r_ref, SPLIT, w_ref[1], lgrad_ref, gw_ref, 0, gv_ref)
 
-    @pl.when(step == pl.num_programs(0) - 1)
+    @pl.when(step < steps - 1)
+    def _():
+        start(SPLIT, step + 1, 3)
+
+    @pl.when(step == steps - 1)
     def _():
         for m in range(SPLIT + 1):
             cut_pieces(out_ref, m, gw_ref, m)
@@ -406,19 +501,109 @@
         cut_pieces(out_ref, SPLIT + 1, gw_ref, 0)
 
 
-def sum_kernel(split, in_ref, out_ref):
-    for m in range(out_ref.shape[0]):
-        total = in_ref[0, m].astype(F32)
-        for f in range(1, in_ref.shape[0]):
-            total = total + in_ref[f, m].astype(F32)
-        if m == split:
-            high, low = split_low(total[:, 0:128] + total[:, 128:256])
-            out_ref[m] = jnp.concatenate([high, low], axis=1)
-        else:
-            out_ref[m] = total.astype(BF16)
+def pack_kernel(
+    stem_ref, table_ref, stem_vec_ref, block_ref, gain_ref, shift_ref, bias_ref, value_ref, chance_ref, front_ref, back_ref, vec_ref
+):
+    layers, shard = block_ref.shape[0], block_ref.shape[1]
+    moves = table_ref.shape[0]
+    vec_ref[...] = jnp.zeros_like(vec_ref)
+    at = 0
+    for ref in (table_ref, stem_vec_ref, gain_ref, shift_ref, bias_ref):
+        vec_ref[at:at + ref.shape[0], 0:shard] = ref[...].astype(F32)
+        at += ref.shape[0]
+    vectors = vec_ref[...].T[0:shard, :]
+    vectors = jnp.concatenate([vectors, jnp.zeros_like(vectors)], axis=1).astype(BF16)
+    for f in range(front_ref.shape[0]):
+        front_ref[f, 0] = vectors
+        front_ref[f, 1] = stem_ref[...]
+        for i in range(SPLIT):
+            front_ref[f, 2 + i] = block_ref[i]
+    for i in range(SPLIT, layers):
+        back_ref[i - SPLIT] = block_ref[i]
+    at = layers - SPLIT
+    back_ref[at:] = jnp.zeros_like(back_ref[at:])
+    nq, nc = value_ref.shape[1], chance_ref.shape[1]
+    for k in range(3):
+        width = min(WIDTH, nq - k * WIDTH)
+        back_ref[at + k, :, 0:width] = value_ref[:, k * WIDTH:k * WIDTH + width]
+    back_ref[at + 2, :, 128:128 + nc] = chance_ref[...]
+
+
+def sum_kernel(mid, mid_ref, end_ref, out_ref):
+    def total_of(ref, m):
+        total = ref[0, m].astype(F32)
+        for f in range(1, ref.shape[0]):
+            total = total + ref[f, m].astype(F32)
+        return total
+
+    for m in range(mid):
+        out_ref[m] = total_of(mid_ref, m).astype(BF16)
+    total = total_of(mid_ref, mid)
+    high, low = split_low(total[0:8] + total[8:16])
+    out_ref[mid] = jnp.zeros_like(out_ref[mid])
+    out_ref[mid, 0:16, :] = jnp.concatenate([high, low], axis=0)
+    count = end_ref.shape[1]
+    for m in range(count - 1):
+        out_ref[mid + 1 + m] = total_of(end_ref, m).astype(BF16)
+    total = total_of(end_ref, count - 1)
+    high, low = split_low(total[:, 0:128] + total[:, 128:256])
+    out_ref[mid + count] = jnp.concatenate([high, low], axis=1)
+
+
+def finish_kernel(
+    count, scale, stem_vec_ref, gain_ref, *refs
+):
+    ins = refs[:count]
+    (
+        loss_ref, stem_ref, table_ref, stem_bias_ref, stem_gain_ref, stem_shift_ref, block_ref, block_gain_ref, block_shift_ref,
+        block_bias_ref, value_ref, value_bias_ref, chance_ref, chance_bias_ref,
+    ) = refs[count:]
+    layers, moves = block_ref.shape[0], table_ref.shape[0]
+    nq, nc = value_ref.shape[1], chance_ref.shape[1]
+    mid = layers - SPLIT + 3
+
+    def total_of(m):
+        total = ins[0][m].astype(F32)
+        for ref in ins[1:]:
+            total = total + ref[m].astype(F32)
+        return total * scale
+
+    for i in range(SPLIT, layers):
+        block_ref[i] = total_of(i - SPLIT)
+    for i in range(SPLIT):
+        block_ref[i] = total_of(mid + 2 + i)
+    stem_ref[...] = total_of(mid + 1)
+    for k in range(3):
+        width = min(WIDTH, nq - k * WIDTH)
+        part = total_of(layers - SPLIT + k)
+        value_ref[:, k * WIDTH:k * WIDTH + width] = part[:, 0:width]
+    chance_ref[...] = part[:, 128:128 + nc]
+    rep = total_of(mid)
+    rep = rep[0:8] + rep[8:16] if rep.shape[0] >= 16 else rep
+    bias = jnp.concatenate([rep[k:k + 1] for k in range(3)], axis=1)
+    value_bias_ref[...] = bias[:, 0:nq]
+    chance_bias_ref[...] = bias[:, 640:640 + nc]
+    loss_ref[...] = jnp.sum(rep[3:4], axis=1, keepdims=True)
+    small = total_of(mid + 2 + SPLIT)
+    small = small[:, 0:128] + small[:, 128:256]
+    shard = small.shape[0]
+    if shard < 128:
+        small = jnp.concatenate([small, jnp.zeros((128 - shard, 128), F32)], axis=0)
+    small = small.T[:, 0:shard]
+    table_ref[...] = small[0:moves]
+    stem_gain = stem_vec_ref[1:2, :].astype(F32)
+    stem_bias_ref[...] = small[moves:moves + 1]
+    stem_gain_ref[...] = small[moves + 1:moves + 2] / stem_gain
+    stem_shift_ref[...] = small[moves + 2:moves + 3] / (16.0 * stem_gain)
+    at = moves + 3
+    gain = gain_ref[...].astype(F32)
+    block_gain_ref[...] = small[at:at + layers] / gain
+    block_shift_ref[...] = small[at + layers:at + 2 * layers] / (16.0 * gain)
+    block_bias_ref[...] = small[at + 2 * layers:at + 3 * layers]
 
 
 VMEM = pl.BlockSpec(memory_space=pltpu.VMEM)
+ANY = pl.BlockSpec(memory_space=pl.ANY)
 
 
 def params(mib):
@@ -459,22 +644,22 @@
     padded = steps * TILE
     fast = shard % 16 == 0 and n_dp & (n_dp - 1) == 0
 
-    vectors = jnp.concatenate(
-        [action_table, stem_bias[None], stem_gain[None], stem_shift[None], block_gain, block_shift, block_bias], axis=0
-    )
-    vectors = jnp.pad(vectors.T, ((0, 0), (0, WIDTH - vectors.shape[0])))
-    head = jnp.concatenate(
-        [value_weight, jnp.zeros((shard, 640 - nq), BF16), chance_weight, jnp.zeros((shard, 128 - nc), BF16)], axis=1
-    )
-    head = jnp.stack([head[:, k * WIDTH:(k + 1) * WIDTH] for k in range(3)])
-    front = jnp.concatenate([vectors[None], stem_weight[None], block_weight[:SPLIT]], axis=0)
-    back = jnp.concatenate([block_weight[SPLIT:], head], axis=0)
+    pieces, piece_rows = (n_fsdp, shard) if fast else (1, WIDTH)
+    stem_vec = jnp.stack([stem_bias, stem_gain, stem_shift])
+    front, back = pl.pallas_call(
+        pack_kernel,
+        in_specs=[VMEM] * 9,
+        out_specs=[VMEM] * 2,
+        out_shape=[
+            struct((pieces, 2 + SPLIT, shard, WIDTH), BF16), struct((layers - SPLIT + 3, shard, WIDTH), BF16),
+        ],
+        scratch_shapes=[pltpu.VMEM((128, max(shard, 128)), F32)],
+        name="pack",
+    )(stem_weight, action_table, stem_vec, block_weight, block_gain, block_shift, block_bias, value_weight, chance_weight)
     if fast:
-        pieces, piece_rows = n_fsdp, shard
-        w_front = lax.all_to_all(jnp.broadcast_to(front[None], (n_fsdp,) + front.shape), "fsdp", 0, 0)
+        w_front = lax.all_to_all(front, "fsdp", 0, 0)
     else:
-        pieces, piece_rows = 1, WIDTH
-        w_front = lax.all_gather(front, "fsdp", axis=1, tiled=True)[None]
+        w_front = lax.all_gather(front, "fsdp", axis=2, tiled=True)
     w_back = lax.all_gather(back, "fsdp", axis=1, tiled=True)
 
     ints = jnp.stack([actions, value_bins >> 5, value_bins & 31, chance_codes, step_mask])
@@ -485,38 +670,40 @@
     head_bias = jnp.broadcast_to(head_bias[None], (8, 3 * WIDTH))
 
     saved = [
-        struct((SPLIT, padded, WIDTH), BF16),
         struct((SPLIT + 1, padded, WIDTH), BF16),
         struct((SPLIT + 1, padded, WIDTH), BF16),
         struct((SPLIT + 1, padded, 128), F32),
+        struct((SPLIT, padded, WIDTH), BF16),
     ]
+    scratch = pltpu.VMEM
+    kept = [scratch((x.shape[0], TILE, x.shape[2]), x.dtype) for x in saved] + [pltpu.SemaphoreType.DMA((SPLIT + 1, 4))]
     stream = struct((padded, WIDTH), F32)
-    scratch = pltpu.VMEM
     front_shape = w_front.shape[1:2] + (WIDTH, WIDTH)
     *held, s_mid, vec = pl.pallas_call(
         functools.partial(first_kernel, layers, rows_dev),
         grid=(steps,),
         in_specs=[tiled((rows_dev, WIDTH), 0), ints_spec, once(w_front.shape)],
-        out_specs=[tiled(x.shape, 1) for x in saved] + [tiled(stream.shape, 0), whole((128, WIDTH))],
+        out_specs=[ANY] * 4 + [tiled(stream.shape, 0), whole((128, WIDTH))],
         out_shape=saved + [stream, struct((128, WIDTH), F32)],
-        scratch_shapes=[scratch(front_shape, BF16), scratch((TILE, WIDTH), BF16), scratch((TILE, 16), BF16)],
+        scratch_shapes=[scratch(front_shape, BF16), scratch((TILE, WIDTH), BF16), scratch((TILE, 16), BF16)] + kept,
         compiler_params=params(62),
         cost_estimate=pl.CostEstimate(flops=rows_dev * WIDTH * WIDTH * 200, bytes_accessed=60 << 20, transcendentals=0),
         name="first",
     )(latent, ints, w_front)
 
     blocks = layers - SPLIT
+    mid_shape = (pieces, blocks + (4 if fast else 3), piece_rows, WIDTH)
     latents, value_logits, chance_logits, ds_mid, gv_mid, rep, parts_mid = pl.pallas_call(
         functools.partial(middle_kernel, layers, nq),
         grid=(steps,),
         in_specs=[tiled(stream.shape, 0), ints_spec, once(vec.shape), once(head_bias.shape), once(w_back.shape)],
         out_specs=[
             tiled((rows_dev, WIDTH), 0), tiled((nq, rows_dev), 1), tiled((nc, rows_dev), 1), tiled(stream.shape, 0),
-            whole((48, WIDTH)), whole((8, WIDTH)), whole((pieces, blocks + 3, piece_rows, WIDTH)),
+            whole((48, WIDTH)), whole((8, WIDTH)), whole(mid_shape),
         ],
         out_shape=[
             struct((rows_dev, WIDTH), BF16), struct((nq, rows_dev), BF16), struct((nc, rows_dev), BF16), stream,
-            struct((48, WIDTH), F32), struct((8, WIDTH), F32), struct((pieces, blocks + 3, piece_rows, WIDTH), BF16),
+            struct((48, WIDTH), F32), struct((8, WIDTH), F32), struct(mid_shape, BF16),
         ],
         scratch_shapes=[
             scratch((3, TILE, 128), F32),
@@ -541,8 +728,7 @@
         functools.partial(last_kernel, layers, rows_dev),
         grid=(steps,),
         in_specs=[tiled((rows_dev, WIDTH), 0), ints_spec, tiled(stream.shape, 0)]
-        + [tiled(x.shape, 1) for x in saved]
-        + [once(w_front.shape), once((48, WIDTH))],
+        + [ANY] * 4 + [once(w_front.shape), once((48, WIDTH))],
         out_specs=[tiled((rows_dev, WIDTH), 0), whole((pieces, SPLIT + 2, piece_rows, WIDTH))],
         out_shape=[struct((rows_dev, WIDTH), BF16), struct((pieces, SPLIT + 2, piece_rows, WIDTH), BF16)],
         scratch_shapes=[
@@ -552,57 +738,68 @@
             scratch((TILE, WIDTH), F32),
             scratch((TILE, WIDTH), BF16),
             scratch((CHUNK, WIDTH), F32),
+        ] + kept[:4] + [
             scratch((SPLIT + 1, WIDTH, WIDTH), F32),
             scratch((48, WIDTH), F32),
-        ],
+        ] + kept[4:],
         compiler_params=params(62),
         cost_estimate=pl.CostEstimate(flops=rows_dev * WIDTH * WIDTH * 150, bytes_accessed=60 << 20, transcendentals=0),
         name="last",
     )(latent, ints, ds_mid, *held, w_front, gv_mid)
 
-    rep = lax.psum(rep, ("dp", "fsdp"))
+    count = blocks + 4 + SPLIT + 2
     if fast:
-        def reduce(parts, split, name):
-            got = lax.all_to_all(parts, "fsdp", 0, 0)
-            mine = pl.pallas_call(
-                functools.partial(sum_kernel, split), in_specs=[VMEM], out_specs=VMEM,
-                out_shape=struct(parts.shape[1:], BF16), name=name,
-            )(got)
-            return sum((y.astype(F32) for y in exchange(mine, "dp", n_dp)), mine.astype(F32))
-
-        mid, end = reduce(parts_mid, -1, "sum_mid"), reduce(parts_end, SPLIT + 1, "sum_end")
+        got_mid = lax.all_to_all(parts_mid, "fsdp", 0, 0)
+        parts_end, got_mid = lax.optimization_barrier((parts_end, got_mid))
+        got_end = lax.all_to_all(parts_end, "fsdp", 0, 0)
+        mine = pl.pallas_call(
+            functools.partial(sum_kernel, blocks + 3),
+            in_specs=[VMEM] * 2,
+            out_specs=VMEM,
+            out_shape=struct((count, shard, WIDTH), BF16),
+            name="sum",
+        )(got_mid, got_end)
+        sums = [mine] + exchange(mine, "dp", n_dp)
     else:
-        scatter = lambda x: lax.psum(
-            lax.psum_scatter(x[0], "fsdp", scatter_dimension=1, tiled=True).astype(F32), "dp"
-        )
-        mid, end = scatter(parts_mid), scatter(parts_end)
-
-    scale = 1.0 / (rows_dev * n_dp * n_fsdp)
-    rep = rep * scale
-    head_grad = jnp.concatenate([mid[blocks + k] for k in range(3)], axis=1) * scale
-    small = (end[SPLIT + 1, :, 0:128] + end[SPLIT + 1, :, 128:256]).T * scale
-    bias_sums = rep[0:3].reshape(3 * WIDTH)
-    at = moves + 3
-    gain = block_gain.astype(F32)
+        scatter = lambda x: lax.psum_scatter(x[0], "fsdp", scatter_dimension=1, tiled=True).astype(F32)
+        sums = jnp.concatenate([scatter(parts_mid), jnp.zeros((1, shard, WIDTH), F32), scatter(parts_end)])
+        rep = lax.psum(rep, ("dp", "fsdp"))
+        sums = lax.psum(sums, "dp").at[blocks + 3, 0:8, :].set(rep)
+        sums = [sums]
+
+    shapes = [
+        (1, 1), (shard, WIDTH), (moves, shard), (1, shard), (1, shard), (1, shard), (layers, shard, WIDTH), (layers, shard),
+        (layers, shard), (layers, shard), (shard, nq), (1, nq), (shard, nc), (1, nc),
+    ]
+    (
+        loss, stem_grad, table_grad, stem_bias_grad, stem_gain_grad, stem_shift_grad, block_grad, gain_grad, shift_grad, bias_grad,
+        value_grad, value_bias_grad, chance_grad, chance_bias_grad,
+    ) = pl.pallas_call(
+        functools.partial(finish_kernel, len(sums), 1.0 / (rows_dev * n_dp * n_fsdp)),
+        in_specs=[VMEM] * (2 + len(sums)),
+        out_specs=[VMEM] * len(shapes),
+        out_shape=[struct(x, F32) for x in shapes],
+        name="finish",
+    )(stem_vec, block_gain, *sums)
     return (
         latents,
         value_logits.T,
         chance_logits.T,
-        jnp.sum(rep[3]),
+        loss.reshape(()),
         latent_grad,
-        end[0] * scale,
-        small[0:moves],
-        small[moves],
-        small[moves + 1] / stem_gain.astype(F32),
-        small[moves + 2] / (16.0 * stem_gain.astype(F32)),
-        jnp.concatenate([end[1:SPLIT + 1], mid[:blocks]], axis=0) * scale,
-        small[at:at + layers] / gain,
-        small[at + layers:at + 2 * layers] / (16.0 * gain),
-        small[at + 2 * layers:at + 3 * layers],
-        head_grad[:, 0:nq],
-        bias_sums[0:nq],
-        head_grad[:, 640:640 + nc],
-        bias_sums[640:640 + nc],
+        stem_grad,
+        table_grad,
+        stem_bias_grad.reshape(shard),
+        stem_gain_grad.reshape(shard),
+        stem_shift_grad.reshape(shard),
+        block_grad,
+        gain_grad,
+        shift_grad,
+        bias_grad,
+        value_grad,
+        value_bias_grad.reshape(nq),
+        chance_grad,
+        chance_bias_grad.reshape(nc),
     )
 
 

time: 338 us -> 273 us (0.81)
  blocking collectives: 72.2 us -> 25.7 us
  local copies, waits for them, and re-layouts: 14.8 us -> 3.87 us
  other arithmetic: 11.1 us -> 6.93 us
  Pallas kernels: 182 us -> 178 us
  waiting for transfers between devices: 27.1 us -> 30.6 us
    psum x1 -> x0, blocking collectives: 48.3 us -> none  [per_device(): rep = lax.psum(rep, ('dp', 'fsdp'))]
    slice x10 -> x0, local copies, waits for them, and re-layouts: 4.33 us -> none  [the longest x1 0.9 us: per_device(): back = jnp.concatenate([block_weight[SPLIT:], head], axis=0)]
    ppermute x6 -> x3, waiting for transfers between devices: 11.5 us -> 12.6 us  [exchange(): lax.ppermute(x, axis, [(i, i ^ k) for i in range(size)])]
  transfers between devices with their start and end apart: 9 -> 6, of which waited for: 5 -> 3; matrix products, arithmetic and copies ran while one was open for 4% -> 2% of each run, Pallas kernels for 13% -> 26%
where the time goes in v3:
time: 273 us; the launch traced here: 272 us
  Pallas kernels  178 us (65%)
  waiting for transfers between devices  30.6 us (11%)
  blocking collectives  25.7 us (9%)
  between operations  14.2 us (5%)
  starting transfers between devices  12.7 us (5%)
  other arithmetic  6.93 us (3%)
  local copies, waits for them, and re-layouts  3.87 us (1%)
    pallas_call x1, Pallas kernels, per_device(): pl.pallas_call(functools.partial(middle_kernel, layers, nq), grid=(steps,...  100 us
    pallas_call x1, Pallas kernels, per_device(): pl.pallas_call(functools.partial(first_kernel, layers, rows_dev), grid=(s...  39.4 us
    pallas_call x1, Pallas kernels, per_device(): pl.pallas_call(functools.partial(last_kernel, layers, rows_dev), grid=(st...  31.8 us
    all_to_all x1, blocking collectives, per_device(): got_end = lax.all_to_all(parts_end, 'fsdp', 0, 0)  25.7 us
    all_to_all x1, waiting for transfers between devices, per_device(): w_front = lax.all_to_all(front, 'fsdp', 0, 0)  17.3 us
    ppermute x3, waiting for transfers between devices, exchange(): lax.ppermute(x, axis, [(i, i ^ k) for i in range(size)])  12.6 us
    all_to_all x1, starting transfers between devices, per_device(): w_front = lax.all_to_all(front, 'fsdp', 0, 0)  7.25 us
  transfers between devices with their start and end apart: 6, of which 3 were waited for; matrix products, arithmetic and copies ran while one was open for 2% of the time, Pallas kernels for 26%

profile of v3, /device:TPU:0, one launch (start us, length us, event | category | flops | bytes accessed | tf_op | source)
XLA Modules:
  0.0 272.0 jit_solution(1947964820890599558)
XLA Ops:
  7.2 1.3 pad_maximum_fusion.1.stem_vec_ref
  8.4 1.9 pack.1
  10.4 7.3 %all-to-all-start = ((bf16[8,6,32,256]{3,2,1,0:T(8,128)(2,1)}), bf16[8,6,32,256]{3,2,1,0:T(8,128)(2,1)S(1)}, u32[]{:S(2)}, u32[]{:S(2)}) async-start(bf16[8,6,32,256]{3,2,1,0:T(8,128)(2,1)} %get-tuple-element.50), calls=%async_computation | async-start | bytes 1572864 | tf_op jit(solution)/shard_map/all_to_all | solution.py:660
  17.6 0.0 all-gather.2.cloned.1.call-start
  17.7 0.7 all-gather.2.cloned.1.call-update
  18.4 0.7 convert_element_type.10
  19.0 0.7 convert_element_type.9
  19.7 0.7 convert.20
  20.5 0.7 convert.23
  21.2 0.7 convert.24
  22.0 0.7 and_convert_fusion
  22.8 0.2 stack.41
  23.0 0.7 copy.39
  23.7 0.1 pad_maximum_fusion
  23.8 17.3 %all-to-all-done.front_ref = bf16[8,6,32,256]{3,2,1,0:T(8,128)(2,1)S(1)} async-done(((bf16[8,6,32,256]{3,2,1,0:T(8,128)(2,1)}), bf16[8,6,32,256]{3,2,1,0:T(8,128)(2,1)S(1)}, u32[]{:S(2)}, u32[]{:S(2)}) %all-to-all-start) | async-done | bytes 786464 | tf_op jit(solution)/shard_map/all_to_all | solution.py:660
  41.1 0.0 copy-start.1
  41.1 0.9 copy-done.1
  42.0 39.4 %first.1 = (bf16[5,5760,256]{2,1,0:T(8,128)(2,1)}, bf16[5,5760,256]{2,1,0:T(8,128)(2,1)}, f32[5,5760,128]{2,1,0:T(8,128)}, bf16[4,5760,256]{2,1,0:T(8,128)(2,1)}...) custom-call(bf16[5696,256]{1,0:T(8,128)(2,1)} %latent_ref.3, bf16[3,16,1920]{2,1,0:T(8,128)(2,1)} %bitcast.18, ...), custom_call_target="tpu_custom_call" | custom-call | flops 74658611200 | bytes 62914560 | tf_op jit(solution)/shard_map/first/pallas_call | solution.py:682
  81.4 0.0 all-gather.2.cloned.1.call-done.w_ref
  81.5 0.6 broadcast_in_dim.14.hb_ref
  82.1 100.2 %middle.1 = (bf16[5696,256]{1,0:T(8,128)(2,1)}, bf16[601,5696]{1,0:T(8,128)(2,1)}, bf16[32,5696]{1,0:T(8,128)(2,1)}, f32[5760,256]{1,0:T(8,128)}, f32[48,256]{1,...) custom-call(f32[5760,256]{1,0:T(8,128)} %get-tuple-element.51.s_in_ref, bf16[3,16,1920]{2,1,0:T(8,128)(2,1)} %bitcast.19, ...), custom_call_target="tpu_custom_call" | custom-call | flops 223975833600 | bytes 41943040 | tf_op jit(solution)/shard_map/middle/pallas_call | solution.py:696
  182.3 3.6 %all-to-all-start.1 = ((bf16[8,10,32,256]{3,2,1,0:T(8,128)(2,1)}), bf16[8,10,32,256]{3,2,1,0:T(8,128)(2,1)S(1)}, u32[]{:S(2)}, u32[]{:S(2)}) async-start(bf16[8,10,32,256]{3,2,1,0:T(8,128)(2,1)} %get-tuple-element.64), calls=%async_computation.1 | async-start | bytes 2621440 | tf_op jit(solution)/shard_map/all_to_all | solution.py:752
  185.9 31.8 %last.1 = (bf16[5696,256]{1,0:T(8,128)(2,1)}, bf16[8,6,32,256]{3,2,1,0:T(8,128)(2,1)}) custom-call(bf16[5696,256]{1,0:T(8,128)(2,1)} %latent_ref.3, bf16[3,16,1920]{2,1,0:T(8,128)(2,1)} %bitcast.20, f32[5760,256]{1,0:T(8,128)} %get-tuple-element.57.ds_in_ref, bf16[5,5760,256]{2,1,0:T(8,128)(2,1)} %get-tuple-element.58.n_in, ...), custom_call_target="tpu_custom_call" | custom-call | flops 55993958400 | bytes 62914560 | tf_op jit(solution)/shard_map/last/pallas_call | solution.py:727
  217.7 0.0 all-to-all-done.1.mid_ref
  217.7 0.0 copy-start
  217.7 25.7 %all_to_all.15.end_ref = bf16[8,6,32,256]{3,2,1,0:T(8,128)(2,1)} all-to-all(bf16[8,6,32,256]{3,2,1,0:T(8,128)(2,1)} %get-tuple-element.66), channel_id=1, replica_groups=mesh['dp'=4,'fsdp'=8] {'fsdp'}, dimensions={0} | all-to-all | bytes 1572864 | tf_op jit(solution)/shard_map/all_to_all | solution.py:754
  243.4 0.0 copy-done
  243.4 2.5 sum.1.refs_0_
  245.9 0.0 collective-permute-start.2
  245.9 1.6 collective-permute-start.1
  247.6 0.2 collective-permute-start
  247.8 6.8 %collective-permute-done.2.refs_3_ = bf16[16,32,256]{2,1,0:T(8,128)(2,1)S(1)} collective-permute-done((bf16[16,32,256]{2,1,0:T(8,128)(2,1)}, bf16[16,32,256]{2,1,0:T(8,128)(2,1)S(1)}, u32[]{:S(2)}, u32[]{:S(2)}) %collective-permute-start.2) | collective-permute-done | bytes 262176 | tf_op jit(solution)/shard_map/ppermute | solution.py:631
  254.6 0.0 copy-start.2
  254.6 5.8 %collective-permute-done.1.refs_2_ = bf16[16,32,256]{2,1,0:T(8,128)(2,1)S(1)} collective-permute-done((bf16[16,32,256]{2,1,0:T(8,128)(2,1)}, bf16[16,32,256]{2,1,0:T(8,128)(2,1)S(1)}, u32[]{:S(2)}, u32[]{:S(2)}) %collective-permute-start.1) | collective-permute-done | bytes 262176 | tf_op jit(solution)/shard_map/ppermute | solution.py:631
  260.4 0.0 copy-start.3
  260.4 0.0 collective-permute-done.refs_1_
  260.4 0.0 copy-done.2
  260.4 0.7 copy-done.3
  261.1 0.0 copy-start.4
  261.1 0.7 copy-done.4
  261.8 2.1 finish.1
  263.9 1.3 reduce
  (8 shorter events, 0.1 us)
Async XLA Ops:
  10.4 30.7 %all-to-all-start = ((bf16[8,6,32,256]{3,2,1,0:T(8,128)(2,1)}), bf16[8,6,32,256]{3,2,1,0:T(8,128)(2,1)S(1)}, u32[]{:S(2)}, u32[]{:S(2)}) async-start(bf16[8,6,32,256]{3,2,1,0:T(8,128)(2,1)} %get-tuple-element.50), calls=%async_computation | async-start | bytes 1572864 | tf_op jit(solution)/shard_map/all_to_all | solution.py:660
  17.6 63.8 %all-gather.2.cloned.1.call-start = ((), (), s32[]{:S(2)}) async-start(), calls=%async_computation.3 | async-start | bytes 1327104 | tf_op jit(solution)/shard_map/all_gather | solution.py:663
  41.1 0.9 copy-start.1
  182.3 35.4 %all-to-all-start.1 = ((bf16[8,10,32,256]{3,2,1,0:T(8,128)(2,1)}), bf16[8,10,32,256]{3,2,1,0:T(8,128)(2,1)S(1)}, u32[]{:S(2)}, u32[]{:S(2)}) async-start(bf16[8,10,32,256]{3,2,1,0:T(8,128)(2,1)} %get-tuple-element.64), calls=%async_computation.1 | async-start | bytes 2621440 | tf_op jit(solution)/shard_map/all_to_all | solution.py:752
  217.7 25.7 %copy-start = (bf16[8,10,32,256]{3,2,1,0:T(8,128)(2,1)}, bf16[8,10,32,256]{3,2,1,0:T(8,128)(2,1)S(1)}, u32[]{:S(2)}) copy-start(bf16[8,10,32,256]{3,2,1,0:T(8,128)(2,1)S(1)} %all-to-all-done.1.mid_ref) | copy-start | bytes 3932164
  245.9 8.7 %collective-permute-start.2 = (bf16[16,32,256]{2,1,0:T(8,128)(2,1)}, bf16[16,32,256]{2,1,0:T(8,128)(2,1)S(1)}, u32[]{:S(2)}, u32[]{:S(2)}) collective-permute-start(bf16[16,32,256]{2,1,0:T(8,128)(2,1)} %sum.1.refs_0_), channel_id=1, source_target_pairs={{0,24},{8,16},{16,8},{24,0},{1,25},{9,17},{17,9},{25,1},{2,26},{10... | collective-permute-start | bytes 786440 | tf_op jit(solution)/shard_map/ppermute | solution.py:631
  245.9 14.4 %collective-permute-start.1 = (bf16[16,32,256]{2,1,0:T(8,128)(2,1)}, bf16[16,32,256]{2,1,0:T(8,128)(2,1)S(1)}, u32[]{:S(2)}, u32[]{:S(2)}) collective-permute-start(bf16[16,32,256]{2,1,0:T(8,128)(2,1)} %sum.1.refs_0_), channel_id=1, source_target_pairs={{0,16},{8,24},{16,0},{24,8},{1,17},{9,25},{17,1},{25,9},{2,18},{10... | collective-permute-start | bytes 786440 | tf_op jit(solution)/shard_map/ppermute | solution.py:631
  247.6 12.8 %collective-permute-start = (bf16[16,32,256]{2,1,0:T(8,128)(2,1)}, bf16[16,32,256]{2,1,0:T(8,128)(2,1)S(1)}, u32[]{:S(2)}, u32[]{:S(2)}) collective-permute-start(bf16[16,32,256]{2,1,0:T(8,128)(2,1)} %sum.1.refs_0_), channel_id=1, source_target_pairs={{0,8},{8,0},{16,24},{24,16},{1,9},{9,1},{17,25},{25,17},{2,10},{10... | collective-permute-start | bytes 786440 | tf_op jit(solution)/shard_map/ppermute | solution.py:631
  254.6 5.8 %copy-start.2 = (bf16[16,32,256]{2,1,0:T(8,128)(2,1)}, bf16[16,32,256]{2,1,0:T(8,128)(2,1)S(1)}, u32[]{:S(2)}) copy-start(bf16[16,32,256]{2,1,0:T(8,128)(2,1)S(1)} %collective-permute-done.2.refs_3_) | copy-start | bytes 786436
  260.4 0.7 copy-start.3
  261.1 0.7 copy-start.4
Sparse Core Ops, SparseCore 0:
  21.2 43.4 all-gather.1

commit v4 on v3

v4 whole, which is shorter than its diff:
```python
import functools
import jax
import jax.numpy as jnp
from jax import lax
from jax.experimental import pallas as pl
from jax.experimental.pallas import tpu as pltpu
from jax.sharding import PartitionSpec as P

F32 = jnp.float32
BF16 = jnp.bfloat16
WIDTH = 256
UNIT = 16
TILE = 1920
CHUNK = 640
PARTS = TILE // CHUNK
HEAD_CHUNK = 384
SPLIT = 4
K0 = 2 * 0.7978845608028654
K1 = 8 * 0.7978845608028654 * 0.044715


def mm(a, b):
    return lax.dot_general(a, b, (((1,), (0,)), ((), ())), preferred_element_type=F32)


def mm_nt(a, b):
    return lax.dot_general(a, b, (((1,), (1,)), ((), ())), preferred_element_type=F32)


def mm_tn(a, b):
    return lax.dot_general(a, b, (((0,), (0,)), ((), ())), preferred_element_type=F32)


def norm_gelu(s, gain8, gain_slope, shift_half):
    mean = jnp.sum(s, axis=1, keepdims=True) * (1.0 / WIDTH)
    center = s - mean
    r = lax.rsqrt(jnp.sum(center * center, axis=1, keepdims=True) + WIDTH * 1e-5)
    n = center * r
    h = n * gain8 + shift_half
    y = h * h
    t = jnp.tanh(h * (K0 + K1 * y))
    e1 = 1.0 + t
    bend = (h * (y + K0 / (3 * K1))) * (1.0 - t)
    slope = (e1 * gain_slope) * (1.0 / (3 * K1) + bend)
    return h * e1, n.astype(BF16), slope.astype(BF16), jnp.broadcast_to(r, (UNIT, 128))


def scales(vec_ref, at, layers):
    gain = vec_ref[pl.ds(at, 1), :]
    return gain * 8.0, gain * (8.0 * 3 * K1), vec_ref[pl.ds(at + layers, 1), :] * 0.5


def norm_back(da, slope, n, r):
    w = da * slope.astype(F32)
    m1 = jnp.sum(w, axis=1, keepdims=True) * (1.0 / WIDTH)
    w16 = w.astype(BF16)
    wn = w16 * n
    wide = (wn[:, 0:128] + wn[:, 128:256]).astype(F32)
    m2 = jnp.sum(wide, axis=1, keepdims=True)
    m1 = jnp.broadcast_to(m1, (UNIT, 128)).astype(BF16)
    m2 = jnp.broadcast_to(m2, (UNIT, 128)).astype(BF16)
    halves = [
        (w[:, k:k + 128] - (m1 + n[:, k:k + 128] * m2).astype(F32)) * r for k in (0, 128)
    ]
    return jnp.concatenate(halves, axis=1), w, wn


def rows_of(c):
    return pl.multiple_of(c * CHUNK, UNIT)


def activate(base, s_ref, save, i, scale):
    act_ref, n_ref, slope_ref, r_ref = save
    for u in range(0, CHUNK, UNIT):
        rows = pl.ds(base + u, UNIT)
        act, n, slope, r = norm_gelu(s_ref[rows, :], *scale)
        act_ref[i, rows, :] = act.astype(BF16)
        n_ref[i, rows, :] = n
        slope_ref[i, rows, :] = slope
        r_ref[i, rows, :] = r


def following(i, c, change):
    end = c == PARTS - 1
    return jnp.where(end, i + change, i), jnp.where(end, 0, c + 1)


def forward_layers(first, last, layers, s_ref, save, vec_ref, w_ref, w_at, save_at, after=None):
    act_ref = save[0]

    def product(i, c):
        return mm(act_ref[i - save_at, pl.ds(rows_of(c), CHUNK), :], w_ref[i - w_at])

    def activation(i, c):
        activate(rows_of(c), s_ref, save, i - save_at, scales(vec_ref, 7 + i, layers))

    def residual(i, base, out):
        bias = vec_ref[pl.ds(7 + 2 * layers + i, 1), :]
        for u in range(0, CHUNK, UNIT):
            rows = pl.ds(base + u, UNIT)
            s_ref[rows, :] = s_ref[rows, :] + (out[u:u + UNIT, :] + bias)

    def body(t, carry):
        before, now = carry
        out = product(*before)
        activation(*now)
        base = rows_of(before[1])
        if spare:
            base = pl.multiple_of(jnp.where(t == 0, TILE, base), UNIT)
        residual(before[0], base, out)
        if after is not None:
            after(*now)
        return now, following(*now, 1)

    spare = s_ref.shape[0] > TILE
    start = jnp.int32(first), jnp.int32(0)
    carry = start, start
    if not spare:
        activation(*start)
        carry = start, following(*start, 1)
    end, _ = lax.fori_loop(0 if spare else 1, (last - first) * PARTS, body, carry)
    residual(end[0], rows_of(end[1]), product(*end))


def column_sums(parts):
    total = parts[0]
    for part in parts[1:]:
        total = total + part
    return total.astype(F32)


GROUP = 4


def fold(x):
    return jnp.sum(x, axis=0, keepdims=True)


def backward_layers(first, last, layers, s_ref, low_ref, da_ref, save, w_ref, w_at, save_at, gw_ref, gv_ref, g_at, after=None):
    act_ref, n_ref, slope_ref, r_ref = save

    def product(i, c):
        return mm_nt(low_ref[pl.ds(rows_of(c), CHUNK), :], w_ref[i - w_at])

    def body(t, carry):
        i, c = carry
        base = rows_of(c)
        next_i, next_c = following(i, c, -1)
        next_i = jnp.maximum(next_i, first)
        next_da = product(next_i, next_c)
        gw_ref[i - g_at] += mm_tn(act_ref[i - save_at, pl.ds(base, CHUNK), :], low_ref[pl.ds(base, CHUNK), :])
        zero = jnp.zeros((UNIT, WIDTH), F32)
        shift, gain, bias = zero, zero, zero
        held = []
        for u in range(0, CHUNK, UNIT):
            rows = pl.ds(base + u, UNIT)
            at = (i - save_at, rows, slice(None))
            d_in, wf, wn = norm_back(da_ref[u:u + UNIT, :], slope_ref[at], n_ref[at], r_ref[at])
            shift = shift + wf
            held.append(wn)
            if len(held) == GROUP:
                gain = gain + column_sums(held)
                held = []
            ds = s_ref[rows, :]
            bias = bias + ds
            ds = ds + d_in
            s_ref[rows, :] = ds
            low_ref[rows, :] = ds.astype(BF16)
        da_ref[...] = next_da
        for k, x in enumerate((gain, shift, bias)):
            gv_ref[pl.ds(7 + k * layers + i, 1), :] += fold(x)
        if after is not None:
            after(i, c)
        return next_i, next_c

    start = jnp.int32(last - 1), jnp.int32(0)
    da_ref[...] = product(*start)
    lax.fori_loop(0, (last - first) * PARTS, body, start)


def columns_of(ints):
    row = lax.broadcasted_iota(jnp.int32, (16, ints.shape[1]), 0)
    parts = (ints[1:2] >> 5, ints[1:2] & 31, ints[2:3], ints[3:4])
    values = jnp.zeros_like(row)
    for k, part in enumerate(parts):
        values = jnp.where(row == k, part, values)
    k = lax.broadcasted_iota(jnp.int32, (16, 384), 0)
    j = lax.broadcasted_iota(jnp.int32, (16, 384), 1) >> 7
    pick = jnp.where((j == 0) & (k == 0), 32.0, 0.0) + jnp.where(
        ((j == 0) & (k == 1)) | ((j == 1) & (k == 2)) | ((j == 2) & (k == 3)), 1.0, 0.0
    )
    return mm_tn(values.astype(F32).astype(BF16), pick.astype(BF16))


def softmax(hb_ref, full_ref, col_ref, top_ref, total_ref, expon_ref, wide_ref, dlog_ref, at, loss_ref):
    units = [slice(u, u + UNIT) for u in range(0, HEAD_CHUNK, UNIT)]
    lane = lax.broadcasted_iota(jnp.int32, (1, 128), 1).astype(F32)
    spread = lambda x: jnp.broadcast_to(x, (UNIT, 128))
    cols = [slice(k * 128, (k + 1) * 128) for k in range(6)]
    for rows in units:
        logits = [full_ref[rows, cols[k]] + hb_ref[0:1, cols[k]].astype(F32) for k in range(6)]
        for k in range(6):
            full_ref[rows, cols[k]] = logits[k]
            wide_ref[k, rows, :] = logits[k].astype(BF16)
        top = functools.reduce(jnp.maximum, logits[:5])
        top_ref[0, rows, :] = spread(jnp.max(top, axis=1, keepdims=True))
        top_ref[1, rows, :] = spread(jnp.max(logits[5], axis=1, keepdims=True))
    for rows in units:
        expon = [jnp.exp(full_ref[rows, cols[k]] - top_ref[k // 5, rows, :]) for k in range(6)]
        for k in range(6):
            expon_ref[rows, cols[k]] = expon[k]
        total_ref[0, rows, :] = spread(jnp.sum(functools.reduce(jnp.add, expon[:5]), axis=1, keepdims=True))
        total_ref[1, rows, :] = spread(jnp.sum(expon[5], axis=1, keepdims=True))
    loss = jnp.zeros((UNIT, 128), F32)
    for rows in units:
        targets, mask = (col_ref[rows, cols[0]], col_ref[rows, cols[1]]), col_ref[rows, cols[2]]
        zero = jnp.zeros_like(mask)
        hits = [zero, zero]
        weights = [mask / total_ref[j, rows, :] for j in range(2)]
        for k in range(6):
            j = k // 5
            hit = lane + 128.0 * (k % 5) == targets[j]
            hits[j] = jnp.where(hit, full_ref[rows, cols[k]], hits[j])
            grad = expon_ref[rows, cols[k]] * weights[j] - jnp.where(hit, mask, zero)
            dlog_ref[pl.ds(at + rows.start, UNIT), cols[k]] = grad.astype(BF16)
        row = jnp.log(total_ref[0, rows, :]) + jnp.log(total_ref[1, rows, :]) + (top_ref[0, rows, :] + top_ref[1, rows, :])
        loss = loss + mask * (row * (1.0 / 128) - (hits[0] + hits[1]))
    loss_ref[...] += loss


def heads(
    nq, ints_ref, s_ref, ds_ref, low_ref, wh_ref, hb_ref, latents_ref, value_ref, chance_ref, turned_ref, dlog_ref, loss_ref, full_ref, col_ref,
    top_ref, total_ref, expon_ref, wide_ref, gw_ref, g_at,
):
    size = HEAD_CHUNK
    count = TILE // size

    def span_of(t):
        return pl.ds(pl.multiple_of(t * size, 128), size)

    def logits(t):
        lat = s_ref[span_of(t), :].astype(BF16)
        latents_ref[span_of(t), :] = lat
        return mm(lat, wh_ref[...]), columns_of(ints_ref[:, span_of(t)])

    def keep(parts):
        full_ref[...], col_ref[...] = parts

    def turn(t):
        for k in range(5):
            height = min(128, nq - k * 128)
            value_ref[k * 128:k * 128 + height, span_of(t)] = wide_ref[k].T[0:height, :]
        chance_ref[:, span_of(t)] = wide_ref[5].T[0:chance_ref.shape[0], :]
        turned_ref[0:WIDTH, span_of(t)] = latents_ref[span_of(t), :].T

    def product(t):
        return mm_nt(dlog_ref[span_of(t), :], wh_ref[...])

    def store(t, ds):
        ds_ref[span_of(t), :] = ds
        low_ref[span_of(t), :] = ds.astype(BF16)

    def body(t, carry):
        before = jnp.maximum(t - 1, 0)
        following = logits(jnp.minimum(t + 1, count - 1))
        turn(before)
        ds = product(before)
        softmax(
            hb_ref, full_ref, col_ref, top_ref, total_ref, expon_ref, wide_ref, dlog_ref, pl.multiple_of(t * size, 128), loss_ref
        )
        store(before, ds)
        keep(following)
        return carry

    keep(logits(jnp.int32(0)))
    lax.fori_loop(0, count, body, 0)
    end = jnp.int32(count - 1)
    turn(end)
    store(end, product(end))

    def grads(k, carry):
        gw_ref[g_at + k] += mm(turned_ref[...], dlog_ref[:, pl.ds(pl.multiple_of(k * WIDTH, WIDTH), WIDTH)])
        return carry

    lax.fori_loop(0, 3, grads, 0)


def unpack_vec(w, vec_ref):
    vec_ref[...] = w[:, 0:128].astype(F32).T


def moves_hot(ints):
    rows = lax.broadcasted_iota(jnp.int32, (16, ints.shape[1]), 0)
    return jnp.where((rows == ints[0:1]) | (rows == 4), 1.0, 0.0).astype(BF16)


def table_of(vec_ref):
    rows = lax.broadcasted_iota(jnp.int32, (16, WIDTH), 0)
    return jnp.where(rows < 5, vec_ref[0:16, :], 0.0).astype(BF16)


def stem_forward(latent_ref, hot_ref, vec_ref, w, s_ref, n_ref, slope_ref, r_ref, pre_ref, n_at):
    table = table_of(vec_ref)
    scale = scales(vec_ref, 5, 1)

    def product(c):
        span = pl.ds(rows_of(c), CHUNK)
        return mm(latent_ref[span, :], w) + mm(hot_ref[span, :], table)

    def body(c, carry):
        following = product(jnp.minimum(c + 1, PARTS - 1))
        for u in range(0, CHUNK, UNIT):
            rows = pl.ds(rows_of(c) + u, UNIT)
            act, n, slope, r = norm_gelu(pre_ref[u:u + UNIT, :], *scale)
            s_ref[rows, :] = act
            n_ref[n_at, rows, :] = n
            slope_ref[n_at, rows, :] = slope
            r_ref[n_at, rows, :] = r
        pre_ref[...] = following
        return carry

    pre_ref[...] = product(jnp.int32(0))
    lax.fori_loop(0, PARTS, body, 0)


def stem_backward(latent_ref, hot_ref, s_ref, low_ref, n_ref, slope_ref, r_ref, n_at, w, lgrad_ref, gw_ref, g_at, gv_ref):
    def products(c):
        span = pl.ds(rows_of(c), CHUNK)
        low = low_ref[...]
        lgrad_ref[span, :] = mm_nt(low, w).astype(BF16)
        gw_ref[g_at] += mm_tn(latent_ref[span, :], low)
        gv_ref[0:16, :] += mm_tn(hot_ref[span, :], low)

    def body(c, carry):
        products(jnp.maximum(c - 1, 0))
        shift = jnp.zeros((UNIT, WIDTH), F32)
        gain = shift
        held = []
        for u in range(0, CHUNK, UNIT):
            rows = pl.ds(rows_of(c) + u, UNIT)
            d_in, wf, wn = norm_back(s_ref[rows, :], slope_ref[n_at, rows, :], n_ref[n_at, rows, :], r_ref[n_at, rows, :])
            shift = shift + wf
            held.append(wn)
            if len(held) == GROUP:
                gain = gain + column_sums(held)
                held = []
            low_ref[u:u + UNIT, :] = d_in.astype(BF16)
        gv_ref[5:6, :] += fold(gain)
        gv_ref[6:7, :] += fold(shift)
        return carry

    low_ref[...] = jnp.zeros_like(low_ref)
    lax.fori_loop(0, PARTS, body, 0)
    products(PARTS - 1)


def clean_latent(latent_ref, lat_ref, rows_dev):
    lat_ref[...] = latent_ref[...]
    steps = -(-rows_dev // TILE)
    tail = rows_dev - (steps - 1) * TILE
    if tail < TILE:
        @pl.when(pl.program_id(0) == steps - 1)
        def _():
            lat_ref[tail:TILE, :] = jnp.zeros((TILE - tail, WIDTH), BF16)


def split_low(x):
    high = x.astype(BF16)
    return high, (x - high.astype(F32)).astype(BF16)


def join_pieces(pieces_ref, w_ref, at):
    rows = WIDTH // pieces_ref.shape[0]
    for f in range(pieces_ref.shape[0]):
        for m in range(pieces_ref.shape[1] // rows):
            w_ref[at + m, f * rows:(f + 1) * rows, :] = pieces_ref[f, m * rows:(m + 1) * rows, :]


def join_front(core_ref, front_refs, w_ref):
    if len(front_refs) == 1:
        join_pieces(front_refs[0], w_ref, 0)
    else:
        half = w_ref.shape[0] // 2
        for core in range(2):
            @pl.when(core_ref[0] == core)
            def _():
                join_pieces(front_refs[core], w_ref, 0)
                join_pieces(front_refs[1 - core], w_ref, half)


def cut_pieces(out_ref, m, matrix):
    rows = WIDTH // out_ref.shape[0]
    at = m * rows if isinstance(m, int) else pl.multiple_of(m * rows, rows)
    for f in range(out_ref.shape[0]):
        out_ref[f, pl.ds(at, rows), :] = matrix[f * rows:(f + 1) * rows, :].astype(BF16)


def cut_vectors(out_ref, at, wide):
    rows = WIDTH // out_ref.shape[0]
    half = rows // 2
    for f in range(out_ref.shape[0]):
        part = wide[f * rows:(f + 1) * rows, :]
        out_ref[f, at:at + half, :] = jnp.concatenate([part[0:half], part[half:rows]], axis=1).astype(BF16)


def copies(refs, away, sems, i, span, inward):
    out = []
    for k, (near, far) in enumerate(zip(refs, away)):
        ends = (far.at[i, span, :], near.at[i]) if inward else (near.at[i], far.at[i, span, :])
        out.append(pltpu.make_async_copy(*ends, sems.at[i, k]))
    return out


def tile_span(step):
    return pl.ds(pl.multiple_of(step * TILE, 128), TILE)


def first_kernel(layers, rows_dev, fronts, core_ref, latent_ref, ints_ref, *refs):
    front_refs = refs[:fronts]
    (
        n_out, slope_out, r_out, act_out, s_ref, vec_ref, w_ref, lat_ref, hot_ref, pre_ref, n_ref, slope_ref, r_ref, act_ref, sems,
    ) = refs[fronts:]
    step, steps = pl.program_id(0), pl.num_programs(0)
    span = tile_span(step)
    refs, away = (n_ref, slope_ref, r_ref, act_ref), (n_out, slope_out, r_out, act_out)

    def start(i, count=4):
        for copy in copies(refs[:count], away, sems, i, span, False):
            copy.start()

    def wait(i, count=4):
        for copy in copies(refs[:count], away, sems, i, span, False):
            copy.wait()

    @pl.when(step == 0)
    def _():
        join_front(core_ref, front_refs, w_ref)
        unpack_vec(w_ref[0], vec_ref)

    clean_latent(latent_ref, lat_ref, rows_dev)
    hot_ref[...] = moves_hot(ints_ref[...]).T

    @pl.when(step > 0)
    def _():
        wait(SPLIT, 3)

    stem_forward(lat_ref, hot_ref, vec_ref, w_ref[1], s_ref, n_ref, slope_ref, r_ref, pre_ref, SPLIT)
    start(SPLIT, 3)

    def after(i, c):
        @pl.when(c == PARTS - 1)
        def _():
            start(i)

            @pl.when((step > 0) & (i < SPLIT - 1))
            def _():
                wait(i + 1)

    @pl.when(step > 0)
    def _():
        wait(0)

    save = (act_ref, n_ref, slope_ref, r_ref)
    forward_layers(0, SPLIT, layers, s_ref, save, vec_ref, w_ref, -2, 0, after)

    @pl.when(step == steps - 1)
    def _():
        wait(SPLIT, 3)
        for i in range(SPLIT):
            wait(i)


def middle_kernel(
    layers, nq, s_in_ref, ints_ref, vec_ref, hb_ref, w_ref,
    latents_ref, value_ref, chance_ref, ds_ref, gv_ref, rep_ref, out_ref,
    wh_ref, s_ref, act_ref, n_ref, slope_ref, r_ref, low_ref, da_ref, turned_ref, dlog_ref, gw_ref, gh_ref, loss_ref, *chunk_refs,
):
    blocks = layers - SPLIT
    step = pl.program_id(0)

    @pl.when(step == 0)
    def _():
        for ref in (gw_ref, gh_ref, gv_ref, loss_ref):
            ref[...] = jnp.zeros_like(ref)
        turned_ref[WIDTH:, :] = jnp.ones_like(turned_ref[WIDTH:, :])
        for k in range(3):
            wh_ref[:, k * WIDTH:(k + 1) * WIDTH] = w_ref[blocks + k]

    s_ref[0:TILE, :] = s_in_ref[...]
    save = (act_ref, n_ref, slope_ref, r_ref)
    forward_layers(SPLIT, layers, layers, s_ref, save, vec_ref, w_ref, SPLIT, SPLIT)
    heads(nq, ints_ref, s_ref, ds_ref, low_ref, wh_ref, hb_ref, latents_ref, value_ref, chance_ref, turned_ref, dlog_ref, loss_ref, *chunk_refs, gh_ref, 0)
    backward_layers(SPLIT, layers, layers, ds_ref, low_ref, da_ref, save, w_ref, SPLIT, SPLIT, gw_ref, gv_ref, SPLIT)

    @pl.when(step == pl.num_programs(0) - 1)
    def _():
        def put(m, carry):
            cut_pieces(out_ref, m, gw_ref.at[m])
            return carry

        lax.fori_loop(0, blocks, put, 0)
        for k in range(3):
            cut_pieces(out_ref, blocks + k, gh_ref.at[k])
        row = lax.broadcasted_iota(jnp.int32, (8, WIDTH), 0)
        total = jnp.where(row == 3, jnp.concatenate([fold(loss_ref[...]), jnp.zeros((1, 128), F32)], axis=1), 0.0)
        for k in range(3):
            total = jnp.where(row == k, gh_ref[k, WIDTH:WIDTH + 1, :], total)
        rep_ref[...] = total
        at = (blocks + 3) * WIDTH // out_ref.shape[0]
        high, low = split_low(total)
        for f in range(out_ref.shape[0]):
            out_ref[f, at:at + 16, :] = jnp.concatenate([high, low], axis=0)


def last_kernel(layers, rows_dev, fronts, core_ref, latent_ref, ints_ref, ds_in_ref, n_in, slope_in, r_in, act_in, gv_in_ref, *refs):
    front_refs = refs[:fronts]
    (
        lgrad_ref, out_ref, w_ref, lat_ref, hot_ref, ds_ref, low_ref, da_ref, chunk_ref, n_ref, slope_ref, r_ref, act_ref, gw_ref, gv_ref,
        sems,
    ) = refs[fronts:]
    step, steps = pl.program_id(0), pl.num_programs(0)
    refs, away = (n_ref, slope_ref, r_ref, act_ref), (n_in, slope_in, r_in, act_in)

    def start(i, to, count=4):
        for copy in copies(refs[:count], away, sems, i, tile_span(to), True):
            copy.start()

    def wait(i, count=4):
        for copy in copies(refs[:count], away, sems, i, tile_span(step), True):
            copy.wait()

    @pl.when(step == 0)
    def _():
        start(SPLIT - 1, 0)
        join_front(core_ref, front_refs, w_ref)
        gw_ref[...] = jnp.zeros_like(gw_ref)
        gv_ref[...] = gv_in_ref[...]

    clean_latent(latent_ref, lat_ref, rows_dev)
    hot_ref[...] = moves_hot(ints_ref[...]).T
    ds_ref[...] = ds_in_ref[...]
    low_ref[...] = ds_in_ref[...].astype(BF16)

    def after(i, c):
        @pl.when(c == PARTS - 1)
        def _():
            @pl.when(step < steps - 1)
            def _():
                start(i, step + 1)

            @pl.when(i > 0)
            def _():
                wait(i - 1)

    wait(SPLIT - 1)

    @pl.when(step == 0)
    def _():
        for i in reversed(range(SPLIT - 1)):
            start(i, 0)
        start(SPLIT, 0, 3)

    save = (act_ref, n_ref, slope_ref, r_ref)
    backward_layers(0, SPLIT, layers, ds_ref, low_ref, da_ref, save, w_ref, -2, 0, gw_ref, gv_ref, -1, after)
    wait(SPLIT, 3)
    stem_backward(lat_ref, hot_ref, ds_ref, chunk_ref, n_ref, slope_ref, r_ref, SPLIT, w_ref[1], lgrad_ref, gw_ref, 0, gv_ref)

    @pl.when(step < steps - 1)
    def _():
        start(SPLIT, step + 1, 3)

    @pl.when(step == steps - 1)
    def _():
        for m in range(SPLIT + 1):
            cut_pieces(out_ref, m, gw_ref[m])
        high, low = split_low(jnp.concatenate([gv_ref[...], jnp.zeros((64 - gv_ref.shape[0], WIDTH), F32)], axis=0))
        wide = jnp.concatenate([high, low], axis=0).astype(F32).T
        cut_vectors(out_ref, (SPLIT + 1) * WIDTH // out_ref.shape[0], wide)


def pack_kernel(
    fronts, core_ref, stem_ref, table_ref, stem_vec_ref, block_ref, gain_ref, shift_ref, bias_ref, value_ref, chance_ref, front_ref,
    back_ref, vec_ref,
):
    layers, shard = block_ref.shape[0], block_ref.shape[1]
    nq, nc = value_ref.shape[1], chance_ref.shape[1]
    vec_ref[...] = jnp.zeros_like(vec_ref)
    at = 0
    for ref in (table_ref, stem_vec_ref, gain_ref, shift_ref, bias_ref):
        vec_ref[at:at + ref.shape[0], 0:shard] = ref[...].astype(F32)
        at += ref.shape[0]
    vectors = vec_ref[...].T[0:shard, :]
    vectors = jnp.concatenate([vectors, jnp.zeros_like(vectors)], axis=1).astype(BF16)
    entries = [lambda: vectors, lambda: stem_ref[...]] + [functools.partial(block_ref.__getitem__, i) for i in range(SPLIT)]
    half = len(entries) // fronts
    for core in range(fronts):
        @pl.when(core_ref[0] == core if fronts > 1 else core_ref[0] >= 0)
        def _():
            for m in range(half):
                entry = entries[core * half + m]()
                for f in range(front_ref.shape[0]):
                    front_ref[f, m * shard:(m + 1) * shard, :] = entry
    for i in range(SPLIT, layers):
        back_ref[i - SPLIT] = block_ref[i]
    at = layers - SPLIT
    back_ref[at:] = jnp.zeros_like(back_ref[at:])
    for k in range(3):
        width = min(WIDTH, nq - k * WIDTH)
        back_ref[at + k, :, 0:width] = value_ref[:, k * WIDTH:k * WIDTH + width]
    back_ref[at + 2, :, 128:128 + nc] = chance_ref[...]


def total_rows(refs, rows):
    total = refs[0][rows, :].astype(F32)
    for ref in refs[1:]:
        total = total + ref[rows, :].astype(F32)
    return total


def sum_mid_kernel(in_ref, out_ref):
    refs = [in_ref.at[f] for f in range(in_ref.shape[0])]
    end = in_ref.shape[1]
    for at in range(0, end - 16, 32):
        out_ref[at:at + 32, :] = total_rows(refs, slice(at, at + 32)).astype(BF16)
    total = total_rows(refs, slice(end - 16, end))
    high, low = split_low(total[0:8] + total[8:16])
    out_ref[end - 16:end, :] = jnp.concatenate([high, low], axis=0)


def sum_end_kernel(in_ref, out_ref):
    refs = [in_ref.at[f] for f in range(in_ref.shape[0])]
    end, vec = in_ref.shape[1], WIDTH // in_ref.shape[0] // 2
    for at in range(0, end - vec, 32):
        out_ref[at:at + 32, :] = total_rows(refs, slice(at, at + 32)).astype(BF16)
    total = total_rows(refs, slice(end - vec, end))
    parts = []
    for k in (0, 128):
        parts += split_low(total[:, k:k + 64] + total[:, k + 64:k + 128])
    out_ref[end - vec:end, :] = jnp.concatenate(parts, axis=1)


def finish_kernel(count, compact, scale, stem_vec_ref, gain_ref, *refs):
    mids, ends = refs[:count], refs[count:2 * count]
    (
        loss_ref, stem_ref, table_ref, stem_bias_ref, stem_gain_ref, stem_shift_ref, block_ref, block_gain_ref, block_shift_ref,
        block_bias_ref, value_ref, value_bias_ref, chance_ref, chance_bias_ref,
    ) = refs[2 * count:]
    layers, shard, moves = block_ref.shape[0], block_ref.shape[1], table_ref.shape[0]
    nq, nc = value_ref.shape[1], chance_ref.shape[1]

    def mid_of(at, rows):
        return total_rows(mids, slice(at, at + rows)) * scale

    def end_of(at, rows):
        return total_rows(ends, slice(at, at + rows)) * scale

    for i in range(SPLIT, layers):
        block_ref[i] = mid_of((i - SPLIT) * shard, shard)
    for i in range(SPLIT):
        block_ref[i] = end_of((1 + i) * shard, shard)
    stem_ref[...] = end_of(0, shard)
    for k in range(3):
        width = min(WIDTH, nq - k * WIDTH)
        part = mid_of((layers - SPLIT + k) * shard, shard)
        value_ref[:, k * WIDTH:k * WIDTH + width] = part[:, 0:width]
    chance_ref[...] = part[:, 128:128 + nc]
    rep = mid_of((layers - SPLIT + 3) * shard, 16)
    rep = rep[0:8] + rep[8:16]
    bias = jnp.concatenate([rep[k:k + 1] for k in range(3)], axis=1)
    value_bias_ref[...] = bias[:, 0:nq]
    chance_bias_ref[...] = bias[:, 640:640 + nc]
    loss_ref[0] = jnp.sum(rep[3:4])
    at = (1 + SPLIT) * shard
    if compact:
        small = end_of(at, shard // 2)
        small = jnp.concatenate([small[:, 0:128], small[:, 128:256]], axis=0)
    else:
        small = end_of(at, shard)[:, 0:128]
    if shard % 128:
        small = jnp.concatenate([small, jnp.zeros((128 - shard, 128), F32)], axis=0)
    small = small.T[:, 0:shard]
    small = small[0:64] + small[64:128]
    table_ref[...] = small[0:moves]
    stem_gain = stem_vec_ref[1:2, :].astype(F32)
    stem_bias_ref[...] = small[moves:moves + 1]
    stem_gain_ref[...] = small[moves + 1:moves + 2] / stem_gain
    stem_shift_ref[...] = small[moves + 2:moves + 3] / (16.0 * stem_gain)
    at = moves + 3
    gain = gain_ref[...].astype(F32)
    block_gain_ref[...] = small[at:at + layers] / gain
    block_shift_ref[...] = small[at + layers:at + 2 * layers] / (16.0 * gain)
    block_bias_ref[...] = small[at + 2 * layers:at + 3 * layers]


SMEM = pl.BlockSpec(memory_space=pltpu.SMEM)
VMEM = pl.BlockSpec(memory_space=pltpu.VMEM)
ANY = pl.BlockSpec(memory_space=pl.ANY)


def params(mib):
    return pltpu.CompilerParams(vmem_limit_bytes=mib << 20)


def tiled(shape, dim):
    block = shape[:dim] + (TILE,) + shape[dim + 1:]
    return pl.BlockSpec(block, lambda i: (0,) * dim + (i,) + (0,) * (len(shape) - dim - 1))


def whole(shape):
    return pl.BlockSpec(shape, lambda i: (0,) * len(shape))


def once(shape):
    return pl.BlockSpec(shape, lambda i: (0,) * len(shape), pipeline_mode=pl.Buffered(1))


def struct(shape, dtype):
    return jax.ShapeDtypeStruct(shape, dtype)


def exchange(x, axis, size):
    return [lax.ppermute(x, axis, [(i, i ^ k) for i in range(size)]) for k in range(1, size)]


def per_device(
    latent, actions, value_bins, chance_codes, step_mask, stem_weight, action_table, stem_bias, stem_gain, stem_shift,
    block_weight, block_gain, block_shift, block_bias, value_weight, value_bias, chance_weight, chance_bias,
):
    n_dp, n_fsdp = lax.axis_size("dp"), lax.axis_size("fsdp")
    rows_dev = latent.shape[0]
    layers, shard = block_weight.shape[0], block_weight.shape[1]
    nq, nc = value_weight.shape[1], chance_weight.shape[1]
    moves = action_table.shape[0]
    steps = -(-rows_dev // TILE)
    padded = steps * TILE
    fast = shard % 16 == 0 and n_dp & (n_dp - 1) == 0

    pieces, piece_rows = (n_fsdp, shard) if fast else (1, WIDTH)
    fronts = 2 if fast and n_dp % 2 == 0 and SPLIT % 2 == 0 else 1
    core = (lax.axis_index("dp") % 2).astype(jnp.int32).reshape(1)
    stem_vec = jnp.stack([stem_bias, stem_gain, stem_shift])
    n_front = (2 + SPLIT) // fronts
    front, back = pl.pallas_call(
        functools.partial(pack_kernel, fronts),
        in_specs=[SMEM] + [VMEM] * 9,
        out_specs=[VMEM] * 2,
        out_shape=[struct((pieces, n_front * shard, WIDTH), BF16), struct((layers - SPLIT + 3, shard, WIDTH), BF16)],
        scratch_shapes=[pltpu.VMEM((128, max(shard, 128)), F32)],
        name="pack",
    )(core, stem_weight, action_table, stem_vec, block_weight, block_gain, block_shift, block_bias, value_weight, chance_weight)
    if fast:
        w_fronts = [lax.all_to_all(front, "fsdp", 0, 0)]
        if fronts > 1:
            w_fronts.append(lax.ppermute(w_fronts[0], "dp", [(i, i ^ 1) for i in range(n_dp)]))
    else:
        front = lax.all_gather(front.reshape(n_front, shard, WIDTH), "fsdp", axis=1, tiled=True)
        w_fronts = [front.reshape(1, n_front * WIDTH, WIDTH)]
    w_back = lax.all_gather(back, "fsdp", axis=1, tiled=True)

    ints = jnp.pad(jnp.stack([actions, value_bins, chance_codes, step_mask]), ((0, 4), (0, padded - rows_dev)))
    ints_spec = pl.BlockSpec((8, TILE), lambda i: (0, i))
    none = lambda n: jnp.full((n,), -1e30, BF16)
    head_bias = jnp.concatenate([value_bias, none(640 - nq), chance_bias, none(128 - nc)])[None]

    saved = [
        struct((SPLIT + 1, padded, WIDTH), BF16),
        struct((SPLIT + 1, padded, WIDTH), BF16),
        struct((SPLIT + 1, padded, 128), F32),
        struct((SPLIT, padded, WIDTH), BF16),
    ]
    scratch = pltpu.VMEM
    kept = [scratch((x.shape[0], TILE, x.shape[2]), x.dtype) for x in saved] + [pltpu.SemaphoreType.DMA((SPLIT + 1, 4))]
    stream = struct((padded, WIDTH), F32)
    front_shape = (2 + SPLIT, WIDTH, WIDTH)
    *held, s_mid, vec = pl.pallas_call(
        functools.partial(first_kernel, layers, rows_dev, fronts),
        grid=(steps,),
        in_specs=[SMEM, tiled((rows_dev, WIDTH), 0), ints_spec] + [once(x.shape) for x in w_fronts],
        out_specs=[ANY] * 4 + [tiled(stream.shape, 0), whole((128, WIDTH))],
        out_shape=saved + [stream, struct((128, WIDTH), F32)],
        scratch_shapes=[scratch(front_shape, BF16), scratch((TILE, WIDTH), BF16), scratch((TILE, 16), BF16), scratch((CHUNK, WIDTH), F32)] + kept,
        compiler_params=params(62),
        cost_estimate=pl.CostEstimate(flops=rows_dev * WIDTH * WIDTH * 200, bytes_accessed=60 << 20, transcendentals=0),
        name="first",
    )(core, latent, ints, *w_fronts)

    blocks = layers - SPLIT
    compact = piece_rows % 32 == 0 and fast
    mid_shape = (pieces, (blocks + 3) * piece_rows + 16, WIDTH)
    end_shape = (pieces, (SPLIT + 1) * piece_rows + piece_rows // 2, WIDTH)
    latents, value_logits, chance_logits, ds_mid, gv_mid, rep, parts_mid = pl.pallas_call(
        functools.partial(middle_kernel, layers, nq),
        grid=(steps,),
        in_specs=[tiled(stream.shape, 0), ints_spec, once(vec.shape), once(head_bias.shape), once(w_back.shape)],
        out_specs=[
            tiled((rows_dev, WIDTH), 0), tiled((nq, rows_dev), 1), tiled((nc, rows_dev), 1), tiled(stream.shape, 0),
            whole((48, WIDTH)), whole((8, WIDTH)), whole(mid_shape),
        ],
        out_shape=[
            struct((rows_dev, WIDTH), BF16), struct((nq, rows_dev), BF16), struct((nc, rows_dev), BF16), stream,
            struct((48, WIDTH), F32), struct((8, WIDTH), F32), struct(mid_shape, BF16),
        ],
        scratch_shapes=[
            scratch((WIDTH, 3 * WIDTH), BF16),
            scratch((TILE + CHUNK, WIDTH), F32),
            scratch((blocks, TILE, WIDTH), BF16),
            scratch((blocks, TILE, WIDTH), BF16),
            scratch((blocks, TILE, WIDTH), BF16),
            scratch((blocks, TILE, 128), F32),
            scratch((TILE, WIDTH), BF16),
            scratch((CHUNK, WIDTH), F32),
            scratch((WIDTH + 16, TILE), BF16),
            scratch((TILE, 3 * WIDTH), BF16),
            scratch((blocks, WIDTH, WIDTH), F32),
            scratch((3, WIDTH + 16, WIDTH), F32),
            scratch((UNIT, 128), F32),
            scratch((HEAD_CHUNK, 3 * WIDTH), F32),
            scratch((HEAD_CHUNK, 384), F32),
            scratch((2, HEAD_CHUNK, 128), F32),
            scratch((2, HEAD_CHUNK, 128), F32),
            scratch((HEAD_CHUNK, 3 * WIDTH), F32),
            scratch((6, HEAD_CHUNK, 128), BF16),
        ],
        compiler_params=params(62),
        cost_estimate=pl.CostEstimate(flops=rows_dev * WIDTH * WIDTH * 600, bytes_accessed=40 << 20, transcendentals=0),
        name="middle",
    )(s_mid, ints, vec, head_bias, w_back)

    latent_grad, parts_end = pl.pallas_call(
        functools.partial(last_kernel, layers, rows_dev, fronts),
        grid=(steps,),
        in_specs=[SMEM, tiled((rows_dev, WIDTH), 0), ints_spec, tiled(stream.shape, 0)]
        + [ANY] * 4 + [once((48, WIDTH))] + [once(x.shape) for x in w_fronts],
        out_specs=[tiled((rows_dev, WIDTH), 0), whole(end_shape)],
        out_shape=[struct((rows_dev, WIDTH), BF16), struct(end_shape, BF16)],
        scratch_shapes=[
            scratch(front_shape, BF16),
            scratch((TILE, WIDTH), BF16),
            scratch((TILE, 16), BF16),
            scratch((TILE, WIDTH), F32),
            scratch((TILE, WIDTH), BF16),
            scratch((CHUNK, WIDTH), F32),
            scratch((CHUNK, WIDTH), BF16),
        ] + kept[:4] + [
            scratch((SPLIT + 1, WIDTH, WIDTH), F32),
            scratch((48, WIDTH), F32),
        ] + kept[4:],
        compiler_params=params(62),
        cost_estimate=pl.CostEstimate(flops=rows_dev * WIDTH * WIDTH * 150, bytes_accessed=60 << 20, transcendentals=0),
        name="last",
    )(core, latent, ints, ds_mid, *held, gv_mid, *w_fronts)

    if fast:
        got_mid = lax.all_to_all(parts_mid, "fsdp", 0, 0)
        parts_end, got_mid = lax.optimization_barrier((parts_end, got_mid))
        got_end = lax.all_to_all(parts_end, "fsdp", 0, 0)

        def add(body, got, name):
            return pl.pallas_call(
                body, in_specs=[VMEM], out_specs=VMEM, out_shape=struct(got.shape[1:], BF16), name=name,
            )(got)

        mine_mid, mine_end = add(sum_mid_kernel, got_mid, "sum_mid"), add(sum_end_kernel, got_end, "sum_end")
        mids = [mine_mid] + exchange(mine_mid, "dp", n_dp)
        ends = [mine_end] + exchange(mine_end, "dp", n_dp)
    else:
        def scatter(x, count):
            x = x[0, :count * WIDTH].reshape(count, WIDTH, WIDTH)
            x = lax.psum_scatter(x, "fsdp", scatter_dimension=1, tiled=True).astype(F32)
            return lax.psum(x, "dp").reshape(count * shard, WIDTH)

        rep = lax.psum(rep, ("dp", "fsdp"))
        vectors = parts_end[0, (SPLIT + 1) * WIDTH:]
        vectors = jnp.concatenate([vectors[:, 0:128], vectors[:, 128:256]], axis=0)
        vectors = jnp.concatenate([vectors, jnp.zeros_like(vectors)], axis=1)
        parts_end = jnp.concatenate([parts_end[:, :(SPLIT + 1) * WIDTH], vectors[None]], axis=1)
        mids = [jnp.concatenate([scatter(parts_mid, blocks + 3), rep, jnp.zeros((8, WIDTH), F32)])]
        ends = [scatter(parts_end, SPLIT + 2)]

    shapes = [
        (1,), (shard, WIDTH), (moves, shard), (1, shard), (1, shard), (1, shard), (layers, shard, WIDTH), (layers, shard),
        (layers, shard), (layers, shard), (shard, nq), (1, nq), (shard, nc), (1, nc),
    ]
    (
        loss, stem_grad, table_grad, stem_bias_grad, stem_gain_grad, stem_shift_grad, block_grad, gain_grad, shift_grad, bias_grad,
        value_grad, value_bias_grad, chance_grad, chance_bias_grad,
    ) = pl.pallas_call(
        functools.partial(finish_kernel, len(mids), compact, 1.0 / (rows_dev * n_dp * n_fsdp)),
        in_specs=[VMEM] * (2 + 2 * len(mids)),
        out_specs=[SMEM] + [VMEM] * (len(shapes) - 1),
        out_shape=[struct(x, F32) for x in shapes],
        name="finish",
    )(stem_vec, block_gain, *mids, *ends)
    return (
        latents,
        value_logits.T,
        chance_logits.T,
        loss.reshape(()),
        latent_grad,
        stem_grad,
        table_grad,
        stem_bias_grad.reshape(shard),
        stem_gain_grad.reshape(shard),
        stem_shift_grad.reshape(shard),
        block_grad,
        gain_grad,
        shift_grad,
        bias_grad,
        value_grad,
        value_bias_grad.reshape(nq),
        chance_grad,
        chance_bias_grad.reshape(nc),
    )


def solution(mesh):
    placed = (
        P(("dp", "fsdp"), None),
        P(("dp", "fsdp")),
        P(("dp", "fsdp")),
        P(("dp", "fsdp")),
        P(("dp", "fsdp")),
        P("fsdp", None),
        P(None, "fsdp"),
        P("fsdp"),
        P("fsdp"),
        P("fsdp"),
        P(None, "fsdp", None),
        P(None, "fsdp"),
        P(None, "fsdp"),
        P(None, "fsdp"),
        P("fsdp", None),
        P(),
        P("fsdp", None),
        P(),
    )
    return jax.shard_map(
        per_device,
        mesh=mesh,
        in_specs=placed,
        out_specs=(
            P(("dp", "fsdp"), None),
            P(("dp", "fsdp"), None),
            P(("dp", "fsdp"), None),
            P(),
            P(("dp", "fsdp"), None),
            P("fsdp", None),
            P(None, "fsdp"),
            P("fsdp"),
            P("fsdp"),
            P("fsdp"),
            P(None, "fsdp", None),
            P(None, "fsdp"),
            P(None, "fsdp"),
            P(None, "fsdp"),
            P("fsdp", None),
            P(),
            P("fsdp", None),
            P(),
        ),
        check_vma=False,
    )
```

time: 273 us -> 248 us (0.908)
  blocking collectives: 25.7 us -> 0 us
  starting transfers between devices: 12.7 us -> 20.7 us
  Pallas kernels: 178 us -> 174 us
  other arithmetic: 6.93 us -> 3.42 us
  local copies, waits for them, and re-layouts: 3.87 us -> 7.21 us
    all_to_all x1 -> x0, blocking collectives: 25.7 us -> none  [per_device(): got_end = lax.all_to_all(parts_end, 'fsdp', 0, 0)]
    ppermute x3 -> x6, waiting for transfers between devices: 12.6 us -> 5.18 us  [exchange(): lax.ppermute(x, axis, [(i, i ^ k) for i in range(size)])]
    all_to_all x1 -> x2, starting transfers between devices: 7.25 us -> 13.3 us  [the longest x1 7.25 us: per_device(): w_fronts = [lax.all_to_all(front, 'fsdp', 0, 0)]]
    pallas_call x1, Pallas kernels: 100 us -> 95.5 us  [per_device(): pl.pallas_call(functools.partial(middle_kernel, layers, nq), grid=(steps,...]
    all_to_all x1 -> x2, waiting for transfers between devices: 17.3 us -> 21.1 us  [the longest x1 14.6 us: per_device(): got_end = lax.all_to_all(parts_end, 'fsdp', 0, 0)]
    another operation x4 -> x1, other arithmetic: 2.98 us -> 0.09 us  [per_device(): jnp.stack([actions, value_bins, chance_codes, step_mask])]
    another operation x6 -> x4, local copies, waits for them, and re-layouts: 0.26 us -> 3.02 us  [per_device(): jnp.stack([actions, value_bins, chance_codes, step_mask])]
    pallas_call x5 -> x6, Pallas kernels: 77.8 us -> 78.4 us  [the longest x1 38.3 us: per_device(): pl.pallas_call(functools.partial(first_kernel, layers, rows_dev, fronts),...]
  transfers between devices with their start and end apart: 6 -> 11, of which waited for: 3 -> 5; matrix products, arithmetic and copies ran while one was open for 2% -> 2% of each run, Pallas kernels for 26% -> 30%
where the time goes in v4:
time: 248 us; the launch traced here: 247 us
  Pallas kernels  174 us (70%)
  waiting for transfers between devices  28 us (11%)
  starting transfers between devices  20.7 us (8%)
  between operations  14.2 us (6%)
  local copies, waits for them, and re-layouts  7.21 us (3%)
  other arithmetic  3.42 us (1%)
    pallas_call x1, Pallas kernels, per_device(): pl.pallas_call(functools.partial(middle_kernel, layers, nq), grid=(steps,...  95.5 us
    pallas_call x1, Pallas kernels, per_device(): pl.pallas_call(functools.partial(first_kernel, layers, rows_dev, fronts),...  38.3 us
    pallas_call x1, Pallas kernels, per_device(): pl.pallas_call(functools.partial(last_kernel, layers, rows_dev, fronts),...  32.1 us
    all_to_all x1, waiting for transfers between devices, per_device(): got_end = lax.all_to_all(parts_end, 'fsdp', 0, 0)  14.6 us
    all_to_all x1, starting transfers between devices, per_device(): w_fronts = [lax.all_to_all(front, 'fsdp', 0, 0)]  7.25 us
    all_to_all x1, waiting for transfers between devices, per_device(): w_fronts = [lax.all_to_all(front, 'fsdp', 0, 0)]  6.55 us
    all_to_all x1, starting transfers between devices, per_device(): got_end = lax.all_to_all(parts_end, 'fsdp', 0, 0)  6 us
    ppermute x6, waiting for transfers between devices, exchange(): lax.ppermute(x, axis, [(i, i ^ k) for i in range(size)])  5.18 us
  transfers between devices with their start and end apart: 11, of which 5 were waited for; matrix products, arithmetic and copies ran while one was open for 2% of the time, Pallas kernels for 30%

profile of v4, /device:TPU:0, one launch (start us, length us, event | category | flops | bytes accessed | tf_op | source)
XLA Modules:
  0.0 247.4 jit_solution(9152954488106472780)
XLA Ops:
  7.2 1.3 pad_maximum_fusion.1.stem_vec_ref
  8.5 1.8 pack.1
  10.3 7.3 %all-to-all-start = ((bf16[8,96,256]{2,1,0:T(8,128)(2,1)}), bf16[8,96,256]{2,1,0:T(8,128)(2,1)S(1)}, u32[]{:S(2)}, u32[]{:S(2)}) async-start(bf16[8,96,256]{2,1,0:T(8,128)(2,1)} %get-tuple-element.50), calls=%async_computation | async-start | bytes 786432 | tf_op jit(solution)/shard_map/all_to_all | solution.py:752
  17.6 0.0 all-gather.2.cloned.1.call-start
  17.6 0.7 all-gather.2.cloned.1.call-update
  18.3 0.8 pad_maximum_fusion
  19.1 0.6 broadcast_in_dim.11.hb_ref
  19.7 0.8 stack.27
  20.4 0.8 stack.28
  21.2 0.8 stack.29
  22.0 0.8 stack.30
  22.7 6.5 %all-to-all-done.refs_0_ = bf16[8,96,256]{2,1,0:T(8,128)(2,1)S(1)} async-done(((bf16[8,96,256]{2,1,0:T(8,128)(2,1)}), bf16[8,96,256]{2,1,0:T(8,128)(2,1)S(1)}, u32[]{:S(2)}, u32[]{:S(2)}) %all-to-all-start) | async-done | bytes 393248 | tf_op jit(solution)/shard_map/all_to_all | solution.py:752
  29.3 0.0 copy-start.2
  29.3 0.0 collective-permute-start
  29.3 0.1 pad_add_fusion
  29.4 0.7 pad.4.ints_ref
  30.1 0.9 collective-permute-done.refs_1_
  31.0 0.0 copy-done.2
  31.0 0.0 copy-start.9
  31.0 0.8 copy-done.9
  31.7 38.3 %first.1 = (bf16[5,5760,256]{2,1,0:T(8,128)(2,1)}, bf16[5,5760,256]{2,1,0:T(8,128)(2,1)}, f32[5,5760,128]{2,1,0:T(8,128)}, bf16[4,5760,256]{2,1,0:T(8,128)(2,1)}...) custom-call(s32[1]{0:T(128)} %bitcast.core_ref, bf16[5696,256]{1,0:T(8,128)(2,1)} %latent_ref.3, s32[8,5760]{1,0:T(8,128)} %pad.4.ints_ref, ...), custom_call_target="tpu_custom_call" | custom-call | flops 74658611200 | bytes 62914560 | tf_op jit(solution)/shard_map/first/pallas_call | solution.py:775
  70.0 0.0 all-gather.2.cloned.1.call-done.w_ref
  70.1 95.5 %middle.1 = (bf16[5696,256]{1,0:T(8,128)(2,1)}, bf16[601,5696]{1,0:T(8,128)(2,1)}, bf16[32,5696]{1,0:T(8,128)(2,1)}, f32[5760,256]{1,0:T(8,128)}, f32[48,256]{1,...) custom-call(f32[5760,256]{1,0:T(8,128)} %get-tuple-element.51.s_in_ref, s32[8,5760]{1,0:T(8,128)} %pad.4.ints_ref, ...), custom_call_target="tpu_custom_call" | custom-call | flops 223975833600 | bytes 41943040 | tf_op jit(solution)/shard_map/middle/pallas_call | solution.py:791
  165.6 3.7 %all-to-all-start.1 = ((bf16[8,304,256]{2,1,0:T(8,128)(2,1)}), bf16[8,304,256]{2,1,0:T(8,128)(2,1)S(1)}, u32[]{:S(2)}, u32[]{:S(2)}) async-start(bf16[8,304,256]{2,1,0:T(8,128)(2,1)} %get-tuple-element.64), calls=%async_computation.1 | async-start | bytes 2490368 | tf_op jit(solution)/shard_map/all_to_all | solution.py:854
  169.3 32.1 %last.1 = (bf16[5696,256]{1,0:T(8,128)(2,1)}, bf16[8,176,256]{2,1,0:T(8,128)(2,1)}) custom-call(s32[1]{0:T(128)} %bitcast.core_ref, bf16[5696,256]{1,0:T(8,128)(2,1)} %latent_ref.3, s32[8,5760]{1,0:T(8,128)} %pad.4.ints_ref, f32[5760,256]{1,0:T(8,128)} %get-tuple-element.57.ds_in_ref, bf16[5,5760,256]{2,1,0:T(8,128)(2,1)} %get-tuple-element.58.n_in, ...), custom_call_target="tpu_custom_call" | custom-call | flops 55993958400 | bytes 62914560 | tf_op jit(solution)/shard_map/last/pallas_call | solution.py:829
  201.3 0.0 all-to-all-done.1.in_ref
  201.4 0.0 copy-start
  201.4 6.0 %all-to-all-start.2 = ((bf16[8,176,256]{2,1,0:T(8,128)(2,1)}), bf16[8,176,256]{2,1,0:T(8,128)(2,1)S(1)}, u32[]{:S(2)}, u32[]{:S(2)}) async-start(bf16[8,176,256]{2,1,0:T(8,128)(2,1)} %get-tuple-element.66), calls=%async_computation.2 | async-start | bytes 1441792 | tf_op jit(solution)/shard_map/all_to_all | solution.py:856
  207.4 0.0 copy-done
  207.4 2.1 sum_mid.1.refs_0_
  209.5 0.5 collective-permute-start.3
  210.0 1.0 collective-permute-start.2
  211.1 0.3 collective-permute-start.1
  211.4 14.6 %all-to-all-done.2.in_ref = bf16[8,176,256]{2,1,0:T(8,128)(2,1)S(1)} async-done(((bf16[8,176,256]{2,1,0:T(8,128)(2,1)}), bf16[8,176,256]{2,1,0:T(8,128)(2,1)S(1)}, u32[]{:S(2)}, u32[]{:S(2)}) %all-to-all-start.2) | async-done | bytes 720928 | tf_op jit(solution)/shard_map/all_to_all | solution.py:856
  226.0 0.0 copy-start.1
  226.0 0.9 copy-done.1
  226.8 1.9 sum_end.1.refs_4_
  228.7 0.0 collective-permute-start.6
  228.7 1.6 collective-permute-start.5
  230.3 0.0 collective-permute-done.3.refs_3_
  230.3 0.0 copy-start.3
  230.3 0.3 collective-permute-start.4
  230.6 0.0 collective-permute-done.2.refs_2_
  230.6 0.0 copy-start.4
  230.6 0.0 collective-permute-done.1.refs_1_
  230.6 0.0 copy-start.5
  230.6 3.2 %collective-permute-done.6.refs_7_ = bf16[176,256]{1,0:T(8,128)(2,1)S(1)} collective-permute-done((bf16[176,256]{1,0:T(8,128)(2,1)}, bf16[176,256]{1,0:T(8,128)(2,1)S(1)}, u32[]{:S(2)}, u32[]{:S(2)}) %collective-permute-start.6) | collective-permute-done | bytes 90144 | tf_op jit(solution)/shard_map/ppermute | solution.py:722
  233.8 0.0 copy-start.6
  233.8 2.0 collective-permute-done.5.refs_6_
  235.8 0.0 copy-start.7
  235.8 0.0 collective-permute-done.4.refs_5_
  235.8 0.0 copy-done.3
  235.8 0.0 copy-done.4
  235.8 0.0 copy-done.5
  235.8 0.0 copy-done.6
  235.8 0.6 copy-done.7
  236.4 0.0 copy-start.8
  236.4 0.6 copy-done.8
  237.1 2.2 finish.1
  239.3 1.3 reduce
  (2 shorter events, 0.0 us)
Async XLA Ops:
  10.3 19.0 %all-to-all-start = ((bf16[8,96,256]{2,1,0:T(8,128)(2,1)}), bf16[8,96,256]{2,1,0:T(8,128)(2,1)S(1)}, u32[]{:S(2)}, u32[]{:S(2)}) async-start(bf16[8,96,256]{2,1,0:T(8,128)(2,1)} %get-tuple-element.50), calls=%async_computation | async-start | bytes 786432 | tf_op jit(solution)/shard_map/all_to_all | solution.py:752
  17.6 52.5 %all-gather.2.cloned.1.call-start = ((), (), s32[]{:S(2)}) async-start(), calls=%async_computation.3 | async-start | bytes 1327104 | tf_op jit(solution)/shard_map/all_gather | solution.py:758
  29.3 1.7 copy-start.2
  29.3 1.7 collective-permute-start
  31.0 0.8 copy-start.9
  165.6 35.8 %all-to-all-start.1 = ((bf16[8,304,256]{2,1,0:T(8,128)(2,1)}), bf16[8,304,256]{2,1,0:T(8,128)(2,1)S(1)}, u32[]{:S(2)}, u32[]{:S(2)}) async-start(bf16[8,304,256]{2,1,0:T(8,128)(2,1)} %get-tuple-element.64), calls=%async_computation.1 | async-start | bytes 2490368 | tf_op jit(solution)/shard_map/all_to_all | solution.py:854
  201.4 6.0 %copy-start = (bf16[8,304,256]{2,1,0:T(8,128)(2,1)}, bf16[8,304,256]{2,1,0:T(8,128)(2,1)S(1)}, u32[]{:S(2)}) copy-start(bf16[8,304,256]{2,1,0:T(8,128)(2,1)S(1)} %all-to-all-done.1.in_ref) | copy-start | bytes 3735556
  201.4 24.6 %all-to-all-start.2 = ((bf16[8,176,256]{2,1,0:T(8,128)(2,1)}), bf16[8,176,256]{2,1,0:T(8,128)(2,1)S(1)}, u32[]{:S(2)}, u32[]{:S(2)}) async-start(bf16[8,176,256]{2,1,0:T(8,128)(2,1)} %get-tuple-element.66), calls=%async_computation.2 | async-start | bytes 1441792 | tf_op jit(solution)/shard_map/all_to_all | solution.py:856
  209.5 20.8 %collective-permute-start.3 = (bf16[304,256]{1,0:T(8,128)(2,1)}, bf16[304,256]{1,0:T(8,128)(2,1)S(1)}, u32[]{:S(2)}, u32[]{:S(2)}) collective-permute-start(bf16[304,256]{1,0:T(8,128)(2,1)} %sum_mid.1.refs_0_), channel_id=1, source_target_pairs={{0,24},{8,16},{16,8},{24,0},{1,25},{9,17},{17,9},{25,1},{2,26},{10... | collective-permute-start | bytes 466952 | tf_op jit(solution)/shard_map/ppermute | solution.py:722
  210.0 20.6 %collective-permute-start.2 = (bf16[304,256]{1,0:T(8,128)(2,1)}, bf16[304,256]{1,0:T(8,128)(2,1)S(1)}, u32[]{:S(2)}, u32[]{:S(2)}) collective-permute-start(bf16[304,256]{1,0:T(8,128)(2,1)} %sum_mid.1.refs_0_), channel_id=1, source_target_pairs={{0,16},{8,24},{16,0},{24,8},{1,17},{9,25},{17,1},{25,9},{2,18},{10... | collective-permute-start | bytes 466952 | tf_op jit(solution)/shard_map/ppermute | solution.py:722
  211.1 19.6 %collective-permute-start.1 = (bf16[304,256]{1,0:T(8,128)(2,1)}, bf16[304,256]{1,0:T(8,128)(2,1)S(1)}, u32[]{:S(2)}, u32[]{:S(2)}) collective-permute-start(bf16[304,256]{1,0:T(8,128)(2,1)} %sum_mid.1.refs_0_), channel_id=1, source_target_pairs={{0,8},{8,0},{16,24},{24,16},{1,9},{9,1},{17,25},{25,17},{2,10},{10... | collective-permute-start | bytes 466952 | tf_op jit(solution)/shard_map/ppermute | solution.py:722
  226.0 0.9 copy-start.1
  228.7 5.0 %collective-permute-start.6 = (bf16[176,256]{1,0:T(8,128)(2,1)}, bf16[176,256]{1,0:T(8,128)(2,1)S(1)}, u32[]{:S(2)}, u32[]{:S(2)}) collective-permute-start(bf16[176,256]{1,0:T(8,128)(2,1)} %sum_end.1.refs_4_), channel_id=1, source_target_pairs={{0,24},{8,16},{16,8},{24,0},{1,25},{9,17},{17,9},{25,1},{2,26},{10... | collective-permute-start | bytes 270344 | tf_op jit(solution)/shard_map/ppermute | solution.py:722
  228.7 7.1 %collective-permute-start.5 = (bf16[176,256]{1,0:T(8,128)(2,1)}, bf16[176,256]{1,0:T(8,128)(2,1)S(1)}, u32[]{:S(2)}, u32[]{:S(2)}) collective-permute-start(bf16[176,256]{1,0:T(8,128)(2,1)} %sum_end.1.refs_4_), channel_id=1, source_target_pairs={{0,16},{8,24},{16,0},{24,8},{1,17},{9,25},{17,1},{25,9},{2,18},{10... | collective-permute-start | bytes 270344 | tf_op jit(solution)/shard_map/ppermute | solution.py:722
  230.3 5.5 %copy-start.3 = (bf16[304,256]{1,0:T(8,128)(2,1)}, bf16[304,256]{1,0:T(8,128)(2,1)S(1)}, u32[]{:S(2)}) copy-start(bf16[304,256]{1,0:T(8,128)(2,1)S(1)} %collective-permute-done.3.refs_3_) | copy-start | bytes 466948
  230.3 5.5 %collective-permute-start.4 = (bf16[176,256]{1,0:T(8,128)(2,1)}, bf16[176,256]{1,0:T(8,128)(2,1)S(1)}, u32[]{:S(2)}, u32[]{:S(2)}) collective-permute-start(bf16[176,256]{1,0:T(8,128)(2,1)} %sum_end.1.refs_4_), channel_id=1, source_target_pairs={{0,8},{8,0},{16,24},{24,16},{1,9},{9,1},{17,25},{25,17},{2,10},{10... | collective-permute-start | bytes 270344 | tf_op jit(solution)/shard_map/ppermute | solution.py:722
  230.6 5.2 %copy-start.4 = (bf16[304,256]{1,0:T(8,128)(2,1)}, bf16[304,256]{1,0:T(8,128)(2,1)S(1)}, u32[]{:S(2)}) copy-start(bf16[304,256]{1,0:T(8,128)(2,1)S(1)} %collective-permute-done.2.refs_2_) | copy-start | bytes 466948
  230.6 5.2 %copy-start.5 = (bf16[304,256]{1,0:T(8,128)(2,1)}, bf16[304,256]{1,0:T(8,128)(2,1)S(1)}, u32[]{:S(2)}) copy-start(bf16[304,256]{1,0:T(8,128)(2,1)S(1)} %collective-permute-done.1.refs_1_) | copy-start | bytes 466948
  233.8 2.0 copy-start.6
  235.8 0.6 copy-start.7
  236.4 0.7 copy-start.8
Sparse Core Ops, SparseCore 0:
  21.2 42.4 all-gather.1

commit v5 on v4

--- a/solution.py
+++ b/solution.py
@@ -11,6 +11,7 @@
 WIDTH = 256
 UNIT = 16
 TILE = 1920
+BACK = 640
 CHUNK = 640
 PARTS = TILE // CHUNK
 HEAD_CHUNK = 384
@@ -42,7 +43,7 @@
     e1 = 1.0 + t
     bend = (h * (y + K0 / (3 * K1))) * (1.0 - t)
     slope = (e1 * gain_slope) * (1.0 / (3 * K1) + bend)
-    return h * e1, n.astype(BF16), slope.astype(BF16), jnp.broadcast_to(r, (UNIT, 128))
+    return h * e1, n.astype(BF16), slope, jnp.broadcast_to(r, (UNIT, 128))
 
 
 def scales(vec_ref, at, layers):
@@ -50,15 +51,17 @@
     return gain * 8.0, gain * (8.0 * 3 * K1), vec_ref[pl.ds(at + layers, 1), :] * 0.5
 
 
+def lane_sums(x):
+    total = lax.reduce_sum(x[:, 0:128] + x[:, 128:256], (1,))
+    return jnp.broadcast_to(total[:, None], (UNIT, 128))
+
+
 def norm_back(da, slope, n, r):
     w = da * slope.astype(F32)
-    m1 = jnp.sum(w, axis=1, keepdims=True) * (1.0 / WIDTH)
     w16 = w.astype(BF16)
     wn = w16 * n
-    wide = (wn[:, 0:128] + wn[:, 128:256]).astype(F32)
-    m2 = jnp.sum(wide, axis=1, keepdims=True)
-    m1 = jnp.broadcast_to(m1, (UNIT, 128)).astype(BF16)
-    m2 = jnp.broadcast_to(m2, (UNIT, 128)).astype(BF16)
+    m1 = lane_sums(w16) * BF16(1.0 / WIDTH)
+    m2 = lane_sums(wn)
     halves = [
         (w[:, k:k + 128] - (m1 + n[:, k:k + 128] * m2).astype(F32)) * r for k in (0, 128)
     ]
@@ -76,23 +79,20 @@
         act, n, slope, r = norm_gelu(s_ref[rows, :], *scale)
         act_ref[i, rows, :] = act.astype(BF16)
         n_ref[i, rows, :] = n
-        slope_ref[i, rows, :] = slope
+        slope_ref[i, rows, :] = slope.astype(slope_ref.dtype)
         r_ref[i, rows, :] = r
 
 
-def following(i, c, change):
-    end = c == PARTS - 1
+def following(i, c, parts, change):
+    end = c == parts - 1
     return jnp.where(end, i + change, i), jnp.where(end, 0, c + 1)
 
 
-def forward_layers(first, last, layers, s_ref, save, vec_ref, w_ref, w_at, save_at, after=None):
+def forward_layers(first, last, layers, s_ref, save, vec_ref, w_ref, w_at, save_at, before_block=None, after_block=None):
     act_ref = save[0]
 
     def product(i, c):
         return mm(act_ref[i - save_at, pl.ds(rows_of(c), CHUNK), :], w_ref[i - w_at])
-
-    def activation(i, c):
-        activate(rows_of(c), s_ref, save, i - save_at, scales(vec_ref, 7 + i, layers))
 
     def residual(i, base, out):
         bias = vec_ref[pl.ds(7 + 2 * layers + i, 1), :]
@@ -100,26 +100,25 @@
             rows = pl.ds(base + u, UNIT)
             s_ref[rows, :] = s_ref[rows, :] + (out[u:u + UNIT, :] + bias)
 
-    def body(t, carry):
-        before, now = carry
-        out = product(*before)
-        activation(*now)
-        base = rows_of(before[1])
-        if spare:
-            base = pl.multiple_of(jnp.where(t == 0, TILE, base), UNIT)
-        residual(before[0], base, out)
-        if after is not None:
-            after(*now)
-        return now, following(*now, 1)
-
-    spare = s_ref.shape[0] > TILE
-    start = jnp.int32(first), jnp.int32(0)
-    carry = start, start
-    if not spare:
-        activation(*start)
-        carry = start, following(*start, 1)
-    end, _ = lax.fori_loop(0 if spare else 1, (last - first) * PARTS, body, carry)
-    residual(end[0], rows_of(end[1]), product(*end))
+    def block(i, carry):
+        if before_block is not None:
+            before_block(i)
+
+        def chunk(c, carry):
+            old_i, old_c, base = carry
+            out = product(old_i, old_c)
+            activate(rows_of(c), s_ref, save, i - save_at, scales(vec_ref, 7 + i, layers))
+            residual(old_i, pl.multiple_of(base, UNIT), out)
+            return i, c, c * CHUNK
+
+        carry = lax.fori_loop(0, PARTS, chunk, carry)
+        if after_block is not None:
+            after_block(i)
+        return carry
+
+    start = jnp.int32(first), jnp.int32(0), jnp.int32(TILE)
+    i, c, base = lax.fori_loop(first, last, block, start)
+    residual(i, pl.multiple_of(base, UNIT), product(i, c))
 
 
 def column_sums(parts):
@@ -129,30 +128,31 @@
     return total.astype(F32)
 
 
-GROUP = 4
+GROUP = 8
 
 
 def fold(x):
     return jnp.sum(x, axis=0, keepdims=True)
 
 
-def backward_layers(first, last, layers, s_ref, low_ref, da_ref, save, w_ref, w_at, save_at, gw_ref, gv_ref, g_at, after=None):
+def backward_layers(first, last, layers, s_ref, low_ref, da_ref, save, w_ref, w_at, save_at, gw_ref, gv_ref, g_at, after_block=None, beside=None):
     act_ref, n_ref, slope_ref, r_ref = save
 
     def product(i, c):
-        return mm_nt(low_ref[pl.ds(rows_of(c), CHUNK), :], w_ref[i - w_at])
-
-    def body(t, carry):
-        i, c = carry
-        base = rows_of(c)
-        next_i, next_c = following(i, c, -1)
+        return mm_nt(low_ref[pl.ds(pl.multiple_of(c * BACK, UNIT), BACK), :], w_ref[i - w_at])
+
+    def chunk(i, c):
+        base = pl.multiple_of(c * BACK, UNIT)
+        next_i, next_c = following(i, c, TILE // BACK, -1)
         next_i = jnp.maximum(next_i, first)
         next_da = product(next_i, next_c)
-        gw_ref[i - g_at] += mm_tn(act_ref[i - save_at, pl.ds(base, CHUNK), :], low_ref[pl.ds(base, CHUNK), :])
+        gw_ref[i - g_at] += mm_tn(act_ref[i - save_at, pl.ds(base, BACK), :], low_ref[pl.ds(base, BACK), :])
+        if beside is not None:
+            beside(last - 1 - i, c)
         zero = jnp.zeros((UNIT, WIDTH), F32)
         shift, gain, bias = zero, zero, zero
         held = []
-        for u in range(0, CHUNK, UNIT):
+        for u in range(0, BACK, UNIT):
             rows = pl.ds(base + u, UNIT)
             at = (i - save_at, rows, slice(None))
             d_in, wf, wn = norm_back(da_ref[u:u + UNIT, :], slope_ref[at], n_ref[at], r_ref[at])
@@ -169,38 +169,26 @@
         da_ref[...] = next_da
         for k, x in enumerate((gain, shift, bias)):
             gv_ref[pl.ds(7 + k * layers + i, 1), :] += fold(x)
-        if after is not None:
-            after(i, c)
-        return next_i, next_c
-
-    start = jnp.int32(last - 1), jnp.int32(0)
-    da_ref[...] = product(*start)
-    lax.fori_loop(0, (last - first) * PARTS, body, start)
-
-
-def columns_of(ints):
-    row = lax.broadcasted_iota(jnp.int32, (16, ints.shape[1]), 0)
-    parts = (ints[1:2] >> 5, ints[1:2] & 31, ints[2:3], ints[3:4])
-    values = jnp.zeros_like(row)
-    for k, part in enumerate(parts):
-        values = jnp.where(row == k, part, values)
-    k = lax.broadcasted_iota(jnp.int32, (16, 384), 0)
-    j = lax.broadcasted_iota(jnp.int32, (16, 384), 1) >> 7
-    pick = jnp.where((j == 0) & (k == 0), 32.0, 0.0) + jnp.where(
-        ((j == 0) & (k == 1)) | ((j == 1) & (k == 2)) | ((j == 2) & (k == 3)), 1.0, 0.0
-    )
-    return mm_tn(values.astype(F32).astype(BF16), pick.astype(BF16))
-
-
-def softmax(hb_ref, full_ref, col_ref, top_ref, total_ref, expon_ref, wide_ref, dlog_ref, at, loss_ref):
+
+    def block(j, carry):
+        i = last - 1 - j
+        lax.fori_loop(0, TILE // BACK, lambda c, carry: chunk(i, c) or carry, 0)
+        if after_block is not None:
+            after_block(i)
+        return carry
+
+    da_ref[...] = product(last - 1, 0)
+    lax.fori_loop(0, last - first, block, 0)
+
+
+def softmax(full_ref, col_ref, top_ref, total_ref, expon_ref, wide_ref, dlog_ref, at, loss_ref):
     units = [slice(u, u + UNIT) for u in range(0, HEAD_CHUNK, UNIT)]
     lane = lax.broadcasted_iota(jnp.int32, (1, 128), 1).astype(F32)
     spread = lambda x: jnp.broadcast_to(x, (UNIT, 128))
     cols = [slice(k * 128, (k + 1) * 128) for k in range(6)]
     for rows in units:
-        logits = [full_ref[rows, cols[k]] + hb_ref[0:1, cols[k]].astype(F32) for k in range(6)]
+        logits = [full_ref[rows, cols[k]] for k in range(6)]
         for k in range(6):
-            full_ref[rows, cols[k]] = logits[k]
             wide_ref[k, rows, :] = logits[k].astype(BF16)
         top = functools.reduce(jnp.maximum, logits[:5])
         top_ref[0, rows, :] = spread(jnp.max(top, axis=1, keepdims=True))
@@ -213,7 +201,7 @@
         total_ref[1, rows, :] = spread(jnp.sum(expon[5], axis=1, keepdims=True))
     loss = jnp.zeros((UNIT, 128), F32)
     for rows in units:
-        targets, mask = (col_ref[rows, cols[0]], col_ref[rows, cols[1]]), col_ref[rows, cols[2]]
+        _, *targets, mask = (spread(col_ref[pl.ds(at + rows.start, UNIT), k:k + 1]) for k in range(4))
         zero = jnp.zeros_like(mask)
         hits = [zero, zero]
         weights = [mask / total_ref[j, rows, :] for j in range(2)]
@@ -230,7 +218,7 @@
 
 def heads(
     nq, ints_ref, s_ref, ds_ref, low_ref, wh_ref, hb_ref, latents_ref, value_ref, chance_ref, turned_ref, dlog_ref, loss_ref, full_ref, col_ref,
-    top_ref, total_ref, expon_ref, wide_ref, gw_ref, g_at,
+    top_ref, total_ref, expon_ref, wide_ref,
 ):
     size = HEAD_CHUNK
     count = TILE // size
@@ -241,10 +229,10 @@
     def logits(t):
         lat = s_ref[span_of(t), :].astype(BF16)
         latents_ref[span_of(t), :] = lat
-        return mm(lat, wh_ref[...]), columns_of(ints_ref[:, span_of(t)])
+        return mm(lat, wh_ref[...])
 
     def keep(parts):
-        full_ref[...], col_ref[...] = parts
+        full_ref[...] = parts + hb_ref[...].astype(F32)
 
     def turn(t):
         for k in range(5):
@@ -265,24 +253,17 @@
         following = logits(jnp.minimum(t + 1, count - 1))
         turn(before)
         ds = product(before)
-        softmax(
-            hb_ref, full_ref, col_ref, top_ref, total_ref, expon_ref, wide_ref, dlog_ref, pl.multiple_of(t * size, 128), loss_ref
-        )
+        softmax(full_ref, col_ref, top_ref, total_ref, expon_ref, wide_ref, dlog_ref, pl.multiple_of(t * size, 128), loss_ref)
         store(before, ds)
         keep(following)
         return carry
 
+    col_ref[...] = ints_ref[...].astype(F32).T
     keep(logits(jnp.int32(0)))
     lax.fori_loop(0, count, body, 0)
     end = jnp.int32(count - 1)
     turn(end)
     store(end, product(end))
-
-    def grads(k, carry):
-        gw_ref[g_at + k] += mm(turned_ref[...], dlog_ref[:, pl.ds(pl.multiple_of(k * WIDTH, WIDTH), WIDTH)])
-        return carry
-
-    lax.fori_loop(0, 3, grads, 0)
 
 
 def unpack_vec(w, vec_ref):
@@ -314,7 +295,7 @@
             act, n, slope, r = norm_gelu(pre_ref[u:u + UNIT, :], *scale)
             s_ref[rows, :] = act
             n_ref[n_at, rows, :] = n
-            slope_ref[n_at, rows, :] = slope
+            slope_ref[n_at, rows, :] = slope.astype(slope_ref.dtype)
             r_ref[n_at, rows, :] = r
         pre_ref[...] = following
         return carry
@@ -329,7 +310,7 @@
         low = low_ref[...]
         lgrad_ref[span, :] = mm_nt(low, w).astype(BF16)
         gw_ref[g_at] += mm_tn(latent_ref[span, :], low)
-        gv_ref[0:16, :] += mm_tn(hot_ref[span, :], low)
+        gv_ref[0:16, :] += mm(hot_ref[:, span], low)
 
     def body(c, carry):
         products(jnp.maximum(c - 1, 0))
@@ -418,7 +399,7 @@
 def first_kernel(layers, rows_dev, fronts, core_ref, latent_ref, ints_ref, *refs):
     front_refs = refs[:fronts]
     (
-        n_out, slope_out, r_out, act_out, s_ref, vec_ref, w_ref, lat_ref, hot_ref, pre_ref, n_ref, slope_ref, r_ref, act_ref, sems,
+        n_out, slope_out, r_out, act_out, s_out_ref, vec_ref, w_ref, lat_ref, hot_ref, pre_ref, s_ref, n_ref, slope_ref, r_ref, act_ref, sems,
     ) = refs[fronts:]
     step, steps = pl.program_id(0), pl.num_programs(0)
     span = tile_span(step)
@@ -447,21 +428,14 @@
     stem_forward(lat_ref, hot_ref, vec_ref, w_ref[1], s_ref, n_ref, slope_ref, r_ref, pre_ref, SPLIT)
     start(SPLIT, 3)
 
-    def after(i, c):
-        @pl.when(c == PARTS - 1)
+    def before_block(i):
+        @pl.when(step > 0)
         def _():
-            start(i)
-
-            @pl.when((step > 0) & (i < SPLIT - 1))
-            def _():
-                wait(i + 1)
-
-    @pl.when(step > 0)
-    def _():
-        wait(0)
+            wait(i)
 
     save = (act_ref, n_ref, slope_ref, r_ref)
-    forward_layers(0, SPLIT, layers, s_ref, save, vec_ref, w_ref, -2, 0, after)
+    forward_layers(0, SPLIT, layers, s_ref, save, vec_ref, w_ref, -2, 0, before_block, start)
+    s_out_ref[...] = s_ref[0:TILE, :]
 
     @pl.when(step == steps - 1)
     def _():
@@ -482,15 +456,22 @@
     def _():
         for ref in (gw_ref, gh_ref, gv_ref, loss_ref):
             ref[...] = jnp.zeros_like(ref)
-        turned_ref[WIDTH:, :] = jnp.ones_like(turned_ref[WIDTH:, :])
+        turned_ref[...] = jnp.ones_like(turned_ref)
+        dlog_ref[TILE:, :] = jnp.zeros_like(dlog_ref[TILE:, :])
         for k in range(3):
             wh_ref[:, k * WIDTH:(k + 1) * WIDTH] = w_ref[blocks + k]
 
     s_ref[0:TILE, :] = s_in_ref[...]
     save = (act_ref, n_ref, slope_ref, r_ref)
     forward_layers(SPLIT, layers, layers, s_ref, save, vec_ref, w_ref, SPLIT, SPLIT)
-    heads(nq, ints_ref, s_ref, ds_ref, low_ref, wh_ref, hb_ref, latents_ref, value_ref, chance_ref, turned_ref, dlog_ref, loss_ref, *chunk_refs, gh_ref, 0)
-    backward_layers(SPLIT, layers, layers, ds_ref, low_ref, da_ref, save, w_ref, SPLIT, SPLIT, gw_ref, gv_ref, SPLIT)
+    heads(nq, ints_ref, s_ref, ds_ref, low_ref, wh_ref, hb_ref, latents_ref, value_ref, chance_ref, turned_ref, dlog_ref, loss_ref, *chunk_refs)
+
+    def beside(j, k):
+        rows = pl.ds(pl.multiple_of(j * HEAD_CHUNK, 128), HEAD_CHUNK)
+        columns = pl.ds(pl.multiple_of(k * WIDTH, WIDTH), WIDTH)
+        gh_ref[k] += mm(turned_ref[:, rows], dlog_ref[rows, columns])
+
+    backward_layers(SPLIT, layers, layers, ds_ref, low_ref, da_ref, save, w_ref, SPLIT, SPLIT, gw_ref, gv_ref, SPLIT, None, beside)
 
     @pl.when(step == pl.num_programs(0) - 1)
     def _():
@@ -537,20 +518,18 @@
         gv_ref[...] = gv_in_ref[...]
 
     clean_latent(latent_ref, lat_ref, rows_dev)
-    hot_ref[...] = moves_hot(ints_ref[...]).T
+    hot_ref[...] = moves_hot(ints_ref[...])
     ds_ref[...] = ds_in_ref[...]
     low_ref[...] = ds_in_ref[...].astype(BF16)
 
-    def after(i, c):
-        @pl.when(c == PARTS - 1)
+    def after_block(i):
+        @pl.when(step < steps - 1)
         def _():
-            @pl.when(step < steps - 1)
-            def _():
-                start(i, step + 1)
-
-            @pl.when(i > 0)
-            def _():
-                wait(i - 1)
+            start(i, step + 1)
+
+        @pl.when(i > 0)
+        def _():
+            wait(i - 1)
 
     wait(SPLIT - 1)
 
@@ -561,7 +540,7 @@
         start(SPLIT, 0, 3)
 
     save = (act_ref, n_ref, slope_ref, r_ref)
-    backward_layers(0, SPLIT, layers, ds_ref, low_ref, da_ref, save, w_ref, -2, 0, gw_ref, gv_ref, -1, after)
+    backward_layers(0, SPLIT, layers, ds_ref, low_ref, da_ref, save, w_ref, -2, 0, gw_ref, gv_ref, -1, after_block)
     wait(SPLIT, 3)
     stem_backward(lat_ref, hot_ref, ds_ref, chunk_ref, n_ref, slope_ref, r_ref, SPLIT, w_ref[1], lgrad_ref, gw_ref, 0, gv_ref)
 
@@ -579,16 +558,18 @@
 
 
 def pack_kernel(
-    fronts, core_ref, stem_ref, table_ref, stem_vec_ref, block_ref, gain_ref, shift_ref, bias_ref, value_ref, chance_ref, front_ref,
+    fronts, core_ref, stem_ref, table_ref, stem_bias_ref, stem_gain_ref, stem_shift_ref, block_ref, gain_ref, shift_ref, bias_ref, value_ref, chance_ref, front_ref,
     back_ref, vec_ref,
 ):
     layers, shard = block_ref.shape[0], block_ref.shape[1]
     nq, nc = value_ref.shape[1], chance_ref.shape[1]
     vec_ref[...] = jnp.zeros_like(vec_ref)
     at = 0
-    for ref in (table_ref, stem_vec_ref, gain_ref, shift_ref, bias_ref):
-        vec_ref[at:at + ref.shape[0], 0:shard] = ref[...].astype(F32)
-        at += ref.shape[0]
+    for ref in (table_ref, stem_bias_ref, stem_gain_ref, stem_shift_ref, gain_ref, shift_ref, bias_ref):
+        rows = ref[...].astype(F32)
+        rows = rows[None] if len(ref.shape) == 1 else rows
+        vec_ref[at:at + rows.shape[0], 0:shard] = rows
+        at += rows.shape[0]
     vectors = vec_ref[...].T[0:shard, :]
     vectors = jnp.concatenate([vectors, jnp.zeros_like(vectors)], axis=1).astype(BF16)
     entries = [lambda: vectors, lambda: stem_ref[...]] + [functools.partial(block_ref.__getitem__, i) for i in range(SPLIT)]
@@ -639,7 +620,7 @@
     out_ref[end - vec:end, :] = jnp.concatenate(parts, axis=1)
 
 
-def finish_kernel(count, compact, scale, stem_vec_ref, gain_ref, *refs):
+def finish_kernel(count, compact, scale, stem_scale_ref, gain_ref, *refs):
     mids, ends = refs[:count], refs[count:2 * count]
     (
         loss_ref, stem_ref, table_ref, stem_bias_ref, stem_gain_ref, stem_shift_ref, block_ref, block_gain_ref, block_shift_ref,
@@ -666,9 +647,10 @@
     chance_ref[...] = part[:, 128:128 + nc]
     rep = mid_of((layers - SPLIT + 3) * shard, 16)
     rep = rep[0:8] + rep[8:16]
-    bias = jnp.concatenate([rep[k:k + 1] for k in range(3)], axis=1)
-    value_bias_ref[...] = bias[:, 0:nq]
-    chance_bias_ref[...] = bias[:, 640:640 + nc]
+    only = lax.broadcasted_iota(jnp.int32, rep.shape, 0)
+    bias = jnp.concatenate([jnp.sum(jnp.where(only == k, rep, 0.0), axis=0) for k in range(3)])
+    value_bias_ref[...] = bias[0:nq]
+    chance_bias_ref[...] = bias[640:640 + nc]
     loss_ref[0] = jnp.sum(rep[3:4])
     at = (1 + SPLIT) * shard
     if compact:
@@ -681,7 +663,7 @@
     small = small.T[:, 0:shard]
     small = small[0:64] + small[64:128]
     table_ref[...] = small[0:moves]
-    stem_gain = stem_vec_ref[1:2, :].astype(F32)
+    stem_gain = stem_scale_ref[...].astype(F32)[None]
     stem_bias_ref[...] = small[moves:moves + 1]
     stem_gain_ref[...] = small[moves + 1:moves + 2] / stem_gain
     stem_shift_ref[...] = small[moves + 2:moves + 3] / (16.0 * stem_gain)
@@ -738,16 +720,18 @@
     pieces, piece_rows = (n_fsdp, shard) if fast else (1, WIDTH)
     fronts = 2 if fast and n_dp % 2 == 0 and SPLIT % 2 == 0 else 1
     core = (lax.axis_index("dp") % 2).astype(jnp.int32).reshape(1)
-    stem_vec = jnp.stack([stem_bias, stem_gain, stem_shift])
     n_front = (2 + SPLIT) // fronts
     front, back = pl.pallas_call(
         functools.partial(pack_kernel, fronts),
-        in_specs=[SMEM] + [VMEM] * 9,
+        in_specs=[SMEM] + [VMEM] * 11,
         out_specs=[VMEM] * 2,
         out_shape=[struct((pieces, n_front * shard, WIDTH), BF16), struct((layers - SPLIT + 3, shard, WIDTH), BF16)],
         scratch_shapes=[pltpu.VMEM((128, max(shard, 128)), F32)],
         name="pack",
-    )(core, stem_weight, action_table, stem_vec, block_weight, block_gain, block_shift, block_bias, value_weight, chance_weight)
+    )(
+        core, stem_weight, action_table, stem_bias, stem_gain, stem_shift, block_weight, block_gain, block_shift, block_bias,
+        value_weight, chance_weight,
+    )
     if fast:
         w_fronts = [lax.all_to_all(front, "fsdp", 0, 0)]
         if fronts > 1:
@@ -778,7 +762,10 @@
         in_specs=[SMEM, tiled((rows_dev, WIDTH), 0), ints_spec] + [once(x.shape) for x in w_fronts],
         out_specs=[ANY] * 4 + [tiled(stream.shape, 0), whole((128, WIDTH))],
         out_shape=saved + [stream, struct((128, WIDTH), F32)],
-        scratch_shapes=[scratch(front_shape, BF16), scratch((TILE, WIDTH), BF16), scratch((TILE, 16), BF16), scratch((CHUNK, WIDTH), F32)] + kept,
+        scratch_shapes=[
+            scratch(front_shape, BF16), scratch((TILE, WIDTH), BF16), scratch((TILE, 16), BF16), scratch((CHUNK, WIDTH), F32),
+            scratch((TILE + CHUNK, WIDTH), F32),
+        ] + kept,
         compiler_params=params(62),
         cost_estimate=pl.CostEstimate(flops=rows_dev * WIDTH * WIDTH * 200, bytes_accessed=60 << 20, transcendentals=0),
         name="first",
@@ -805,17 +792,17 @@
             scratch((TILE + CHUNK, WIDTH), F32),
             scratch((blocks, TILE, WIDTH), BF16),
             scratch((blocks, TILE, WIDTH), BF16),
-            scratch((blocks, TILE, WIDTH), BF16),
+            scratch((blocks, TILE, WIDTH), F32),
             scratch((blocks, TILE, 128), F32),
             scratch((TILE, WIDTH), BF16),
-            scratch((CHUNK, WIDTH), F32),
-            scratch((WIDTH + 16, TILE), BF16),
-            scratch((TILE, 3 * WIDTH), BF16),
+            scratch((BACK, WIDTH), F32),
+            scratch((WIDTH + 16, max(blocks * HEAD_CHUNK, TILE)), BF16),
+            scratch((max(blocks * HEAD_CHUNK, TILE), 3 * WIDTH), BF16),
             scratch((blocks, WIDTH, WIDTH), F32),
             scratch((3, WIDTH + 16, WIDTH), F32),
             scratch((UNIT, 128), F32),
             scratch((HEAD_CHUNK, 3 * WIDTH), F32),
-            scratch((HEAD_CHUNK, 384), F32),
+            scratch((TILE, 8), F32),
             scratch((2, HEAD_CHUNK, 128), F32),
             scratch((2, HEAD_CHUNK, 128), F32),
             scratch((HEAD_CHUNK, 3 * WIDTH), F32),
@@ -836,10 +823,10 @@
         scratch_shapes=[
             scratch(front_shape, BF16),
             scratch((TILE, WIDTH), BF16),
-            scratch((TILE, 16), BF16),
+            scratch((16, TILE), BF16),
             scratch((TILE, WIDTH), F32),
             scratch((TILE, WIDTH), BF16),
-            scratch((CHUNK, WIDTH), F32),
+            scratch((BACK, WIDTH), F32),
             scratch((CHUNK, WIDTH), BF16),
         ] + kept[:4] + [
             scratch((SPLIT + 1, WIDTH, WIDTH), F32),
@@ -879,7 +866,7 @@
 
     shapes = [
         (1,), (shard, WIDTH), (moves, shard), (1, shard), (1, shard), (1, shard), (layers, shard, WIDTH), (layers, shard),
-        (layers, shard), (layers, shard), (shard, nq), (1, nq), (shard, nc), (1, nc),
+        (layers, shard), (layers, shard), (shard, nq), (nq,), (shard, nc), (nc,),
     ]
     (
         loss, stem_grad, table_grad, stem_bias_grad, stem_gain_grad, stem_shift_grad, block_grad, gain_grad, shift_grad, bias_grad,
@@ -890,7 +877,7 @@
         out_specs=[SMEM] + [VMEM] * (len(shapes) - 1),
         out_shape=[struct(x, F32) for x in shapes],
         name="finish",
-    )(stem_vec, block_gain, *mids, *ends)
+    )(stem_gain, block_gain, *mids, *ends)
     return (
         latents,
         value_logits.T,
@@ -907,9 +894,9 @@
         shift_grad,
         bias_grad,
         value_grad,
-        value_bias_grad.reshape(nq),
+        value_bias_grad,
         chance_grad,
-        chance_bias_grad.reshape(nc),
+        chance_bias_grad,
     )
 
 

time: 248 us -> 242 us (0.976)
  Pallas kernels: 174 us -> 170 us
  other arithmetic: 3.42 us -> 0.87 us
    pallas_call x1, Pallas kernels: 95.5 us -> 91.8 us  [per_device(): pl.pallas_call(functools.partial(middle_kernel, layers, nq), grid=(steps,...]
  transfers between devices with their start and end apart: 11 -> 11, of which waited for: 5 -> 5; matrix products, arithmetic and copies ran while one was open for 2% -> 2% of each run, Pallas kernels for 30% -> 31%
where the time goes in v5:
time: 242 us; the launch traced here: 241 us
  Pallas kernels  170 us (70%)
  waiting for transfers between devices  28 us (12%)
  starting transfers between devices  20.7 us (9%)
  between operations  14.2 us (6%)
  local copies, waits for them, and re-layouts  7.18 us (3%)
    pallas_call x1, Pallas kernels, per_device(): pl.pallas_call(functools.partial(middle_kernel, layers, nq), grid=(steps,...  91.8 us
    pallas_call x1, Pallas kernels, per_device(): pl.pallas_call(functools.partial(first_kernel, layers, rows_dev, fronts),...  38.2 us
    pallas_call x1, Pallas kernels, per_device(): pl.pallas_call(functools.partial(last_kernel, layers, rows_dev, fronts),...  31.9 us
    all_to_all x1, waiting for transfers between devices, per_device(): got_end = lax.all_to_all(parts_end, 'fsdp', 0, 0)  14.6 us
    all_to_all x1, starting transfers between devices, per_device(): w_fronts = [lax.all_to_all(front, 'fsdp', 0, 0)]  7.25 us
    all_to_all x1, waiting for transfers between devices, per_device(): w_fronts = [lax.all_to_all(front, 'fsdp', 0, 0)]  6.55 us
    all_to_all x1, starting transfers between devices, per_device(): got_end = lax.all_to_all(parts_end, 'fsdp', 0, 0)  6.03 us
    ppermute x6, waiting for transfers between devices, exchange(): lax.ppermute(x, axis, [(i, i ^ k) for i in range(size)])  5.18 us
  transfers between devices with their start and end apart: 11, of which 5 were waited for; matrix products, arithmetic and copies ran while one was open for 2% of the time, Pallas kernels for 31%

profile of v5, /device:TPU:0, one launch (start us, length us, event | category | flops | bytes accessed | tf_op | source)
XLA Modules:
  0.0 241.1 jit_solution(7601715491429372567)
XLA Ops:
  7.2 1.8 pack.1
  9.0 7.3 %all-to-all-start = ((bf16[8,96,256]{2,1,0:T(8,128)(2,1)}), bf16[8,96,256]{2,1,0:T(8,128)(2,1)S(1)}, u32[]{:S(2)}, u32[]{:S(2)}) async-start(bf16[8,96,256]{2,1,0:T(8,128)(2,1)} %get-tuple-element.50), calls=%async_computation | async-start | bytes 786432 | tf_op jit(solution)/shard_map/all_to_all | solution.py:736
  16.3 0.0 all-gather.2.cloned.1.call-start
  16.3 0.7 all-gather.2.cloned.1.call-update
  17.1 0.8 pad_maximum_fusion
  17.8 0.6 broadcast_in_dim.11.hb_ref
  18.4 0.8 stack.15
  19.2 0.8 stack.16
  19.9 0.8 stack.17
  20.7 0.8 stack.18
  21.5 6.5 %all-to-all-done.refs_0_ = bf16[8,96,256]{2,1,0:T(8,128)(2,1)S(1)} async-done(((bf16[8,96,256]{2,1,0:T(8,128)(2,1)}), bf16[8,96,256]{2,1,0:T(8,128)(2,1)S(1)}, u32[]{:S(2)}, u32[]{:S(2)}) %all-to-all-start) | async-done | bytes 393248 | tf_op jit(solution)/shard_map/all_to_all | solution.py:736
  28.0 0.0 copy-start.2
  28.0 0.0 collective-permute-start
  28.0 0.1 pad_add_fusion
  28.1 0.7 pad.4.ints_ref
  28.8 0.9 collective-permute-done.refs_1_
  29.7 0.0 copy-done.2
  29.7 0.0 copy-start.9
  29.7 0.8 copy-done.9
  30.5 38.2 %first.1 = (bf16[5,5760,256]{2,1,0:T(8,128)(2,1)}, bf16[5,5760,256]{2,1,0:T(8,128)(2,1)}, f32[5,5760,128]{2,1,0:T(8,128)}, bf16[4,5760,256]{2,1,0:T(8,128)(2,1)}...) custom-call(s32[1]{0:T(128)} %bitcast.core_ref, bf16[5696,256]{1,0:T(8,128)(2,1)} %latent_ref.3, s32[8,5760]{1,0:T(8,128)} %pad.4.ints_ref, ...), custom_call_target="tpu_custom_call" | custom-call | flops 74658611200 | bytes 62914560 | tf_op jit(solution)/shard_map/first/pallas_call | solution.py:759
  68.7 0.0 all-gather.2.cloned.1.call-done.w_ref
  68.8 91.8 %middle.1 = (bf16[5696,256]{1,0:T(8,128)(2,1)}, bf16[601,5696]{1,0:T(8,128)(2,1)}, bf16[32,5696]{1,0:T(8,128)(2,1)}, f32[5760,256]{1,0:T(8,128)}, f32[48,256]{1,...) custom-call(f32[5760,256]{1,0:T(8,128)} %get-tuple-element.51.s_in_ref, s32[8,5760]{1,0:T(8,128)} %pad.4.ints_ref, ...), custom_call_target="tpu_custom_call" | custom-call | flops 223975833600 | bytes 41943040 | tf_op jit(solution)/shard_map/middle/pallas_call | solution.py:778
  160.6 3.7 %all-to-all-start.1 = ((bf16[8,304,256]{2,1,0:T(8,128)(2,1)}), bf16[8,304,256]{2,1,0:T(8,128)(2,1)S(1)}, u32[]{:S(2)}, u32[]{:S(2)}) async-start(bf16[8,304,256]{2,1,0:T(8,128)(2,1)} %get-tuple-element.64), calls=%async_computation.1 | async-start | bytes 2490368 | tf_op jit(solution)/shard_map/all_to_all | solution.py:841
  164.3 31.9 %last.1 = (bf16[5696,256]{1,0:T(8,128)(2,1)}, bf16[8,176,256]{2,1,0:T(8,128)(2,1)}) custom-call(s32[1]{0:T(128)} %bitcast.core_ref, bf16[5696,256]{1,0:T(8,128)(2,1)} %latent_ref.3, s32[8,5760]{1,0:T(8,128)} %pad.4.ints_ref, f32[5760,256]{1,0:T(8,128)} %get-tuple-element.57.ds_in_ref, bf16[5,5760,256]{2,1,0:T(8,128)(2,1)} %get-tuple-element.58.n_in, ...), custom_call_target="tpu_custom_call" | custom-call | flops 55993958400 | bytes 62914560 | tf_op jit(solution)/shard_map/last/pallas_call | solution.py:816
  196.2 0.0 all-to-all-done.1.in_ref
  196.3 0.0 copy-start
  196.3 6.0 %all-to-all-start.2 = ((bf16[8,176,256]{2,1,0:T(8,128)(2,1)}), bf16[8,176,256]{2,1,0:T(8,128)(2,1)S(1)}, u32[]{:S(2)}, u32[]{:S(2)}) async-start(bf16[8,176,256]{2,1,0:T(8,128)(2,1)} %get-tuple-element.66), calls=%async_computation.2 | async-start | bytes 1441792 | tf_op jit(solution)/shard_map/all_to_all | solution.py:843
  202.3 0.0 copy-done
  202.3 2.1 sum_mid.1.refs_0_
  204.4 0.5 collective-permute-start.3
  205.0 1.0 collective-permute-start.2
  206.0 0.3 collective-permute-start.1
  206.3 14.6 %all-to-all-done.2.in_ref = bf16[8,176,256]{2,1,0:T(8,128)(2,1)S(1)} async-done(((bf16[8,176,256]{2,1,0:T(8,128)(2,1)}), bf16[8,176,256]{2,1,0:T(8,128)(2,1)S(1)}, u32[]{:S(2)}, u32[]{:S(2)}) %all-to-all-start.2) | async-done | bytes 720928 | tf_op jit(solution)/shard_map/all_to_all | solution.py:843
  220.9 0.0 copy-start.1
  220.9 0.9 copy-done.1
  221.8 1.9 sum_end.1.refs_4_
  223.7 0.0 collective-permute-start.6
  223.7 1.5 collective-permute-start.5
  225.2 0.0 collective-permute-done.3.refs_3_
  225.2 0.0 copy-start.3
  225.2 0.3 collective-permute-start.4
  225.5 0.0 collective-permute-done.2.refs_2_
  225.6 0.0 copy-start.4
  225.6 0.0 collective-permute-done.1.refs_1_
  225.6 0.0 copy-start.5
  225.6 3.2 %collective-permute-done.6.refs_7_ = bf16[176,256]{1,0:T(8,128)(2,1)S(1)} collective-permute-done((bf16[176,256]{1,0:T(8,128)(2,1)}, bf16[176,256]{1,0:T(8,128)(2,1)S(1)}, u32[]{:S(2)}, u32[]{:S(2)}) %collective-permute-start.6) | collective-permute-done | bytes 90144 | tf_op jit(solution)/shard_map/ppermute | solution.py:704
  228.7 0.0 copy-start.6
  228.7 2.0 collective-permute-done.5.refs_6_
  230.7 0.0 copy-start.7
  230.7 0.0 collective-permute-done.4.refs_5_
  230.7 0.0 copy-done.3
  230.8 0.0 copy-done.4
  230.8 0.0 copy-done.5
  230.8 0.0 copy-done.6
  230.8 0.6 copy-done.7
  231.4 0.0 copy-start.8
  231.4 0.6 copy-done.8
  232.0 2.2 finish.1
  (2 shorter events, 0.0 us)
Async XLA Ops:
  9.0 19.0 %all-to-all-start = ((bf16[8,96,256]{2,1,0:T(8,128)(2,1)}), bf16[8,96,256]{2,1,0:T(8,128)(2,1)S(1)}, u32[]{:S(2)}, u32[]{:S(2)}) async-start(bf16[8,96,256]{2,1,0:T(8,128)(2,1)} %get-tuple-element.50), calls=%async_computation | async-start | bytes 786432 | tf_op jit(solution)/shard_map/all_to_all | solution.py:736
  16.3 52.5 %all-gather.2.cloned.1.call-start = ((), (), s32[]{:S(2)}) async-start(), calls=%async_computation.3 | async-start | bytes 1327104 | tf_op jit(solution)/shard_map/all_gather | solution.py:742
  28.0 1.7 copy-start.2
  28.0 1.7 collective-permute-start
  29.7 0.8 copy-start.9
  160.6 35.7 %all-to-all-start.1 = ((bf16[8,304,256]{2,1,0:T(8,128)(2,1)}), bf16[8,304,256]{2,1,0:T(8,128)(2,1)S(1)}, u32[]{:S(2)}, u32[]{:S(2)}) async-start(bf16[8,304,256]{2,1,0:T(8,128)(2,1)} %get-tuple-element.64), calls=%async_computation.1 | async-start | bytes 2490368 | tf_op jit(solution)/shard_map/all_to_all | solution.py:841
  196.3 6.0 %copy-start = (bf16[8,304,256]{2,1,0:T(8,128)(2,1)}, bf16[8,304,256]{2,1,0:T(8,128)(2,1)S(1)}, u32[]{:S(2)}) copy-start(bf16[8,304,256]{2,1,0:T(8,128)(2,1)S(1)} %all-to-all-done.1.in_ref) | copy-start | bytes 3735556
  196.3 24.6 %all-to-all-start.2 = ((bf16[8,176,256]{2,1,0:T(8,128)(2,1)}), bf16[8,176,256]{2,1,0:T(8,128)(2,1)S(1)}, u32[]{:S(2)}, u32[]{:S(2)}) async-start(bf16[8,176,256]{2,1,0:T(8,128)(2,1)} %get-tuple-element.66), calls=%async_computation.2 | async-start | bytes 1441792 | tf_op jit(solution)/shard_map/all_to_all | solution.py:843
  204.4 20.8 %collective-permute-start.3 = (bf16[304,256]{1,0:T(8,128)(2,1)}, bf16[304,256]{1,0:T(8,128)(2,1)S(1)}, u32[]{:S(2)}, u32[]{:S(2)}) collective-permute-start(bf16[304,256]{1,0:T(8,128)(2,1)} %sum_mid.1.refs_0_), channel_id=1, source_target_pairs={{0,24},{8,16},{16,8},{24,0},{1,25},{9,17},{17,9},{25,1},{2,26},{10... | collective-permute-start | bytes 466952 | tf_op jit(solution)/shard_map/ppermute | solution.py:704
  205.0 20.6 %collective-permute-start.2 = (bf16[304,256]{1,0:T(8,128)(2,1)}, bf16[304,256]{1,0:T(8,128)(2,1)S(1)}, u32[]{:S(2)}, u32[]{:S(2)}) collective-permute-start(bf16[304,256]{1,0:T(8,128)(2,1)} %sum_mid.1.refs_0_), channel_id=1, source_target_pairs={{0,16},{8,24},{16,0},{24,8},{1,17},{9,25},{17,1},{25,9},{2,18},{10... | collective-permute-start | bytes 466952 | tf_op jit(solution)/shard_map/ppermute | solution.py:704
  206.0 19.6 %collective-permute-start.1 = (bf16[304,256]{1,0:T(8,128)(2,1)}, bf16[304,256]{1,0:T(8,128)(2,1)S(1)}, u32[]{:S(2)}, u32[]{:S(2)}) collective-permute-start(bf16[304,256]{1,0:T(8,128)(2,1)} %sum_mid.1.refs_0_), channel_id=1, source_target_pairs={{0,8},{8,0},{16,24},{24,16},{1,9},{9,1},{17,25},{25,17},{2,10},{10... | collective-permute-start | bytes 466952 | tf_op jit(solution)/shard_map/ppermute | solution.py:704
  220.9 0.9 copy-start.1
  223.7 5.1 %collective-permute-start.6 = (bf16[176,256]{1,0:T(8,128)(2,1)}, bf16[176,256]{1,0:T(8,128)(2,1)S(1)}, u32[]{:S(2)}, u32[]{:S(2)}) collective-permute-start(bf16[176,256]{1,0:T(8,128)(2,1)} %sum_end.1.refs_4_), channel_id=1, source_target_pairs={{0,24},{8,16},{16,8},{24,0},{1,25},{9,17},{17,9},{25,1},{2,26},{10... | collective-permute-start | bytes 270344 | tf_op jit(solution)/shard_map/ppermute | solution.py:704
  223.7 7.1 %collective-permute-start.5 = (bf16[176,256]{1,0:T(8,128)(2,1)}, bf16[176,256]{1,0:T(8,128)(2,1)S(1)}, u32[]{:S(2)}, u32[]{:S(2)}) collective-permute-start(bf16[176,256]{1,0:T(8,128)(2,1)} %sum_end.1.refs_4_), channel_id=1, source_target_pairs={{0,16},{8,24},{16,0},{24,8},{1,17},{9,25},{17,1},{25,9},{2,18},{10... | collective-permute-start | bytes 270344 | tf_op jit(solution)/shard_map/ppermute | solution.py:704
  225.2 5.5 %copy-start.3 = (bf16[304,256]{1,0:T(8,128)(2,1)}, bf16[304,256]{1,0:T(8,128)(2,1)S(1)}, u32[]{:S(2)}) copy-start(bf16[304,256]{1,0:T(8,128)(2,1)S(1)} %collective-permute-done.3.refs_3_) | copy-start | bytes 466948
  225.2 5.5 %collective-permute-start.4 = (bf16[176,256]{1,0:T(8,128)(2,1)}, bf16[176,256]{1,0:T(8,128)(2,1)S(1)}, u32[]{:S(2)}, u32[]{:S(2)}) collective-permute-start(bf16[176,256]{1,0:T(8,128)(2,1)} %sum_end.1.refs_4_), channel_id=1, source_target_pairs={{0,8},{8,0},{16,24},{24,16},{1,9},{9,1},{17,25},{25,17},{2,10},{10... | collective-permute-start | bytes 270344 | tf_op jit(solution)/shard_map/ppermute | solution.py:704
  225.6 5.2 %copy-start.4 = (bf16[304,256]{1,0:T(8,128)(2,1)}, bf16[304,256]{1,0:T(8,128)(2,1)S(1)}, u32[]{:S(2)}) copy-start(bf16[304,256]{1,0:T(8,128)(2,1)S(1)} %collective-permute-done.2.refs_2_) | copy-start | bytes 466948
  225.6 5.2 %copy-start.5 = (bf16[304,256]{1,0:T(8,128)(2,1)}, bf16[304,256]{1,0:T(8,128)(2,1)S(1)}, u32[]{:S(2)}) copy-start(bf16[304,256]{1,0:T(8,128)(2,1)S(1)} %collective-permute-done.1.refs_1_) | copy-start | bytes 466948
  228.7 2.0 copy-start.6
  230.7 0.6 copy-start.7
  231.4 0.6 copy-start.8
Sparse Core Ops, SparseCore 0:
  19.9 42.4 all-gather.1

commit v6 on v5

--- a/solution.py
+++ b/solution.py
@@ -42,13 +42,21 @@
     t = jnp.tanh(h * (K0 + K1 * y))
     e1 = 1.0 + t
     bend = (h * (y + K0 / (3 * K1))) * (1.0 - t)
-    slope = (e1 * gain_slope) * (1.0 / (3 * K1) + bend)
+    slope = e1 * (1.0 / (3 * K1) + bend)
+    if gain_slope is not None:
+        slope = slope * gain_slope
     return h * e1, n.astype(BF16), slope, jnp.broadcast_to(r, (UNIT, 128))
 
 
-def scales(vec_ref, at, layers):
+def scales(vec_ref, at, layers, slope):
     gain = vec_ref[pl.ds(at, 1), :]
-    return gain * 8.0, gain * (8.0 * 3 * K1), vec_ref[pl.ds(at + layers, 1), :] * 0.5
+    return gain * 8.0, gain * (8.0 * 3 * K1) if slope else None, vec_ref[pl.ds(at + layers, 1), :] * 0.5
+
+
+def gained(w, columns, at):
+    lane = lax.broadcasted_iota(jnp.int32, columns.shape, 1)
+    gain = jnp.sum(jnp.where(lane == at, columns, 0.0), axis=1, keepdims=True)
+    return (w.astype(F32) * (gain * (8.0 * 3 * K1))).astype(BF16)
 
 
 def lane_sums(x):
@@ -107,7 +115,7 @@
         def chunk(c, carry):
             old_i, old_c, base = carry
             out = product(old_i, old_c)
-            activate(rows_of(c), s_ref, save, i - save_at, scales(vec_ref, 7 + i, layers))
+            activate(rows_of(c), s_ref, save, i - save_at, scales(vec_ref, 7 + i, layers, False))
             residual(old_i, pl.multiple_of(base, UNIT), out)
             return i, c, c * CHUNK
 
@@ -181,15 +189,13 @@
     lax.fori_loop(0, last - first, block, 0)
 
 
-def softmax(full_ref, col_ref, top_ref, total_ref, expon_ref, wide_ref, dlog_ref, at, loss_ref):
+def softmax(full_ref, col_ref, top_ref, total_ref, expon_ref, dlog_ref, at, loss_ref):
     units = [slice(u, u + UNIT) for u in range(0, HEAD_CHUNK, UNIT)]
     lane = lax.broadcasted_iota(jnp.int32, (1, 128), 1).astype(F32)
     spread = lambda x: jnp.broadcast_to(x, (UNIT, 128))
     cols = [slice(k * 128, (k + 1) * 128) for k in range(6)]
     for rows in units:
         logits = [full_ref[rows, cols[k]] for k in range(6)]
-        for k in range(6):
-            wide_ref[k, rows, :] = logits[k].astype(BF16)
         top = functools.reduce(jnp.maximum, logits[:5])
         top_ref[0, rows, :] = spread(jnp.max(top, axis=1, keepdims=True))
         top_ref[1, rows, :] = spread(jnp.max(logits[5], axis=1, keepdims=True))
@@ -217,8 +223,8 @@
 
 
 def heads(
-    nq, ints_ref, s_ref, ds_ref, low_ref, wh_ref, hb_ref, latents_ref, value_ref, chance_ref, turned_ref, dlog_ref, loss_ref, full_ref, col_ref,
-    top_ref, total_ref, expon_ref, wide_ref,
+    ints_ref, s_ref, ds_ref, low_ref, wh_ref, hb_ref, latents_ref, turned_ref, dlog_ref, loss_ref, full_ref, col_ref, top_ref, total_ref,
+    expon_ref,
 ):
     size = HEAD_CHUNK
     count = TILE // size
@@ -235,10 +241,6 @@
         full_ref[...] = parts + hb_ref[...].astype(F32)
 
     def turn(t):
-        for k in range(5):
-            height = min(128, nq - k * 128)
-            value_ref[k * 128:k * 128 + height, span_of(t)] = wide_ref[k].T[0:height, :]
-        chance_ref[:, span_of(t)] = wide_ref[5].T[0:chance_ref.shape[0], :]
         turned_ref[0:WIDTH, span_of(t)] = latents_ref[span_of(t), :].T
 
     def product(t):
@@ -253,7 +255,7 @@
         following = logits(jnp.minimum(t + 1, count - 1))
         turn(before)
         ds = product(before)
-        softmax(full_ref, col_ref, top_ref, total_ref, expon_ref, wide_ref, dlog_ref, pl.multiple_of(t * size, 128), loss_ref)
+        softmax(full_ref, col_ref, top_ref, total_ref, expon_ref, dlog_ref, pl.multiple_of(t * size, 128), loss_ref)
         store(before, ds)
         keep(following)
         return carry
@@ -282,7 +284,7 @@
 
 def stem_forward(latent_ref, hot_ref, vec_ref, w, s_ref, n_ref, slope_ref, r_ref, pre_ref, n_at):
     table = table_of(vec_ref)
-    scale = scales(vec_ref, 5, 1)
+    scale = scales(vec_ref, 5, 1, True)
 
     def product(c):
         span = pl.ds(rows_of(c), CHUNK)
@@ -304,11 +306,10 @@
     lax.fori_loop(0, PARTS, body, 0)
 
 
-def stem_backward(latent_ref, hot_ref, s_ref, low_ref, n_ref, slope_ref, r_ref, n_at, w, lgrad_ref, gw_ref, g_at, gv_ref):
+def stem_backward(latent_ref, hot_ref, s_ref, low_ref, n_ref, slope_ref, r_ref, n_at, d_pre_ref, gw_ref, g_at, gv_ref):
     def products(c):
         span = pl.ds(rows_of(c), CHUNK)
         low = low_ref[...]
-        lgrad_ref[span, :] = mm_nt(low, w).astype(BF16)
         gw_ref[g_at] += mm_tn(latent_ref[span, :], low)
         gv_ref[0:16, :] += mm(hot_ref[:, span], low)
 
@@ -325,7 +326,9 @@
             if len(held) == GROUP:
                 gain = gain + column_sums(held)
                 held = []
-            low_ref[u:u + UNIT, :] = d_in.astype(BF16)
+            low = d_in.astype(BF16)
+            low_ref[u:u + UNIT, :] = low
+            d_pre_ref[rows, :] = low
         gv_ref[5:6, :] += fold(gain)
         gv_ref[6:7, :] += fold(shift)
         return carry
@@ -445,9 +448,8 @@
 
 
 def middle_kernel(
-    layers, nq, s_in_ref, ints_ref, vec_ref, hb_ref, w_ref,
-    latents_ref, value_ref, chance_ref, ds_ref, gv_ref, rep_ref, out_ref,
-    wh_ref, s_ref, act_ref, n_ref, slope_ref, r_ref, low_ref, da_ref, turned_ref, dlog_ref, gw_ref, gh_ref, loss_ref, *chunk_refs,
+    layers, s_in_ref, ints_ref, vec_ref, hb_ref, w_ref, latents_ref, ds_ref, gv_ref, rep_ref, out_ref,
+    wh_ref, wg_ref, s_ref, act_ref, n_ref, slope_ref, r_ref, low_ref, da_ref, turned_ref, dlog_ref, gw_ref, gh_ref, loss_ref, *chunk_refs,
 ):
     blocks = layers - SPLIT
     step = pl.program_id(0)
@@ -460,18 +462,25 @@
         dlog_ref[TILE:, :] = jnp.zeros_like(dlog_ref[TILE:, :])
         for k in range(3):
             wh_ref[:, k * WIDTH:(k + 1) * WIDTH] = w_ref[blocks + k]
+        columns = vec_ref[...].T
+
+        def scale(i, carry):
+            wg_ref[i] = gained(w_ref[i], columns, 7 + SPLIT + i)
+            return carry
+
+        lax.fori_loop(0, blocks, scale, 0)
 
     s_ref[0:TILE, :] = s_in_ref[...]
     save = (act_ref, n_ref, slope_ref, r_ref)
     forward_layers(SPLIT, layers, layers, s_ref, save, vec_ref, w_ref, SPLIT, SPLIT)
-    heads(nq, ints_ref, s_ref, ds_ref, low_ref, wh_ref, hb_ref, latents_ref, value_ref, chance_ref, turned_ref, dlog_ref, loss_ref, *chunk_refs)
+    heads(ints_ref, s_ref, ds_ref, low_ref, wh_ref, hb_ref, latents_ref, turned_ref, dlog_ref, loss_ref, *chunk_refs)
 
     def beside(j, k):
         rows = pl.ds(pl.multiple_of(j * HEAD_CHUNK, 128), HEAD_CHUNK)
         columns = pl.ds(pl.multiple_of(k * WIDTH, WIDTH), WIDTH)
         gh_ref[k] += mm(turned_ref[:, rows], dlog_ref[rows, columns])
 
-    backward_layers(SPLIT, layers, layers, ds_ref, low_ref, da_ref, save, w_ref, SPLIT, SPLIT, gw_ref, gv_ref, SPLIT, None, beside)
+    backward_layers(SPLIT, layers, layers, ds_ref, low_ref, da_ref, save, wg_ref, SPLIT, SPLIT, gw_ref, gv_ref, SPLIT, None, beside)
 
     @pl.when(step == pl.num_programs(0) - 1)
     def _():
@@ -496,7 +505,7 @@
 def last_kernel(layers, rows_dev, fronts, core_ref, latent_ref, ints_ref, ds_in_ref, n_in, slope_in, r_in, act_in, gv_in_ref, *refs):
     front_refs = refs[:fronts]
     (
-        lgrad_ref, out_ref, w_ref, lat_ref, hot_ref, ds_ref, low_ref, da_ref, chunk_ref, n_ref, slope_ref, r_ref, act_ref, gw_ref, gv_ref,
+        d_pre_ref, out_ref, stem_ref, w_ref, lat_ref, hot_ref, ds_ref, low_ref, da_ref, chunk_ref, n_ref, slope_ref, r_ref, act_ref, gw_ref, gv_ref,
         sems,
     ) = refs[fronts:]
     step, steps = pl.program_id(0), pl.num_programs(0)
@@ -514,6 +523,14 @@
     def _():
         start(SPLIT - 1, 0)
         join_front(core_ref, front_refs, w_ref)
+        stem_ref[...] = w_ref[1]
+        columns = w_ref[0, :, 0:128].astype(F32)
+
+        def scale(i, carry):
+            w_ref[2 + i] = gained(w_ref[2 + i], columns, 7 + i)
+            return carry
+
+        lax.fori_loop(0, SPLIT, scale, 0)
         gw_ref[...] = jnp.zeros_like(gw_ref)
         gv_ref[...] = gv_in_ref[...]
 
@@ -542,7 +559,7 @@
     save = (act_ref, n_ref, slope_ref, r_ref)
     backward_layers(0, SPLIT, layers, ds_ref, low_ref, da_ref, save, w_ref, -2, 0, gw_ref, gv_ref, -1, after_block)
     wait(SPLIT, 3)
-    stem_backward(lat_ref, hot_ref, ds_ref, chunk_ref, n_ref, slope_ref, r_ref, SPLIT, w_ref[1], lgrad_ref, gw_ref, 0, gv_ref)
+    stem_backward(lat_ref, hot_ref, ds_ref, chunk_ref, n_ref, slope_ref, r_ref, SPLIT, d_pre_ref, gw_ref, 0, gv_ref)
 
     @pl.when(step < steps - 1)
     def _():
@@ -589,6 +606,32 @@
         width = min(WIDTH, nq - k * WIDTH)
         back_ref[at + k, :, 0:width] = value_ref[:, k * WIDTH:k * WIDTH + width]
     back_ref[at + 2, :, 128:128 + nc] = chance_ref[...]
+
+
+def outputs_kernel(latents_ref, d_pre_ref, w_ref, hb_ref, stem_ref, value_ref, chance_ref, lgrad_ref, turned_ref, bias_ref):
+    count = turned_ref.shape[0] // WIDTH
+
+    @pl.when(pl.program_id(0) == 0)
+    def _():
+        at = w_ref.shape[0] - count
+        for k in range(count):
+            turned_ref[k * WIDTH:(k + 1) * WIDTH, :] = w_ref[at + k].T
+        columns = jnp.broadcast_to(hb_ref[...].astype(F32), (8, count * WIDTH)).T
+        bias_ref[...] = jnp.broadcast_to(columns[:, 0:1], bias_ref.shape)
+
+    nq, nc = value_ref.shape[0], chance_ref.shape[0]
+    wide = [slice(k, k + 128) for k in range(0, HEAD_CHUNK, 128)]
+
+    def chunk(c, carry):
+        span = pl.ds(pl.multiple_of(c * HEAD_CHUNK, 128), HEAD_CHUNK)
+        logits = mm_nt(turned_ref[...], latents_ref[span, :])
+        logits = jnp.concatenate([logits[:, x] + bias_ref[...] for x in wide], axis=1).astype(BF16)
+        value_ref[:, span] = logits[0:nq]
+        chance_ref[:, span] = logits[640:640 + nc]
+        lgrad_ref[span, :] = mm_nt(d_pre_ref[span, :], stem_ref[...]).astype(BF16)
+        return carry
+
+    lax.fori_loop(0, TILE // HEAD_CHUNK, chunk, 0)
 
 
 def total_rows(refs, rows):
@@ -732,20 +775,20 @@
         core, stem_weight, action_table, stem_bias, stem_gain, stem_shift, block_weight, block_gain, block_shift, block_bias,
         value_weight, chance_weight,
     )
+    ints = jnp.pad(jnp.stack([actions, value_bins, chance_codes, step_mask]), ((0, 4), (0, padded - rows_dev)))
+    none = lambda n: jnp.full((n,), -1e30, BF16)
+    head_bias = jnp.concatenate([value_bias, none(640 - nq), chance_bias, none(128 - nc)])[None]
     if fast:
         w_fronts = [lax.all_to_all(front, "fsdp", 0, 0)]
         if fronts > 1:
+            w_fronts[0], ints, head_bias = lax.optimization_barrier((w_fronts[0], ints, head_bias))
             w_fronts.append(lax.ppermute(w_fronts[0], "dp", [(i, i ^ 1) for i in range(n_dp)]))
     else:
         front = lax.all_gather(front.reshape(n_front, shard, WIDTH), "fsdp", axis=1, tiled=True)
         w_fronts = [front.reshape(1, n_front * WIDTH, WIDTH)]
     w_back = lax.all_gather(back, "fsdp", axis=1, tiled=True)
 
-    ints = jnp.pad(jnp.stack([actions, value_bins, chance_codes, step_mask]), ((0, 4), (0, padded - rows_dev)))
     ints_spec = pl.BlockSpec((8, TILE), lambda i: (0, i))
-    none = lambda n: jnp.full((n,), -1e30, BF16)
-    head_bias = jnp.concatenate([value_bias, none(640 - nq), chance_bias, none(128 - nc)])[None]
-
     saved = [
         struct((SPLIT + 1, padded, WIDTH), BF16),
         struct((SPLIT + 1, padded, WIDTH), BF16),
@@ -775,20 +818,19 @@
     compact = piece_rows % 32 == 0 and fast
     mid_shape = (pieces, (blocks + 3) * piece_rows + 16, WIDTH)
     end_shape = (pieces, (SPLIT + 1) * piece_rows + piece_rows // 2, WIDTH)
-    latents, value_logits, chance_logits, ds_mid, gv_mid, rep, parts_mid = pl.pallas_call(
-        functools.partial(middle_kernel, layers, nq),
+    latents, ds_mid, gv_mid, rep, parts_mid = pl.pallas_call(
+        functools.partial(middle_kernel, layers),
         grid=(steps,),
         in_specs=[tiled(stream.shape, 0), ints_spec, once(vec.shape), once(head_bias.shape), once(w_back.shape)],
         out_specs=[
-            tiled((rows_dev, WIDTH), 0), tiled((nq, rows_dev), 1), tiled((nc, rows_dev), 1), tiled(stream.shape, 0),
-            whole((48, WIDTH)), whole((8, WIDTH)), whole(mid_shape),
+            tiled((rows_dev, WIDTH), 0), tiled(stream.shape, 0), whole((48, WIDTH)), whole((8, WIDTH)), whole(mid_shape),
         ],
         out_shape=[
-            struct((rows_dev, WIDTH), BF16), struct((nq, rows_dev), BF16), struct((nc, rows_dev), BF16), stream,
-            struct((48, WIDTH), F32), struct((8, WIDTH), F32), struct(mid_shape, BF16),
+            struct((rows_dev, WIDTH), BF16), stream, struct((48, WIDTH), F32), struct((8, WIDTH), F32), struct(mid_shape, BF16),
         ],
         scratch_shapes=[
             scratch((WIDTH, 3 * WIDTH), BF16),
+            scratch((blocks, WIDTH, WIDTH), BF16),
             scratch((TILE + CHUNK, WIDTH), F32),
             scratch((blocks, TILE, WIDTH), BF16),
             scratch((blocks, TILE, WIDTH), BF16),
@@ -806,20 +848,19 @@
             scratch((2, HEAD_CHUNK, 128), F32),
             scratch((2, HEAD_CHUNK, 128), F32),
             scratch((HEAD_CHUNK, 3 * WIDTH), F32),
-            scratch((6, HEAD_CHUNK, 128), BF16),
         ],
         compiler_params=params(62),
         cost_estimate=pl.CostEstimate(flops=rows_dev * WIDTH * WIDTH * 600, bytes_accessed=40 << 20, transcendentals=0),
         name="middle",
     )(s_mid, ints, vec, head_bias, w_back)
 
-    latent_grad, parts_end = pl.pallas_call(
+    d_pre, parts_end, w_stem = pl.pallas_call(
         functools.partial(last_kernel, layers, rows_dev, fronts),
         grid=(steps,),
         in_specs=[SMEM, tiled((rows_dev, WIDTH), 0), ints_spec, tiled(stream.shape, 0)]
         + [ANY] * 4 + [once((48, WIDTH))] + [once(x.shape) for x in w_fronts],
-        out_specs=[tiled((rows_dev, WIDTH), 0), whole(end_shape)],
-        out_shape=[struct((rows_dev, WIDTH), BF16), struct(end_shape, BF16)],
+        out_specs=[tiled((padded, WIDTH), 0), whole(end_shape), whole((WIDTH, WIDTH))],
+        out_shape=[struct((padded, WIDTH), BF16), struct(end_shape, BF16), struct((WIDTH, WIDTH), BF16)],
         scratch_shapes=[
             scratch(front_shape, BF16),
             scratch((TILE, WIDTH), BF16),
@@ -837,10 +878,26 @@
         name="last",
     )(core, latent, ints, ds_mid, *held, gv_mid, *w_fronts)
 
+    def outputs_of(states):
+        return pl.pallas_call(
+            outputs_kernel,
+            grid=(steps,),
+            in_specs=[tiled((rows_dev, WIDTH), 0), tiled((padded, WIDTH), 0)]
+            + [once(x.shape) for x in (w_back, head_bias, w_stem)],
+            out_specs=[tiled((nq, rows_dev), 1), tiled((nc, rows_dev), 1), tiled((rows_dev, WIDTH), 0)],
+            out_shape=[struct((nq, rows_dev), BF16), struct((nc, rows_dev), BF16), struct((rows_dev, WIDTH), BF16)],
+            scratch_shapes=[scratch((3 * WIDTH, WIDTH), BF16), scratch((3 * WIDTH, 128), F32)],
+            compiler_params=params(48),
+            cost_estimate=pl.CostEstimate(flops=rows_dev * WIDTH * WIDTH * 20, bytes_accessed=16 << 20, transcendentals=0),
+            name="outputs",
+        )(states, d_pre, w_back, head_bias, w_stem)
+
     if fast:
         got_mid = lax.all_to_all(parts_mid, "fsdp", 0, 0)
-        parts_end, got_mid = lax.optimization_barrier((parts_end, got_mid))
+        parts_end, got_mid, states = lax.optimization_barrier((parts_end, got_mid, latents))
         got_end = lax.all_to_all(parts_end, "fsdp", 0, 0)
+        outputs = outputs_of(states)
+        got_end, outputs = lax.optimization_barrier((got_end, outputs))
 
         def add(body, got, name):
             return pl.pallas_call(
@@ -851,6 +908,8 @@
         mids = [mine_mid] + exchange(mine_mid, "dp", n_dp)
         ends = [mine_end] + exchange(mine_end, "dp", n_dp)
     else:
+        outputs = outputs_of(latents)
+
         def scatter(x, count):
             x = x[0, :count * WIDTH].reshape(count, WIDTH, WIDTH)
             x = lax.psum_scatter(x, "fsdp", scatter_dimension=1, tiled=True).astype(F32)
@@ -864,6 +923,7 @@
         mids = [jnp.concatenate([scatter(parts_mid, blocks + 3), rep, jnp.zeros((8, WIDTH), F32)])]
         ends = [scatter(parts_end, SPLIT + 2)]
 
+    value_logits, chance_logits, latent_grad = outputs
     shapes = [
         (1,), (shard, WIDTH), (moves, shard), (1, shard), (1, shard), (1, shard), (layers, shard, WIDTH), (layers, shard),
         (layers, shard), (layers, shard), (shard, nq), (nq,), (shard, nc), (nc,),

time: 242 us -> 238 us (0.983)
  waiting for transfers between devices: 28 us -> 15.6 us
  Pallas kernels: 170 us -> 176 us
  local copies, waits for them, and re-layouts: 7.18 us -> 9.93 us
    all_to_all x1, waiting for transfers between devices: 14.6 us -> 1.61 us  [per_device(): got_end = lax.all_to_all(parts_end, 'fsdp', 0, 0)]
    pallas_call x1 -> x2, Pallas kernels: 91.8 us -> 98.6 us  [the longest x1 88.8 us: per_device(): pl.pallas_call(functools.partial(middle_kernel, layers), grid=(steps,), i...]
    unnamed x20 -> x26, local copies, waits for them, and re-layouts: 2.86 us -> 5.63 us
  transfers between devices with their start and end apart: 11 -> 11, of which waited for: 5 -> 6; matrix products, arithmetic and copies ran while one was open for 2% -> 2% of each run, Pallas kernels for 31% -> 35%
where the time goes in v6:
time: 238 us
  Pallas kernels  176 us (74%)
  starting transfers between devices  21.2 us (9%)
  waiting for transfers between devices  15.6 us (7%)
  between operations  14.2 us (6%)
  local copies, waits for them, and re-layouts  9.93 us (4%)
    pallas_call x1, Pallas kernels, per_device(): pl.pallas_call(functools.partial(middle_kernel, layers), grid=(steps,), i...  88.8 us
    pallas_call x1, Pallas kernels, per_device(): pl.pallas_call(functools.partial(first_kernel, layers, rows_dev, fronts),...  37.3 us
    pallas_call x1, Pallas kernels, per_device(): pl.pallas_call(functools.partial(last_kernel, layers, rows_dev, fronts),...  31.7 us
    pallas_call x1, Pallas kernels, outputs_of(): pl.pallas_call(outputs_kernel, grid=(steps,), in_specs=[tiled((rows_dev,...  9.88 us
    all_to_all x1, starting transfers between devices, per_device(): w_fronts = [lax.all_to_all(front, 'fsdp', 0, 0)]  7.25 us
    all_to_all x1, waiting for transfers between devices, per_device(): w_fronts = [lax.all_to_all(front, 'fsdp', 0, 0)]  6.45 us
    all_to_all x1, starting transfers between devices, per_device(): got_end = lax.all_to_all(parts_end, 'fsdp', 0, 0)  5.89 us
    unnamed x26, local copies, waits for them, and re-layouts  5.63 us
  transfers between devices with their start and end apart: 11, of which 6 were waited for; matrix products, arithmetic and copies ran while one was open for 2% of the time, Pallas kernels for 35%

profile of v6, /device:TPU:0, one launch (start us, length us, event | category | flops | bytes accessed | tf_op | source)
XLA Modules:
  0.0 237.5 jit_solution(3012771503158820911)
XLA Ops:
  7.2 1.8 pack.1
  9.0 7.3 %all-to-all-start = ((bf16[8,96,256]{2,1,0:T(8,128)(2,1)}), bf16[8,96,256]{2,1,0:T(8,128)(2,1)S(1)}, u32[]{:S(2)}, u32[]{:S(2)}) async-start(bf16[8,96,256]{2,1,0:T(8,128)(2,1)} %get-tuple-element.60), calls=%async_computation | async-start | bytes 786432 | tf_op jit(solution)/shard_map/all_to_all | solution.py:782
  16.3 0.0 all-gather.2.cloned.1.call-start
  16.4 0.8 pad_maximum_fusion
  17.1 0.6 broadcast_in_dim.11.hb_ref
  17.7 0.8 stack.15
  18.5 0.8 stack.16
  19.2 0.8 stack.17
  20.0 0.8 stack.18
  20.8 0.1 pad_add_fusion
  20.9 0.7 pad.4.ints_ref
  21.6 6.4 %all-to-all-done.refs_0_ = bf16[8,96,256]{2,1,0:T(8,128)(2,1)S(1)} async-done(((bf16[8,96,256]{2,1,0:T(8,128)(2,1)}), bf16[8,96,256]{2,1,0:T(8,128)(2,1)S(1)}, u32[]{:S(2)}, u32[]{:S(2)}) %all-to-all-start) | async-done | bytes 393248 | tf_op jit(solution)/shard_map/all_to_all | solution.py:782
  28.0 0.0 copy-start.5
  28.0 0.0 collective-permute-start
  28.0 0.0 all-gather.2.cloned.1.call-update
  28.0 1.7 collective-permute-done.refs_1_
  29.7 0.0 copy-done.5
  29.7 0.0 copy-start.12
  29.7 0.7 copy-done.12
  30.5 37.3 %first.1 = (bf16[5,5760,256]{2,1,0:T(8,128)(2,1)}, bf16[5,5760,256]{2,1,0:T(8,128)(2,1)}, f32[5,5760,128]{2,1,0:T(8,128)}, bf16[4,5760,256]{2,1,0:T(8,128)(2,1)}...) custom-call(s32[1]{0:T(128)} %bitcast.core_ref, bf16[5696,256]{1,0:T(8,128)(2,1)} %latent_ref.3, s32[8,5760]{1,0:T(8,128)} %pad.4.ints_ref, ...), custom_call_target="tpu_custom_call" | custom-call | flops 74658611200 | bytes 62914560 | tf_op jit(solution)/shard_map/first/pallas_call | solution.py:802
  67.8 0.6 all-gather.2.cloned.1.call-done.w_ref
  68.5 88.8 %middle.1 = (bf16[5696,256]{1,0:T(8,128)(2,1)}, f32[5760,256]{1,0:T(8,128)}, f32[48,256]{1,0:T(8,128)}, f32[8,256]{1,0:T(8,128)}, bf16[8,304,256]{2,1,0:T(8,128)(2,1)}) custom-call(f32[5760,256]{1,0:T(8,128)} %get-tuple-element.63.s_in_ref, s32[8,5760]{1,0:T(8,128)} %pad.4.ints_ref, f32[128,256]{1,0:T(8,128)} %get-tuple-element.64.vec_ref, ...), custom_call_target="tpu_custom_call" | custom-call | flops 223975833600 | bytes 41943040 | tf_op jit(solution)/shard_map/middle/pallas_call | solution.py:821
  157.2 4.3 %all-to-all-start.1 = ((bf16[8,304,256]{2,1,0:T(8,128)(2,1)}), bf16[8,304,256]{2,1,0:T(8,128)(2,1)}, u32[]{:S(2)}, u32[]{:S(2)}) async-start(bf16[8,304,256]{2,1,0:T(8,128)(2,1)} %get-tuple-element.75), calls=%async_computation.1 | async-start | bytes 2490368 | tf_op jit(solution)/shard_map/all_to_all | solution.py:896
  161.5 0.0 copy-start
  161.5 0.0 copy-start.1
  161.5 31.7 %last.1 = (bf16[5760,256]{1,0:T(8,128)(2,1)}, bf16[8,176,256]{2,1,0:T(8,128)(2,1)}, bf16[256,256]{1,0:T(8,128)(2,1)}) custom-call(s32[1]{0:T(128)} %bitcast.core_ref, bf16[5696,256]{1,0:T(8,128)(2,1)} %latent_ref.3, s32[8,5760]{1,0:T(8,128)} %pad.4.ints_ref, f32[5760,256]{1,0:T(8,128)} %get-tuple-element.68.ds_in_ref, ...), custom_call_target="tpu_custom_call" | custom-call | flops 55993958400 | bytes 62914560 | tf_op jit(solution)/shard_map/last/pallas_call | solution.py:857
  193.2 0.0 all-to-all-done.1.in_ref
  193.2 5.9 %all-to-all-start.2 = ((bf16[8,176,256]{2,1,0:T(8,128)(2,1)}), bf16[8,176,256]{2,1,0:T(8,128)(2,1)S(1)}, u32[]{:S(2)}, u32[]{:S(2)}) async-start(bf16[8,176,256]{2,1,0:T(8,128)(2,1)} %get-tuple-element.76), calls=%async_computation.2 | async-start | bytes 1441792 | tf_op jit(solution)/shard_map/all_to_all | solution.py:898
  199.1 2.1 sum_mid.1.refs_0_
  201.2 0.1 collective-permute-start.3
  201.3 1.4 collective-permute-start.2
  202.7 0.4 collective-permute-start.1
  203.1 0.0 copy-done
  203.1 0.0 copy-done.1
  203.1 0.0 copy-start.2
  203.1 1.8 copy-done.2
  204.9 0.0 copy-start.3
  204.9 0.9 copy-done.3
  205.8 9.9 %outputs.1 = (bf16[601,5696]{1,0:T(8,128)(2,1)}, bf16[32,5696]{1,0:T(8,128)(2,1)}, bf16[5696,256]{1,0:T(8,128)(2,1)}) custom-call(bf16[5696,256]{1,0:T(8,128)(2,1)S(1)} %copy-done.2, bf16[5760,256]{1,0:T(8,128)(2,1)} %get-tuple-element.78.d_pre_ref, bf16[9,256,256]{2,1,0:T(8,128)(2,1)S(1)} %copy-done.1, bf16[1,768]{1,0:T(2,128)(2,1)S(1)} %copy-done, ...), custom_call_target="tpu_custom_call" | custom-call | flops 7465861120 | bytes 16777216 | tf_op jit(solution)/shard_map/outputs/pallas_call | solution.py:882
  215.7 1.6 all-to-all-done.2.in_ref
  217.3 0.0 copy-start.4
  217.3 0.9 copy-done.4
  218.2 1.9 sum_end.1.refs_4_
  220.1 0.0 collective-permute-start.6
  220.1 1.5 collective-permute-start.5
  221.7 0.0 collective-permute-done.3.refs_3_
  221.7 0.0 copy-start.6
  221.7 0.3 collective-permute-start.4
  222.0 0.0 collective-permute-done.2.refs_2_
  222.0 0.0 collective-permute-done.1.refs_1_
  222.0 0.0 copy-start.8
  222.0 3.2 %collective-permute-done.6.refs_7_ = bf16[176,256]{1,0:T(8,128)(2,1)S(1)} collective-permute-done((bf16[176,256]{1,0:T(8,128)(2,1)}, bf16[176,256]{1,0:T(8,128)(2,1)S(1)}, u32[]{:S(2)}, u32[]{:S(2)}) %collective-permute-start.6) | collective-permute-done | bytes 90144 | tf_op jit(solution)/shard_map/ppermute | solution.py:747
  225.2 0.0 copy-start.9
  225.2 2.0 collective-permute-done.5.refs_6_
  227.2 0.0 copy-start.10
  227.2 0.0 collective-permute-done.4.refs_5_
  227.2 0.0 copy-done.6
  227.2 0.0 copy-done.7
  227.2 0.0 copy-done.8
  227.2 0.0 copy-done.9
  227.2 0.6 copy-done.10
  227.8 0.0 copy-start.11
  227.8 0.6 copy-done.11
  228.4 2.2 finish.1
  (3 shorter events, 0.0 us)
Async XLA Ops:
  9.0 19.0 %all-to-all-start = ((bf16[8,96,256]{2,1,0:T(8,128)(2,1)}), bf16[8,96,256]{2,1,0:T(8,128)(2,1)S(1)}, u32[]{:S(2)}, u32[]{:S(2)}) async-start(bf16[8,96,256]{2,1,0:T(8,128)(2,1)} %get-tuple-element.60), calls=%async_computation | async-start | bytes 786432 | tf_op jit(solution)/shard_map/all_to_all | solution.py:782
  16.3 52.2 %all-gather.2.cloned.1.call-start = ((), (), s32[]{:S(2)}) async-start(), calls=%async_computation.3 | async-start | bytes 1327104 | tf_op jit(solution)/shard_map/all_gather | solution.py:789
  28.0 1.7 copy-start.5
  28.0 1.7 collective-permute-start
  29.7 0.8 copy-start.12
  157.2 36.0 %all-to-all-start.1 = ((bf16[8,304,256]{2,1,0:T(8,128)(2,1)}), bf16[8,304,256]{2,1,0:T(8,128)(2,1)}, u32[]{:S(2)}, u32[]{:S(2)}) async-start(bf16[8,304,256]{2,1,0:T(8,128)(2,1)} %get-tuple-element.75), calls=%async_computation.1 | async-start | bytes 2490368 | tf_op jit(solution)/shard_map/all_to_all | solution.py:896
  161.5 41.6 %copy-start = (bf16[1,768]{1,0:T(2,128)(2,1)S(1)}, bf16[1,768]{1,0:T(2,128)(2,1)}, u32[]{:S(2)}) copy-start(bf16[1,768]{1,0:T(2,128)(2,1)} %broadcast_in_dim.11.hb_ref) | copy-start | bytes 4612
  161.5 41.6 %copy-start.1 = (bf16[9,256,256]{2,1,0:T(8,128)(2,1)S(1)}, bf16[9,256,256]{2,1,0:T(8,128)(2,1)}, u32[]{:S(2)}) copy-start(bf16[9,256,256]{2,1,0:T(8,128)(2,1)} %all-gather.2.cloned.1.call-done.w_ref) | copy-start | bytes 3538948
  193.2 24.1 %all-to-all-start.2 = ((bf16[8,176,256]{2,1,0:T(8,128)(2,1)}), bf16[8,176,256]{2,1,0:T(8,128)(2,1)S(1)}, u32[]{:S(2)}, u32[]{:S(2)}) async-start(bf16[8,176,256]{2,1,0:T(8,128)(2,1)} %get-tuple-element.76), calls=%async_computation.2 | async-start | bytes 1441792 | tf_op jit(solution)/shard_map/all_to_all | solution.py:898
  201.2 20.4 %collective-permute-start.3 = (bf16[304,256]{1,0:T(8,128)(2,1)}, bf16[304,256]{1,0:T(8,128)(2,1)S(1)}, u32[]{:S(2)}, u32[]{:S(2)}) collective-permute-start(bf16[304,256]{1,0:T(8,128)(2,1)} %sum_mid.1.refs_0_), channel_id=1, source_target_pairs={{0,24},{8,16},{16,8},{24,0},{1,25},{9,17},{17,9},{25,1},{2,26},{10... | collective-permute-start | bytes 466952 | tf_op jit(solution)/shard_map/ppermute | solution.py:747
  201.3 20.6 %collective-permute-start.2 = (bf16[304,256]{1,0:T(8,128)(2,1)}, bf16[304,256]{1,0:T(8,128)(2,1)S(1)}, u32[]{:S(2)}, u32[]{:S(2)}) collective-permute-start(bf16[304,256]{1,0:T(8,128)(2,1)} %sum_mid.1.refs_0_), channel_id=1, source_target_pairs={{0,16},{8,24},{16,0},{24,8},{1,17},{9,25},{17,1},{25,9},{2,18},{10... | collective-permute-start | bytes 466952 | tf_op jit(solution)/shard_map/ppermute | solution.py:747
  202.7 19.2 %collective-permute-start.1 = (bf16[304,256]{1,0:T(8,128)(2,1)}, bf16[304,256]{1,0:T(8,128)(2,1)S(1)}, u32[]{:S(2)}, u32[]{:S(2)}) collective-permute-start(bf16[304,256]{1,0:T(8,128)(2,1)} %sum_mid.1.refs_0_), channel_id=1, source_target_pairs={{0,8},{8,0},{16,24},{24,16},{1,9},{9,1},{17,25},{25,17},{2,10},{10... | collective-permute-start | bytes 466952 | tf_op jit(solution)/shard_map/ppermute | solution.py:747
  203.1 1.8 copy-start.2
  204.9 0.9 copy-start.3
  217.3 0.9 copy-start.4
  220.1 5.1 %collective-permute-start.6 = (bf16[176,256]{1,0:T(8,128)(2,1)}, bf16[176,256]{1,0:T(8,128)(2,1)S(1)}, u32[]{:S(2)}, u32[]{:S(2)}) collective-permute-start(bf16[176,256]{1,0:T(8,128)(2,1)} %sum_end.1.refs_4_), channel_id=1, source_target_pairs={{0,24},{8,16},{16,8},{24,0},{1,25},{9,17},{17,9},{25,1},{2,26},{10... | collective-permute-start | bytes 270344 | tf_op jit(solution)/shard_map/ppermute | solution.py:747
  220.1 7.1 %collective-permute-start.5 = (bf16[176,256]{1,0:T(8,128)(2,1)}, bf16[176,256]{1,0:T(8,128)(2,1)S(1)}, u32[]{:S(2)}, u32[]{:S(2)}) collective-permute-start(bf16[176,256]{1,0:T(8,128)(2,1)} %sum_end.1.refs_4_), channel_id=1, source_target_pairs={{0,16},{8,24},{16,0},{24,8},{1,17},{9,25},{17,1},{25,9},{2,18},{10... | collective-permute-start | bytes 270344 | tf_op jit(solution)/shard_map/ppermute | solution.py:747
  221.7 5.5 %copy-start.6 = (bf16[304,256]{1,0:T(8,128)(2,1)}, bf16[304,256]{1,0:T(8,128)(2,1)S(1)}, u32[]{:S(2)}) copy-start(bf16[304,256]{1,0:T(8,128)(2,1)S(1)} %collective-permute-done.3.refs_3_) | copy-start | bytes 466948
  221.7 5.5 %collective-permute-start.4 = (bf16[176,256]{1,0:T(8,128)(2,1)}, bf16[176,256]{1,0:T(8,128)(2,1)S(1)}, u32[]{:S(2)}, u32[]{:S(2)}) collective-permute-start(bf16[176,256]{1,0:T(8,128)(2,1)} %sum_end.1.refs_4_), channel_id=1, source_target_pairs={{0,8},{8,0},{16,24},{24,16},{1,9},{9,1},{17,25},{25,17},{2,10},{10... | collective-permute-start | bytes 270344 | tf_op jit(solution)/shard_map/ppermute | solution.py:747
  222.0 5.2 %copy-start.7 = (bf16[304,256]{1,0:T(8,128)(2,1)}, bf16[304,256]{1,0:T(8,128)(2,1)S(1)}, u32[]{:S(2)}) copy-start(bf16[304,256]{1,0:T(8,128)(2,1)S(1)} %collective-permute-done.2.refs_2_) | copy-start | bytes 466948
  222.0 5.2 %copy-start.8 = (bf16[304,256]{1,0:T(8,128)(2,1)}, bf16[304,256]{1,0:T(8,128)(2,1)S(1)}, u32[]{:S(2)}) copy-start(bf16[304,256]{1,0:T(8,128)(2,1)S(1)} %collective-permute-done.1.refs_1_) | copy-start | bytes 466948
  225.2 2.0 copy-start.9
  227.2 0.6 copy-start.10
  227.8 0.6 copy-start.11
Sparse Core Ops, SparseCore 0:
  28.2 40.2 all-gather.1

commit v7 on v6

--- a/solution.py
+++ b/solution.py
@@ -10,6 +10,7 @@
 BF16 = jnp.bfloat16
 WIDTH = 256
 UNIT = 16
+WIDE = 32
 TILE = 1920
 BACK = 640
 CHUNK = 640
@@ -45,7 +46,7 @@
     slope = e1 * (1.0 / (3 * K1) + bend)
     if gain_slope is not None:
         slope = slope * gain_slope
-    return h * e1, n.astype(BF16), slope, jnp.broadcast_to(r, (UNIT, 128))
+    return h * e1, n.astype(BF16), slope, jnp.broadcast_to(r, (s.shape[0], 128))
 
 
 def scales(vec_ref, at, layers, slope):
@@ -61,7 +62,7 @@
 
 def lane_sums(x):
     total = lax.reduce_sum(x[:, 0:128] + x[:, 128:256], (1,))
-    return jnp.broadcast_to(total[:, None], (UNIT, 128))
+    return jnp.broadcast_to(total[:, None], (x.shape[0], 128))
 
 
 def norm_back(da, slope, n, r):
@@ -82,8 +83,8 @@
 
 def activate(base, s_ref, save, i, scale):
     act_ref, n_ref, slope_ref, r_ref = save
-    for u in range(0, CHUNK, UNIT):
-        rows = pl.ds(base + u, UNIT)
+    for u in range(0, CHUNK, WIDE):
+        rows = pl.ds(base + u, WIDE)
         act, n, slope, r = norm_gelu(s_ref[rows, :], *scale)
         act_ref[i, rows, :] = act.astype(BF16)
         n_ref[i, rows, :] = n
@@ -104,9 +105,9 @@
 
     def residual(i, base, out):
         bias = vec_ref[pl.ds(7 + 2 * layers + i, 1), :]
-        for u in range(0, CHUNK, UNIT):
-            rows = pl.ds(base + u, UNIT)
-            s_ref[rows, :] = s_ref[rows, :] + (out[u:u + UNIT, :] + bias)
+        for u in range(0, CHUNK, WIDE):
+            rows = pl.ds(base + u, WIDE)
+            s_ref[rows, :] = s_ref[rows, :] + (out[u:u + WIDE, :] + bias)
 
     def block(i, carry):
         if before_block is not None:
@@ -136,7 +137,7 @@
     return total.astype(F32)
 
 
-GROUP = 8
+GROUP = 4
 
 
 def fold(x):
@@ -157,13 +158,13 @@
         gw_ref[i - g_at] += mm_tn(act_ref[i - save_at, pl.ds(base, BACK), :], low_ref[pl.ds(base, BACK), :])
         if beside is not None:
             beside(last - 1 - i, c)
-        zero = jnp.zeros((UNIT, WIDTH), F32)
+        zero = jnp.zeros((WIDE, WIDTH), F32)
         shift, gain, bias = zero, zero, zero
         held = []
-        for u in range(0, BACK, UNIT):
-            rows = pl.ds(base + u, UNIT)
+        for u in range(0, BACK, WIDE):
+            rows = pl.ds(base + u, WIDE)
             at = (i - save_at, rows, slice(None))
-            d_in, wf, wn = norm_back(da_ref[u:u + UNIT, :], slope_ref[at], n_ref[at], r_ref[at])
+            d_in, wf, wn = norm_back(da_ref[u:u + WIDE, :], slope_ref[at], n_ref[at], r_ref[at])
             shift = shift + wf
             held.append(wn)
             if len(held) == GROUP:
@@ -292,9 +293,9 @@
 
     def body(c, carry):
         following = product(jnp.minimum(c + 1, PARTS - 1))
-        for u in range(0, CHUNK, UNIT):
-            rows = pl.ds(rows_of(c) + u, UNIT)
-            act, n, slope, r = norm_gelu(pre_ref[u:u + UNIT, :], *scale)
+        for u in range(0, CHUNK, WIDE):
+            rows = pl.ds(rows_of(c) + u, WIDE)
+            act, n, slope, r = norm_gelu(pre_ref[u:u + WIDE, :], *scale)
             s_ref[rows, :] = act
             n_ref[n_at, rows, :] = n
             slope_ref[n_at, rows, :] = slope.astype(slope_ref.dtype)
@@ -315,11 +316,11 @@
 
     def body(c, carry):
         products(jnp.maximum(c - 1, 0))
-        shift = jnp.zeros((UNIT, WIDTH), F32)
+        shift = jnp.zeros((WIDE, WIDTH), F32)
         gain = shift
         held = []
-        for u in range(0, CHUNK, UNIT):
-            rows = pl.ds(rows_of(c) + u, UNIT)
+        for u in range(0, CHUNK, WIDE):
+            rows = pl.ds(rows_of(c) + u, WIDE)
             d_in, wf, wn = norm_back(s_ref[rows, :], slope_ref[n_at, rows, :], n_ref[n_at, rows, :], r_ref[n_at, rows, :])
             shift = shift + wf
             held.append(wn)
@@ -327,7 +328,7 @@
                 gain = gain + column_sums(held)
                 held = []
             low = d_in.astype(BF16)
-            low_ref[u:u + UNIT, :] = low
+            low_ref[u:u + WIDE, :] = low
             d_pre_ref[rows, :] = low
         gv_ref[5:6, :] += fold(gain)
         gv_ref[6:7, :] += fold(shift)
@@ -458,7 +459,8 @@
     def _():
         for ref in (gw_ref, gh_ref, gv_ref, loss_ref):
             ref[...] = jnp.zeros_like(ref)
-        turned_ref[...] = jnp.ones_like(turned_ref)
+        turned_ref[WIDTH:, :] = jnp.ones_like(turned_ref[WIDTH:, :])
+        turned_ref[0:WIDTH, TILE:] = jnp.zeros_like(turned_ref[0:WIDTH, TILE:])
         dlog_ref[TILE:, :] = jnp.zeros_like(dlog_ref[TILE:, :])
         for k in range(3):
             wh_ref[:, k * WIDTH:(k + 1) * WIDTH] = w_ref[blocks + k]

time: 238 us -> 237 us (level)
  no operation moved by 1% of the time
where the time goes in v7:
time: 237 us; the launch traced here: 236 us
  Pallas kernels  174 us (73%)
  starting transfers between devices  21.2 us (9%)
  waiting for transfers between devices  15.6 us (7%)
  between operations  14.2 us (6%)
  local copies, waits for them, and re-layouts  9.93 us (4%)
    pallas_call x1, Pallas kernels, per_device(): pl.pallas_call(functools.partial(middle_kernel, layers), grid=(steps,), i...  87.9 us
    pallas_call x1, Pallas kernels, per_device(): pl.pallas_call(functools.partial(first_kernel, layers, rows_dev, fronts),...  36.8 us
    pallas_call x1, Pallas kernels, per_device(): pl.pallas_call(functools.partial(last_kernel, layers, rows_dev, fronts),...  31.8 us
    pallas_call x1, Pallas kernels, outputs_of(): pl.pallas_call(outputs_kernel, grid=(steps,), in_specs=[tiled((rows_dev,...  9.87 us
    all_to_all x1, starting transfers between devices, per_device(): w_fronts = [lax.all_to_all(front, 'fsdp', 0, 0)]  7.25 us
    all_to_all x1, waiting for transfers between devices, per_device(): w_fronts = [lax.all_to_all(front, 'fsdp', 0, 0)]  6.45 us
    all_to_all x1, starting transfers between devices, per_device(): got_end = lax.all_to_all(parts_end, 'fsdp', 0, 0)  5.89 us
    unnamed x26, local copies, waits for them, and re-layouts  5.63 us
  transfers between devices with their start and end apart: 11, of which 6 were waited for; matrix products, arithmetic and copies ran while one was open for 2% of the time, Pallas kernels for 35%

profile of v7, /device:TPU:0, one launch (start us, length us, event | category | flops | bytes accessed | tf_op | source)
XLA Modules:
  0.0 236.2 jit_solution(18014667723038753001)
XLA Ops:
  7.2 1.8 pack.1
  9.0 7.3 %all-to-all-start = ((bf16[8,96,256]{2,1,0:T(8,128)(2,1)}), bf16[8,96,256]{2,1,0:T(8,128)(2,1)S(1)}, u32[]{:S(2)}, u32[]{:S(2)}) async-start(bf16[8,96,256]{2,1,0:T(8,128)(2,1)} %get-tuple-element.60), calls=%async_computation | async-start | bytes 786432 | tf_op jit(solution)/shard_map/all_to_all | solution.py:784
  16.3 0.0 all-gather.2.cloned.1.call-start
  16.4 0.8 pad_maximum_fusion
  17.1 0.6 broadcast_in_dim.11.hb_ref
  17.7 0.8 stack.15
  18.5 0.8 stack.16
  19.2 0.8 stack.17
  20.0 0.8 stack.18
  20.8 0.1 pad_add_fusion
  20.9 0.7 pad.4.ints_ref
  21.6 6.4 %all-to-all-done.refs_0_ = bf16[8,96,256]{2,1,0:T(8,128)(2,1)S(1)} async-done(((bf16[8,96,256]{2,1,0:T(8,128)(2,1)}), bf16[8,96,256]{2,1,0:T(8,128)(2,1)S(1)}, u32[]{:S(2)}, u32[]{:S(2)}) %all-to-all-start) | async-done | bytes 393248 | tf_op jit(solution)/shard_map/all_to_all | solution.py:784
  28.0 0.0 copy-start.5
  28.0 0.0 collective-permute-start
  28.0 0.0 all-gather.2.cloned.1.call-update
  28.0 1.7 collective-permute-done.refs_1_
  29.7 0.0 copy-done.5
  29.7 0.0 copy-start.12
  29.7 0.7 copy-done.12
  30.5 36.8 %first.1 = (bf16[5,5760,256]{2,1,0:T(8,128)(2,1)}, bf16[5,5760,256]{2,1,0:T(8,128)(2,1)}, f32[5,5760,128]{2,1,0:T(8,128)}, bf16[4,5760,256]{2,1,0:T(8,128)(2,1)}...) custom-call(s32[1]{0:T(128)} %bitcast.core_ref, bf16[5696,256]{1,0:T(8,128)(2,1)} %latent_ref.3, s32[8,5760]{1,0:T(8,128)} %pad.4.ints_ref, ...), custom_call_target="tpu_custom_call" | custom-call | flops 74658611200 | bytes 62914560 | tf_op jit(solution)/shard_map/first/pallas_call | solution.py:804
  67.3 1.2 all-gather.2.cloned.1.call-done.w_ref
  68.5 87.9 %middle.1 = (bf16[5696,256]{1,0:T(8,128)(2,1)}, f32[5760,256]{1,0:T(8,128)}, f32[48,256]{1,0:T(8,128)}, f32[8,256]{1,0:T(8,128)}, bf16[8,304,256]{2,1,0:T(8,128)(2,1)}) custom-call(f32[5760,256]{1,0:T(8,128)} %get-tuple-element.63.s_in_ref, s32[8,5760]{1,0:T(8,128)} %pad.4.ints_ref, f32[128,256]{1,0:T(8,128)} %get-tuple-element.64.vec_ref, ...), custom_call_target="tpu_custom_call" | custom-call | flops 223975833600 | bytes 41943040 | tf_op jit(solution)/shard_map/middle/pallas_call | solution.py:823
  156.4 4.3 %all-to-all-start.1 = ((bf16[8,304,256]{2,1,0:T(8,128)(2,1)}), bf16[8,304,256]{2,1,0:T(8,128)(2,1)}, u32[]{:S(2)}, u32[]{:S(2)}) async-start(bf16[8,304,256]{2,1,0:T(8,128)(2,1)} %get-tuple-element.75), calls=%async_computation.1 | async-start | bytes 2490368 | tf_op jit(solution)/shard_map/all_to_all | solution.py:898
  160.7 0.0 copy-start
  160.7 0.0 copy-start.1
  160.7 31.8 %last.1 = (bf16[5760,256]{1,0:T(8,128)(2,1)}, bf16[8,176,256]{2,1,0:T(8,128)(2,1)}, bf16[256,256]{1,0:T(8,128)(2,1)}) custom-call(s32[1]{0:T(128)} %bitcast.core_ref, bf16[5696,256]{1,0:T(8,128)(2,1)} %latent_ref.3, s32[8,5760]{1,0:T(8,128)} %pad.4.ints_ref, f32[5760,256]{1,0:T(8,128)} %get-tuple-element.68.ds_in_ref, ...), custom_call_target="tpu_custom_call" | custom-call | flops 55993958400 | bytes 62914560 | tf_op jit(solution)/shard_map/last/pallas_call | solution.py:859
  192.5 0.0 all-to-all-done.1.in_ref
  192.5 5.9 %all-to-all-start.2 = ((bf16[8,176,256]{2,1,0:T(8,128)(2,1)}), bf16[8,176,256]{2,1,0:T(8,128)(2,1)S(1)}, u32[]{:S(2)}, u32[]{:S(2)}) async-start(bf16[8,176,256]{2,1,0:T(8,128)(2,1)} %get-tuple-element.76), calls=%async_computation.2 | async-start | bytes 1441792 | tf_op jit(solution)/shard_map/all_to_all | solution.py:900
  198.4 2.1 sum_mid.1.refs_0_
  200.5 0.0 collective-permute-start.3
  200.5 1.5 collective-permute-start.2
  202.0 0.4 collective-permute-start.1
  202.4 0.0 copy-done
  202.4 0.0 copy-done.1
  202.4 0.0 copy-start.2
  202.4 1.8 copy-done.2
  204.2 0.0 copy-start.3
  204.2 0.9 copy-done.3
  205.1 9.9 %outputs.1 = (bf16[601,5696]{1,0:T(8,128)(2,1)}, bf16[32,5696]{1,0:T(8,128)(2,1)}, bf16[5696,256]{1,0:T(8,128)(2,1)}) custom-call(bf16[5696,256]{1,0:T(8,128)(2,1)S(1)} %copy-done.2, bf16[5760,256]{1,0:T(8,128)(2,1)} %get-tuple-element.78.d_pre_ref, bf16[9,256,256]{2,1,0:T(8,128)(2,1)S(1)} %copy-done.1, bf16[1,768]{1,0:T(2,128)(2,1)S(1)} %copy-done, ...), custom_call_target="tpu_custom_call" | custom-call | flops 7465861120 | bytes 16777216 | tf_op jit(solution)/shard_map/outputs/pallas_call | solution.py:884
  215.0 1.1 all-to-all-done.2.in_ref
  216.0 0.0 copy-start.4
  216.0 0.9 copy-done.4
  216.9 1.9 sum_end.1.refs_4_
  218.8 0.0 collective-permute-start.6
  218.8 1.5 collective-permute-start.5
  220.4 0.0 collective-permute-done.3.refs_3_
  220.4 0.0 copy-start.6
  220.4 0.3 collective-permute-start.4
  220.7 0.0 collective-permute-done.2.refs_2_
  220.7 0.0 copy-start.7
  220.7 0.0 collective-permute-done.1.refs_1_
  220.7 0.0 copy-start.8
  220.7 3.2 %collective-permute-done.6.refs_7_ = bf16[176,256]{1,0:T(8,128)(2,1)S(1)} collective-permute-done((bf16[176,256]{1,0:T(8,128)(2,1)}, bf16[176,256]{1,0:T(8,128)(2,1)S(1)}, u32[]{:S(2)}, u32[]{:S(2)}) %collective-permute-start.6) | collective-permute-done | bytes 90144 | tf_op jit(solution)/shard_map/ppermute | solution.py:749
  223.9 0.0 copy-start.9
  223.9 2.0 collective-permute-done.5.refs_6_
  225.9 0.0 copy-start.10
  225.9 0.0 collective-permute-done.4.refs_5_
  225.9 0.0 copy-done.6
  225.9 0.0 copy-done.7
  225.9 0.0 copy-done.8
  225.9 0.0 copy-done.9
  225.9 0.6 copy-done.10
  226.5 0.6 copy-done.11
  227.1 2.2 finish.1
  (3 shorter events, 0.0 us)
Async XLA Ops:
  9.0 19.0 %all-to-all-start = ((bf16[8,96,256]{2,1,0:T(8,128)(2,1)}), bf16[8,96,256]{2,1,0:T(8,128)(2,1)S(1)}, u32[]{:S(2)}, u32[]{:S(2)}) async-start(bf16[8,96,256]{2,1,0:T(8,128)(2,1)} %get-tuple-element.60), calls=%async_computation | async-start | bytes 786432 | tf_op jit(solution)/shard_map/all_to_all | solution.py:784
  16.3 52.2 %all-gather.2.cloned.1.call-start = ((), (), s32[]{:S(2)}) async-start(), calls=%async_computation.3 | async-start | bytes 1327104 | tf_op jit(solution)/shard_map/all_gather | solution.py:791
  28.0 1.7 copy-start.5
  28.0 1.7 collective-permute-start
  29.7 0.8 copy-start.12
  156.4 36.1 %all-to-all-start.1 = ((bf16[8,304,256]{2,1,0:T(8,128)(2,1)}), bf16[8,304,256]{2,1,0:T(8,128)(2,1)}, u32[]{:S(2)}, u32[]{:S(2)}) async-start(bf16[8,304,256]{2,1,0:T(8,128)(2,1)} %get-tuple-element.75), calls=%async_computation.1 | async-start | bytes 2490368 | tf_op jit(solution)/shard_map/all_to_all | solution.py:898
  160.7 41.7 %copy-start = (bf16[1,768]{1,0:T(2,128)(2,1)S(1)}, bf16[1,768]{1,0:T(2,128)(2,1)}, u32[]{:S(2)}) copy-start(bf16[1,768]{1,0:T(2,128)(2,1)} %broadcast_in_dim.11.hb_ref) | copy-start | bytes 4612
  160.7 41.7 %copy-start.1 = (bf16[9,256,256]{2,1,0:T(8,128)(2,1)S(1)}, bf16[9,256,256]{2,1,0:T(8,128)(2,1)}, u32[]{:S(2)}) copy-start(bf16[9,256,256]{2,1,0:T(8,128)(2,1)} %all-gather.2.cloned.1.call-done.w_ref) | copy-start | bytes 3538948
  192.5 23.5 %all-to-all-start.2 = ((bf16[8,176,256]{2,1,0:T(8,128)(2,1)}), bf16[8,176,256]{2,1,0:T(8,128)(2,1)S(1)}, u32[]{:S(2)}, u32[]{:S(2)}) async-start(bf16[8,176,256]{2,1,0:T(8,128)(2,1)} %get-tuple-element.76), calls=%async_computation.2 | async-start | bytes 1441792 | tf_op jit(solution)/shard_map/all_to_all | solution.py:900
  200.5 19.9 %collective-permute-start.3 = (bf16[304,256]{1,0:T(8,128)(2,1)}, bf16[304,256]{1,0:T(8,128)(2,1)S(1)}, u32[]{:S(2)}, u32[]{:S(2)}) collective-permute-start(bf16[304,256]{1,0:T(8,128)(2,1)} %sum_mid.1.refs_0_), channel_id=1, source_target_pairs={{0,24},{8,16},{16,8},{24,0},{1,25},{9,17},{17,9},{25,1},{2,26},{10... | collective-permute-start | bytes 466952 | tf_op jit(solution)/shard_map/ppermute | solution.py:749
  200.5 20.2 %collective-permute-start.2 = (bf16[304,256]{1,0:T(8,128)(2,1)}, bf16[304,256]{1,0:T(8,128)(2,1)S(1)}, u32[]{:S(2)}, u32[]{:S(2)}) collective-permute-start(bf16[304,256]{1,0:T(8,128)(2,1)} %sum_mid.1.refs_0_), channel_id=1, source_target_pairs={{0,16},{8,24},{16,0},{24,8},{1,17},{9,25},{17,1},{25,9},{2,18},{10... | collective-permute-start | bytes 466952 | tf_op jit(solution)/shard_map/ppermute | solution.py:749
  202.0 18.7 %collective-permute-start.1 = (bf16[304,256]{1,0:T(8,128)(2,1)}, bf16[304,256]{1,0:T(8,128)(2,1)S(1)}, u32[]{:S(2)}, u32[]{:S(2)}) collective-permute-start(bf16[304,256]{1,0:T(8,128)(2,1)} %sum_mid.1.refs_0_), channel_id=1, source_target_pairs={{0,8},{8,0},{16,24},{24,16},{1,9},{9,1},{17,25},{25,17},{2,10},{10... | collective-permute-start | bytes 466952 | tf_op jit(solution)/shard_map/ppermute | solution.py:749
  202.4 1.8 copy-start.2
  204.2 0.9 copy-start.3
  216.0 0.9 copy-start.4
  218.8 5.1 %collective-permute-start.6 = (bf16[176,256]{1,0:T(8,128)(2,1)}, bf16[176,256]{1,0:T(8,128)(2,1)S(1)}, u32[]{:S(2)}, u32[]{:S(2)}) collective-permute-start(bf16[176,256]{1,0:T(8,128)(2,1)} %sum_end.1.refs_4_), channel_id=1, source_target_pairs={{0,24},{8,16},{16,8},{24,0},{1,25},{9,17},{17,9},{25,1},{2,26},{10... | collective-permute-start | bytes 270344 | tf_op jit(solution)/shard_map/ppermute | solution.py:749
  218.8 7.0 %collective-permute-start.5 = (bf16[176,256]{1,0:T(8,128)(2,1)}, bf16[176,256]{1,0:T(8,128)(2,1)S(1)}, u32[]{:S(2)}, u32[]{:S(2)}) collective-permute-start(bf16[176,256]{1,0:T(8,128)(2,1)} %sum_end.1.refs_4_), channel_id=1, source_target_pairs={{0,16},{8,24},{16,0},{24,8},{1,17},{9,25},{17,1},{25,9},{2,18},{10... | collective-permute-start | bytes 270344 | tf_op jit(solution)/shard_map/ppermute | solution.py:749
  220.4 5.5 %copy-start.6 = (bf16[304,256]{1,0:T(8,128)(2,1)}, bf16[304,256]{1,0:T(8,128)(2,1)S(1)}, u32[]{:S(2)}) copy-start(bf16[304,256]{1,0:T(8,128)(2,1)S(1)} %collective-permute-done.3.refs_3_) | copy-start | bytes 466948
  220.4 5.5 %collective-permute-start.4 = (bf16[176,256]{1,0:T(8,128)(2,1)}, bf16[176,256]{1,0:T(8,128)(2,1)S(1)}, u32[]{:S(2)}, u32[]{:S(2)}) collective-permute-start(bf16[176,256]{1,0:T(8,128)(2,1)} %sum_end.1.refs_4_), channel_id=1, source_target_pairs={{0,8},{8,0},{16,24},{24,16},{1,9},{9,1},{17,25},{25,17},{2,10},{10... | collective-permute-start | bytes 270344 | tf_op jit(solution)/shard_map/ppermute | solution.py:749
  220.7 5.2 %copy-start.7 = (bf16[304,256]{1,0:T(8,128)(2,1)}, bf16[304,256]{1,0:T(8,128)(2,1)S(1)}, u32[]{:S(2)}) copy-start(bf16[304,256]{1,0:T(8,128)(2,1)S(1)} %collective-permute-done.2.refs_2_) | copy-start | bytes 466948
  220.7 5.2 %copy-start.8 = (bf16[304,256]{1,0:T(8,128)(2,1)}, bf16[304,256]{1,0:T(8,128)(2,1)S(1)}, u32[]{:S(2)}) copy-start(bf16[304,256]{1,0:T(8,128)(2,1)S(1)} %collective-permute-done.1.refs_1_) | copy-start | bytes 466948
  223.9 2.0 copy-start.9
  225.9 0.6 copy-start.10
  226.5 0.6 copy-start.11
Sparse Core Ops, SparseCore 0:
  28.2 40.2 all-gather.1

commit v8 on v7

--- a/solution.py
+++ b/solution.py
@@ -400,10 +400,10 @@
     return pl.ds(pl.multiple_of(step * TILE, 128), TILE)
 
 
-def first_kernel(layers, rows_dev, fronts, core_ref, latent_ref, ints_ref, *refs):
+def first_kernel(layers, rows_dev, fronts, nq, nc, core_ref, latent_ref, ints_ref, *refs):
     front_refs = refs[:fronts]
     (
-        n_out, slope_out, r_out, act_out, s_out_ref, vec_ref, w_ref, lat_ref, hot_ref, pre_ref, s_ref, n_ref, slope_ref, r_ref, act_ref, sems,
+        n_out, slope_out, r_out, act_out, s_out_ref, vec_ref, head_ref, w_ref, lat_ref, hot_ref, pre_ref, s_ref, n_ref, slope_ref, r_ref, act_ref, sems,
     ) = refs[fronts:]
     step, steps = pl.program_id(0), pl.num_programs(0)
     span = tile_span(step)
@@ -421,6 +421,12 @@
     def _():
         join_front(core_ref, front_refs, w_ref)
         unpack_vec(w_ref[0], vec_ref)
+        tail = w_ref[0, :, 128:256]
+        lane = lax.broadcasted_iota(jnp.int32, (1, 128), 1)
+        head_ref[:, 0:128] = jnp.where(lane < nq - 2 * WIDTH, tail.astype(F32), 0.0).astype(BF16)
+        row = lax.broadcasted_iota(jnp.int32, (128, 128), 0)
+        pick = (row == lane + (128 - nc)) & (lane < nc)
+        head_ref[:, 128:256] = mm(tail, jnp.where(pick, 1.0, 0.0).astype(BF16)).astype(BF16)
 
     clean_latent(latent_ref, lat_ref, rows_dev)
     hot_ref[...] = moves_hot(ints_ref[...]).T
@@ -449,7 +455,7 @@
 
 
 def middle_kernel(
-    layers, s_in_ref, ints_ref, vec_ref, hb_ref, w_ref, latents_ref, ds_ref, gv_ref, rep_ref, out_ref,
+    layers, s_in_ref, ints_ref, vec_ref, hb_ref, w_ref, head_ref, latents_ref, ds_ref, gv_ref, rep_ref, out_ref,
     wh_ref, wg_ref, s_ref, act_ref, n_ref, slope_ref, r_ref, low_ref, da_ref, turned_ref, dlog_ref, gw_ref, gh_ref, loss_ref, *chunk_refs,
 ):
     blocks = layers - SPLIT
@@ -463,7 +469,7 @@
         turned_ref[0:WIDTH, TILE:] = jnp.zeros_like(turned_ref[0:WIDTH, TILE:])
         dlog_ref[TILE:, :] = jnp.zeros_like(dlog_ref[TILE:, :])
         for k in range(3):
-            wh_ref[:, k * WIDTH:(k + 1) * WIDTH] = w_ref[blocks + k]
+            wh_ref[:, k * WIDTH:(k + 1) * WIDTH] = w_ref[blocks + k] if k < 2 else head_ref[...]
         columns = vec_ref[...].T
 
         def scale(i, carry):
@@ -574,6 +580,11 @@
         high, low = split_low(jnp.concatenate([gv_ref[...], jnp.zeros((64 - gv_ref.shape[0], WIDTH), F32)], axis=0))
         wide = jnp.concatenate([high, low], axis=0).astype(F32).T
         cut_vectors(out_ref, (SPLIT + 1) * WIDTH // out_ref.shape[0], wide)
+
+
+def shifted_eye(rows, columns, shift):
+    row = lax.broadcasted_iota(jnp.int32, (rows, columns), 0)
+    return jnp.where(row + shift == lax.broadcasted_iota(jnp.int32, (rows, columns), 1), 1.0, 0.0).astype(BF16)
 
 
 def pack_kernel(
@@ -589,8 +600,11 @@
         rows = rows[None] if len(ref.shape) == 1 else rows
         vec_ref[at:at + rows.shape[0], 0:shard] = rows
         at += rows.shape[0]
-    vectors = vec_ref[...].T[0:shard, :]
-    vectors = jnp.concatenate([vectors, jnp.zeros_like(vectors)], axis=1).astype(BF16)
+    vectors = vec_ref[0:128, :].T[0:shard, :]
+    vec_ref[...] = jnp.zeros_like(vec_ref)
+    vec_ref[0:shard, 0:nq - 2 * WIDTH] = value_ref[:, 2 * WIDTH:].astype(F32)
+    tail = vec_ref[0:shard, 0:128] + mm(chance_ref[...], shifted_eye(nc, 128, 128 - nc))
+    vectors = jnp.concatenate([vectors, tail], axis=1).astype(BF16)
     entries = [lambda: vectors, lambda: stem_ref[...]] + [functools.partial(block_ref.__getitem__, i) for i in range(SPLIT)]
     half = len(entries) // fronts
     for core in range(fronts):
@@ -603,21 +617,18 @@
     for i in range(SPLIT, layers):
         back_ref[i - SPLIT] = block_ref[i]
     at = layers - SPLIT
-    back_ref[at:] = jnp.zeros_like(back_ref[at:])
-    for k in range(3):
-        width = min(WIDTH, nq - k * WIDTH)
-        back_ref[at + k, :, 0:width] = value_ref[:, k * WIDTH:k * WIDTH + width]
-    back_ref[at + 2, :, 128:128 + nc] = chance_ref[...]
-
-
-def outputs_kernel(latents_ref, d_pre_ref, w_ref, hb_ref, stem_ref, value_ref, chance_ref, lgrad_ref, turned_ref, bias_ref):
+    for k in range(2):
+        back_ref[at + k] = value_ref[:, k * WIDTH:(k + 1) * WIDTH]
+
+
+def outputs_kernel(latents_ref, d_pre_ref, w_ref, head_ref, hb_ref, stem_ref, value_ref, chance_ref, lgrad_ref, turned_ref, bias_ref):
     count = turned_ref.shape[0] // WIDTH
 
     @pl.when(pl.program_id(0) == 0)
     def _():
-        at = w_ref.shape[0] - count
+        at = w_ref.shape[0] - 2
         for k in range(count):
-            turned_ref[k * WIDTH:(k + 1) * WIDTH, :] = w_ref[at + k].T
+            turned_ref[k * WIDTH:(k + 1) * WIDTH, :] = (w_ref[at + k] if k < 2 else head_ref[...]).T
         columns = jnp.broadcast_to(hb_ref[...].astype(F32), (8, count * WIDTH)).T
         bias_ref[...] = jnp.broadcast_to(columns[:, 0:1], bias_ref.shape)
 
@@ -770,8 +781,8 @@
         functools.partial(pack_kernel, fronts),
         in_specs=[SMEM] + [VMEM] * 11,
         out_specs=[VMEM] * 2,
-        out_shape=[struct((pieces, n_front * shard, WIDTH), BF16), struct((layers - SPLIT + 3, shard, WIDTH), BF16)],
-        scratch_shapes=[pltpu.VMEM((128, max(shard, 128)), F32)],
+        out_shape=[struct((pieces, n_front * shard, WIDTH), BF16), struct((layers - SPLIT + 2, shard, WIDTH), BF16)],
+        scratch_shapes=[pltpu.VMEM((max(shard, 128), max(shard, 128)), F32)],
         name="pack",
     )(
         core, stem_weight, action_table, stem_bias, stem_gain, stem_shift, block_weight, block_gain, block_shift, block_bias,
@@ -801,12 +812,12 @@
     kept = [scratch((x.shape[0], TILE, x.shape[2]), x.dtype) for x in saved] + [pltpu.SemaphoreType.DMA((SPLIT + 1, 4))]
     stream = struct((padded, WIDTH), F32)
     front_shape = (2 + SPLIT, WIDTH, WIDTH)
-    *held, s_mid, vec = pl.pallas_call(
-        functools.partial(first_kernel, layers, rows_dev, fronts),
+    *held, s_mid, vec, w_head = pl.pallas_call(
+        functools.partial(first_kernel, layers, rows_dev, fronts, nq, nc),
         grid=(steps,),
         in_specs=[SMEM, tiled((rows_dev, WIDTH), 0), ints_spec] + [once(x.shape) for x in w_fronts],
-        out_specs=[ANY] * 4 + [tiled(stream.shape, 0), whole((128, WIDTH))],
-        out_shape=saved + [stream, struct((128, WIDTH), F32)],
+        out_specs=[ANY] * 4 + [tiled(stream.shape, 0), whole((128, WIDTH)), whole((WIDTH, WIDTH))],
+        out_shape=saved + [stream, struct((128, WIDTH), F32), struct((WIDTH, WIDTH), BF16)],
         scratch_shapes=[
             scratch(front_shape, BF16), scratch((TILE, WIDTH), BF16), scratch((TILE, 16), BF16), scratch((CHUNK, WIDTH), F32),
             scratch((TILE + CHUNK, WIDTH), F32),
@@ -823,7 +834,8 @@
     latents, ds_mid, gv_mid, rep, parts_mid = pl.pallas_call(
         functools.partial(middle_kernel, layers),
         grid=(steps,),
-        in_specs=[tiled(stream.shape, 0), ints_spec, once(vec.shape), once(head_bias.shape), once(w_back.shape)],
+        in_specs=[tiled(stream.shape, 0), ints_spec, once(vec.shape), once(head_bias.shape), once(w_back.shape),
+            once(w_head.shape)],
         out_specs=[
             tiled((rows_dev, WIDTH), 0), tiled(stream.shape, 0), whole((48, WIDTH)), whole((8, WIDTH)), whole(mid_shape),
         ],
@@ -854,7 +866,7 @@
         compiler_params=params(62),
         cost_estimate=pl.CostEstimate(flops=rows_dev * WIDTH * WIDTH * 600, bytes_accessed=40 << 20, transcendentals=0),
         name="middle",
-    )(s_mid, ints, vec, head_bias, w_back)
+    )(s_mid, ints, vec, head_bias, w_back, w_head)
 
     d_pre, parts_end, w_stem = pl.pallas_call(
         functools.partial(last_kernel, layers, rows_dev, fronts),
@@ -885,14 +897,14 @@
             outputs_kernel,
             grid=(steps,),
             in_specs=[tiled((rows_dev, WIDTH), 0), tiled((padded, WIDTH), 0)]
-            + [once(x.shape) for x in (w_back, head_bias, w_stem)],
+            + [once(x.shape) for x in (w_back, w_head, head_bias, w_stem)],
             out_specs=[tiled((nq, rows_dev), 1), tiled((nc, rows_dev), 1), tiled((rows_dev, WIDTH), 0)],
             out_shape=[struct((nq, rows_dev), BF16), struct((nc, rows_dev), BF16), struct((rows_dev, WIDTH), BF16)],
             scratch_shapes=[scratch((3 * WIDTH, WIDTH), BF16), scratch((3 * WIDTH, 128), F32)],
             compiler_params=params(48),
             cost_estimate=pl.CostEstimate(flops=rows_dev * WIDTH * WIDTH * 20, bytes_accessed=16 << 20, transcendentals=0),
             name="outputs",
-        )(states, d_pre, w_back, head_bias, w_stem)
+        )(states, d_pre, w_back, w_head, head_bias, w_stem)
 
     if fast:
         got_mid = lax.all_to_all(parts_mid, "fsdp", 0, 0)

time: 237 us -> 237 us (level)
    unnamed x26 -> x28, local copies, waits for them, and re-layouts: 5.63 us -> 5.6 us
where the time goes in v8:
time: 237 us
  Pallas kernels  175 us (74%)
  starting transfers between devices  21.2 us (9%)
  waiting for transfers between devices  15.6 us (7%)
  between operations  14.2 us (6%)
  local copies, waits for them, and re-layouts  9.9 us (4%)
    pallas_call x1, Pallas kernels, per_device(): pl.pallas_call(functools.partial(middle_kernel, layers), grid=(steps,), i...  87.9 us
    pallas_call x1, Pallas kernels, per_device(): pl.pallas_call(functools.partial(first_kernel, layers, rows_dev, fronts,...  37 us
    pallas_call x1, Pallas kernels, per_device(): pl.pallas_call(functools.partial(last_kernel, layers, rows_dev, fronts),...  32 us
    pallas_call x1, Pallas kernels, outputs_of(): pl.pallas_call(outputs_kernel, grid=(steps,), in_specs=[tiled((rows_dev,...  9.87 us
    all_to_all x1, starting transfers between devices, per_device(): w_fronts = [lax.all_to_all(front, 'fsdp', 0, 0)]  7.25 us
    all_to_all x1, waiting for transfers between devices, per_device(): w_fronts = [lax.all_to_all(front, 'fsdp', 0, 0)]  6.45 us
    all_to_all x1, starting transfers between devices, per_device(): got_end = lax.all_to_all(parts_end, 'fsdp', 0, 0)  5.92 us
    unnamed x28, local copies, waits for them, and re-layouts  5.6 us
  transfers between devices with their start and end apart: 11, of which 6 were waited for; matrix products, arithmetic and copies ran while one was open for 2% of the time, Pallas kernels for 35%

profile of v8, /device:TPU:0, one launch (start us, length us, event | category | flops | bytes accessed | tf_op | source)
XLA Modules:
  0.0 236.6 jit_solution(387679953049591482)
XLA Ops:
  7.2 1.9 pack.1
  9.1 7.3 %all-to-all-start = ((bf16[8,96,256]{2,1,0:T(8,128)(2,1)}), bf16[8,96,256]{2,1,0:T(8,128)(2,1)S(1)}, u32[]{:S(2)}, u32[]{:S(2)}) async-start(bf16[8,96,256]{2,1,0:T(8,128)(2,1)} %get-tuple-element.61), calls=%async_computation | async-start | bytes 786432 | tf_op jit(solution)/shard_map/all_to_all | solution.py:795
  16.3 0.0 all-gather.2.cloned.1.call-start
  16.4 0.8 pad_maximum_fusion
  17.2 0.6 broadcast_in_dim.11.hb_ref
  17.8 0.8 stack.15
  18.5 0.8 stack.16
  19.3 0.8 stack.17
  20.0 0.8 stack.18
  20.8 0.1 pad_add_fusion
  20.9 0.7 pad.4.ints_ref
  21.6 6.4 %all-to-all-done.refs_0_ = bf16[8,96,256]{2,1,0:T(8,128)(2,1)S(1)} async-done(((bf16[8,96,256]{2,1,0:T(8,128)(2,1)}), bf16[8,96,256]{2,1,0:T(8,128)(2,1)S(1)}, u32[]{:S(2)}, u32[]{:S(2)}) %all-to-all-start) | async-done | bytes 393248 | tf_op jit(solution)/shard_map/all_to_all | solution.py:795
  28.0 0.0 copy-start.6
  28.0 0.0 collective-permute-start
  28.0 0.0 all-gather.2.cloned.1.call-update
  28.1 1.7 collective-permute-done.refs_1_
  29.8 0.0 copy-done.6
  29.8 0.0 copy-start.13
  29.8 0.7 copy-done.13
  30.5 37.0 %first.1 = (bf16[5,5760,256]{2,1,0:T(8,128)(2,1)}, bf16[5,5760,256]{2,1,0:T(8,128)(2,1)}, f32[5,5760,128]{2,1,0:T(8,128)}, bf16[4,5760,256]{2,1,0:T(8,128)(2,1)}...) custom-call(s32[1]{0:T(128)} %bitcast.core_ref, bf16[5696,256]{1,0:T(8,128)(2,1)} %latent_ref.3, ...), custom_call_target="tpu_custom_call" | custom-call | flops 74658611200 | bytes 62914560 | tf_op jit(solution)/shard_map/first/pallas_call | solution.py:815
  67.5 0.1 all-gather.2.cloned.1.call-done.w_ref
  67.6 87.9 %middle.1 = (bf16[5696,256]{1,0:T(8,128)(2,1)}, f32[5760,256]{1,0:T(8,128)}, f32[48,256]{1,0:T(8,128)}, f32[8,256]{1,0:T(8,128)}, bf16[8,304,256]{2,1,0:T(8,128)(2,1)}) custom-call(f32[5760,256]{1,0:T(8,128)} %get-tuple-element.64.s_in_ref, s32[8,5760]{1,0:T(8,128)} %pad.4.ints_ref, f32[128,256]{1,0:T(8,128)} %get-tuple-element.65.vec_ref, ...), custom_call_target="tpu_custom_call" | custom-call | flops 223975833600 | bytes 41943040 | tf_op jit(solution)/shard_map/middle/pallas_call | solution.py:834
  155.5 4.3 %all-to-all-start.1 = ((bf16[8,304,256]{2,1,0:T(8,128)(2,1)}), bf16[8,304,256]{2,1,0:T(8,128)(2,1)}, u32[]{:S(2)}, u32[]{:S(2)}) async-start(bf16[8,304,256]{2,1,0:T(8,128)(2,1)} %get-tuple-element.77), calls=%async_computation.1 | async-start | bytes 2490368 | tf_op jit(solution)/shard_map/all_to_all | solution.py:910
  159.8 0.0 copy-start
  159.8 0.0 copy-start.1
  159.8 0.0 copy-start.3
  159.8 32.0 %last.1 = (bf16[5760,256]{1,0:T(8,128)(2,1)}, bf16[8,176,256]{2,1,0:T(8,128)(2,1)}, bf16[256,256]{1,0:T(8,128)(2,1)}) custom-call(s32[1]{0:T(128)} %bitcast.core_ref, bf16[5696,256]{1,0:T(8,128)(2,1)} %latent_ref.3, s32[8,5760]{1,0:T(8,128)} %pad.4.ints_ref, f32[5760,256]{1,0:T(8,128)} %get-tuple-element.70.ds_in_ref, ...), custom_call_target="tpu_custom_call" | custom-call | flops 55993958400 | bytes 62914560 | tf_op jit(solution)/shard_map/last/pallas_call | solution.py:871
  191.8 0.0 all-to-all-done.1.in_ref
  191.8 5.9 %all-to-all-start.2 = ((bf16[8,176,256]{2,1,0:T(8,128)(2,1)}), bf16[8,176,256]{2,1,0:T(8,128)(2,1)S(1)}, u32[]{:S(2)}, u32[]{:S(2)}) async-start(bf16[8,176,256]{2,1,0:T(8,128)(2,1)} %get-tuple-element.78), calls=%async_computation.2 | async-start | bytes 1441792 | tf_op jit(solution)/shard_map/all_to_all | solution.py:912
  197.7 2.1 sum_mid.1.refs_0_
  199.8 0.6 collective-permute-start.3
  200.5 0.9 collective-permute-start.2
  201.3 0.4 collective-permute-start.1
  201.7 0.0 copy-done
  201.7 0.0 copy-done.1
  201.7 0.0 copy-done.3
  201.7 1.8 copy-done.2
  203.5 0.0 copy-start.4
  203.5 0.9 copy-done.4
  204.4 9.9 %outputs.1 = (bf16[601,5696]{1,0:T(8,128)(2,1)}, bf16[32,5696]{1,0:T(8,128)(2,1)}, bf16[5696,256]{1,0:T(8,128)(2,1)}) custom-call(bf16[5696,256]{1,0:T(8,128)(2,1)S(1)} %copy-done.2, bf16[5760,256]{1,0:T(8,128)(2,1)} %get-tuple-element.80.d_pre_ref, bf16[8,256,256]{2,1,0:T(8,128)(2,1)S(1)} %copy-done.1, bf16[256,256]{1,0:T(8,128)(2,1)S(1)} %copy-done.3, ...), custom_call_target="tpu_custom_call" | custom-call | flops 7465861120 | bytes 16777216 | tf_op jit(solution)/shard_map/outputs/pallas_call | solution.py:896
  214.3 2.1 all-to-all-done.2.in_ref
  216.4 0.0 copy-start.5
  216.4 0.9 copy-done.5
  217.3 1.9 sum_end.1.refs_4_
  219.2 0.0 collective-permute-start.6
  219.2 1.5 collective-permute-start.5
  220.7 0.0 collective-permute-done.3.refs_3_
  220.7 0.0 copy-start.7
  220.7 0.3 collective-permute-start.4
  221.1 0.0 collective-permute-done.2.refs_2_
  221.1 0.0 copy-start.8
  221.1 0.0 collective-permute-done.1.refs_1_
  221.1 0.0 copy-start.9
  221.1 3.2 %collective-permute-done.6.refs_7_ = bf16[176,256]{1,0:T(8,128)(2,1)S(1)} collective-permute-done((bf16[176,256]{1,0:T(8,128)(2,1)}, bf16[176,256]{1,0:T(8,128)(2,1)S(1)}, u32[]{:S(2)}, u32[]{:S(2)}) %collective-permute-start.6) | collective-permute-done | bytes 90144 | tf_op jit(solution)/shard_map/ppermute | solution.py:760
  224.3 0.0 copy-start.10
  224.3 2.0 collective-permute-done.5.refs_6_
  226.3 0.0 collective-permute-done.4.refs_5_
  226.3 0.0 copy-done.7
  226.3 0.0 copy-done.8
  226.3 0.0 copy-done.9
  226.3 0.0 copy-done.10
  226.3 0.6 copy-done.11
  226.9 0.6 copy-done.12
  227.5 2.2 finish.1
  (5 shorter events, 0.0 us)
Async XLA Ops:
  9.1 19.0 %all-to-all-start = ((bf16[8,96,256]{2,1,0:T(8,128)(2,1)}), bf16[8,96,256]{2,1,0:T(8,128)(2,1)S(1)}, u32[]{:S(2)}, u32[]{:S(2)}) async-start(bf16[8,96,256]{2,1,0:T(8,128)(2,1)} %get-tuple-element.61), calls=%async_computation | async-start | bytes 786432 | tf_op jit(solution)/shard_map/all_to_all | solution.py:795
  16.3 51.3 %all-gather.2.cloned.1.call-start = ((), (), s32[]{:S(2)}) async-start(), calls=%async_computation.3 | async-start | bytes 1179648 | tf_op jit(solution)/shard_map/all_gather | solution.py:802
  28.0 1.7 copy-start.6
  28.0 1.7 collective-permute-start
  29.8 0.7 copy-start.13
  155.5 36.3 %all-to-all-start.1 = ((bf16[8,304,256]{2,1,0:T(8,128)(2,1)}), bf16[8,304,256]{2,1,0:T(8,128)(2,1)}, u32[]{:S(2)}, u32[]{:S(2)}) async-start(bf16[8,304,256]{2,1,0:T(8,128)(2,1)} %get-tuple-element.77), calls=%async_computation.1 | async-start | bytes 2490368 | tf_op jit(solution)/shard_map/all_to_all | solution.py:910
  159.8 41.9 %copy-start = (bf16[1,768]{1,0:T(2,128)(2,1)S(1)}, bf16[1,768]{1,0:T(2,128)(2,1)}, u32[]{:S(2)}) copy-start(bf16[1,768]{1,0:T(2,128)(2,1)} %broadcast_in_dim.11.hb_ref) | copy-start | bytes 4612
  159.8 41.9 %copy-start.1 = (bf16[8,256,256]{2,1,0:T(8,128)(2,1)S(1)}, bf16[8,256,256]{2,1,0:T(8,128)(2,1)}, u32[]{:S(2)}) copy-start(bf16[8,256,256]{2,1,0:T(8,128)(2,1)} %all-gather.2.cloned.1.call-done.w_ref) | copy-start | bytes 3145732
  159.8 41.9 %copy-start.3 = (bf16[256,256]{1,0:T(8,128)(2,1)S(1)}, bf16[256,256]{1,0:T(8,128)(2,1)}, u32[]{:S(2)}) copy-start(bf16[256,256]{1,0:T(8,128)(2,1)} %get-tuple-element.68.head_ref) | copy-start | bytes 393220
  191.8 24.6 %all-to-all-start.2 = ((bf16[8,176,256]{2,1,0:T(8,128)(2,1)}), bf16[8,176,256]{2,1,0:T(8,128)(2,1)S(1)}, u32[]{:S(2)}, u32[]{:S(2)}) async-start(bf16[8,176,256]{2,1,0:T(8,128)(2,1)} %get-tuple-element.78), calls=%async_computation.2 | async-start | bytes 1441792 | tf_op jit(solution)/shard_map/all_to_all | solution.py:912
  199.8 20.9 %collective-permute-start.3 = (bf16[304,256]{1,0:T(8,128)(2,1)}, bf16[304,256]{1,0:T(8,128)(2,1)S(1)}, u32[]{:S(2)}, u32[]{:S(2)}) collective-permute-start(bf16[304,256]{1,0:T(8,128)(2,1)} %sum_mid.1.refs_0_), channel_id=1, source_target_pairs={{0,24},{8,16},{16,8},{24,0},{1,25},{9,17},{17,9},{25,1},{2,26},{10... | collective-permute-start | bytes 466952 | tf_op jit(solution)/shard_map/ppermute | solution.py:760
  200.5 20.6 %collective-permute-start.2 = (bf16[304,256]{1,0:T(8,128)(2,1)}, bf16[304,256]{1,0:T(8,128)(2,1)S(1)}, u32[]{:S(2)}, u32[]{:S(2)}) collective-permute-start(bf16[304,256]{1,0:T(8,128)(2,1)} %sum_mid.1.refs_0_), channel_id=1, source_target_pairs={{0,16},{8,24},{16,0},{24,8},{1,17},{9,25},{17,1},{25,9},{2,18},{10... | collective-permute-start | bytes 466952 | tf_op jit(solution)/shard_map/ppermute | solution.py:760
  201.3 19.8 %collective-permute-start.1 = (bf16[304,256]{1,0:T(8,128)(2,1)}, bf16[304,256]{1,0:T(8,128)(2,1)S(1)}, u32[]{:S(2)}, u32[]{:S(2)}) collective-permute-start(bf16[304,256]{1,0:T(8,128)(2,1)} %sum_mid.1.refs_0_), channel_id=1, source_target_pairs={{0,8},{8,0},{16,24},{24,16},{1,9},{9,1},{17,25},{25,17},{2,10},{10... | collective-permute-start | bytes 466952 | tf_op jit(solution)/shard_map/ppermute | solution.py:760
  201.7 1.8 copy-start.2
  203.5 0.9 copy-start.4
  216.4 0.9 copy-start.5
  219.2 5.1 %collective-permute-start.6 = (bf16[176,256]{1,0:T(8,128)(2,1)}, bf16[176,256]{1,0:T(8,128)(2,1)S(1)}, u32[]{:S(2)}, u32[]{:S(2)}) collective-permute-start(bf16[176,256]{1,0:T(8,128)(2,1)} %sum_end.1.refs_4_), channel_id=1, source_target_pairs={{0,24},{8,16},{16,8},{24,0},{1,25},{9,17},{17,9},{25,1},{2,26},{10... | collective-permute-start | bytes 270344 | tf_op jit(solution)/shard_map/ppermute | solution.py:760
  219.2 7.1 %collective-permute-start.5 = (bf16[176,256]{1,0:T(8,128)(2,1)}, bf16[176,256]{1,0:T(8,128)(2,1)S(1)}, u32[]{:S(2)}, u32[]{:S(2)}) collective-permute-start(bf16[176,256]{1,0:T(8,128)(2,1)} %sum_end.1.refs_4_), channel_id=1, source_target_pairs={{0,16},{8,24},{16,0},{24,8},{1,17},{9,25},{17,1},{25,9},{2,18},{10... | collective-permute-start | bytes 270344 | tf_op jit(solution)/shard_map/ppermute | solution.py:760
  220.7 5.5 %copy-start.7 = (bf16[304,256]{1,0:T(8,128)(2,1)}, bf16[304,256]{1,0:T(8,128)(2,1)S(1)}, u32[]{:S(2)}) copy-start(bf16[304,256]{1,0:T(8,128)(2,1)S(1)} %collective-permute-done.3.refs_3_) | copy-start | bytes 466948
  220.7 5.5 %collective-permute-start.4 = (bf16[176,256]{1,0:T(8,128)(2,1)}, bf16[176,256]{1,0:T(8,128)(2,1)S(1)}, u32[]{:S(2)}, u32[]{:S(2)}) collective-permute-start(bf16[176,256]{1,0:T(8,128)(2,1)} %sum_end.1.refs_4_), channel_id=1, source_target_pairs={{0,8},{8,0},{16,24},{24,16},{1,9},{9,1},{17,25},{25,17},{2,10},{10... | collective-permute-start | bytes 270344 | tf_op jit(solution)/shard_map/ppermute | solution.py:760
  221.1 5.2 %copy-start.8 = (bf16[304,256]{1,0:T(8,128)(2,1)}, bf16[304,256]{1,0:T(8,128)(2,1)S(1)}, u32[]{:S(2)}) copy-start(bf16[304,256]{1,0:T(8,128)(2,1)S(1)} %collective-permute-done.2.refs_2_) | copy-start | bytes 466948
  221.1 5.2 %copy-start.9 = (bf16[304,256]{1,0:T(8,128)(2,1)}, bf16[304,256]{1,0:T(8,128)(2,1)S(1)}, u32[]{:S(2)}) copy-start(bf16[304,256]{1,0:T(8,128)(2,1)S(1)} %collective-permute-done.1.refs_1_) | copy-start | bytes 466948
  224.3 2.0 copy-start.10
  226.3 0.6 copy-start.11
  226.9 0.6 copy-start.12
Sparse Core Ops, SparseCore 0:
  28.2 39.3 all-gather.1

commit v9 on v8

--- a/solution.py
+++ b/solution.py
@@ -757,7 +757,7 @@
 
 
 def exchange(x, axis, size):
-    return [lax.ppermute(x, axis, [(i, i ^ k) for i in range(size)]) for k in range(1, size)]
+    return [lax.ppermute(x, axis, [(i, i ^ k) for i in range(size)]) for k in reversed(range(1, size))]
 
 
 def per_device(

time: 237 us -> 237 us (level)
  no operation moved by 1% of the time
where the time goes in v9:
time: 237 us; the launch traced here: 236 us
  Pallas kernels  175 us (74%)
  starting transfers between devices  21.2 us (9%)
  waiting for transfers between devices  15.3 us (6%)
  between operations  14.3 us (6%)
  local copies, waits for them, and re-layouts  9.31 us (4%)
    pallas_call x1, Pallas kernels, per_device(): pl.pallas_call(functools.partial(middle_kernel, layers), grid=(steps,), i...  87.9 us
    pallas_call x1, Pallas kernels, per_device(): pl.pallas_call(functools.partial(first_kernel, layers, rows_dev, fronts,...  37 us
    pallas_call x1, Pallas kernels, per_device(): pl.pallas_call(functools.partial(last_kernel, layers, rows_dev, fronts),...  32 us
    pallas_call x1, Pallas kernels, outputs_of(): pl.pallas_call(outputs_kernel, grid=(steps,), in_specs=[tiled((rows_dev,...  9.87 us
    all_to_all x1, starting transfers between devices, per_device(): w_fronts = [lax.all_to_all(front, 'fsdp', 0, 0)]  7.25 us
    all_to_all x1, waiting for transfers between devices, per_device(): w_fronts = [lax.all_to_all(front, 'fsdp', 0, 0)]  6.45 us
    all_to_all x1, starting transfers between devices, per_device(): got_end = lax.all_to_all(parts_end, 'fsdp', 0, 0)  5.92 us
    unnamed x28, local copies, waits for them, and re-layouts  5 us
  transfers between devices with their start and end apart: 11, of which 6 were waited for; matrix products, arithmetic and copies ran while one was open for 2% of the time, Pallas kernels for 35%

profile of v9, /device:TPU:0, one launch (start us, length us, event | category | flops | bytes accessed | tf_op | source)
XLA Modules:
  0.0 235.7 jit_solution(7002176592652409283)
XLA Ops:
  7.2 1.9 pack.1
  9.1 7.3 %all-to-all-start = ((bf16[8,96,256]{2,1,0:T(8,128)(2,1)}), bf16[8,96,256]{2,1,0:T(8,128)(2,1)S(1)}, u32[]{:S(2)}, u32[]{:S(2)}) async-start(bf16[8,96,256]{2,1,0:T(8,128)(2,1)} %get-tuple-element.61), calls=%async_computation | async-start | bytes 786432 | tf_op jit(solution)/shard_map/all_to_all | solution.py:795
  16.3 0.0 all-gather.2.cloned.1.call-start
  16.4 0.8 pad_maximum_fusion
  17.2 0.6 broadcast_in_dim.11.hb_ref
  17.8 0.8 stack.15
  18.5 0.8 stack.16
  19.3 0.8 stack.17
  20.0 0.8 stack.18
  20.8 0.1 pad_add_fusion
  20.9 0.7 pad.4.ints_ref
  21.6 6.4 %all-to-all-done.refs_0_ = bf16[8,96,256]{2,1,0:T(8,128)(2,1)S(1)} async-done(((bf16[8,96,256]{2,1,0:T(8,128)(2,1)}), bf16[8,96,256]{2,1,0:T(8,128)(2,1)S(1)}, u32[]{:S(2)}, u32[]{:S(2)}) %all-to-all-start) | async-done | bytes 393248 | tf_op jit(solution)/shard_map/all_to_all | solution.py:795
  28.0 0.0 copy-start.6
  28.0 0.0 collective-permute-start
  28.0 0.0 all-gather.2.cloned.1.call-update
  28.1 1.7 collective-permute-done.refs_1_
  29.8 0.0 copy-done.6
  29.8 0.0 copy-start.13
  29.8 0.7 copy-done.13
  30.5 37.0 %first.1 = (bf16[5,5760,256]{2,1,0:T(8,128)(2,1)}, bf16[5,5760,256]{2,1,0:T(8,128)(2,1)}, f32[5,5760,128]{2,1,0:T(8,128)}, bf16[4,5760,256]{2,1,0:T(8,128)(2,1)}...) custom-call(s32[1]{0:T(128)} %bitcast.core_ref, bf16[5696,256]{1,0:T(8,128)(2,1)} %latent_ref.3, ...), custom_call_target="tpu_custom_call" | custom-call | flops 74658611200 | bytes 62914560 | tf_op jit(solution)/shard_map/first/pallas_call | solution.py:815
  67.5 0.1 all-gather.2.cloned.1.call-done.w_ref
  67.6 87.9 %middle.1 = (bf16[5696,256]{1,0:T(8,128)(2,1)}, f32[5760,256]{1,0:T(8,128)}, f32[48,256]{1,0:T(8,128)}, f32[8,256]{1,0:T(8,128)}, bf16[8,304,256]{2,1,0:T(8,128)(2,1)}) custom-call(f32[5760,256]{1,0:T(8,128)} %get-tuple-element.64.s_in_ref, s32[8,5760]{1,0:T(8,128)} %pad.4.ints_ref, f32[128,256]{1,0:T(8,128)} %get-tuple-element.65.vec_ref, ...), custom_call_target="tpu_custom_call" | custom-call | flops 223975833600 | bytes 41943040 | tf_op jit(solution)/shard_map/middle/pallas_call | solution.py:834
  155.5 4.3 %all-to-all-start.1 = ((bf16[8,304,256]{2,1,0:T(8,128)(2,1)}), bf16[8,304,256]{2,1,0:T(8,128)(2,1)}, u32[]{:S(2)}, u32[]{:S(2)}) async-start(bf16[8,304,256]{2,1,0:T(8,128)(2,1)} %get-tuple-element.77), calls=%async_computation.1 | async-start | bytes 2490368 | tf_op jit(solution)/shard_map/all_to_all | solution.py:910
  159.8 0.0 copy-start
  159.8 0.0 copy-start.1
  159.8 0.0 copy-start.3
  159.8 32.0 %last.1 = (bf16[5760,256]{1,0:T(8,128)(2,1)}, bf16[8,176,256]{2,1,0:T(8,128)(2,1)}, bf16[256,256]{1,0:T(8,128)(2,1)}) custom-call(s32[1]{0:T(128)} %bitcast.core_ref, bf16[5696,256]{1,0:T(8,128)(2,1)} %latent_ref.3, s32[8,5760]{1,0:T(8,128)} %pad.4.ints_ref, f32[5760,256]{1,0:T(8,128)} %get-tuple-element.70.ds_in_ref, ...), custom_call_target="tpu_custom_call" | custom-call | flops 55993958400 | bytes 62914560 | tf_op jit(solution)/shard_map/last/pallas_call | solution.py:871
  191.8 0.0 all-to-all-done.1.in_ref
  191.8 5.9 %all-to-all-start.2 = ((bf16[8,176,256]{2,1,0:T(8,128)(2,1)}), bf16[8,176,256]{2,1,0:T(8,128)(2,1)S(1)}, u32[]{:S(2)}, u32[]{:S(2)}) async-start(bf16[8,176,256]{2,1,0:T(8,128)(2,1)} %get-tuple-element.78), calls=%async_computation.2 | async-start | bytes 1441792 | tf_op jit(solution)/shard_map/all_to_all | solution.py:912
  197.7 2.1 sum_mid.1.refs_0_
  199.8 0.0 collective-permute-start.3
  199.8 1.5 collective-permute-start.2
  201.3 0.4 collective-permute-start.1
  201.7 0.0 copy-done
  201.7 0.0 copy-done.1
  201.7 0.0 copy-done.3
  201.7 0.0 copy-start.2
  201.7 1.8 copy-done.2
  203.5 0.0 copy-start.4
  203.5 0.9 copy-done.4
  204.4 9.9 %outputs.1 = (bf16[601,5696]{1,0:T(8,128)(2,1)}, bf16[32,5696]{1,0:T(8,128)(2,1)}, bf16[5696,256]{1,0:T(8,128)(2,1)}) custom-call(bf16[5696,256]{1,0:T(8,128)(2,1)S(1)} %copy-done.2, bf16[5760,256]{1,0:T(8,128)(2,1)} %get-tuple-element.80.d_pre_ref, bf16[8,256,256]{2,1,0:T(8,128)(2,1)S(1)} %copy-done.1, bf16[256,256]{1,0:T(8,128)(2,1)S(1)} %copy-done.3, ...), custom_call_target="tpu_custom_call" | custom-call | flops 7465861120 | bytes 16777216 | tf_op jit(solution)/shard_map/outputs/pallas_call | solution.py:896
  214.3 2.1 all-to-all-done.2.in_ref
  216.4 0.0 copy-start.5
  216.4 0.9 copy-done.5
  217.3 1.9 sum_end.1.refs_4_
  219.2 0.0 collective-permute-start.6
  219.2 1.5 collective-permute-start.5
  220.7 0.0 collective-permute-done.3.refs_3_
  220.7 0.4 collective-permute-start.4
  221.1 0.0 collective-permute-done.2.refs_2_
  221.1 0.0 collective-permute-done.1.refs_1_
  221.1 0.0 copy-start.9
  221.1 0.0 collective-permute-done.6.refs_7_
  221.1 0.0 copy-start.10
  221.1 3.7 %collective-permute-done.5.refs_6_ = bf16[176,256]{1,0:T(8,128)(2,1)S(1)} collective-permute-done((bf16[176,256]{1,0:T(8,128)(2,1)}, bf16[176,256]{1,0:T(8,128)(2,1)S(1)}, u32[]{:S(2)}, u32[]{:S(2)}) %collective-permute-start.5) | collective-permute-done | bytes 90144 | tf_op jit(solution)/shard_map/ppermute | solution.py:760
  224.8 1.2 collective-permute-done.4.refs_5_
  226.0 0.0 copy-done.7
  226.0 0.0 copy-done.8
  226.0 0.0 copy-done.9
  226.0 0.0 copy-done.10
  226.0 0.0 copy-done.11
  226.0 0.0 copy-start.12
  226.0 0.6 copy-done.12
  226.6 2.2 finish.1
  (5 shorter events, 0.0 us)
Async XLA Ops:
  9.1 19.0 %all-to-all-start = ((bf16[8,96,256]{2,1,0:T(8,128)(2,1)}), bf16[8,96,256]{2,1,0:T(8,128)(2,1)S(1)}, u32[]{:S(2)}, u32[]{:S(2)}) async-start(bf16[8,96,256]{2,1,0:T(8,128)(2,1)} %get-tuple-element.61), calls=%async_computation | async-start | bytes 786432 | tf_op jit(solution)/shard_map/all_to_all | solution.py:795
  16.3 51.3 %all-gather.2.cloned.1.call-start = ((), (), s32[]{:S(2)}) async-start(), calls=%async_computation.3 | async-start | bytes 1179648 | tf_op jit(solution)/shard_map/all_gather | solution.py:802
  28.0 1.7 copy-start.6
  28.0 1.7 collective-permute-start
  29.8 0.7 copy-start.13
  155.5 36.3 %all-to-all-start.1 = ((bf16[8,304,256]{2,1,0:T(8,128)(2,1)}), bf16[8,304,256]{2,1,0:T(8,128)(2,1)}, u32[]{:S(2)}, u32[]{:S(2)}) async-start(bf16[8,304,256]{2,1,0:T(8,128)(2,1)} %get-tuple-element.77), calls=%async_computation.1 | async-start | bytes 2490368 | tf_op jit(solution)/shard_map/all_to_all | solution.py:910
  159.8 41.9 %copy-start = (bf16[1,768]{1,0:T(2,128)(2,1)S(1)}, bf16[1,768]{1,0:T(2,128)(2,1)}, u32[]{:S(2)}) copy-start(bf16[1,768]{1,0:T(2,128)(2,1)} %broadcast_in_dim.11.hb_ref) | copy-start | bytes 4612
  159.8 41.9 %copy-start.1 = (bf16[8,256,256]{2,1,0:T(8,128)(2,1)S(1)}, bf16[8,256,256]{2,1,0:T(8,128)(2,1)}, u32[]{:S(2)}) copy-start(bf16[8,256,256]{2,1,0:T(8,128)(2,1)} %all-gather.2.cloned.1.call-done.w_ref) | copy-start | bytes 3145732
  159.8 41.9 %copy-start.3 = (bf16[256,256]{1,0:T(8,128)(2,1)S(1)}, bf16[256,256]{1,0:T(8,128)(2,1)}, u32[]{:S(2)}) copy-start(bf16[256,256]{1,0:T(8,128)(2,1)} %get-tuple-element.68.head_ref) | copy-start | bytes 393220
  191.8 24.6 %all-to-all-start.2 = ((bf16[8,176,256]{2,1,0:T(8,128)(2,1)}), bf16[8,176,256]{2,1,0:T(8,128)(2,1)S(1)}, u32[]{:S(2)}, u32[]{:S(2)}) async-start(bf16[8,176,256]{2,1,0:T(8,128)(2,1)} %get-tuple-element.78), calls=%async_computation.2 | async-start | bytes 1441792 | tf_op jit(solution)/shard_map/all_to_all | solution.py:912
  199.8 20.9 %collective-permute-start.3 = (bf16[304,256]{1,0:T(8,128)(2,1)}, bf16[304,256]{1,0:T(8,128)(2,1)S(1)}, u32[]{:S(2)}, u32[]{:S(2)}) collective-permute-start(bf16[304,256]{1,0:T(8,128)(2,1)} %sum_mid.1.refs_0_), channel_id=1, source_target_pairs={{0,8},{8,0},{16,24},{24,16},{1,9},{9,1},{17,25},{25,17},{2,10},{10... | collective-permute-start | bytes 466952 | tf_op jit(solution)/shard_map/ppermute | solution.py:760
  199.8 21.2 %collective-permute-start.2 = (bf16[304,256]{1,0:T(8,128)(2,1)}, bf16[304,256]{1,0:T(8,128)(2,1)S(1)}, u32[]{:S(2)}, u32[]{:S(2)}) collective-permute-start(bf16[304,256]{1,0:T(8,128)(2,1)} %sum_mid.1.refs_0_), channel_id=1, source_target_pairs={{0,16},{8,24},{16,0},{24,8},{1,17},{9,25},{17,1},{25,9},{2,18},{10... | collective-permute-start | bytes 466952 | tf_op jit(solution)/shard_map/ppermute | solution.py:760
  201.3 19.8 %collective-permute-start.1 = (bf16[304,256]{1,0:T(8,128)(2,1)}, bf16[304,256]{1,0:T(8,128)(2,1)S(1)}, u32[]{:S(2)}, u32[]{:S(2)}) collective-permute-start(bf16[304,256]{1,0:T(8,128)(2,1)} %sum_mid.1.refs_0_), channel_id=1, source_target_pairs={{0,24},{8,16},{16,8},{24,0},{1,25},{9,17},{17,9},{25,1},{2,26},{10... | collective-permute-start | bytes 466952 | tf_op jit(solution)/shard_map/ppermute | solution.py:760
  201.7 1.8 copy-start.2
  203.5 0.9 copy-start.4
  216.4 0.9 copy-start.5
  219.2 1.9 collective-permute-start.6
  219.2 5.6 %collective-permute-start.5 = (bf16[176,256]{1,0:T(8,128)(2,1)}, bf16[176,256]{1,0:T(8,128)(2,1)S(1)}, u32[]{:S(2)}, u32[]{:S(2)}) collective-permute-start(bf16[176,256]{1,0:T(8,128)(2,1)} %sum_end.1.refs_4_), channel_id=1, source_target_pairs={{0,16},{8,24},{16,0},{24,8},{1,17},{9,25},{17,1},{25,9},{2,18},{10... | collective-permute-start | bytes 270344 | tf_op jit(solution)/shard_map/ppermute | solution.py:760
  220.7 5.3 %copy-start.7 = (bf16[304,256]{1,0:T(8,128)(2,1)}, bf16[304,256]{1,0:T(8,128)(2,1)S(1)}, u32[]{:S(2)}) copy-start(bf16[304,256]{1,0:T(8,128)(2,1)S(1)} %collective-permute-done.3.refs_3_) | copy-start | bytes 466948
  220.7 5.3 %collective-permute-start.4 = (bf16[176,256]{1,0:T(8,128)(2,1)}, bf16[176,256]{1,0:T(8,128)(2,1)S(1)}, u32[]{:S(2)}, u32[]{:S(2)}) collective-permute-start(bf16[176,256]{1,0:T(8,128)(2,1)} %sum_end.1.refs_4_), channel_id=1, source_target_pairs={{0,24},{8,16},{16,8},{24,0},{1,25},{9,17},{17,9},{25,1},{2,26},{10... | collective-permute-start | bytes 270344 | tf_op jit(solution)/shard_map/ppermute | solution.py:760
  221.1 4.9 %copy-start.8 = (bf16[304,256]{1,0:T(8,128)(2,1)}, bf16[304,256]{1,0:T(8,128)(2,1)S(1)}, u32[]{:S(2)}) copy-start(bf16[304,256]{1,0:T(8,128)(2,1)S(1)} %collective-permute-done.2.refs_2_) | copy-start | bytes 466948
  221.1 4.9 %copy-start.9 = (bf16[304,256]{1,0:T(8,128)(2,1)}, bf16[304,256]{1,0:T(8,128)(2,1)S(1)}, u32[]{:S(2)}) copy-start(bf16[304,256]{1,0:T(8,128)(2,1)S(1)} %collective-permute-done.1.refs_1_) | copy-start | bytes 466948
  221.1 4.9 %copy-start.10 = (bf16[176,256]{1,0:T(8,128)(2,1)}, bf16[176,256]{1,0:T(8,128)(2,1)S(1)}, u32[]{:S(2)}) copy-start(bf16[176,256]{1,0:T(8,128)(2,1)S(1)} %collective-permute-done.6.refs_7_) | copy-start | bytes 270340
  224.8 1.2 copy-start.11
  226.0 0.6 copy-start.12
Sparse Core Ops, SparseCore 0:
  28.2 39.3 all-gather.1
